TPU v7x, 32 devices: a whole 2x2x4 slice. The times are simulated.
32 devices in a mesh: seq: 16 (over z, x, core), head: 2 (over y).
Axes of the slice: x: 2, y: 2, z: 4, core: 2. Of those that a mesh axis runs over, the one named last changes fastest.
Arguments:
- tokens: bfloat16 [2048, 4096], P('seq', 'head')
- gain: float32 [4096], replicated, may hold values from 0.25 to 1.75
- w_query: bfloat16 [4096, 2048], P('seq', 'head'), may hold values from -0.09375 to 0.09375
- w_key: bfloat16 [4096, 2048], P('seq', 'head'), may hold values from -0.09375 to 0.09375
- w_value: bfloat16 [4096, 2048], P('seq', 'head'), may hold values from -0.09375 to 0.09375
- w_out: bfloat16 [2048, 4096], P('head', 'seq'), may hold values from -0.125 to 0.125
- mem_query: bfloat16 [128, 2048], P(None, 'head'), may hold values from -12 to 12
- score_scale: float32 [16], P('head'), may hold values from 1.5 to 4
- decay: float32 [16, 16], P('seq', 'head'), may hold values from 0 to 1, as said below
- seg_len: int32 [16], P('seq'), may hold values from 32 to 128, as said below
Outputs:
- branch: bfloat16 [2048, 4096], P('seq', 'head')
Inputs may be any that keep to these rules, and one draw needn't show every extreme that they name: `decay`: retention lies strictly between 0 and 1. `seg_len`: at least one segment is full and at least one holds exactly 32 valid tokens.
All inputs are finite; a program needn't handle non-finite values.
Results may differ from a plain program's by a relative error of at most 0.015.
Values may be sent and summed in bfloat16 or wider, within the bound.
No kernel may reach another device: no remote copies, remote signals or barrier semaphores. Data moves between devices by JAX's collectives and lax.ppermute only.
A program may use at most 64 MiB of HBM per device.

v0:
```python
import math

import jax
import jax.numpy as jnp
from jax import lax
from jax.sharding import PartitionSpec as P

DH = 128


def carried_in(part, axis, combine, identity):
    place = lax.axis_index(axis)
    gathered = jax.tree.map(lambda a: lax.all_gather(a, axis), part)
    state = jax.tree.map(lambda a, e: jnp.zeros_like(a) + jnp.asarray(e, a.dtype), part, identity)

    def one(lap, state):
        return combine(
            state, jax.tree.map(lambda a: lax.dynamic_index_in_dim(a, lap, 0, False), gathered)
        )

    return lax.fori_loop(0, place, one, state)


def body(tokens, gain, w_query, w_key, w_value, w_out, mem_query, score_scale, decay, seg_len):
    seg_rows, feat_local = tokens.shape
    col_local = w_query.shape[1]
    head_size = DH
    heads_local = col_local // head_size
    slot_count = mem_query.shape[0]
    valid_len = seg_len[0]
    inverse_root_scale = 1.0 / math.sqrt(head_size)
    score_bias = math.log(slot_count + seg_rows)
    whole = lax.all_gather(tokens, "head", axis=1, tiled=True)
    wide = whole.astype(jnp.float32)
    mean_squares = jnp.mean(wide * wide, axis=1, keepdims=True)
    normed = (wide * lax.rsqrt(mean_squares + 1e-05) * gain).astype(jnp.bfloat16)
    pieces = (
        lax.all_gather(w_query, "seq", axis=0, tiled=True),
        lax.all_gather(w_key, "seq", axis=0, tiled=True),
        lax.all_gather(w_value, "seq", axis=0, tiled=True),
    )
    query_sum, key_sum, value_sum = tuple(
        (jnp.dot(normed, piece, preferred_element_type=jnp.float32) for piece in pieces)
    )
    query_head_split = query_sum.astype(jnp.bfloat16).reshape(seg_rows, heads_local, head_size)
    key_head_split = key_sum.astype(jnp.bfloat16).reshape(seg_rows, heads_local, head_size)
    value_head_split = value_sum.astype(jnp.bfloat16).reshape(seg_rows, heads_local, head_size)
    positions = jnp.arange(seg_rows, dtype=jnp.int32)
    valid_keys = (positions < valid_len).astype(jnp.float32)
    memory_head_split = mem_query.reshape(slot_count, heads_local, head_size)
    memory_write_scores = (
        jnp.einsum(
            "bia,sia->ibs", memory_head_split, key_head_split, preferred_element_type=jnp.float32
        )
        * inverse_root_scale
    )
    memory_write_weights = (
        jax.nn.sigmoid(memory_write_scores - math.log(seg_rows)) * valid_keys[None, None, :]
    ).astype(jnp.bfloat16)
    memory_written_keys = jnp.einsum(
        "elz,zek->lek", memory_write_weights, key_head_split, preferred_element_type=jnp.float32
    )
    memory_written_values = jnp.einsum(
        "elz,zek->lek", memory_write_weights, value_head_split, preferred_element_type=jnp.float32
    )
    written = jnp.stack(
        [
            memory_written_keys.reshape(slot_count, col_local),
            memory_written_values.reshape(slot_count, col_local),
        ]
    )

    def combine_state(earlier, later):
        return (
            earlier[0] * later[0],
            jnp.repeat(later[0], head_size)[None, None, :] * earlier[1] + later[1],
        )

    retain = decay[0]
    identity = (jnp.ones_like(retain), jnp.zeros_like(written))
    _, memory_in = carried_in((retain, written), "seq", combine_state, identity)
    mem_split = memory_in.reshape(2, slot_count, heads_local, head_size)
    memory_unit_rows = (
        mem_split * lax.rsqrt(jnp.mean(jnp.square(mem_split), axis=3, keepdims=True) + 1e-06)
    ).astype(jnp.bfloat16)
    head_scale_factors = (score_scale * inverse_root_scale)[:, None, None]
    memory_score_matrix = (
        jnp.einsum(
            "zul,rul->uzr",
            query_head_split,
            memory_unit_rows[0],
            preferred_element_type=jnp.float32,
        )
        * head_scale_factors
    )
    tok_scores = (
        jnp.einsum(
            "thd,shd->hts", query_head_split, key_head_split, preferred_element_type=jnp.float32
        )
        * head_scale_factors
    )
    allowed = (positions[None, :] <= positions[:, None]).astype(jnp.float32) * valid_keys[None, :]
    memory_attention_weights = jax.nn.sigmoid(memory_score_matrix - score_bias).astype(jnp.bfloat16)
    token_attention_weights = (
        jax.nn.sigmoid(tok_scores - score_bias) * allowed[None, :, :]
    ).astype(jnp.bfloat16)
    attended_output = jnp.einsum(
        "krf,fku->rku",
        memory_attention_weights,
        memory_unit_rows[1],
        preferred_element_type=jnp.float32,
    )
    attended_output = attended_output + jnp.einsum(
        "ymo,oyl->myl",
        token_attention_weights,
        value_head_split,
        preferred_element_type=jnp.float32,
    )
    attended_output = (
        (attended_output * valid_keys[:, None, None])
        .astype(jnp.bfloat16)
        .reshape(seg_rows, col_local)
    )
    partial_rows = jnp.dot(
        attended_output,
        lax.all_gather(w_out, "seq", axis=1, tiled=True),
        preferred_element_type=jnp.float32,
    )
    branch = lax.psum_scatter(
        partial_rows.astype(jnp.bfloat16), "head", scatter_dimension=1, tiled=True
    )
    return branch


def solution(mesh):
    return jax.shard_map(
        body,
        mesh=mesh,
        in_specs=(
            P("seq", "head"),
            P(),
            P("seq", "head"),
            P("seq", "head"),
            P("seq", "head"),
            P("head", "seq"),
            P(None, "head"),
            P("head"),
            P("seq", "head"),
            P("seq"),
        ),
        out_specs=P("seq", "head"),
        check_vma=False,
    )
```

profile of v0, /device:TPU:0, one launch (start us, length us, event | category | flops | bytes accessed | tf_op | source)
XLA Modules:
  0.0 497.3 jit_solution(4196374657746008414)
XLA Ops:
  6.5 0.7 all-gather.9.cloned.1.call-update
  7.3 0.7 all-gather.11.cloned.1.call-update
  8.1 0.7 all-gather.13.cloned.1.call-update
  8.8 0.5 all-gather.15.cloned.1.call-update
  10.0 22.9 %all-gather.9.cloned.1.call-done = bf16[128,4096]{1,0:T(8,128)(2,1)} async-done(((bf16[128,2048]{1,0:T(8,128)(2,1)}), bf16[128,4096]{1,0:T(8,128)(2,1)}) %all-gather.9.cloned.1.call-update) | async-done | bytes 1048592 | tf_op jit(solution)/shard_map/all_gather | solution.py:33
  32.9 1.5 fusion
  34.5 75.5 %all-gather.11.cloned.1.call-done = bf16[4096,1024]{1,0:T(8,128)(2,1)} async-done(((bf16[256,1024]{1,0:T(8,128)(2,1)}), bf16[4096,1024]{1,0:T(8,128)(2,1)}) %all-gather.11.cloned.1.call-update) | async-done | bytes 8388624 | tf_op jit(solution)/shard_map/all_gather | solution.py:39
  110.0 5.0 %convolution_convert_fusion.3 = bf16[128,1024]{1,0:T(8,128)(2,1)S(1)} fusion(bf16[4096,1024]{1,0:T(8,128)(2,1)} %all-gather.11.cloned.1.call-done, bf16[128,4096]{1,0:T(8,128)(2,1)} %all-gather.9.cloned.1.call-done, f32[4096]{0:T(1024)} %param.13, f32[128]{0:T(128)S(1)} %add_rsqrt_fusion.1), kind=kOutput, calls=%fused_computation.37 | convolution fusion | flops 1075970048 | bytes 9716224 | tf_op jit(solution)/shard_map/dot_general | solution.py:43
  115.3 0.4 fusion.22
  116.1 69.3 %all-gather.13.cloned.1.call-done = bf16[4096,1024]{1,0:T(8,128)(2,1)} async-done(((bf16[256,1024]{1,0:T(8,128)(2,1)}), bf16[4096,1024]{1,0:T(8,128)(2,1)}) %all-gather.13.cloned.1.call-update) | async-done | bytes 8388624 | tf_op jit(solution)/shard_map/all_gather | solution.py:40
  185.4 4.7 convolution_convert_fusion.2
  190.2 0.2 fusion.53
  190.7 1.1 pad_maximum_fusion
  191.8 0.5 all-gather.17.cloned.1.call-update
  192.4 18.8 %all-gather.1 = f32[16,1,8]{2,1,0:T(1,128)S(1)} all-gather(f32[1,1,8]{2,1,0:T(1,128)S(1)} %bitcast.76), channel_id=1, replica_groups=mesh['seq'=16,'head'=2] {'seq'}, dimensions={0}, use_global_device_ids=true | all-gather | bytes 544 | tf_op jit(solution)/shard_map/all_gather | solution.py:13
  211.2 49.4 %all-gather.15.cloned.1.call-done = bf16[4096,1024]{1,0:T(8,128)(2,1)} async-done(((bf16[256,1024]{1,0:T(8,128)(2,1)}), bf16[4096,1024]{1,0:T(8,128)(2,1)}) %all-gather.15.cloned.1.call-update) | async-done | bytes 8388624 | tf_op jit(solution)/shard_map/all_gather | solution.py:38
  260.6 5.4 %fusion.25 = bf16[16,8,8,128]{3,2,1,0:T(8,128)(2,1)} fusion(bf16[4096,1024]{1,0:T(8,128)(2,1)} %all-gather.15.cloned.1.call-done, bf16[128,4096]{1,0:T(8,128)(2,1)S(1)} %copy-done.1, f32[4096]{0:T(1024)S(1)} %copy-done.3, f32[128]{0:T(128)S(1)} %add_rsqrt_fusion.1), kind=kOutput, calls=%fused_computation.38 | convolution fusion | flops 1075970048 | bytes 9716224 | tf_op jit(solution)/shard_map/dot_general | solution.py:43
  266.0 121.8 %all-gather.19.cloned.1.call-done = f32[32,128,1024]{2,1,0:T(8,128)} async-done(((f32[2,128,1024]{2,1,0:T(8,128)}), f32[32,128,1024]{2,1,0:T(8,128)}) %all-gather.19.cloned.1.call-update) | async-done | bytes 16777232 | tf_op jit(solution)/shard_map/all_gather | solution.py:13
  387.9 0.3 copy.28
  388.5 1.4 fusion.26
  389.9 1.5 fusion.24
  391.4 74.7 %all-gather.17.cloned.1.call-done = bf16[1024,4096]{1,0:T(8,128)(2,1)} async-done(((bf16[1024,256]{1,0:T(8,128)(2,1)}), bf16[1024,4096]{1,0:T(8,128)(2,1)}) %all-gather.17.cloned.1.call-update) | async-done | bytes 8388624 | tf_op jit(solution)/shard_map/all_gather | solution.py:126
  466.1 5.6 %convolution_convert_fusion = bf16[128,4096]{1,0:T(8,128)(2,1)} fusion(bf16[128,1024]{0,1:T(8,128)(2,1)S(1)} %bitcast.74, bf16[1024,4096]{1,0:T(8,128)(2,1)} %all-gather.17.cloned.1.call-done), kind=kOutput, calls=%fused_computation.3 | convolution fusion | flops 1074266112 | bytes 9699328 | tf_op jit(solution)/shard_map/dot_general | solution.py:124
  471.8 18.7 %reduce-scatter.2.cloned.1.call-done = bf16[128,2048]{1,0:T(8,128)(2,1)} async-done(((bf16[128,4096]{1,0:T(8,128)(2,1)}), bf16[128,2048]{1,0:T(8,128)(2,1)}) %reduce-scatter.2.cloned.1.call-update) | async-done | bytes 524304 | tf_op jit(solution)/shard_map/reduce_scatter | solution.py:129
  (33 shorter events, 1.6 us)
Async XLA Ops:
  6.5 108.7 %copy-start = (bf16[128,1024]{1,0:T(8,128)(2,1)S(1)}, bf16[128,1024]{1,0:T(8,128)(2,1)}, u32[]{:S(2)}) copy-start(bf16[128,1024]{1,0:T(8,128)(2,1)} %param.18) | copy-start | bytes 786436
  6.5 26.4 %all-gather.9.cloned.1.call-start = ((), (), s32[]{:S(2)}) async-start(), calls=%async_computation.1 | async-start | bytes 1572864 | tf_op jit(solution)/shard_map/all_gather | solution.py:33
  7.3 102.8 %all-gather.11.cloned.1.call-start = ((), (), s32[]{:S(2)}) async-start(), calls=%async_computation.2 | async-start | bytes 8912896 | tf_op jit(solution)/shard_map/all_gather | solution.py:39
  8.0 177.4 %all-gather.13.cloned.1.call-start = ((), (), s32[]{:S(2)}) async-start(), calls=%async_computation.3 | async-start | bytes 8912896 | tf_op jit(solution)/shard_map/all_gather | solution.py:40
  8.7 251.9 %all-gather.15.cloned.1.call-start = ((), (), s32[]{:S(2)}) async-start(), calls=%async_computation.4 | async-start | bytes 8912896 | tf_op jit(solution)/shard_map/all_gather | solution.py:38
  9.3 378.5 %all-gather.19.cloned.1.call-start = ((), (), s32[]{:S(2)}) async-start(), calls=%async_computation.7 | async-start | bytes 17825792 | tf_op jit(solution)/shard_map/all_gather | solution.py:13
  34.5 150.9 %copy-start.1 = (bf16[128,4096]{1,0:T(8,128)(2,1)S(1)}, bf16[128,4096]{1,0:T(8,128)(2,1)}, u32[]{:S(2)}) copy-start(bf16[128,4096]{1,0:T(8,128)(2,1)} %all-gather.9.cloned.1.call-done) | copy-start | bytes 3145732
  34.5 150.9 %copy-start.3 = (f32[4096]{0:T(1024)S(1)}, f32[4096]{0:T(1024)}, u32[]{:S(2)}) copy-start(f32[4096]{0:T(1024)} %param.13) | copy-start | bytes 49156
  116.1 76.3 %copy-start.2 = (f32[1,8]{1,0:T(1,128)S(1)}, f32[1,8]{1,0:T(1,128)}, u32[]{:S(2)}) copy-start(f32[1,8]{1,0:T(1,128)} %param.20) | copy-start | bytes 100
  116.1 95.2 %copy-start.4 = (f32[8]{0:T(128)S(1)}, f32[8]{0:T(128)}, u32[]{:S(2)}) copy-start(f32[8]{0:T(128)} %param.19) | copy-start | bytes 100
  191.8 274.3 %all-gather.17.cloned.1.call-start = ((), (), s32[]{:S(2)}) async-start(), calls=%async_computation.5 | async-start | bytes 8912896 | tf_op jit(solution)/shard_map/all_gather | solution.py:126
  192.4 298.1 %reduce-scatter.2.cloned.1.call-start = ((), (), s32[]{:S(2)}) async-start(), calls=%async_computation.6 | async-start | bytes 1572864 | tf_op jit(solution)/shard_map/reduce_scatter | solution.py:129
Sparse Core Ops, SparseCore 0:
  8.9 23.9 all-gather.8
  35.1 74.8 all-gather.10
  112.2 73.1 all-gather.12
  187.4 73.1 all-gather.14
  262.6 125.1 all-gather.18
  389.8 76.2 all-gather.16
  471.9 18.4 reduce-scatter.1
where the time goes:
time: 498 us; the launch traced here: 497 us
  waiting for transfers between devices  435 us (87%)
  matrix products  24.5 us (5%)
  blocking collectives  18.8 us (4%)
  between operations  14.3 us (3%)
    all_gather x1, waiting for transfers between devices, carried_in(): gathered = jax.tree.map(lambda a: lax.all_gather(a, axis), part)  122 us
    all_gather x1, waiting for transfers between devices, body(): lax.all_gather(w_key, 'seq', axis=0, tiled=True)  75.5 us
    all_gather x1, waiting for transfers between devices, body(): lax.all_gather(w_out, 'seq', axis=1, tiled=True)  74.7 us
    all_gather x1, waiting for transfers between devices, body(): lax.all_gather(w_value, 'seq', axis=0, tiled=True)  69.3 us
    all_gather x1, waiting for transfers between devices, body(): lax.all_gather(w_query, 'seq', axis=0, tiled=True)  49.4 us
    all_gather x1, waiting for transfers between devices, body(): whole = lax.all_gather(tokens, 'head', axis=1, tiled=True)  22.9 us
    all_gather x1, blocking collectives, carried_in(): gathered = jax.tree.map(lambda a: lax.all_gather(a, axis), part)  18.8 us
    reduce_scatter x1, waiting for transfers between devices, body(): lax.psum_scatter(partial_rows.astype(jnp.bfloat16), 'head', scatter_dimen...  18.7 us
  transfers between devices with their start and end apart: 7, of which 7 were waited for; matrix products, arithmetic and copies ran while one was open for 5% of the time, Pallas kernels for 0%

commit v1 on v0

v1 whole, which is shorter than its diff:
```python
import math

import jax
import jax.numpy as jnp
from jax import lax
from jax.sharding import PartitionSpec as P

DH = 128


def pick(a, i):
    return lax.dynamic_index_in_dim(a, i, 0, False)


def body(tokens, gain, w_query, w_key, w_value, w_out, mem_query, score_scale, decay, seg_len):
    n_seq = lax.axis_size("seq")
    n_head = lax.axis_size("head")
    seg_rows, feat_local = tokens.shape
    width = gain.shape[0]
    w_rows, col_local = w_query.shape
    heads = col_local // DH
    slots = mem_query.shape[0]
    cn = 2 if heads % 2 == 0 else 1
    zn = heads // cn
    xn = n_seq // heads
    place = lax.axis_index("seq")
    y = lax.axis_index("head")
    c = place % cn
    x = place // cn % xn
    z = place // (cn * xn)

    def split(s):
        return s // (cn * xn), s // cn % xn, s % cn

    def join(a, b, d):
        return (a * xn + b) * cn + d

    def over_z(a, j):
        pairs = [(s, join(split(s)[0] ^ j, *split(s)[1:])) for s in range(n_seq)]
        return lax.ppermute(a, "seq", pairs)

    def over_x(a, k):
        pairs = []
        for s in range(n_seq):
            sz, sx, sc = split(s)
            pairs.append((s, join(sz, (sx + k) % xn, sc)))
        return lax.ppermute(a, "seq", pairs)

    def over_c(a, m):
        pairs = [(s, s ^ m) for s in range(n_seq)]
        return lax.ppermute(a, "seq", pairs)

    def over_y(a, k):
        return lax.ppermute(a, "head", [(h, (h + k) % n_head) for h in range(n_head)])

    def gather_z(a):
        got = {0: a}
        bit = zn // 2
        while bit:
            for j in sorted(got):
                got[j | bit] = over_z(got[j], bit)
            bit //= 2
        return [got[j] for j in range(zn)]

    normed = []
    for part in gather_z(tokens):
        own = [part] + [over_y(part, k) for k in range(1, n_head)]
        rows = []
        for m in range(cn):
            full = jnp.zeros((seg_rows, width), tokens.dtype)
            for k, piece in enumerate(own):
                piece = over_c(piece, m) if m else piece
                full = lax.dynamic_update_slice(full, piece, (0, (y - k) % n_head * feat_local))
            rows.append(full)
        wide = jnp.concatenate(rows).astype(jnp.float32)
        mean_squares = jnp.mean(wide * wide, axis=1, keepdims=True)
        normed.append((wide * lax.rsqrt(mean_squares + 1e-05) * gain).astype(jnp.bfloat16))

    blocks = jnp.concatenate(
        [
            w.reshape(w_rows, heads, DH).transpose(1, 0, 2)
            for w in (w_query, w_key, w_value)
        ],
        axis=2,
    ).reshape(zn, cn, w_rows, 3 * DH)
    weight = jnp.zeros((zn, xn, cn, w_rows, 3 * DH), w_query.dtype)
    for j in range(zn):
        block = pick(blocks, z ^ j)
        block = over_z(block, j) if j else block
        pair = jnp.zeros((cn, w_rows, 3 * DH), w_query.dtype)
        for m in range(cn):
            piece = pick(block, c ^ m)
            piece = over_c(piece, m) if m else piece
            pair = lax.dynamic_update_slice(pair, piece[None], (c ^ m, 0, 0))
        for k in range(xn):
            got = over_x(pair, k) if k else pair
            weight = lax.dynamic_update_slice(
                weight, got[None, None], (z ^ j, (x - k) % xn, 0, 0, 0)
            )
    weight = weight.reshape(width, 3 * DH)

    meta = jnp.concatenate([decay, seg_len.astype(jnp.float32)[:, None]], axis=1)
    table = jnp.zeros((zn, xn, cn, heads + 1), jnp.float32)
    for j, by_z in enumerate(gather_z(meta)):
        for k in range(xn):
            by_x = over_x(by_z, k) if k else by_z
            for m in range(cn):
                got = over_c(by_x, m) if m else by_x
                table = lax.dynamic_update_slice(
                    table, got[None, None], (z ^ j, (x - k) % xn, c ^ m, 0)
                )
    head = z * cn + c
    retain = lax.dynamic_index_in_dim(table, head, 3, False)
    lens = lax.dynamic_index_in_dim(table[..., heads], x, 1, False)
    retain_own = lax.dynamic_index_in_dim(retain, x, 1, False)

    sums = jnp.stack(
        [
            jnp.dot(rows, weight, preferred_element_type=jnp.float32)
            .astype(jnp.bfloat16)
            .reshape(cn, seg_rows, 3 * DH)
            for rows in normed
        ]
    )
    order = [pick(sums, z ^ i) for i in range(zn)]
    sums = jnp.stack([jnp.stack([pick(o, c ^ i) for i in range(cn)]) for o in order])
    query, keys, values = jnp.split(sums, 3, axis=3)

    inverse_root_scale = 1.0 / math.sqrt(DH)
    score_bias = math.log(slots + seg_rows)
    positions = jnp.arange(seg_rows, dtype=jnp.float32)
    valid = (positions < lens[..., None]).astype(jnp.float32)
    own_query = lax.dynamic_slice_in_dim(mem_query, head * DH, DH, 1)
    f32 = dict(preferred_element_type=jnp.float32)
    write_scores = jnp.einsum("md,zctd->zcmt", own_query, keys, **f32) * inverse_root_scale
    write_weights = (
        jax.nn.sigmoid(write_scores - math.log(seg_rows)) * valid[:, :, None, :]
    ).astype(jnp.bfloat16)
    written = jnp.einsum("zcmt,zctd->zcmd", write_weights, sums[..., DH:], **f32)

    group = written[:, 0]
    for i in range(1, cn):
        group = retain_own[:, i, None, None] * group + written[:, i]
    groups = jnp.zeros((xn,) + group.shape, jnp.float32)
    for k in range(xn):
        got = over_x(group.astype(jnp.bfloat16), k).astype(jnp.float32) if k else group
        groups = lax.dynamic_update_slice(groups, got[None], ((x - k) % xn, 0, 0, 0))
    group_retain = jnp.prod(retain, axis=2)
    memory = jnp.zeros_like(group[0])
    memory_in = []
    for i in range(zn):
        entry = memory
        for k in range(xn):
            if k:
                entry = jnp.where(x == k, memory, entry)
            memory = group_retain[i, k] * memory + groups[k, i]
        inner = []
        for m in range(cn):
            inner.append(entry)
            entry = retain_own[i, m] * entry + written[i, m]
        memory_in.append(jnp.stack(inner))
    memory_in = jnp.stack(memory_in).reshape(zn, cn, slots, 2, DH)
    unit = (
        memory_in * lax.rsqrt(jnp.mean(jnp.square(memory_in), axis=4, keepdims=True) + 1e-06)
    ).astype(jnp.bfloat16)

    scale = pick(score_scale, head) * inverse_root_scale
    mem_scores = jnp.einsum("zctd,zcmd->zctm", query, unit[:, :, :, 0], **f32) * scale
    tok_scores = jnp.einsum("zctd,zcsd->zcts", query, keys, **f32) * scale
    allowed = (positions[None, :] <= positions[:, None]).astype(jnp.float32) * valid[:, :, None, :]
    mem_weights = jax.nn.sigmoid(mem_scores - score_bias).astype(jnp.bfloat16)
    tok_weights = (jax.nn.sigmoid(tok_scores - score_bias) * allowed).astype(jnp.bfloat16)
    attended = jnp.einsum("zctm,zcmd->zctd", mem_weights, unit[:, :, :, 1], **f32)
    attended = attended + jnp.einsum("zcts,zcsd->zctd", tok_weights, values, **f32)
    attended = (attended * valid[..., None]).astype(jnp.bfloat16)

    rows = jnp.zeros((seg_rows, zn, cn, DH), jnp.bfloat16)
    for j in range(zn):
        block = pick(attended, z ^ j)
        block = over_z(block, j) if j else block
        for m in range(cn):
            piece = pick(block, c ^ m)
            piece = over_c(piece, m) if m else piece
            rows = lax.dynamic_update_slice(rows, piece[:, None, None], (0, z ^ j, c ^ m, 0))
    rows = rows.reshape(seg_rows, heads * DH)

    tied, _ = lax.optimization_barrier((w_out, weight))
    out_cols = w_out.shape[1]
    partial = jnp.zeros((seg_rows, n_seq * out_cols), jnp.bfloat16)
    for j, by_z in enumerate(gather_z(tied)):
        for k in range(xn):
            by_x = over_x(by_z, k) if k else by_z
            for m in range(cn):
                got = over_c(by_x, m) if m else by_x
                product = jnp.dot(rows, got, **f32).astype(jnp.bfloat16)
                source = join(z ^ j, (x - k) % xn, c ^ m)
                partial = lax.dynamic_update_slice(partial, product, (0, source * out_cols))
    branch = lax.dynamic_slice_in_dim(partial, y * feat_local, feat_local, 1).astype(jnp.float32)
    for k in range(1, n_head):
        share = lax.dynamic_slice_in_dim(partial, (y + k) % n_head * feat_local, feat_local, 1)
        branch = branch + over_y(share, k).astype(jnp.float32)
    return branch.astype(jnp.bfloat16)


def solution(mesh):
    return jax.shard_map(
        body,
        mesh=mesh,
        in_specs=(
            P("seq", "head"),
            P(),
            P("seq", "head"),
            P("seq", "head"),
            P("seq", "head"),
            P("head", "seq"),
            P(None, "head"),
            P("head"),
            P("seq", "head"),
            P("seq"),
        ),
        out_specs=P("seq", "head"),
        check_vma=False,
    )
```

time: 498 us -> 289 us (0.58)
  waiting for transfers between devices: 435 us -> 184 us
  starting transfers between devices: 0.23 us -> 37.8 us
  local copies, waits for them, and re-layouts: 1.2 us -> 31.5 us
  blocking collectives: 18.8 us -> 0 us
  other arithmetic: 2.83 us -> 15.3 us
  between operations: 14.3 us -> 3.62 us
  matrix products: 24.5 us -> 16.2 us
    all_gather x6 -> x0, waiting for transfers between devices: 414 us -> none  [the longest x1 122 us: carried_in(): gathered = jax.tree.map(lambda a: lax.all_gather(a, axis), part)]
    ppermute x0 -> x65, waiting for transfers between devices: none -> 184 us  [the longest x15 87.8 us: over_z(): return lax.ppermute(a, 'seq', pairs)]
    ppermute x0 -> x65, starting transfers between devices: none -> 37.8 us  [the longest x15 16.1 us: over_z(): return lax.ppermute(a, 'seq', pairs)]
    all_gather x1 -> x0, blocking collectives: 18.8 us -> none  [carried_in(): gathered = jax.tree.map(lambda a: lax.all_gather(a, axis), part)]
    reduce_scatter x1 -> x0, waiting for transfers between devices: 18.7 us -> none  [body(): lax.psum_scatter(partial_rows.astype(jnp.bfloat16), 'head', scatter_dimen...]
    dynamic_update_slice x0 -> x55, local copies, waits for them, and re-layouts: none -> 14.1 us  [the longest x16 10.5 us: body(): lax.dynamic_update_slice(table, got[None, None], (z ^ j, (x - k) % xn, c...]
    dot_general x9 -> x23, matrix products: 24.5 us -> 16.2 us  [the longest x16 8.57 us: body(): product = jnp.dot(rows, got, **f32).astype(jnp.bfloat16)]
    add x0 -> x4, other arithmetic: none -> 6.46 us  [the longest x3 6.34 us: body(): entry = retain_own[i, m] * entry + written[i, m]]
  transfers between devices with their start and end apart: 7 -> 65, of which waited for: 7 -> 29; matrix products, arithmetic and copies ran while one was open for 5% -> 21% of each run, Pallas kernels for 0% -> 0%
where the time goes in v1:
time: 289 us; the launch traced here: 288 us
  waiting for transfers between devices  184 us (64%)
  starting transfers between devices  37.8 us (13%)
  local copies, waits for them, and re-layouts  31.5 us (11%)
  matrix products  16.2 us (6%)
  other arithmetic  15.3 us (5%)
  between operations  3.62 us (1%)
    ppermute x15, waiting for transfers between devices, over_z(): return lax.ppermute(a, 'seq', pairs)  87.8 us
    ppermute x13, waiting for transfers between devices, over_x(): return lax.ppermute(a, 'seq', pairs)  54.6 us
    ppermute x5, waiting for transfers between devices, over_y(): lax.ppermute(a, 'head', [(h, (h + k) % n_head) for h in range(n_head)])  31.8 us
    ppermute x15, starting transfers between devices, over_z(): return lax.ppermute(a, 'seq', pairs)  16.1 us
    dynamic_update_slice x16, local copies, waits for them, and re-layouts, body(): lax.dynamic_update_slice(table, got[None, None], (z ^ j, (x - k) % xn, c...  10.5 us
    ppermute x32, waiting for transfers between devices, over_c(): return lax.ppermute(a, 'seq', pairs)  9.62 us
    ppermute x13, starting transfers between devices, over_x(): return lax.ppermute(a, 'seq', pairs)  9.04 us
    dot_general x16, matrix products, body(): product = jnp.dot(rows, got, **f32).astype(jnp.bfloat16)  8.57 us
  transfers between devices with their start and end apart: 65, of which 29 were waited for; matrix products, arithmetic and copies ran while one was open for 21% of the time, Pallas kernels for 0%

profile of v1, /device:TPU:0, one launch (start us, length us, event | category | flops | bytes accessed | tf_op | source)
XLA Modules:
  0.0 288.4 jit_solution(4793242251006416419)
XLA Ops:
  1.9 2.5 collective-permute-start.27
  6.0 2.6 collective-permute-start.33
  18.8 2.2 collective-permute-start.5
  24.3 2.9 %collective-permute-done.31 = f32[1,9]{1,0:T(1,128)S(1)} collective-permute-done((f32[1,9]{1,0:T(1,128)S(1)}, f32[1,9]{1,0:T(1,128)S(1)}, u32[]{:S(2)}, u32[]{:S(2)}) %collective-permute-start.31) | collective-permute-done | bytes 68 | tf_op jit(solution)/shard_map/ppermute | solution.py:47
  28.9 2.9 %collective-permute-done.35 = f32[1,9]{1,0:T(1,128)S(1)} collective-permute-done((f32[1,9]{1,0:T(1,128)S(1)}, f32[1,9]{1,0:T(1,128)S(1)}, u32[]{:S(2)}, u32[]{:S(2)}) %collective-permute-start.35) | collective-permute-done | bytes 68 | tf_op jit(solution)/shard_map/ppermute | solution.py:47
  33.2 2.2 collective-permute-done.37
  44.7 2.5 collective-permute-done.39
  64.1 19.6 %collective-permute-done.8 = bf16[2,256,384]{2,1,0:T(8,128)(2,1)} collective-permute-done((bf16[2,256,384]{2,1,0:T(8,128)(2,1)}, bf16[2,256,384]{2,1,0:T(8,128)(2,1)}, u32[]{:S(2)}, u32[]{:S(2)}) %collective-permute-start.8) | collective-permute-done | bytes 393248 | tf_op jit(solution)/shard_map/ppermute | solution.py:40
  87.6 26.9 %collective-permute-done.18 = bf16[128,2048]{1,0:T(8,128)(2,1)S(1)} collective-permute-done((bf16[128,2048]{1,0:T(8,128)(2,1)S(1)}, bf16[128,2048]{1,0:T(8,128)(2,1)S(1)}, u32[]{:S(2)}, u32[]{:S(2)}) %collective-permute-start.18) | collective-permute-done | bytes 524320 | tf_op jit(solution)/shard_map/ppermute | solution.py:40
  118.4 10.4 %collective-permute-done.7 = bf16[2,256,384]{2,1,0:T(8,128)(2,1)S(1)} collective-permute-done((bf16[2,256,384]{2,1,0:T(8,128)(2,1)S(1)}, bf16[2,256,384]{2,1,0:T(8,128)(2,1)S(1)}, u32[]{:S(2)}, u32[]{:S(2)}) %collective-permute-start.7) | collective-permute-done | bytes 393248 | tf_op jit(solution)/shard_map/ppermute | solution.py:47
  129.5 9.5 %collective-permute-done.10 = bf16[2,256,384]{2,1,0:T(8,128)(2,1)S(1)} collective-permute-done((bf16[2,256,384]{2,1,0:T(8,128)(2,1)S(1)}, bf16[2,256,384]{2,1,0:T(8,128)(2,1)S(1)}, u32[]{:S(2)}, u32[]{:S(2)}) %collective-permute-start.10) | collective-permute-done | bytes 393248 | tf_op jit(solution)/shard_map/ppermute | solution.py:47
  139.7 8.6 %collective-permute-done.13 = bf16[2,256,384]{2,1,0:T(8,128)(2,1)S(1)} collective-permute-done((bf16[2,256,384]{2,1,0:T(8,128)(2,1)S(1)}, bf16[2,256,384]{2,1,0:T(8,128)(2,1)S(1)}, u32[]{:S(2)}, u32[]{:S(2)}) %collective-permute-start.13) | collective-permute-done | bytes 393248 | tf_op jit(solution)/shard_map/ppermute | solution.py:47
  152.7 6.8 %collective-permute-done.19 = bf16[128,2048]{1,0:T(8,128)(2,1)S(1)} collective-permute-done((bf16[128,2048]{1,0:T(8,128)(2,1)S(1)}, bf16[128,2048]{1,0:T(8,128)(2,1)S(1)}, u32[]{:S(2)}, u32[]{:S(2)}) %collective-permute-start.19) | collective-permute-done | bytes 524320 | tf_op jit(solution)/shard_map/ppermute | solution.py:54
  159.5 4.3 %collective-permute-done.22 = bf16[128,2048]{1,0:T(8,128)(2,1)S(1)} collective-permute-done((bf16[128,2048]{1,0:T(8,128)(2,1)S(1)}, bf16[128,2048]{1,0:T(8,128)(2,1)S(1)}, u32[]{:S(2)}, u32[]{:S(2)}) %collective-permute-start.22) | collective-permute-done | bytes 524320 | tf_op jit(solution)/shard_map/ppermute | solution.py:40
  167.5 12.3 %collective-permute-done.23 = bf16[128,2048]{1,0:T(8,128)(2,1)S(1)} collective-permute-done((bf16[128,2048]{1,0:T(8,128)(2,1)S(1)}, bf16[128,2048]{1,0:T(8,128)(2,1)S(1)}, u32[]{:S(2)}, u32[]{:S(2)}) %collective-permute-start.23) | collective-permute-done | bytes 524320 | tf_op jit(solution)/shard_map/ppermute | solution.py:54
  189.1 7.4 %collective-permute-done.41 = bf16[4,128,256]{2,1,0:T(8,128)(2,1)} collective-permute-done((bf16[4,128,256]{2,1,0:T(8,128)(2,1)S(1)}, bf16[4,128,256]{2,1,0:T(8,128)(2,1)}, u32[]{:S(2)}, u32[]{:S(2)}) %collective-permute-start.41) | collective-permute-done | bytes 262176 | tf_op jit(solution)/shard_map/ppermute | solution.py:47
  199.8 3.1 %bitcast_add_fusion.2 = (f32[1,1,128,2,128]{4,2,1,0,3:T(8,128)S(1)}, f32[1,1,128,2,128]{4,2,1,0,3:T(8,128)S(1)}, f32[1,1,128,2,128]{4,2,1,0,3:T(8,128)S(1)}, f32...) fusion(f32[1,1,16,2,8,128]{5,4,3,2,1,0:T(8,128)S(1)} %get-tuple-element.27, f32[]{:T(128)} %bitcast.75, ...), kind=kLoop, calls=%fused_computation.166 | loop fusion | flops 393216 | bytes 1441813 | tf_op jit(solution)/shard_map/add | solution.py:160
  202.9 2.6 bitcast_add_fusion
  210.8 3.0 %collective-permute-done.43 = bf16[2,128,128]{2,1,0:T(8,128)(2,1)S(1)} collective-permute-done((bf16[2,128,128]{2,1,0:T(8,128)(2,1)S(1)}, bf16[2,128,128]{2,1,0:T(8,128)(2,1)S(1)}, u32[]{:S(2)}, u32[]{:S(2)}) %collective-permute-start.43) | collective-permute-done | bytes 65568 | tf_op jit(solution)/shard_map/ppermute | solution.py:40
  216.7 3.9 %collective-permute-done.47 = bf16[2,128,128]{2,1,0:T(8,128)(2,1)S(1)} collective-permute-done((bf16[2,128,128]{2,1,0:T(8,128)(2,1)S(1)}, bf16[2,128,128]{2,1,0:T(8,128)(2,1)S(1)}, u32[]{:S(2)}, u32[]{:S(2)}) %collective-permute-start.47) | collective-permute-done | bytes 65568 | tf_op jit(solution)/shard_map/ppermute | solution.py:40
  223.7 18.8 %collective-permute-done.56 = bf16[1024,256]{1,0:T(8,128)(2,1)S(1)} collective-permute-done((bf16[1024,256]{1,0:T(8,128)(2,1)}, bf16[1024,256]{1,0:T(8,128)(2,1)S(1)}, u32[]{:S(2)}, u32[]{:S(2)}) %collective-permute-start.56) | collective-permute-done | bytes 524320 | tf_op jit(solution)/shard_map/ppermute | solution.py:40
  247.7 9.1 %collective-permute-done.60 = bf16[1024,256]{1,0:T(8,128)(2,1)S(1)} collective-permute-done((bf16[1024,256]{1,0:T(8,128)(2,1)S(1)}, bf16[1024,256]{1,0:T(8,128)(2,1)S(1)}, u32[]{:S(2)}, u32[]{:S(2)}) %collective-permute-start.60) | collective-permute-done | bytes 524320 | tf_op jit(solution)/shard_map/ppermute | solution.py:40
  260.1 10.3 %collective-permute-done.62 = bf16[1024,256]{1,0:T(8,128)(2,1)S(1)} collective-permute-done((bf16[1024,256]{1,0:T(8,128)(2,1)S(1)}, bf16[1024,256]{1,0:T(8,128)(2,1)S(1)}, u32[]{:S(2)}, u32[]{:S(2)}) %collective-permute-start.62) | collective-permute-done | bytes 524320 | tf_op jit(solution)/shard_map/ppermute | solution.py:47
  274.6 12.8 %collective-permute-done.64 = bf16[128,2048]{1,0:T(8,128)(2,1)S(1)} collective-permute-done((bf16[128,2048]{1,0:T(8,128)(2,1)S(1)}, bf16[128,2048]{1,0:T(8,128)(2,1)S(1)}, u32[]{:S(2)}, u32[]{:S(2)}) %collective-permute-start.64) | collective-permute-done | bytes 524320 | tf_op jit(solution)/shard_map/ppermute | solution.py:54
  (307 shorter events, 97.6 us)
Async XLA Ops:
  8.6 77.0 %collective-permute-start.14 = (bf16[128,2048]{1,0:T(8,128)(2,1)}, bf16[128,2048]{1,0:T(8,128)(2,1)}, u32[]{:S(2)}, u32[]{:S(2)}) collective-permute-start(bf16[128,2048]{1,0:T(8,128)(2,1)} %param.10), channel_id=1, source_target_pairs={{0,8},{2,10},{4,12},{6,14},{8,0},{10,2},{12,4},{14,6},{16,24},{18,... | collective-permute-start | bytes 1572872 | tf_op jit(solution)/shard_map/ppermute | solution.py:40
  18.0 68.9 %collective-permute-start.1 = (bf16[128,2048]{1,0:T(8,128)(2,1)S(1)}, bf16[128,2048]{1,0:T(8,128)(2,1)S(1)}, u32[]{:S(2)}, u32[]{:S(2)}) collective-permute-start(bf16[128,2048]{1,0:T(8,128)(2,1)S(1)} %copy-done.3), channel_id=1, source_target_pairs={{0,2},{2,0},{4,6},{6,4},{8,10},{10,8},{12,14},{14,12},{16,18},{18,... | collective-permute-start | bytes 1572872 | tf_op jit(solution)/shard_map/ppermute | solution.py:51
  18.2 40.6 %collective-permute-start.3 = (bf16[256,384]{1,0:T(8,128)(2,1)}, bf16[256,384]{1,0:T(8,128)(2,1)}, u32[]{:S(2)}, u32[]{:S(2)}) collective-permute-start(bf16[256,384]{1,0:T(8,128)(2,1)} %dynamic-slice_bitcast_fusion.6), channel_id=1, source_target_pairs={{0,2},{2,0},{4,6},{6,4},{8,10},{10,8},{12,14},{14,12},{16,18},{18,... | collective-permute-start | bytes 589832 | tf_op jit(solution)/shard_map/ppermute | solution.py:51
  18.8 42.6 %collective-permute-start.5 = (bf16[2,256,384]{2,1,0:T(8,128)(2,1)}, bf16[2,256,384]{2,1,0:T(8,128)(2,1)}, u32[]{:S(2)}, u32[]{:S(2)}) collective-permute-start(bf16[2,256,384]{2,1,0:T(8,128)(2,1)} %get-tuple-element.16), channel_id=1, source_target_pairs={{0,8},{2,10},{4,12},{6,14},{8,0},{10,2},{12,4},{14,6},{16,24},{18,... | collective-permute-start | bytes 1179656 | tf_op jit(solution)/shard_map/ppermute | solution.py:40
  55.5 28.2 %collective-permute-start.8 = (bf16[2,256,384]{2,1,0:T(8,128)(2,1)}, bf16[2,256,384]{2,1,0:T(8,128)(2,1)}, u32[]{:S(2)}, u32[]{:S(2)}) collective-permute-start(bf16[2,256,384]{2,1,0:T(8,128)(2,1)} %get-tuple-element.15), channel_id=1, source_target_pairs={{0,16},{2,18},{4,20},{6,22},{8,24},{10,26},{12,28},{14,30},{16,0},... | collective-permute-start | bytes 1179656 | tf_op jit(solution)/shard_map/ppermute | solution.py:40
  58.7 26.1 %collective-permute-start.11 = (bf16[2,256,384]{2,1,0:T(8,128)(2,1)S(1)}, bf16[2,256,384]{2,1,0:T(8,128)(2,1)S(1)}, u32[]{:S(2)}, u32[]{:S(2)}) collective-permute-start(bf16[2,256,384]{2,1,0:T(8,128)(2,1)S(1)} %get-tuple-element.14), channel_id=1, source_target_pairs={{0,24},{2,26},{4,28},{6,30},{8,16},{10,18},{12,20},{14,22},{16,8},... | collective-permute-start | bytes 1179656 | tf_op jit(solution)/shard_map/ppermute | solution.py:40
  61.4 53.3 %collective-permute-start = (bf16[128,2048]{1,0:T(8,128)(2,1)S(1)}, bf16[128,2048]{1,0:T(8,128)(2,1)S(1)}, u32[]{:S(2)}, u32[]{:S(2)}) collective-permute-start(bf16[128,2048]{1,0:T(8,128)(2,1)S(1)} %copy-done.3), channel_id=1, source_target_pairs={{0,1},{1,0},{2,3},{3,2},{4,5},{5,4},{6,7},{7,6},{8,9},{9,8},{10,11... | collective-permute-start | bytes 1572872 | tf_op jit(solution)/shard_map/ppermute | solution.py:54
  83.7 30.7 %collective-permute-start.18 = (bf16[128,2048]{1,0:T(8,128)(2,1)S(1)}, bf16[128,2048]{1,0:T(8,128)(2,1)S(1)}, u32[]{:S(2)}, u32[]{:S(2)}) collective-permute-start(bf16[128,2048]{1,0:T(8,128)(2,1)S(1)} %copy-done.3), channel_id=1, source_target_pairs={{0,16},{2,18},{4,20},{6,22},{8,24},{10,26},{12,28},{14,30},{16,0},... | collective-permute-start | bytes 1572872 | tf_op jit(solution)/shard_map/ppermute | solution.py:40
  84.9 30.4 %collective-permute-start.4 = (bf16[2,256,384]{2,1,0:T(8,128)(2,1)S(1)}, bf16[2,256,384]{2,1,0:T(8,128)(2,1)S(1)}, u32[]{:S(2)}, u32[]{:S(2)}) collective-permute-start(bf16[2,256,384]{2,1,0:T(8,128)(2,1)S(1)} %bitcast_dynamic-update-slice_fusion.11), channel_id=1, source_target_pairs={{0,4},{2,6},{4,0},{6,2},{8,12},{10,14},{12,8},{14,10},{16,20},{18,... | collective-permute-start | bytes 1179656 | tf_op jit(solution)/shard_map/ppermute | solution.py:47
  85.6 31.3 %collective-permute-start.6 = (bf16[256,384]{1,0:T(8,128)(2,1)S(1)}, bf16[256,384]{1,0:T(8,128)(2,1)S(1)}, u32[]{:S(2)}, u32[]{:S(2)}) collective-permute-start(bf16[256,384]{1,0:T(8,128)(2,1)S(1)} %get-tuple-element.40), channel_id=1, source_target_pairs={{0,2},{2,0},{4,6},{6,4},{8,10},{10,8},{12,14},{14,12},{16,18},{18,... | collective-permute-start | bytes 589832 | tf_op jit(solution)/shard_map/ppermute | solution.py:51
  86.9 30.2 %collective-permute-start.9 = (bf16[256,384]{1,0:T(8,128)(2,1)S(1)}, bf16[256,384]{1,0:T(8,128)(2,1)S(1)}, u32[]{:S(2)}, u32[]{:S(2)}) collective-permute-start(bf16[256,384]{1,0:T(8,128)(2,1)S(1)} %get-tuple-element.38), channel_id=1, source_target_pairs={{0,2},{2,0},{4,6},{6,4},{8,10},{10,8},{12,14},{14,12},{16,18},{18,... | collective-permute-start | bytes 589832 | tf_op jit(solution)/shard_map/ppermute | solution.py:51
  114.7 34.2 %collective-permute-start.16 = (bf16[128,2048]{1,0:T(8,128)(2,1)}, bf16[128,2048]{1,0:T(8,128)(2,1)S(1)}, u32[]{:S(2)}, u32[]{:S(2)}) collective-permute-start(bf16[128,2048]{1,0:T(8,128)(2,1)} %collective-permute-done.14), channel_id=1, source_target_pairs={{0,2},{2,0},{4,6},{6,4},{8,10},{10,8},{12,14},{14,12},{16,18},{18,... | collective-permute-start | bytes 1572872 | tf_op jit(solution)/shard_map/ppermute | solution.py:51
  115.3 33.8 %collective-permute-start.15 = (bf16[128,2048]{1,0:T(8,128)(2,1)}, bf16[128,2048]{1,0:T(8,128)(2,1)S(1)}, u32[]{:S(2)}, u32[]{:S(2)}) collective-permute-start(bf16[128,2048]{1,0:T(8,128)(2,1)} %collective-permute-done.14), channel_id=1, source_target_pairs={{0,1},{1,0},{2,3},{3,2},{4,5},{5,4},{6,7},{7,6},{8,9},{9,8},{10,11... | collective-permute-start | bytes 1572872 | tf_op jit(solution)/shard_map/ppermute | solution.py:54
  117.0 32.3 %collective-permute-start.2 = (bf16[128,2048]{1,0:T(8,128)(2,1)S(1)}, bf16[128,2048]{1,0:T(8,128)(2,1)S(1)}, u32[]{:S(2)}, u32[]{:S(2)}) collective-permute-start(bf16[128,2048]{1,0:T(8,128)(2,1)S(1)} %collective-permute-done), channel_id=1, source_target_pairs={{0,2},{2,0},{4,6},{6,4},{8,10},{10,8},{12,14},{14,12},{16,18},{18,... | collective-permute-start | bytes 1572872 | tf_op jit(solution)/shard_map/ppermute | solution.py:51
  117.1 33.3 %collective-permute-start.20 = (bf16[128,2048]{1,0:T(8,128)(2,1)S(1)}, bf16[128,2048]{1,0:T(8,128)(2,1)S(1)}, u32[]{:S(2)}, u32[]{:S(2)}) collective-permute-start(bf16[128,2048]{1,0:T(8,128)(2,1)S(1)} %collective-permute-done.18), channel_id=1, source_target_pairs={{0,2},{2,0},{4,6},{6,4},{8,10},{10,8},{12,14},{14,12},{16,18},{18,... | collective-permute-start | bytes 1572872 | tf_op jit(solution)/shard_map/ppermute | solution.py:51
  149.1 94.8 %collective-permute-start.49 = (bf16[1024,256]{1,0:T(8,128)(2,1)}, bf16[1024,256]{1,0:T(8,128)(2,1)}, u32[]{:S(2)}, u32[]{:S(2)}) collective-permute-start(bf16[1024,256]{1,0:T(8,128)(2,1)} %param.15), channel_id=1, source_target_pairs={{0,2},{2,0},{4,6},{6,4},{8,10},{10,8},{12,14},{14,12},{16,18},{18,... | collective-permute-start | bytes 1572872 | tf_op jit(solution)/shard_map/ppermute | solution.py:51
  149.3 74.0 %collective-permute-start.50 = (bf16[1024,256]{1,0:T(8,128)(2,1)}, bf16[1024,256]{1,0:T(8,128)(2,1)}, u32[]{:S(2)}, u32[]{:S(2)}) collective-permute-start(bf16[1024,256]{1,0:T(8,128)(2,1)} %param.15), channel_id=1, source_target_pairs={{0,4},{2,6},{4,0},{6,2},{8,12},{10,14},{12,8},{14,10},{16,20},{18,... | collective-permute-start | bytes 1572872 | tf_op jit(solution)/shard_map/ppermute | solution.py:47
  150.4 65.3 %collective-permute-start.52 = (bf16[1024,256]{1,0:T(8,128)(2,1)}, bf16[1024,256]{1,0:T(8,128)(2,1)}, u32[]{:S(2)}, u32[]{:S(2)}) collective-permute-start(bf16[1024,256]{1,0:T(8,128)(2,1)} %param.15), channel_id=1, source_target_pairs={{0,8},{2,10},{4,12},{6,14},{8,0},{10,2},{12,4},{14,6},{16,24},{18,... | collective-permute-start | bytes 1572872 | tf_op jit(solution)/shard_map/ppermute | solution.py:40
  215.8 26.7 %collective-permute-start.56 = (bf16[1024,256]{1,0:T(8,128)(2,1)}, bf16[1024,256]{1,0:T(8,128)(2,1)S(1)}, u32[]{:S(2)}, u32[]{:S(2)}) collective-permute-start(bf16[1024,256]{1,0:T(8,128)(2,1)} %param.15), channel_id=1, source_target_pairs={{0,16},{2,18},{4,20},{6,22},{8,24},{10,26},{12,28},{14,30},{16,0},... | collective-permute-start | bytes 1572872 | tf_op jit(solution)/shard_map/ppermute | solution.py:40
  216.7 42.2 %collective-permute-start.53 = (bf16[1024,256]{1,0:T(8,128)(2,1)}, bf16[1024,256]{1,0:T(8,128)(2,1)S(1)}, u32[]{:S(2)}, u32[]{:S(2)}) collective-permute-start(bf16[1024,256]{1,0:T(8,128)(2,1)} %collective-permute-done.52), channel_id=1, source_target_pairs={{0,2},{2,0},{4,6},{6,4},{8,10},{10,8},{12,14},{14,12},{16,18},{18,... | collective-permute-start | bytes 1572872 | tf_op jit(solution)/shard_map/ppermute | solution.py:51
  223.0 19.5 %collective-permute-start.48 = (bf16[128,128]{0,1:T(8,128)(2,1)S(1)}, bf16[128,128]{0,1:T(8,128)(2,1)S(1)}, u32[]{:S(2)}, u32[]{:S(2)}) collective-permute-start(bf16[128,128]{0,1:T(8,128)(2,1)S(1)} %bitcast.280), channel_id=1, source_target_pairs={{0,2},{2,0},{4,6},{6,4},{8,10},{10,8},{12,14},{14,12},{16,18},{18,... | collective-permute-start | bytes 98312 | tf_op jit(solution)/shard_map/ppermute | solution.py:51
  223.2 24.2 %collective-permute-start.54 = (bf16[1024,256]{1,0:T(8,128)(2,1)}, bf16[1024,256]{1,0:T(8,128)(2,1)S(1)}, u32[]{:S(2)}, u32[]{:S(2)}) collective-permute-start(bf16[1024,256]{1,0:T(8,128)(2,1)} %collective-permute-done.52), channel_id=1, source_target_pairs={{0,4},{2,6},{4,0},{6,2},{8,12},{10,14},{12,8},{14,10},{16,20},{18,... | collective-permute-start | bytes 1572872 | tf_op jit(solution)/shard_map/ppermute | solution.py:47
  247.2 23.8 %collective-permute-start.57 = (bf16[1024,256]{1,0:T(8,128)(2,1)S(1)}, bf16[1024,256]{1,0:T(8,128)(2,1)S(1)}, u32[]{:S(2)}, u32[]{:S(2)}) collective-permute-start(bf16[1024,256]{1,0:T(8,128)(2,1)S(1)} %collective-permute-done.56), channel_id=1, source_target_pairs={{0,2},{2,0},{4,6},{6,4},{8,10},{10,8},{12,14},{14,12},{16,18},{18,... | collective-permute-start | bytes 1572872 | tf_op jit(solution)/shard_map/ppermute | solution.py:51
  247.4 23.0 %collective-permute-start.55 = (bf16[1024,256]{1,0:T(8,128)(2,1)S(1)}, bf16[1024,256]{1,0:T(8,128)(2,1)S(1)}, u32[]{:S(2)}, u32[]{:S(2)}) collective-permute-start(bf16[1024,256]{1,0:T(8,128)(2,1)S(1)} %collective-permute-done.54), channel_id=1, source_target_pairs={{0,2},{2,0},{4,6},{6,4},{8,10},{10,8},{12,14},{14,12},{16,18},{18,... | collective-permute-start | bytes 1572872 | tf_op jit(solution)/shard_map/ppermute | solution.py:51
  (51 other events, 358.1 us)

commit v2 on v0

v2 whole, which is shorter than its diff:
```python
import functools
import math

import jax
import jax.numpy as jnp
from jax import lax
from jax.experimental import pallas as pl
from jax.experimental.pallas import tpu as pltpu
from jax.sharding import PartitionSpec as P

DH = 128
F32 = jnp.float32
BF16 = jnp.bfloat16
VMEM = pl.BlockSpec(memory_space=pltpu.VMEM)
SMEM = pl.BlockSpec(memory_space=pltpu.SMEM)


def dot(a, b, contract=(1, 0)):
    dims = (((contract[0],), (contract[1],)), ((), ()))
    return lax.dot_general(a, b, dims, preferred_element_type=F32)


def call(kernel, ins, outs, scratch=(), flops=0, scalars=1):
    moved = sum(math.prod(a.shape) * a.dtype.itemsize for a in (*ins, *outs))
    return pl.pallas_call(
        kernel,
        in_specs=[SMEM] * scalars + [VMEM] * (len(ins) - scalars),
        out_specs=[VMEM] * len(outs),
        out_shape=outs,
        scratch_shapes=scratch,
        compiler_params=pltpu.CompilerParams(vmem_limit_bytes=48 * 2**20),
        cost_estimate=pl.CostEstimate(flops=flops, bytes_accessed=moved, transcendentals=0),
    )(*ins)


def lanes(index, size):
    return pl.ds(pl.multiple_of(index * size, size), size)


def cut_kernel(zn, cn, at, *refs):
    weights, outs = refs[:3], refs[3:]
    z, c = at[0], at[2]
    for m, out in enumerate(outs):
        for j in range(zn):
            head = (z ^ j) * cn + (c ^ m)
            for i, w in enumerate(weights):
                out[j, :, i * DH : (i + 1) * DH] = w[:, lanes(head, DH)]


def pack_kernel(zn, cn, *refs):
    for j in range(zn):
        for m in range(cn):
            refs[cn + j][m] = refs[m][j]


def norm_kernel(n_head, at, gain, *refs):
    parts, out = refs[:n_head], refs[n_head]
    feat = parts[0].shape[1]
    wide = [part[...].astype(F32) for part in parts]
    squares = sum(jnp.sum(w * w, axis=1, keepdims=True) for w in wide)
    inverse = lax.rsqrt(squares / (feat * n_head) + 1e-05)
    for k, w in enumerate(wide):
        half = lanes(lax.rem(at[3] + n_head - k, n_head), feat)
        out[:, half] = (w * inverse * gain[:, half]).astype(BF16)


def project(zn, xn, cn, j, at, rows, weights, chunk, each):
    z, x, c = at[0], at[1], at[2]
    w_rows = weights[0].shape[1]
    for k, w in enumerate(weights):
        for m in range(cn):
            spot = lax.rem(x + xn - k, xn) * cn + (c ^ m)
            chunk[pl.ds(pl.multiple_of(spot * w_rows, w_rows), w_rows), :] = w[m]
    size = chunk.shape[0]
    for i in range(zn):
        left = jnp.concatenate([rows[i * cn + m][:, lanes(z ^ j, size)] for m in range(cn)])
        each(i, dot(left, chunk[...]))


def project_kernel(zn, xn, cn, steps, at, *refs):
    rows = refs[: zn * cn]
    weights = refs[zn * cn : zn * cn + len(steps) * xn]
    out, chunk = refs[-2:]
    for n, j in enumerate(steps):

        def each(i, sums):
            out[i] = sums if n == 0 else out[i] + sums

        project(zn, xn, cn, j, at, rows, weights[n * xn : (n + 1) * xn], chunk.at[n], each)


def segment_info(xn, cn, heads, at, table):
    width = heads + 1
    z, x, c = at[0], at[1], at[2]
    head = z * cn + c

    def row(zi, xi, ci):
        return (((z ^ zi) * xn + lax.rem(x + xn - xi, xn)) * cn + (c ^ ci)) * width

    def retain(zi, xi, ci):
        return table[row(zi, xi, ci) + head]

    def length(zi, ci):
        return table[row(zi, x, ci) + heads]

    return retain, length


def write_kernel(zn, xn, cn, heads, step, at, table, *refs):
    rows = refs[: zn * cn]
    weights = refs[zn * cn : zn * cn + xn]
    query = refs[zn * cn + xn]
    before = refs[zn * cn + xn + 1] if zn > 1 else None
    sums, written, group, group16, chunk = refs[-5:]
    z, x, c = at[0], at[1], at[2]
    retain, length = segment_info(xn, cn, heads, at, table)
    seg_rows = sums.shape[2]

    def each(i, add):
        add = add if before is None else add + before[i]
        add = add.astype(BF16).reshape(cn, seg_rows, 3 * DH)
        for m in range(cn):
            sums[z ^ i, c ^ m] = add[m]

    project(zn, xn, cn, step, at, rows, weights, chunk.at[0], each)
    own = query[:, lanes(z * cn + c, DH)]
    slots = own.shape[0]
    position = lax.broadcasted_iota(jnp.int32, (slots, seg_rows), 1).astype(F32)
    for i in range(zn):
        total = None
        for m in range(cn):
            keys = sums[i, m, :, DH : 2 * DH]
            scores = dot(own, keys, (1, 1)) * (1.0 / math.sqrt(DH))
            gate = jax.nn.sigmoid(scores - math.log(seg_rows))
            gate = jnp.where(position < length(i, m), gate, 0.0).astype(BF16)
            new = dot(gate, sums[i, m, :, DH:])
            written[i, m] = new
            total = new if total is None else retain(i, x, m) * total + new
        group[i] = total
        group16[i] = total.astype(BF16)


def token_kernel(zn, xn, cn, heads, slots, at, table, scale, sums, out):
    _, length = segment_info(xn, cn, heads, at, table)
    seg_rows = sums.shape[2]
    shape = (seg_rows, seg_rows)
    row = lax.broadcasted_iota(jnp.int32, shape, 0)
    column = lax.broadcasted_iota(jnp.int32, shape, 1)
    factor = scale[at[0] * cn + at[2]] * (1.0 / math.sqrt(DH))
    for i in range(zn):
        for m in range(cn):
            query, keys, values = (sums[i, m, :, n * DH : (n + 1) * DH] for n in range(3))
            scores = dot(query, keys, (1, 1)) * factor
            gate = jax.nn.sigmoid(scores - math.log(slots + seg_rows))
            allowed = (column <= row) & (column.astype(F32) < length(i, m))
            out[i, m] = dot(jnp.where(allowed, gate, 0.0).astype(BF16), values)


def memory_kernel(zn, xn, cn, heads, at, table, scale, sums, token, written, group, *refs):
    others = refs[: xn - 1]
    outs = refs[xn - 1 : xn - 1 + zn]
    groups, done = refs[-2:]
    z, x, c = at[0], at[1], at[2]
    retain, length = segment_info(xn, cn, heads, at, table)
    slots, seg_rows = group.shape[1], sums.shape[2]
    factor = scale[z * cn + c] * (1.0 / math.sqrt(DH))
    bias = math.log(slots + seg_rows)
    row = lax.broadcasted_iota(jnp.int32, (seg_rows, DH), 0).astype(F32)
    groups[x] = group[...]
    for k, other in enumerate(others, 1):
        groups[lax.rem(x + xn - k, xn)] = other[...].astype(F32)
    memory = jnp.zeros(group.shape[1:], F32)
    for i in range(zn):
        entry = memory
        for k in range(xn):
            if k:
                entry = jnp.where(x == k, memory, entry)
            kept = retain(i, k, 0)
            for m in range(1, cn):
                kept = kept * retain(i, k, m)
            memory = kept * memory + groups[k, i]
        for m in range(cn):
            units = []
            for n in range(2):
                part = entry[:, n * DH : (n + 1) * DH]
                mean = jnp.mean(part * part, axis=1, keepdims=True)
                units.append((part * lax.rsqrt(mean + 1e-06)).astype(BF16))
            scores = dot(sums[i, m, :, :DH], units[0], (1, 1)) * factor
            gate = jax.nn.sigmoid(scores - bias).astype(BF16)
            total = dot(gate, units[1]) + token[i, m]
            done[i, m] = jnp.where(row < length(i, m), total, 0.0).astype(BF16)
            if m + 1 < cn:
                entry = retain(i, x, m) * entry + written[i, m]
    for j in range(zn):
        for m in range(cn):
            outs[j][m] = done[z ^ j, c ^ m]


def out_kernel(zn, xn, cn, n_head, at, *refs):
    attended = refs[: zn * cn]
    weights = refs[zn * cn : zn * cn + zn * xn]
    outs, rows = refs[-1 - cn * n_head : -1], refs[-1]
    z, x, c, y = at[0], at[1], at[2], at[3]
    seg_rows = attended[0].shape[1]
    for j in range(zn):
        for e in range(cn):
            for m in range(cn):
                rows[m * seg_rows : (m + 1) * seg_rows, lanes((z ^ j) * cn + (c ^ e), DH)] = (
                    attended[j * cn + e][m ^ e]
                )
    blocks = outs[0].shape[0]
    for j in range(zn):
        for k in range(xn):
            product = dot(rows[...], weights[j * xn + k][...]).astype(BF16)
            spot = (z ^ j) * xn + lax.rem(x + xn - k, xn)
            turn = lax.rem(spot // blocks + n_head - y, n_head)
            for r in range(n_head):

                @pl.when(turn == r)
                def _():
                    for m in range(cn):
                        outs[r * cn + m][lax.rem(spot, blocks)] = product[
                            m * seg_rows : (m + 1) * seg_rows
                        ]


def sum_kernel(n_head, cn, at, *refs):
    out = refs[-1]
    blocks, _, size = refs[0].shape
    for b in range(blocks):
        totals = [
            sum(refs[r * cn + e][b].astype(F32) for r in range(n_head)).astype(BF16)
            for e in range(cn)
        ]
        for m in range(cn):
            total = totals[0]
            for e in range(1, cn):
                total = jnp.where((at[2] ^ e) == m, totals[e], total)
            first = (b * cn + m) * size
            out[:, first : first + size] = total


def body(tokens, gain, w_query, w_key, w_value, w_out, mem_query, score_scale, decay, seg_len):
    n_seq = lax.axis_size("seq")
    n_head = lax.axis_size("head")
    seg_rows, feat_local = tokens.shape
    width = gain.shape[0]
    w_rows, col_local = w_query.shape
    heads = col_local // DH
    slots = mem_query.shape[0]
    cn = 2 if heads % 2 == 0 else 1
    zn = heads // cn
    xn = n_seq // heads
    place = lax.axis_index("seq")
    y = lax.axis_index("head")
    at = jnp.stack([place // (cn * xn), place // cn % xn, place % cn, y]).astype(jnp.int32)

    def shape(dims, dtype=BF16):
        return jax.ShapeDtypeStruct(dims, dtype)

    def split(s):
        return s // (cn * xn), s // cn % xn, s % cn

    def join(a, b, d):
        return (a * xn + b) * cn + d

    def over_z(a, j):
        pairs = [(s, join(split(s)[0] ^ j, *split(s)[1:])) for s in range(n_seq)]
        return lax.ppermute(a, "seq", pairs)

    def over_x(a, k):
        pairs = []
        for s in range(n_seq):
            sz, sx, sc = split(s)
            pairs.append((s, join(sz, (sx + k) % xn, sc)))
        return lax.ppermute(a, "seq", pairs)

    def over_c(a, m):
        return lax.ppermute(a, "seq", [(s, s ^ m) for s in range(n_seq)])

    def over_y(a, k):
        return lax.ppermute(a, "head", [(h, (h + k) % n_head) for h in range(n_head)])

    def gather_z(a):
        got = {0: a}
        bit = zn // 2
        while bit:
            for j in sorted(got):
                got[j | bit] = over_z(got[j], bit)
            bit //= 2
        return [got[j] for j in range(zn)]

    def after(a, *done):
        return lax.optimization_barrier((a,) + done)[0]

    tok = gather_z(tokens)
    rows = []
    for part in tok:
        parts = [part] + [over_y(part, k) for k in range(1, n_head)]
        (normed,) = call(
            functools.partial(norm_kernel, n_head),
            (at, gain[None], *parts),
            [shape((seg_rows, width))],
        )
        rows += [over_c(normed, m) if m else normed for m in range(cn)]

    cuts = call(
        functools.partial(cut_kernel, zn, cn),
        (at, w_query, w_key, w_value),
        [shape((zn, w_rows, 3 * DH))] * cn,
    )
    cuts = [over_c(cut, m) if m else cut for m, cut in enumerate(cuts)]
    packs = call(
        functools.partial(pack_kernel, zn, cn),
        cuts,
        [shape((cn, w_rows, 3 * DH))] * zn,
        scalars=0,
    )
    pieces = []
    for j, pack in enumerate(packs):
        if j:
            pack = over_z(after(pack, tok[1 if j < 3 else 2]), j)
        pieces.append([over_x(pack, k) if k else pack for k in range(xn)])

    meta = after(jnp.concatenate([decay[0], seg_len.astype(F32)]), tok[zn // 2])
    meta = jnp.stack([over_c(meta, m) if m else meta for m in range(cn)])
    meta = jnp.stack([over_x(meta, k) if k else meta for k in range(xn)])
    table = jnp.stack(gather_z(meta)).reshape(-1)

    def chunks(count):
        return [pltpu.VMEM((count, xn * cn * w_rows, 3 * DH), BF16)]

    flops = 2 * zn * cn * seg_rows * width * 3 * DH
    last = zn - 1
    before = []
    if last:
        before = call(
            functools.partial(project_kernel, zn, xn, cn, range(last)),
            (at, *rows, *sum(pieces[:last], [])),
            [shape((zn, cn * seg_rows, 3 * DH), F32)],
            chunks(last),
            flops * last // zn,
        )
    sums, written, group, group16 = call(
        functools.partial(write_kernel, zn, xn, cn, heads, last),
        (at, table, *rows, *pieces[last], mem_query, *before),
        [
            shape((zn, cn, seg_rows, 3 * DH)),
            shape((zn, cn, slots, 2 * DH), F32),
            shape((zn, slots, 2 * DH), F32),
            shape((zn, slots, 2 * DH)),
        ],
        chunks(1),
        flops // zn,
        scalars=2,
    )
    others = [over_x(group16, k) for k in range(1, xn)]
    (token,) = call(
        functools.partial(token_kernel, zn, xn, cn, heads, slots),
        (at, table, score_scale, sums),
        [shape((zn, cn, seg_rows, DH), F32)],
        scalars=3,
    )
    attended = call(
        functools.partial(memory_kernel, zn, xn, cn, heads),
        (at, table, score_scale, sums, token, written, group, *others),
        [shape((cn, seg_rows, DH))] * zn,
        [
            pltpu.VMEM((xn, zn, slots, 2 * DH), F32),
            pltpu.VMEM((zn, cn, seg_rows, DH), BF16),
        ],
        scalars=3,
    )

    here = []
    for j, block in enumerate(attended):
        block = over_z(block, j) if j else block
        here += [over_c(block, m) if m else block for m in range(cn)]

    columns = []
    for part in gather_z(after(w_out, pieces[last][0])):
        columns += [over_x(part, k) if k else part for k in range(xn)]
    out_cols = w_out.shape[1]
    blocks = feat_local // (cn * out_cols)
    products = call(
        functools.partial(out_kernel, zn, xn, cn, n_head),
        (at, *here, *columns),
        [shape((blocks, seg_rows, out_cols))] * (cn * n_head),
        [pltpu.VMEM((cn * seg_rows, heads * DH), BF16)],
        2 * cn * seg_rows * heads * DH * zn * xn * out_cols,
    )
    mine = []
    for r in range(n_head):
        for m in range(cn):
            block = products[r * cn + m]
            block = over_c(block, m) if m else block
            mine.append(over_y(block, r) if r else block)
    (branch,) = call(
        functools.partial(sum_kernel, n_head, cn),
        (at, *mine),
        [shape((seg_rows, feat_local))],
    )
    return branch


def solution(mesh):
    return jax.shard_map(
        body,
        mesh=mesh,
        in_specs=(
            P("seq", "head"),
            P(),
            P("seq", "head"),
            P("seq", "head"),
            P("seq", "head"),
            P("head", "seq"),
            P(None, "head"),
            P("head"),
            P("seq", "head"),
            P("seq"),
        ),
        out_specs=P("seq", "head"),
        check_vma=False,
    )
```

time: 498 us -> 220 us (0.44)
  waiting for transfers between devices: 435 us -> 131 us
  starting transfers between devices: 0.23 us -> 45.7 us
  Pallas kernels: 0 us -> 29.6 us
  matrix products: 24.5 us -> 0 us
  blocking collectives: 18.8 us -> 0 us
  between operations: 14.3 us -> 0.93 us
  local copies, waits for them, and re-layouts: 1.2 us -> 11.7 us
    all_gather x6 -> x0, waiting for transfers between devices: 414 us -> none  [the longest x1 122 us: carried_in(): gathered = jax.tree.map(lambda a: lax.all_gather(a, axis), part)]
    ppermute x0 -> x43, waiting for transfers between devices: none -> 131 us  [the longest x15 82.2 us: over_z(): return lax.ppermute(a, 'seq', pairs)]
    ppermute x0 -> x43, starting transfers between devices: none -> 45.7 us  [the longest x15 24.4 us: over_z(): return lax.ppermute(a, 'seq', pairs)]
    pallas_call x0 -> x12, Pallas kernels: none -> 29.6 us  [call(): pl.pallas_call(kernel, in_specs=[SMEM] * scalars + [VMEM] * (len(ins) - s...]
    dot_general x9 -> x0, matrix products: 24.5 us -> none  [the longest x3 15.1 us: body(): jnp.dot(normed, piece, preferred_element_type=jnp.float32)]
    all_gather x1 -> x0, blocking collectives: 18.8 us -> none  [carried_in(): gathered = jax.tree.map(lambda a: lax.all_gather(a, axis), part)]
    reduce_scatter x1 -> x0, waiting for transfers between devices: 18.7 us -> none  [body(): lax.psum_scatter(partial_rows.astype(jnp.bfloat16), 'head', scatter_dimen...]
    unnamed x10 -> x50, local copies, waits for them, and re-layouts: 0.03 us -> 11.6 us
  transfers between devices with their start and end apart: 7 -> 43, of which waited for: 7 -> 20; matrix products, arithmetic and copies ran while one was open for 5% -> 0% of each run, Pallas kernels for 0% -> 11%
where the time goes in v2:
time: 220 us; the launch traced here: 219 us
  waiting for transfers between devices  131 us (60%)
  starting transfers between devices  45.7 us (21%)
  Pallas kernels  29.6 us (13%)
  local copies, waits for them, and re-layouts  11.7 us (5%)
    ppermute x15, waiting for transfers between devices, over_z(): return lax.ppermute(a, 'seq', pairs)  82.2 us
    ppermute x10, waiting for transfers between devices, over_x(): return lax.ppermute(a, 'seq', pairs)  34 us
    pallas_call x12, Pallas kernels, call(): pl.pallas_call(kernel, in_specs=[SMEM] * scalars + [VMEM] * (len(ins) - s...  29.6 us
    ppermute x15, starting transfers between devices, over_z(): return lax.ppermute(a, 'seq', pairs)  24.4 us
    ppermute x6, waiting for transfers between devices, over_y(): lax.ppermute(a, 'head', [(h, (h + k) % n_head) for h in range(n_head)])  13.2 us
    ppermute x10, starting transfers between devices, over_x(): return lax.ppermute(a, 'seq', pairs)  11.9 us
    unnamed x50, local copies, waits for them, and re-layouts  11.6 us
    ppermute x6, starting transfers between devices, over_y(): lax.ppermute(a, 'head', [(h, (h + k) % n_head) for h in range(n_head)])  7.6 us
  transfers between devices with their start and end apart: 43, of which 20 were waited for; matrix products, arithmetic and copies ran while one was open for 0% of the time, Pallas kernels for 11%

profile of v2, /device:TPU:0, one launch (start us, length us, event | category | flops | bytes accessed | tf_op | source)
XLA Modules:
  0.0 219.0 jit_solution(14569070127619027823)
XLA Ops:
  0.0 4.0 %collective-permute-start = (bf16[128,2048]{1,0:T(8,128)(2,1)}, bf16[128,2048]{1,0:T(8,128)(2,1)S(1)}, u32[]{:S(2)}, u32[]{:S(2)}) collective-permute-start(bf16[128,2048]{1,0:T(8,128)(2,1)} %refs_0_.2), channel_id=1, source_target_pairs={{0,16},{2,18},{4,20},{6,22},{8,24},{10,26},{12,28},{14,30},{16,0},... | collective-permute-start | bytes 1572872 | tf_op jit(solution)/shard_map/ppermute | solution.py:269
  11.5 16.1 %collective-permute-done.refs_0_ = bf16[128,2048]{1,0:T(8,128)(2,1)S(1)} collective-permute-done((bf16[128,2048]{1,0:T(8,128)(2,1)}, bf16[128,2048]{1,0:T(8,128)(2,1)S(1)}, u32[]{:S(2)}, u32[]{:S(2)}) %collective-permute-start) | collective-permute-done | bytes 524320 | tf_op jit(solution)/shard_map/ppermute | solution.py:269
  36.7 8.8 %collective-permute-done.3 = f32[2,2,9]{2,1,0:T(2,128)S(1)} collective-permute-done((f32[2,2,9]{2,1,0:T(2,128)S(1)}, f32[2,2,9]{2,1,0:T(2,128)S(1)}, u32[]{:S(2)}, u32[]{:S(2)}) %collective-permute-start.3) | collective-permute-done | bytes 176 | tf_op jit(solution)/shard_map/ppermute | solution.py:269
  46.6 3.9 %collective-permute-done.4 = f32[2,2,9]{2,1,0:T(2,128)S(1)} collective-permute-done((f32[2,2,9]{2,1,0:T(2,128)S(1)}, f32[2,2,9]{2,1,0:T(2,128)S(1)}, u32[]{:S(2)}, u32[]{:S(2)}) %collective-permute-start.4) | collective-permute-done | bytes 176 | tf_op jit(solution)/shard_map/ppermute | solution.py:269
  50.6 3.6 %collective-permute-done.5 = f32[2,2,9]{2,1,0:T(2,128)S(1)} collective-permute-done((f32[2,2,9]{2,1,0:T(2,128)S(1)}, f32[2,2,9]{2,1,0:T(2,128)S(1)}, u32[]{:S(2)}, u32[]{:S(2)}) %collective-permute-start.5) | collective-permute-done | bytes 176 | tf_op jit(solution)/shard_map/ppermute | solution.py:269
  55.0 2.0 collective-permute-start.20
  60.4 2.4 %collective-permute-start.17 = (bf16[2,256,384]{2,1,0:T(8,128)(2,1)S(1)}, bf16[2,256,384]{2,1,0:T(8,128)(2,1)}, u32[]{:S(2)}, u32[]{:S(2)}) collective-permute-start(bf16[2,256,384]{2,1,0:T(8,128)(2,1)S(1)} %get-tuple-element.32), channel_id=1, source_target_pairs={{0,24},{2,26},{4,28},{6,30},{8,16},{10,18},{12,20},{14,22},{16,8},... | collective-permute-start | bytes 1179656 | tf_op jit(solution)/shard_map/ppermute | solution.py:269
  62.8 12.3 %collective-permute-done.22.refs_12_ = bf16[2,256,384]{2,1,0:T(8,128)(2,1)S(1)} collective-permute-done((bf16[2,256,384]{2,1,0:T(8,128)(2,1)S(1)}, bf16[2,256,384]{2,1,0:T(8,128)(2,1)S(1)}, u32[]{:S(2)}, u32[]{:S(2)}) %collective-permute-start.22) | collective-permute-done | bytes 393248 | tf_op jit(solution)/shard_map/ppermute | solution.py:269
  76.6 3.7 %collective-permute-done.20.refs_10_ = bf16[2,256,384]{2,1,0:T(8,128)(2,1)S(1)} collective-permute-done((bf16[2,256,384]{2,1,0:T(8,128)(2,1)S(1)}, bf16[2,256,384]{2,1,0:T(8,128)(2,1)S(1)}, u32[]{:S(2)}, u32[]{:S(2)}) %collective-permute-start.20) | collective-permute-done | bytes 393248 | tf_op jit(solution)/shard_map/ppermute | solution.py:269
  84.3 2.8 %collective-permute-done.19.refs_9_ = bf16[2,256,384]{2,1,0:T(8,128)(2,1)S(1)} collective-permute-done((bf16[2,256,384]{2,1,0:T(8,128)(2,1)S(1)}, bf16[2,256,384]{2,1,0:T(8,128)(2,1)S(1)}, u32[]{:S(2)}, u32[]{:S(2)}) %collective-permute-start.19) | collective-permute-done | bytes 393248 | tf_op jit(solution)/shard_map/ppermute | solution.py:276
  88.4 6.5 %collective-permute-start.35 = (bf16[1024,256]{1,0:T(8,128)(2,1)S(1)}, bf16[1024,256]{1,0:T(8,128)(2,1)}, u32[]{:S(2)}, u32[]{:S(2)}) collective-permute-start(bf16[1024,256]{1,0:T(8,128)(2,1)S(1)} %copy-done.6), channel_id=1, source_target_pairs={{0,16},{2,18},{4,20},{6,22},{8,24},{10,26},{12,28},{14,30},{16,0},... | collective-permute-start | bytes 1572872 | tf_op jit(solution)/shard_map/ppermute | solution.py:269
  97.6 5.2 %collective-permute-done.21.refs_11_ = bf16[2,256,384]{2,1,0:T(8,128)(2,1)S(1)} collective-permute-done((bf16[2,256,384]{2,1,0:T(8,128)(2,1)S(1)}, bf16[2,256,384]{2,1,0:T(8,128)(2,1)S(1)}, u32[]{:S(2)}, u32[]{:S(2)}) %collective-permute-start.21) | collective-permute-done | bytes 393248 | tf_op jit(solution)/shard_map/ppermute | solution.py:276
  103.5 14.9 %collective-permute-done.35.refs_12_ = bf16[1024,256]{1,0:T(8,128)(2,1)} collective-permute-done((bf16[1024,256]{1,0:T(8,128)(2,1)S(1)}, bf16[1024,256]{1,0:T(8,128)(2,1)}, u32[]{:S(2)}, u32[]{:S(2)}) %collective-permute-start.35) | collective-permute-done | bytes 524320 | tf_op jit(solution)/shard_map/ppermute | solution.py:269
  118.4 10.0 %collective-permute-done.33.refs_10_ = bf16[1024,256]{1,0:T(8,128)(2,1)} collective-permute-done((bf16[1024,256]{1,0:T(8,128)(2,1)S(1)}, bf16[1024,256]{1,0:T(8,128)(2,1)}, u32[]{:S(2)}, u32[]{:S(2)}) %collective-permute-start.33) | collective-permute-done | bytes 524320 | tf_op jit(solution)/shard_map/ppermute | solution.py:269
  131.8 5.9 %collective-permute-done.37.refs_14_ = bf16[1024,256]{1,0:T(8,128)(2,1)} collective-permute-done((bf16[1024,256]{1,0:T(8,128)(2,1)}, bf16[1024,256]{1,0:T(8,128)(2,1)}, u32[]{:S(2)}, u32[]{:S(2)}) %collective-permute-start.37) | collective-permute-done | bytes 524320 | tf_op jit(solution)/shard_map/ppermute | solution.py:269
  145.9 7.4 %shard_map.106.refs_11_ = f32[4,256,384]{2,1,0:T(8,128)} custom-call(s32[4]{0:T(128)S(1)} %pad_add_fusion.at, bf16[128,4096]{1,0:T(8,128)(2,1)S(1)} %shard_map.100.refs_0_, bf16[128,4096]{1,0:T(8,128)(2,1)S(1)} %copy-done.3, bf16[128,4096]{1,0:T(8,128)(2,1)S(1)} %shard_map.101.refs_2_, bf16[128,4096]{1,0:T(8,128)(2,1)} %collective-permute-done.10.refs_3_, ...), custom_call_target="tpu_custom_call" | custom-call | flops 2415919104 | bytes 12320784 | tf_op jit(solution)/shard_map/pallas_call | solution.py:25
  153.3 5.6 %shard_map.107 = (bf16[4,2,128,384]{3,2,1,0:T(8,128)(2,1)S(1)}, f32[4,2,128,256]{3,2,1,0:T(8,128)S(1)}, f32[4,128,256]{2,1,0:T(8,128)S(1)}, bf16[4,128,256]{2,1,0:T(8,128)(2,1)S(1)}) custom-call(s32[4]{0:T(128)S(1)} %pad_add_fusion.at, f32[144]{0:T(256)S(1)} %reshape.3.table, bf16[128,4096]{1,0:T(8,128)(2,1)S(1)} %shard_map.100.refs_0_, ...), custom_call_target="tpu_custom_call" | custom-call | flops 805306368 | bytes 13632080 | tf_op jit(solution)/shard_map/pallas_call | solution.py:25
  162.4 24.0 %collective-permute-done.24.refs_0_ = bf16[4,128,256]{2,1,0:T(8,128)(2,1)S(1)} collective-permute-done((bf16[4,128,256]{2,1,0:T(8,128)(2,1)S(1)}, bf16[4,128,256]{2,1,0:T(8,128)(2,1)S(1)}, u32[]{:S(2)}, u32[]{:S(2)}) %collective-permute-start.24) | collective-permute-done | bytes 262176 | tf_op jit(solution)/shard_map/ppermute | solution.py:276
  186.4 2.3 %shard_map.109 = (bf16[2,128,128]{2,1,0:T(8,128)(2,1)S(1)}, bf16[2,128,128]{2,1,0:T(8,128)(2,1)S(1)}, bf16[2,128,128]{2,1,0:T(8,128)(2,1)S(1)}, bf16[2,128,128]{2,1,0:T(8,128)(2,1)S(1)}) custom-call(s32[4]{0:T(128)S(1)} %pad_add_fusion.at, f32[144]{0:T(256)S(1)} %reshape.3.table, f32[8]{0:T(128)S(1)} %copy-done.23, ...), custom_call_target="tpu_custom_call" | custom-call | bytes 3408496 | tf_op jit(solution)/shard_map/pallas_call | solution.py:25
  190.7 2.5 %collective-permute-start.30 = (bf16[2,128,128]{2,1,0:T(8,128)(2,1)S(1)}, bf16[2,128,128]{2,1,0:T(8,128)(2,1)S(1)}, u32[]{:S(2)}, u32[]{:S(2)}) collective-permute-start(bf16[2,128,128]{2,1,0:T(8,128)(2,1)S(1)} %get-tuple-element.45), channel_id=1, source_target_pairs={{0,24},{2,26},{4,28},{6,30},{8,16},{10,18},{12,20},{14,22},{16,8},... | collective-permute-start | bytes 196616 | tf_op jit(solution)/shard_map/ppermute | solution.py:269
  194.1 2.7 %collective-permute-done.30.refs_6_ = bf16[2,128,128]{2,1,0:T(8,128)(2,1)S(1)} collective-permute-done((bf16[2,128,128]{2,1,0:T(8,128)(2,1)S(1)}, bf16[2,128,128]{2,1,0:T(8,128)(2,1)S(1)}, u32[]{:S(2)}, u32[]{:S(2)}) %collective-permute-start.30) | collective-permute-done | bytes 65568 | tf_op jit(solution)/shard_map/ppermute | solution.py:269
  198.0 4.9 %shard_map.110 = (bf16[4,128,256]{2,1,0:T(8,128)(2,1)S(1)}, bf16[4,128,256]{2,1,0:T(8,128)(2,1)S(1)}, bf16[4,128,256]{2,1,0:T(8,128)(2,1)S(1)}, bf16[4,128,256]{2,1,0:T(8,128)(2,1)S(1)}) custom-call(s32[4]{0:T(128)S(1)} %pad_add_fusion.at, bf16[2,128,128]{2,1,0:T(8,128)(2,1)S(1)} %get-tuple-element.42.refs_0_, ...), custom_call_target="tpu_custom_call" | custom-call | flops 1073741824 | bytes 5767184 | tf_op jit(solution)/shard_map/pallas_call | solution.py:25
  206.1 6.6 %collective-permute-done.40.refs_2_ = bf16[4,128,256]{2,1,0:T(8,128)(2,1)S(1)} collective-permute-done((bf16[4,128,256]{2,1,0:T(8,128)(2,1)S(1)}, bf16[4,128,256]{2,1,0:T(8,128)(2,1)S(1)}, u32[]{:S(2)}, u32[]{:S(2)}) %collective-permute-start.40) | collective-permute-done | bytes 262176 | tf_op jit(solution)/shard_map/ppermute | solution.py:282
  212.7 4.8 %collective-permute-done.42.refs_3_ = bf16[4,128,256]{2,1,0:T(8,128)(2,1)S(1)} collective-permute-done((bf16[4,128,256]{2,1,0:T(8,128)(2,1)S(1)}, bf16[4,128,256]{2,1,0:T(8,128)(2,1)S(1)}, u32[]{:S(2)}, u32[]{:S(2)}) %collective-permute-start.42) | collective-permute-done | bytes 262176 | tf_op jit(solution)/shard_map/ppermute | solution.py:282
  (130 shorter events, 55.1 us)
Async XLA Ops:
  0.0 27.6 %collective-permute-start = (bf16[128,2048]{1,0:T(8,128)(2,1)}, bf16[128,2048]{1,0:T(8,128)(2,1)S(1)}, u32[]{:S(2)}, u32[]{:S(2)}) collective-permute-start(bf16[128,2048]{1,0:T(8,128)(2,1)} %refs_0_.2), channel_id=1, source_target_pairs={{0,16},{2,18},{4,20},{6,22},{8,24},{10,26},{12,28},{14,30},{16,0},... | collective-permute-start | bytes 1572872 | tf_op jit(solution)/shard_map/ppermute | solution.py:269
  4.0 25.0 %collective-permute-start.6 = (bf16[128,2048]{1,0:T(8,128)(2,1)}, bf16[128,2048]{1,0:T(8,128)(2,1)S(1)}, u32[]{:S(2)}, u32[]{:S(2)}) collective-permute-start(bf16[128,2048]{1,0:T(8,128)(2,1)} %refs_0_.2), channel_id=1, source_target_pairs={{0,1},{1,0},{2,3},{3,2},{4,5},{5,4},{6,7},{7,6},{8,9},{9,8},{10,11... | collective-permute-start | bytes 1572872 | tf_op jit(solution)/shard_map/ppermute | solution.py:282
  9.7 36.3 %collective-permute-start.16 = (bf16[4,256,384]{2,1,0:T(8,128)(2,1)S(1)}, bf16[4,256,384]{2,1,0:T(8,128)(2,1)S(1)}, u32[]{:S(2)}, u32[]{:S(2)}) collective-permute-start(bf16[4,256,384]{2,1,0:T(8,128)(2,1)S(1)} %get-tuple-element.30), channel_id=1, source_target_pairs={{0,2},{2,0},{4,6},{6,4},{8,10},{10,8},{12,14},{14,12},{16,18},{18,... | collective-permute-start | bytes 2359304 | tf_op jit(solution)/shard_map/ppermute | solution.py:279
  9.8 25.5 %collective-permute-start.8 = (bf16[128,2048]{1,0:T(8,128)(2,1)S(1)}, bf16[128,2048]{1,0:T(8,128)(2,1)S(1)}, u32[]{:S(2)}, u32[]{:S(2)}) collective-permute-start(bf16[128,2048]{1,0:T(8,128)(2,1)S(1)} %copy-done.5), channel_id=1, source_target_pairs={{0,8},{2,10},{4,12},{6,14},{8,0},{10,2},{12,4},{14,6},{16,24},{18,... | collective-permute-start | bytes 1572872 | tf_op jit(solution)/shard_map/ppermute | solution.py:269
  27.6 27.5 %collective-permute-start.13 = (bf16[128,2048]{1,0:T(8,128)(2,1)S(1)}, bf16[128,2048]{1,0:T(8,128)(2,1)S(1)}, u32[]{:S(2)}, u32[]{:S(2)}) collective-permute-start(bf16[128,2048]{1,0:T(8,128)(2,1)S(1)} %collective-permute-done.refs_0_), channel_id=1, source_target_pairs={{0,8},{2,10},{4,12},{6,14},{8,0},{10,2},{12,4},{14,6},{16,24},{18,... | collective-permute-start | bytes 1572872 | tf_op jit(solution)/shard_map/ppermute | solution.py:269
  31.7 56.6 %collective-permute-start.7 = (bf16[128,4096]{1,0:T(8,128)(2,1)S(1)}, bf16[128,4096]{1,0:T(8,128)(2,1)S(1)}, u32[]{:S(2)}, u32[]{:S(2)}) collective-permute-start(bf16[128,4096]{1,0:T(8,128)(2,1)S(1)} %shard_map.100.refs_0_), channel_id=1, source_target_pairs={{0,2},{2,0},{4,6},{6,4},{8,10},{10,8},{12,14},{14,12},{16,18},{18,... | collective-permute-start | bytes 3145736 | tf_op jit(solution)/shard_map/ppermute | solution.py:279
  33.8 23.3 %collective-permute-start.11 = (bf16[128,2048]{1,0:T(8,128)(2,1)S(1)}, bf16[128,2048]{1,0:T(8,128)(2,1)S(1)}, u32[]{:S(2)}, u32[]{:S(2)}) collective-permute-start(bf16[128,2048]{1,0:T(8,128)(2,1)S(1)} %collective-permute-done.refs_0_), channel_id=1, source_target_pairs={{0,1},{1,0},{2,3},{3,2},{4,5},{5,4},{6,7},{7,6},{8,9},{9,8},{10,11... | collective-permute-start | bytes 1572872 | tf_op jit(solution)/shard_map/ppermute | solution.py:282
  54.1 21.0 %collective-permute-start.22 = (bf16[2,256,384]{2,1,0:T(8,128)(2,1)S(1)}, bf16[2,256,384]{2,1,0:T(8,128)(2,1)S(1)}, u32[]{:S(2)}, u32[]{:S(2)}) collective-permute-start(bf16[2,256,384]{2,1,0:T(8,128)(2,1)S(1)} %get-tuple-element.37), channel_id=1, source_target_pairs={{0,16},{2,18},{4,20},{6,22},{8,24},{10,26},{12,28},{14,30},{16,0},... | collective-permute-start | bytes 1179656 | tf_op jit(solution)/shard_map/ppermute | solution.py:269
  55.0 25.2 %collective-permute-start.20 = (bf16[2,256,384]{2,1,0:T(8,128)(2,1)S(1)}, bf16[2,256,384]{2,1,0:T(8,128)(2,1)S(1)}, u32[]{:S(2)}, u32[]{:S(2)}) collective-permute-start(bf16[2,256,384]{2,1,0:T(8,128)(2,1)S(1)} %get-tuple-element.35), channel_id=1, source_target_pairs={{0,8},{2,10},{4,12},{6,14},{8,0},{10,2},{12,4},{14,6},{16,24},{18,... | collective-permute-start | bytes 1179656 | tf_op jit(solution)/shard_map/ppermute | solution.py:269
  57.1 30.8 %collective-permute-start.14 = (bf16[128,2048]{1,0:T(8,128)(2,1)S(1)}, bf16[128,2048]{1,0:T(8,128)(2,1)S(1)}, u32[]{:S(2)}, u32[]{:S(2)}) collective-permute-start(bf16[128,2048]{1,0:T(8,128)(2,1)S(1)} %collective-permute-done.13.refs_0_), channel_id=1, source_target_pairs={{0,1},{1,0},{2,3},{3,2},{4,5},{5,4},{6,7},{7,6},{8,9},{9,8},{10,11... | collective-permute-start | bytes 1572872 | tf_op jit(solution)/shard_map/ppermute | solution.py:282
  60.4 21.4 %collective-permute-start.17 = (bf16[2,256,384]{2,1,0:T(8,128)(2,1)S(1)}, bf16[2,256,384]{2,1,0:T(8,128)(2,1)}, u32[]{:S(2)}, u32[]{:S(2)}) collective-permute-start(bf16[2,256,384]{2,1,0:T(8,128)(2,1)S(1)} %get-tuple-element.32), channel_id=1, source_target_pairs={{0,24},{2,26},{4,28},{6,30},{8,16},{10,18},{12,20},{14,22},{16,8},... | collective-permute-start | bytes 1179656 | tf_op jit(solution)/shard_map/ppermute | solution.py:269
  81.8 21.0 %collective-permute-start.21 = (bf16[2,256,384]{2,1,0:T(8,128)(2,1)S(1)}, bf16[2,256,384]{2,1,0:T(8,128)(2,1)S(1)}, u32[]{:S(2)}, u32[]{:S(2)}) collective-permute-start(bf16[2,256,384]{2,1,0:T(8,128)(2,1)S(1)} %collective-permute-done.20.refs_10_), channel_id=1, source_target_pairs={{0,4},{2,6},{4,0},{6,2},{8,12},{10,14},{12,8},{14,10},{16,20},{18,... | collective-permute-start | bytes 1179656 | tf_op jit(solution)/shard_map/ppermute | solution.py:276
  87.8 41.8 %collective-permute-start.10 = (bf16[128,4096]{1,0:T(8,128)(2,1)S(1)}, bf16[128,4096]{1,0:T(8,128)(2,1)}, u32[]{:S(2)}, u32[]{:S(2)}) collective-permute-start(bf16[128,4096]{1,0:T(8,128)(2,1)S(1)} %shard_map.101.refs_2_), channel_id=1, source_target_pairs={{0,2},{2,0},{4,6},{6,4},{8,10},{10,8},{12,14},{14,12},{16,18},{18,... | collective-permute-start | bytes 3145736 | tf_op jit(solution)/shard_map/ppermute | solution.py:279
  87.8 42.8 %collective-permute-start.12 = (bf16[128,4096]{1,0:T(8,128)(2,1)S(1)}, bf16[128,4096]{1,0:T(8,128)(2,1)}, u32[]{:S(2)}, u32[]{:S(2)}) collective-permute-start(bf16[128,4096]{1,0:T(8,128)(2,1)S(1)} %shard_map.102.refs_4_), channel_id=1, source_target_pairs={{0,2},{2,0},{4,6},{6,4},{8,10},{10,8},{12,14},{14,12},{16,18},{18,... | collective-permute-start | bytes 3145736 | tf_op jit(solution)/shard_map/ppermute | solution.py:279
  88.4 30.0 %collective-permute-start.35 = (bf16[1024,256]{1,0:T(8,128)(2,1)S(1)}, bf16[1024,256]{1,0:T(8,128)(2,1)}, u32[]{:S(2)}, u32[]{:S(2)}) collective-permute-start(bf16[1024,256]{1,0:T(8,128)(2,1)S(1)} %copy-done.6), channel_id=1, source_target_pairs={{0,16},{2,18},{4,20},{6,22},{8,24},{10,26},{12,28},{14,30},{16,0},... | collective-permute-start | bytes 1572872 | tf_op jit(solution)/shard_map/ppermute | solution.py:269
  97.6 41.6 %collective-permute-start.15 = (bf16[128,4096]{1,0:T(8,128)(2,1)}, bf16[128,4096]{1,0:T(8,128)(2,1)}, u32[]{:S(2)}, u32[]{:S(2)}) collective-permute-start(bf16[128,4096]{1,0:T(8,128)(2,1)} %shard_map.103.refs_6_), channel_id=1, source_target_pairs={{0,2},{2,0},{4,6},{6,4},{8,10},{10,8},{12,14},{14,12},{16,18},{18,... | collective-permute-start | bytes 3145736 | tf_op jit(solution)/shard_map/ppermute | solution.py:279
  103.5 24.9 %collective-permute-start.33 = (bf16[1024,256]{1,0:T(8,128)(2,1)S(1)}, bf16[1024,256]{1,0:T(8,128)(2,1)}, u32[]{:S(2)}, u32[]{:S(2)}) collective-permute-start(bf16[1024,256]{1,0:T(8,128)(2,1)S(1)} %copy-done.6), channel_id=1, source_target_pairs={{0,8},{2,10},{4,12},{6,14},{8,0},{10,2},{12,4},{14,6},{16,24},{18,... | collective-permute-start | bytes 1572872 | tf_op jit(solution)/shard_map/ppermute | solution.py:269
  118.4 19.3 %collective-permute-start.37 = (bf16[1024,256]{1,0:T(8,128)(2,1)}, bf16[1024,256]{1,0:T(8,128)(2,1)}, u32[]{:S(2)}, u32[]{:S(2)}) collective-permute-start(bf16[1024,256]{1,0:T(8,128)(2,1)} %collective-permute-done.35.refs_12_), channel_id=1, source_target_pairs={{0,8},{2,10},{4,12},{6,14},{8,0},{10,2},{12,4},{14,6},{16,24},{18,... | collective-permute-start | bytes 1572872 | tf_op jit(solution)/shard_map/ppermute | solution.py:269
  128.4 24.9 %collective-permute-start.18 = (bf16[2,256,384]{2,1,0:T(8,128)(2,1)}, bf16[2,256,384]{2,1,0:T(8,128)(2,1)}, u32[]{:S(2)}, u32[]{:S(2)}) collective-permute-start(bf16[2,256,384]{2,1,0:T(8,128)(2,1)} %collective-permute-done.17.refs_8_), channel_id=1, source_target_pairs={{0,4},{2,6},{4,0},{6,2},{8,12},{10,14},{12,8},{14,10},{16,20},{18,... | collective-permute-start | bytes 1179656 | tf_op jit(solution)/shard_map/ppermute | solution.py:276
  129.7 59.2 %collective-permute-start.32 = (bf16[1024,256]{1,0:T(8,128)(2,1)}, bf16[1024,256]{1,0:T(8,128)(2,1)S(1)}, u32[]{:S(2)}, u32[]{:S(2)}) collective-permute-start(bf16[1024,256]{1,0:T(8,128)(2,1)} %refs_8_), channel_id=1, source_target_pairs={{0,4},{2,6},{4,0},{6,2},{8,12},{10,14},{12,8},{14,10},{16,20},{18,... | collective-permute-start | bytes 1572872 | tf_op jit(solution)/shard_map/ppermute | solution.py:276
  130.6 60.1 %collective-permute-start.36 = (bf16[1024,256]{1,0:T(8,128)(2,1)}, bf16[1024,256]{1,0:T(8,128)(2,1)S(1)}, u32[]{:S(2)}, u32[]{:S(2)}) collective-permute-start(bf16[1024,256]{1,0:T(8,128)(2,1)} %collective-permute-done.35.refs_12_), channel_id=1, source_target_pairs={{0,4},{2,6},{4,0},{6,2},{8,12},{10,14},{12,8},{14,10},{16,20},{18,... | collective-permute-start | bytes 1572872 | tf_op jit(solution)/shard_map/ppermute | solution.py:276
  137.6 55.6 %collective-permute-start.34 = (bf16[1024,256]{1,0:T(8,128)(2,1)}, bf16[1024,256]{1,0:T(8,128)(2,1)S(1)}, u32[]{:S(2)}, u32[]{:S(2)}) collective-permute-start(bf16[1024,256]{1,0:T(8,128)(2,1)} %collective-permute-done.33.refs_10_), channel_id=1, source_target_pairs={{0,4},{2,6},{4,0},{6,2},{8,12},{10,14},{12,8},{14,10},{16,20},{18,... | collective-permute-start | bytes 1572872 | tf_op jit(solution)/shard_map/ppermute | solution.py:276
  139.1 57.6 %collective-permute-start.38 = (bf16[1024,256]{1,0:T(8,128)(2,1)}, bf16[1024,256]{1,0:T(8,128)(2,1)S(1)}, u32[]{:S(2)}, u32[]{:S(2)}) collective-permute-start(bf16[1024,256]{1,0:T(8,128)(2,1)} %collective-permute-done.37.refs_14_), channel_id=1, source_target_pairs={{0,4},{2,6},{4,0},{6,2},{8,12},{10,14},{12,8},{14,10},{16,20},{18,... | collective-permute-start | bytes 1572872 | tf_op jit(solution)/shard_map/ppermute | solution.py:276
  158.9 27.5 %collective-permute-start.24 = (bf16[4,128,256]{2,1,0:T(8,128)(2,1)S(1)}, bf16[4,128,256]{2,1,0:T(8,128)(2,1)S(1)}, u32[]{:S(2)}, u32[]{:S(2)}) collective-permute-start(bf16[4,128,256]{2,1,0:T(8,128)(2,1)S(1)} %get-tuple-element.41), channel_id=1, source_target_pairs={{0,4},{2,6},{4,0},{6,2},{8,12},{10,14},{12,8},{14,10},{16,20},{18,... | collective-permute-start | bytes 786440 | tf_op jit(solution)/shard_map/ppermute | solution.py:276
  (44 other events, 324.7 us)

commit v3 on v2

v3 whole, which is shorter than its diff:
```python
import functools
import math

import jax
import jax.numpy as jnp
from jax import lax
from jax.experimental import pallas as pl
from jax.experimental.pallas import tpu as pltpu
from jax.sharding import PartitionSpec as P

DH = 128
META = 16
F32 = jnp.float32
BF16 = jnp.bfloat16


def dot(a, b, contract=(1, 0)):
    dims = (((contract[0],), (contract[1],)), ((), ()))
    return lax.dot_general(a, b, dims, preferred_element_type=F32)


def call(kernel, ins, outs, scratch=(), flops=0, scalars=1, column=None, room=20):
    moved = sum(math.prod(a.shape) * a.dtype.itemsize for a in (*ins, *outs))

    def whole(a):
        return pl.BlockSpec(a.shape, lambda i, *_: (0,) * len(a.shape))

    def spec(a):
        if column and a.shape[-1] > column[0] and a.ndim == 2 and a.dtype == BF16:
            pick = column[1]
            return pl.BlockSpec((a.shape[0], column[0]), lambda i, at, *_: (0, pick(at)))
        return whole(a)

    return pl.pallas_call(
        kernel,
        grid_spec=pltpu.PrefetchScalarGridSpec(
            num_scalar_prefetch=scalars,
            grid=(1,),
            in_specs=[spec(a) for a in ins[scalars:]],
            out_specs=[whole(a) for a in outs],
            scratch_shapes=scratch,
        ),
        out_shape=outs,
        compiler_params=pltpu.CompilerParams(vmem_limit_bytes=room * 2**20),
        cost_estimate=pl.CostEstimate(flops=flops, bytes_accessed=moved, transcendentals=0),
    )(*ins)


def lanes(index, size):
    return pl.ds(pl.multiple_of(index * size, size), size)


def cut_kernel(cn, at, decay, seg_len, *refs):
    weights, outs = refs[:3], refs[3:]
    w_rows = weights[0].shape[0]
    row = lax.broadcasted_iota(jnp.int32, (META, DH), 0)
    length = jnp.full((META, DH), seg_len[0], jnp.int32).astype(F32)
    for j, out in enumerate(outs):
        for e in range(cn):
            head = (at[0] ^ j) * cn + e
            rest = jnp.full((META, DH), decay[head], F32)
            for i, w in enumerate(weights):
                first = (e * 3 + i) * DH
                out[:w_rows, first : first + DH] = w[:, lanes(head, DH)]
                term = rest.astype(BF16).astype(F32)
                rest = rest - term
                out[w_rows:, first : first + DH] = jnp.where(row < META // 2, term, length).astype(BF16)


def norm_kernel(n_head, at, gain, *refs):
    parts, out = refs[:n_head], refs[n_head]
    feat = parts[0].shape[1]
    wide = [part[...].astype(F32) for part in parts]
    squares = sum(jnp.sum(w * w, axis=1, keepdims=True) for w in wide)
    inverse = lax.rsqrt(squares / (feat * n_head) + 1e-05)
    for k, w in enumerate(wide):
        half = lanes(lax.rem(at[3] + n_head - k, n_head), feat)
        out[:, half] = (w * inverse * gain[:, half]).astype(BF16)


def project(xn, cn, at, rows, weights, chunk, meta, each):
    x, c = at[1], at[2]
    w_rows = weights[0].shape[0] - META
    row = lax.broadcasted_iota(jnp.int32, (META, DH), 0)
    for n, w in enumerate(weights):
        xi, ci = lax.rem(x + xn - n // cn, xn), c ^ (n % cn)
        chunk[pl.ds(pl.multiple_of((xi * cn + ci) * w_rows, w_rows), w_rows), :] = w[:w_rows]
        tail = w[w_rows:].astype(F32)
        terms = tail[:, : 3 * DH]
        for e in range(1, cn):
            terms = jnp.where(c == e, tail[:, e * 3 * DH : (e + 1) * 3 * DH], terms)
        total = terms[:, :DH] + terms[:, DH : 2 * DH] + terms[:, 2 * DH :]
        meta[xi, ci] = jnp.where(row < META // 2, total, terms[:, :DH])
    for first in range(0, len(rows), 2):
        pair = range(first, min(first + 2, len(rows)))
        sums = dot(jnp.concatenate([rows[i][...] for i in pair]), chunk[...])
        for n, i in enumerate(pair):
            size = sums.shape[0] // len(pair)
            each(i, sums[n * size : (n + 1) * size])


def project_kernel(zn, xn, cn, steps, at, *refs):
    rows = refs[:zn]
    weights = refs[zn : zn + len(steps) * xn * cn]
    out, meta, chunk = refs[-3:]
    size = chunk.shape[1]
    for n, j in enumerate(steps):

        def each(i, sums):
            out[i] = sums if n == 0 else out[i] + sums

        part = [row.at[:, lanes(at[0] ^ j, size)] for row in rows]
        few = weights[n * xn * cn : (n + 1) * xn * cn]
        project(xn, cn, at, part, few, chunk.at[n], meta.at[n], each)


def finish_kernel(zn, xn, cn, at, *refs):
    rows = refs[:zn]
    weights = refs[zn : zn + xn * cn]
    before = refs[zn + xn * cn] if zn > 1 else None
    outs, meta, chunk = refs[-2 - cn : -2], refs[-2], refs[-1]
    c = at[2]

    def each(i, sums):
        sums = (sums if before is None else sums + before[i]).astype(BF16)
        heads = [sums[:, e * 3 * DH : (e + 1) * 3 * DH] for e in range(cn)]
        for m, out in enumerate(outs):
            pick = heads[m]
            for e in range(cn):
                if e != m:
                    pick = jnp.where((c ^ m) == e, heads[e], pick)
            out[i] = pick

    project(xn, cn, at, rows, weights, chunk, meta.at[0], each)


def segment_info(table):
    def retain(zi, xi, ci):
        return table[zi, xi, ci, 0:1, 0:1]

    def length(zi, xi, ci):
        return table[zi, xi, ci, META // 2 : META // 2 + 1, 0:1]

    return retain, length


def write_kernel(zn, xn, cn, at, *refs):
    parts, query, metas = refs[:cn], refs[cn], refs[cn + 1 : -5]
    sums, written, group, group16, table = refs[-5:]
    z, x, c = at[0], at[1], at[2]
    j = 0
    for meta in metas:
        for n in range(meta.shape[0]):
            table[z ^ j] = meta[n]
            j += 1
    retain, length = segment_info(table)
    seg_rows = sums.shape[2]
    for i in range(zn):
        for m in range(cn):
            sums[z ^ i, c ^ m] = parts[m][i]
    own = query[:, lanes(z * cn + c, DH)]
    slots = own.shape[0]
    position = lax.broadcasted_iota(jnp.int32, (slots, seg_rows), 1).astype(F32)
    for i in range(zn):
        keys = sums[i, :, :, DH : 2 * DH].reshape(cn * seg_rows, DH)
        scores = dot(own, keys, (1, 1)) * (1.0 / math.sqrt(DH))
        gates = jax.nn.sigmoid(scores - math.log(seg_rows))
        total = None
        for m in range(cn):
            gate = gates[:, m * seg_rows : (m + 1) * seg_rows]
            gate = jnp.where(position < length(i, x, m), gate, 0.0).astype(BF16)
            new = dot(gate, sums[i, m, :, DH:])
            written[i, m] = new
            total = new if total is None else retain(i, x, m) * total + new
        group[i] = total
        group16[i] = total.astype(BF16)


def token_kernel(zn, cn, slots, at, scale, table, sums, out):
    _, length = segment_info(table)
    seg_rows = sums.shape[2]
    shape = (seg_rows, seg_rows)
    row = lax.broadcasted_iota(jnp.int32, shape, 0)
    column = lax.broadcasted_iota(jnp.int32, shape, 1)
    factor = scale[at[0] * cn + at[2]] * (1.0 / math.sqrt(DH))
    for i in range(zn):
        for m in range(cn):
            query, keys, values = (sums[i, m, :, n * DH : (n + 1) * DH] for n in range(3))
            scores = dot(query, keys, (1, 1)) * factor
            gate = jax.nn.sigmoid(scores - math.log(slots + seg_rows))
            allowed = (column <= row) & (column.astype(F32) < length(i, at[1], m))
            out[i, m] = dot(jnp.where(allowed, gate, 0.0).astype(BF16), values)


def memory_kernel(zn, xn, cn, at, scale, table, sums, token, written, group, *refs):
    others = refs[: xn - 1]
    outs = refs[xn - 1 : xn - 1 + zn]
    groups, done = refs[-2:]
    z, x, c = at[0], at[1], at[2]
    retain, length = segment_info(table)
    slots, seg_rows = group.shape[1], sums.shape[2]
    factor = scale[z * cn + c] * (1.0 / math.sqrt(DH))
    bias = math.log(slots + seg_rows)
    row = lax.broadcasted_iota(jnp.int32, (seg_rows, DH), 0).astype(F32)
    groups[x] = group[...]
    for k, other in enumerate(others, 1):
        groups[lax.rem(x + xn - k, xn)] = other[...].astype(F32)
    memory = jnp.zeros(group.shape[1:], F32)
    for i in range(zn):
        entry = memory
        for k in range(xn):
            if k:
                entry = jnp.where(x == k, memory, entry)
            kept = retain(i, k, 0)
            for m in range(1, cn):
                kept = kept * retain(i, k, m)
            memory = kept * memory + groups[k, i]
        for m in range(cn):
            units = []
            for n in range(2):
                part = entry[:, n * DH : (n + 1) * DH]
                mean = jnp.mean(part * part, axis=1, keepdims=True)
                units.append((part * lax.rsqrt(mean + 1e-06)).astype(BF16))
            scores = dot(sums[i, m, :, :DH], units[0], (1, 1)) * factor
            gate = jax.nn.sigmoid(scores - bias).astype(BF16)
            total = dot(gate, units[1]) + token[i, m]
            done[i, m] = jnp.where(row < length(i, x, m), total, 0.0).astype(BF16)
            if m + 1 < cn:
                entry = retain(i, x, m) * entry + written[i, m]
    for j in range(zn):
        for m in range(cn):
            outs[j][m] = done[z ^ j, c ^ m]


def out_kernel(zn, xn, cn, n_head, at, *refs):
    attended = refs[: zn * cn]
    weights = refs[zn * cn : zn * cn + zn * xn]
    outs, rows = refs[-1 - cn * n_head : -1], refs[-1]
    z, x, c, y = at[0], at[1], at[2], at[3]
    seg_rows = attended[0].shape[1]
    for j in range(zn):
        for e in range(cn):
            for m in range(cn):
                rows[m * seg_rows : (m + 1) * seg_rows, lanes((z ^ j) * cn + (c ^ e), DH)] = (
                    attended[j * cn + e][m ^ e]
                )
    blocks = outs[0].shape[0]
    for j in range(zn):
        for k in range(xn):
            product = dot(rows[...], weights[j * xn + k][...]).astype(BF16)
            spot = (z ^ j) * xn + lax.rem(x + xn - k, xn)
            turn = lax.rem(spot // blocks + n_head - y, n_head)
            for r in range(n_head):

                @pl.when(turn == r)
                def _():
                    for m in range(cn):
                        outs[r * cn + m][lax.rem(spot, blocks)] = product[
                            m * seg_rows : (m + 1) * seg_rows
                        ]


def sum_kernel(n_head, cn, at, *refs):
    out = refs[-1]
    blocks, _, size = refs[0].shape
    for b in range(blocks):
        totals = [
            sum(refs[r * cn + e][b].astype(F32) for r in range(n_head)).astype(BF16)
            for e in range(cn)
        ]
        for m in range(cn):
            total = totals[0]
            for e in range(1, cn):
                total = jnp.where((at[2] ^ e) == m, totals[e], total)
            first = (b * cn + m) * size
            out[:, first : first + size] = total


def body(tokens, gain, w_query, w_key, w_value, w_out, mem_query, score_scale, decay, seg_len):
    n_seq = lax.axis_size("seq")
    n_head = lax.axis_size("head")
    seg_rows, feat_local = tokens.shape
    width = gain.shape[0]
    w_rows, col_local = w_query.shape
    heads = col_local // DH
    slots = mem_query.shape[0]
    cn = 2 if heads % 2 == 0 else 1
    zn = heads // cn
    xn = n_seq // heads
    place = lax.axis_index("seq")
    y = lax.axis_index("head")
    at = jnp.stack([place // (cn * xn), place // cn % xn, place % cn, y]).astype(jnp.int32)

    def shape(dims, dtype=BF16):
        return jax.ShapeDtypeStruct(dims, dtype)

    def split(s):
        return s // (cn * xn), s // cn % xn, s % cn

    def join(a, b, d):
        return (a * xn + b) * cn + d

    def over_z(a, j):
        pairs = [(s, join(split(s)[0] ^ j, *split(s)[1:])) for s in range(n_seq)]
        return lax.ppermute(a, "seq", pairs)

    def over_x(a, k):
        pairs = []
        for s in range(n_seq):
            sz, sx, sc = split(s)
            pairs.append((s, join(sz, (sx + k) % xn, sc)))
        return lax.ppermute(a, "seq", pairs)

    def over_c(a, m):
        return lax.ppermute(a, "seq", [(s, s ^ m) for s in range(n_seq)])

    def over_y(a, k):
        return lax.ppermute(a, "head", [(h, (h + k) % n_head) for h in range(n_head)])

    chain = []

    def mark(a):
        chain[:] = [a]
        return a

    def done(a):
        return mark(lax.optimization_barrier((a, *chain))[0])

    def done_all(parts):
        parts = lax.optimization_barrier((*parts, *chain))[: len(parts)]
        mark(parts[-1])
        return parts

    def after(a, b):
        return lax.optimization_barrier((a, b))[0]

    last = zn - 1
    tok, packs, pieces, rows = {0: tokens}, {}, {}, {}
    started, columns, out_z = {}, {}, {0: w_out}

    def begin_tok(j):
        low = j & -j
        if j < zn and j not in started and j ^ low in tok:
            started[j] = over_z(tok[j ^ low], low)

    def begin_y(j):
        started["y", j] = [over_y(tok[j], k) for k in range(1, n_head)]

    def end_y(j):
        parts = [tok[j]] + [done(part) for part in started["y", j]]
        (rows[j],) = call(
            functools.partial(norm_kernel, n_head),
            (at, gain[None], *parts),
            [shape((seg_rows, width))],
        )
        mark(rows[j])

    def both(a):
        return [over_c(a, m) if m else a for m in range(cn)]

    def begin_x(j):
        started["x", j] = [over_x(packs[j], k) for k in range(1, xn)]
        pieces[j] = both(packs[j])

    def end_x(j):
        for part in started["x", j]:
            pieces[j] += both(done(part))

    def begin_out(j, source):
        started["o", j] = [over_x(source, k) for k in range(1, xn)]
        columns[j] = [source]

    def end_out(j):
        columns[j] += [done(part) for part in started["o", j]]

    for bit in range(zn.bit_length() - 2, -1, -1):
        begin_tok(1 << bit)
    begin_y(0)
    begin_out(0, w_out)
    sent = call(
        functools.partial(cut_kernel, cn),
        (at, decay[0], seg_len, w_query, w_key, w_value),
        [shape((w_rows + META, cn * 3 * DH))] * zn,
        scalars=3,
    )
    packs[0] = sent[0]
    begin_x(0)
    if last:
        started["w", 1] = over_z(sent[1], 1)

    bits = [1 << n for n in range(zn.bit_length() - 1)]
    more = [j for j in range(1, zn) if j not in bits]
    if bits:
        for b, part in zip(bits, done_all([started[b] for b in bits])):
            tok[b] = part
            begin_y(b)
    for j in more:
        begin_tok(j)
    for j in range(2, min(3, zn)):
        started["w", j] = over_z(after(sent[j], tok[1]), j)
    end_y(0)
    ready = []
    for j in range(1, zn):
        if j == 2:
            ready = done_all([started["w", 2], *(started[i] for i in more)])
            packs[2] = ready[0]
            for i, part in zip(more, ready[1:]):
                tok[i] = part
                begin_y(i)
        elif j == last:
            first = over_z(after(w_out, packs[j - 1]), 1)
            packs[j], out_z[1] = done_all([started["w", j], first])
        else:
            packs[j] = done(started["w", j])
        begin_x(j)
        if j > 1 and j + 1 < zn:
            started["w", j + 1] = over_z(after(sent[j + 1], packs[j]), j + 1)
        end_y(j)
        end_x(j - 1)
        if j == 1:
            end_out(0)
    for b in bits[1:]:
        started["oz", b] = over_z(after(w_out, packs[last]), b)
    if not last:
        end_out(0)
    rows = [rows[j] for j in range(zn)]

    chunk_rows = xn * cn * w_rows
    flops = 2 * zn * seg_rows * chunk_rows * cn * 3 * DH
    before = []
    if last:
        before = call(
            functools.partial(project_kernel, zn, xn, cn, range(last)),
            (at, *rows, *sum((pieces[j] for j in range(last)), [])),
            [
                shape((zn, seg_rows, cn * 3 * DH), F32),
                shape((last, xn, cn, META, DH), F32),
            ],
            [pltpu.VMEM((last, chunk_rows, cn * 3 * DH), BF16)],
            flops * last,
            room=48,
        )
        mark(before[0])
    end_x(last)
    *parts, meta = call(
        functools.partial(finish_kernel, zn, xn, cn),
        (at, *rows, *pieces[last], *before[:1]),
        [shape((zn, seg_rows, 3 * DH))] * cn + [shape((1, xn, cn, META, DH), F32)],
        [pltpu.VMEM((chunk_rows, cn * 3 * DH), BF16)],
        flops,
        column=(chunk_rows, lambda at: at[0] ^ last),
        room=32,
    )
    if last:
        begin_out(1, out_z[1])
    parts = [done(over_c(part, m)) if m else part for m, part in enumerate(parts)]
    sums, written, group, group16, table = call(
        functools.partial(write_kernel, zn, xn, cn),
        (at, *parts, mem_query, *before[1:], meta),
        [
            shape((zn, cn, seg_rows, 3 * DH)),
            shape((zn, cn, slots, 2 * DH), F32),
            shape((zn, slots, 2 * DH), F32),
            shape((zn, slots, 2 * DH)),
            shape((zn, xn, cn, META, DH), F32),
        ],
    )
    others = [over_x(group16, k) for k in range(1, xn)]
    (token,) = call(
        functools.partial(token_kernel, zn, cn, slots),
        (at, score_scale, table, sums),
        [shape((zn, cn, seg_rows, DH), F32)],
        scalars=2,
    )
    mark(token)
    others = [done(other) for other in others]
    attended = call(
        functools.partial(memory_kernel, zn, xn, cn),
        (at, score_scale, table, sums, token, written, group, *others),
        [shape((cn, seg_rows, DH))] * zn,
        [
            pltpu.VMEM((xn, zn, slots, 2 * DH), F32),
            pltpu.VMEM((zn, cn, seg_rows, DH), BF16),
        ],
        scalars=2,
    )

    here = [over_z(block, j) if j else block for j, block in enumerate(attended)]
    swapped = {}
    for j in range(zn):
        here[j] = done(here[j]) if j else here[j]
        swapped[j] = [over_c(here[j], m) for m in range(1, cn)]
    for b in bits[1:]:
        out_z[b] = done(started["oz", b])
        begin_out(b, out_z[b])
    for j in range(1, zn):
        if j not in out_z:
            low = j & -j
            out_z[j] = done(over_z(out_z[j ^ low], low))
            begin_out(j, out_z[j])
    here = sum(([here[j]] + [done(a) for a in swapped[j]] for j in range(zn)), [])

    for j in range(1, zn):
        end_out(j)
    columns = sum((columns[j] for j in range(zn)), [])
    out_cols = w_out.shape[1]
    blocks = feat_local // (cn * out_cols)
    products = call(
        functools.partial(out_kernel, zn, xn, cn, n_head),
        (at, *here, *columns),
        [shape((blocks, seg_rows, out_cols))] * (cn * n_head),
        [pltpu.VMEM((cn * seg_rows, heads * DH), BF16)],
        2 * cn * seg_rows * heads * DH * zn * xn * out_cols,
        room=32,
    )
    mine = []
    for r in range(n_head):
        for m in range(cn):
            block = products[r * cn + m]
            block = over_c(block, m) if m else block
            mine.append(over_y(block, r) if r else block)
    (branch,) = call(
        functools.partial(sum_kernel, n_head, cn),
        (at, *mine),
        [shape((seg_rows, feat_local))],
    )
    return branch


def solution(mesh):
    return jax.shard_map(
        body,
        mesh=mesh,
        in_specs=(
            P("seq", "head"),
            P(),
            P("seq", "head"),
            P("seq", "head"),
            P("seq", "head"),
            P("head", "seq"),
            P(None, "head"),
            P("head"),
            P("seq", "head"),
            P("seq"),
        ),
        out_specs=P("seq", "head"),
        check_vma=False,
    )
```

time: 220 us -> 189 us (0.86)
  waiting for transfers between devices: 131 us -> 111 us
  Pallas kernels: 29.6 us -> 24 us
  local copies, waits for them, and re-layouts: 11.7 us -> 8.16 us
    ppermute x15 -> x12, waiting for transfers between devices: 82.2 us -> 67.1 us  [over_z(): return lax.ppermute(a, 'seq', pairs)]
    ppermute x10 -> x9, waiting for transfers between devices: 34 us -> 28 us  [over_x(): return lax.ppermute(a, 'seq', pairs)]
    pallas_call x12, Pallas kernels: 29.6 us -> 24 us  [call(): pl.pallas_call(kernel, grid_spec=pltpu.PrefetchScalarGridSpec(num_scalar_...]
    ppermute x15 -> x12, starting transfers between devices: 24.4 us -> 20.4 us  [over_z(): return lax.ppermute(a, 'seq', pairs)]
    unnamed x50 -> x32, local copies, waits for them, and re-layouts: 11.6 us -> 8.16 us
    ppermute x12 -> x15, waiting for transfers between devices: 1.38 us -> 4.77 us  [over_c(): return lax.ppermute(a, 'seq', [(s, s ^ m) for s in range(n_seq)])]
    ppermute x10 -> x9, starting transfers between devices: 11.9 us -> 12.6 us  [over_x(): return lax.ppermute(a, 'seq', pairs)]
  transfers between devices with their start and end apart: 43 -> 42, of which waited for: 20 -> 22; matrix products, arithmetic and copies ran while one was open for 0% -> 0% of each run, Pallas kernels for 11% -> 9%
where the time goes in v3:
time: 189 us
  waiting for transfers between devices  111 us (59%)
  starting transfers between devices  44.4 us (23%)
  Pallas kernels  24 us (13%)
  local copies, waits for them, and re-layouts  8.16 us (4%)
    ppermute x12, waiting for transfers between devices, over_z(): return lax.ppermute(a, 'seq', pairs)  67.1 us
    ppermute x9, waiting for transfers between devices, over_x(): return lax.ppermute(a, 'seq', pairs)  28 us
    pallas_call x12, Pallas kernels, call(): pl.pallas_call(kernel, grid_spec=pltpu.PrefetchScalarGridSpec(num_scalar_...  24 us
    ppermute x12, starting transfers between devices, over_z(): return lax.ppermute(a, 'seq', pairs)  20.4 us
    ppermute x9, starting transfers between devices, over_x(): return lax.ppermute(a, 'seq', pairs)  12.6 us
    ppermute x6, waiting for transfers between devices, over_y(): lax.ppermute(a, 'head', [(h, (h + k) % n_head) for h in range(n_head)])  11.4 us
    ppermute x6, starting transfers between devices, over_y(): lax.ppermute(a, 'head', [(h, (h + k) % n_head) for h in range(n_head)])  8.62 us
    unnamed x32, local copies, waits for them, and re-layouts  8.16 us
  transfers between devices with their start and end apart: 42, of which 22 were waited for; matrix products, arithmetic and copies ran while one was open for 0% of the time, Pallas kernels for 9%

profile of v3, /device:TPU:0, one launch (start us, length us, event | category | flops | bytes accessed | tf_op | source)
XLA Modules:
  0.0 188.9 jit_solution(1415884704601559907)
XLA Ops:
  0.0 3.0 %collective-permute-start.1 = (bf16[128,2048]{1,0:T(8,128)(2,1)}, bf16[128,2048]{1,0:T(8,128)(2,1)S(1)}, u32[]{:S(2)}, u32[]{:S(2)}) collective-permute-start(bf16[128,2048]{1,0:T(8,128)(2,1)} %refs_0_.2), channel_id=1, source_target_pairs={{0,8},{2,10},{4,12},{6,14},{8,0},{10,2},{12,4},{14,6},{16,24},{18,... | collective-permute-start | bytes 1572872 | tf_op jit(solution)/shard_map/ppermute | solution.py:305
  3.0 2.6 %collective-permute-start.2 = (bf16[128,2048]{1,0:T(8,128)(2,1)}, bf16[128,2048]{1,0:T(8,128)(2,1)S(1)}, u32[]{:S(2)}, u32[]{:S(2)}) collective-permute-start(bf16[128,2048]{1,0:T(8,128)(2,1)} %refs_0_.2), channel_id=1, source_target_pairs={{0,16},{2,18},{4,20},{6,22},{8,24},{10,26},{12,28},{14,30},{16,0},... | collective-permute-start | bytes 1572872 | tf_op jit(solution)/shard_map/ppermute | solution.py:305
  14.6 12.5 %collective-permute-done.1.refs_0_ = bf16[128,2048]{1,0:T(8,128)(2,1)S(1)} collective-permute-done((bf16[128,2048]{1,0:T(8,128)(2,1)}, bf16[128,2048]{1,0:T(8,128)(2,1)S(1)}, u32[]{:S(2)}, u32[]{:S(2)}) %collective-permute-start.1) | collective-permute-done | bytes 524320 | tf_op jit(solution)/shard_map/ppermute | solution.py:305
  30.9 4.5 %collective-permute-done.4.refs_8_ = bf16[272,768]{1,0:T(8,128)(2,1)S(1)} collective-permute-done((bf16[272,768]{1,0:T(8,128)(2,1)S(1)}, bf16[272,768]{1,0:T(8,128)(2,1)S(1)}, u32[]{:S(2)}, u32[]{:S(2)}) %collective-permute-start.4) | collective-permute-done | bytes 417824 | tf_op jit(solution)/shard_map/ppermute | solution.py:305
  35.3 1.8 collective-permute-start.7
  37.1 2.5 %collective-permute-start.6 = (bf16[272,768]{1,0:T(8,128)(2,1)S(1)}, bf16[272,768]{1,0:T(8,128)(2,1)S(1)}, u32[]{:S(2)}, u32[]{:S(2)}) collective-permute-start(bf16[272,768]{1,0:T(8,128)(2,1)S(1)} %get-tuple-element.68), channel_id=1, source_target_pairs={{0,16},{2,18},{4,20},{6,22},{8,24},{10,26},{12,28},{14,30},{16,0},... | collective-permute-start | bytes 1253384 | tf_op jit(solution)/shard_map/ppermute | solution.py:305
  45.7 10.7 %collective-permute-done.6.refs_12_ = bf16[272,768]{1,0:T(8,128)(2,1)S(1)} collective-permute-done((bf16[272,768]{1,0:T(8,128)(2,1)S(1)}, bf16[272,768]{1,0:T(8,128)(2,1)S(1)}, u32[]{:S(2)}, u32[]{:S(2)}) %collective-permute-start.6) | collective-permute-done | bytes 417824 | tf_op jit(solution)/shard_map/ppermute | solution.py:305
  57.4 3.5 %collective-permute-start.11 = (bf16[272,768]{1,0:T(8,128)(2,1)S(1)}, bf16[272,768]{1,0:T(8,128)(2,1)S(1)}, u32[]{:S(2)}, u32[]{:S(2)}) collective-permute-start(bf16[272,768]{1,0:T(8,128)(2,1)S(1)} %get-tuple-element.76), channel_id=1, source_target_pairs={{0,24},{2,26},{4,28},{6,30},{8,16},{10,18},{12,20},{14,22},{16,8},... | collective-permute-start | bytes 1253384 | tf_op jit(solution)/shard_map/ppermute | solution.py:305
  63.9 7.9 %collective-permute-done.11.refs_4_ = bf16[272,768]{1,0:T(8,128)(2,1)S(1)} collective-permute-done((bf16[272,768]{1,0:T(8,128)(2,1)S(1)}, bf16[272,768]{1,0:T(8,128)(2,1)S(1)}, u32[]{:S(2)}, u32[]{:S(2)}) %collective-permute-start.11) | collective-permute-done | bytes 417824 | tf_op jit(solution)/shard_map/ppermute | solution.py:305
  73.8 7.1 %collective-permute-done.12.refs_10_ = bf16[1024,256]{1,0:T(8,128)(2,1)S(1)} collective-permute-done((bf16[1024,256]{1,0:T(8,128)(2,1)S(1)}, bf16[1024,256]{1,0:T(8,128)(2,1)S(1)}, u32[]{:S(2)}, u32[]{:S(2)}) %collective-permute-start.12) | collective-permute-done | bytes 524320 | tf_op jit(solution)/shard_map/ppermute | solution.py:305
  85.8 6.4 %shard_map.105 = (f32[4,128,768]{2,1,0:T(8,128)}, f32[3,2,2,16,128]{4,3,2,1,0:T(8,128)S(1)}) custom-call(s32[4]{0:T(128)S(1)} %pad_add_fusion.at, bf16[128,4096]{1,0:T(8,128)(2,1)S(1)} %shard_map.100.refs_0_, bf16[128,4096]{1,0:T(8,128)(2,1)} %copy-done, bf16[128,4096]{1,0:T(8,128)(2,1)} %copy-done.2, bf16[128,4096]{1,0:T(8,128)(2,1)} %copy-done.4, ...), custom_call_target="tpu_custom_call" | custom-call | flops 2415919104 | bytes 10878992 | tf_op jit(solution)/shard_map/pallas_call | solution.py:34
  92.2 3.4 %collective-permute-done.15.refs_6_ = bf16[272,768]{1,0:T(8,128)(2,1)S(1)} collective-permute-done((bf16[272,768]{1,0:T(8,128)(2,1)S(1)}, bf16[272,768]{1,0:T(8,128)(2,1)S(1)}, u32[]{:S(2)}, u32[]{:S(2)}) %collective-permute-start.15) | collective-permute-done | bytes 417824 | tf_op jit(solution)/shard_map/ppermute | solution.py:312
  95.6 1.7 collective-permute-done.23.refs_7_
  105.2 2.0 %shard_map.108.token = f32[4,2,128,128]{3,2,1,0:T(8,128)S(1)} custom-call(s32[4]{0:T(128)S(1)} %pad_add_fusion.at, f32[8]{0:T(128)S(1)} %copy-done.14, f32[4,2,2,16,128]{4,3,2,1,0:T(8,128)S(1)} %get-tuple-element.90.table, bf16[4,2,128,384]{3,2,1,0:T(8,128)(2,1)S(1)} %get-tuple-element.91.sums), custom_call_target="tpu_custom_call" | custom-call | bytes 1441840 | tf_op jit(solution)/shard_map/pallas_call | solution.py:34
  107.1 4.9 %collective-permute-done.25.refs_0_ = bf16[4,128,256]{2,1,0:T(8,128)(2,1)S(1)} collective-permute-done((bf16[4,128,256]{2,1,0:T(8,128)(2,1)S(1)}, bf16[4,128,256]{2,1,0:T(8,128)(2,1)S(1)}, u32[]{:S(2)}, u32[]{:S(2)}) %collective-permute-start.25) | collective-permute-done | bytes 262176 | tf_op jit(solution)/shard_map/ppermute | solution.py:312
  112.0 2.2 %shard_map.109 = (bf16[2,128,128]{2,1,0:T(8,128)(2,1)S(1)}, bf16[2,128,128]{2,1,0:T(8,128)(2,1)S(1)}, bf16[2,128,128]{2,1,0:T(8,128)(2,1)S(1)}, bf16[2,128,128]{2,1,0:T(8,128)(2,1)S(1)}) custom-call(s32[4]{0:T(128)S(1)} %pad_add_fusion.at, f32[8]{0:T(128)S(1)} %copy-done.14, f32[4,2,2,16,128]{4,3,2,1,0:T(8,128)S(1)} %get-tuple-element.90.table, ...), custom_call_target="tpu_custom_call" | custom-call | bytes 3538992 | tf_op jit(solution)/shard_map/pallas_call | solution.py:34
  114.2 1.8 collective-permute-start.30
  119.4 12.3 %collective-permute-done.29.refs_4_ = bf16[2,128,128]{2,1,0:T(8,128)(2,1)S(1)} collective-permute-done((bf16[2,128,128]{2,1,0:T(8,128)(2,1)S(1)}, bf16[2,128,128]{2,1,0:T(8,128)(2,1)S(1)}, u32[]{:S(2)}, u32[]{:S(2)}) %collective-permute-start.29) | collective-permute-done | bytes 65568 | tf_op jit(solution)/shard_map/ppermute | solution.py:305
  135.2 9.6 %collective-permute-done.31.refs_14_ = bf16[1024,256]{1,0:T(8,128)(2,1)S(1)} collective-permute-done((bf16[1024,256]{1,0:T(8,128)(2,1)S(1)}, bf16[1024,256]{1,0:T(8,128)(2,1)S(1)}, u32[]{:S(2)}, u32[]{:S(2)}) %collective-permute-start.31) | collective-permute-done | bytes 524320 | tf_op jit(solution)/shard_map/ppermute | solution.py:305
  149.0 10.3 %collective-permute-done.36.refs_13_ = bf16[1024,256]{1,0:T(8,128)(2,1)S(1)} collective-permute-done((bf16[1024,256]{1,0:T(8,128)(2,1)S(1)}, bf16[1024,256]{1,0:T(8,128)(2,1)S(1)}, u32[]{:S(2)}, u32[]{:S(2)}) %collective-permute-start.36) | collective-permute-done | bytes 524320 | tf_op jit(solution)/shard_map/ppermute | solution.py:312
  159.3 9.5 %collective-permute-done.37.refs_15_ = bf16[1024,256]{1,0:T(8,128)(2,1)S(1)} collective-permute-done((bf16[1024,256]{1,0:T(8,128)(2,1)S(1)}, bf16[1024,256]{1,0:T(8,128)(2,1)S(1)}, u32[]{:S(2)}, u32[]{:S(2)}) %collective-permute-start.37) | collective-permute-done | bytes 524320 | tf_op jit(solution)/shard_map/ppermute | solution.py:312
  168.7 4.1 %shard_map.110 = (bf16[4,128,256]{2,1,0:T(8,128)(2,1)S(1)}, bf16[4,128,256]{2,1,0:T(8,128)(2,1)S(1)}, bf16[4,128,256]{2,1,0:T(8,128)(2,1)S(1)}, bf16[4,128,256]{2,1,0:T(8,128)(2,1)S(1)}) custom-call(s32[4]{0:T(128)S(1)} %pad_add_fusion.at, bf16[2,128,128]{2,1,0:T(8,128)(2,1)S(1)} %get-tuple-element.96.refs_0_, ...), custom_call_target="tpu_custom_call" | custom-call | flops 1073741824 | bytes 5767184 | tf_op jit(solution)/shard_map/pallas_call | solution.py:34
  176.0 6.6 %collective-permute-done.39.refs_2_ = bf16[4,128,256]{2,1,0:T(8,128)(2,1)S(1)} collective-permute-done((bf16[4,128,256]{2,1,0:T(8,128)(2,1)S(1)}, bf16[4,128,256]{2,1,0:T(8,128)(2,1)S(1)}, u32[]{:S(2)}, u32[]{:S(2)}) %collective-permute-start.39) | collective-permute-done | bytes 262176 | tf_op jit(solution)/shard_map/ppermute | solution.py:318
  182.6 4.7 %collective-permute-done.41.refs_3_ = bf16[4,128,256]{2,1,0:T(8,128)(2,1)S(1)} collective-permute-done((bf16[4,128,256]{2,1,0:T(8,128)(2,1)S(1)}, bf16[4,128,256]{2,1,0:T(8,128)(2,1)S(1)}, u32[]{:S(2)}, u32[]{:S(2)}) %collective-permute-start.41) | collective-permute-done | bytes 262176 | tf_op jit(solution)/shard_map/ppermute | solution.py:318
  (105 shorter events, 52.4 us)
Async XLA Ops:
  0.0 27.1 %collective-permute-start.1 = (bf16[128,2048]{1,0:T(8,128)(2,1)}, bf16[128,2048]{1,0:T(8,128)(2,1)S(1)}, u32[]{:S(2)}, u32[]{:S(2)}) collective-permute-start(bf16[128,2048]{1,0:T(8,128)(2,1)} %refs_0_.2), channel_id=1, source_target_pairs={{0,8},{2,10},{4,12},{6,14},{8,0},{10,2},{12,4},{14,6},{16,24},{18,... | collective-permute-start | bytes 1572872 | tf_op jit(solution)/shard_map/ppermute | solution.py:305
  3.0 24.8 %collective-permute-start.2 = (bf16[128,2048]{1,0:T(8,128)(2,1)}, bf16[128,2048]{1,0:T(8,128)(2,1)S(1)}, u32[]{:S(2)}, u32[]{:S(2)}) collective-permute-start(bf16[128,2048]{1,0:T(8,128)(2,1)} %refs_0_.2), channel_id=1, source_target_pairs={{0,16},{2,18},{4,20},{6,22},{8,24},{10,26},{12,28},{14,30},{16,0},... | collective-permute-start | bytes 1572872 | tf_op jit(solution)/shard_map/ppermute | solution.py:305
  11.1 24.2 %collective-permute-start.4 = (bf16[272,768]{1,0:T(8,128)(2,1)S(1)}, bf16[272,768]{1,0:T(8,128)(2,1)S(1)}, u32[]{:S(2)}, u32[]{:S(2)}) collective-permute-start(bf16[272,768]{1,0:T(8,128)(2,1)S(1)} %get-tuple-element.64), channel_id=1, source_target_pairs={{0,8},{2,10},{4,12},{6,14},{8,0},{10,2},{12,4},{14,6},{16,24},{18,... | collective-permute-start | bytes 1253384 | tf_op jit(solution)/shard_map/ppermute | solution.py:305
  11.6 28.1 %collective-permute-start = (bf16[128,2048]{1,0:T(8,128)(2,1)S(1)}, bf16[128,2048]{1,0:T(8,128)(2,1)S(1)}, u32[]{:S(2)}, u32[]{:S(2)}) collective-permute-start(bf16[128,2048]{1,0:T(8,128)(2,1)S(1)} %copy-done.10), channel_id=1, source_target_pairs={{0,1},{1,0},{2,3},{3,2},{4,5},{5,4},{6,7},{7,6},{8,9},{9,8},{10,11... | collective-permute-start | bytes 1572872 | tf_op jit(solution)/shard_map/ppermute | solution.py:318
  13.1 24.0 %collective-permute-start.9 = (bf16[272,768]{1,0:T(8,128)(2,1)S(1)}, bf16[272,768]{1,0:T(8,128)(2,1)S(1)}, u32[]{:S(2)}, u32[]{:S(2)}) collective-permute-start(bf16[272,768]{1,0:T(8,128)(2,1)S(1)} %get-tuple-element.69.refs_4_), channel_id=1, source_target_pairs={{0,4},{2,6},{4,0},{6,2},{8,12},{10,14},{12,8},{14,10},{16,20},{18,... | collective-permute-start | bytes 1253384 | tf_op jit(solution)/shard_map/ppermute | solution.py:312
  27.9 14.3 %collective-permute-start.3 = (bf16[128,2048]{1,0:T(8,128)(2,1)S(1)}, bf16[128,2048]{1,0:T(8,128)(2,1)S(1)}, u32[]{:S(2)}, u32[]{:S(2)}) collective-permute-start(bf16[128,2048]{1,0:T(8,128)(2,1)S(1)} %collective-permute-done.1.refs_0_), channel_id=1, source_target_pairs={{0,1},{1,0},{2,3},{3,2},{4,5},{5,4},{6,7},{7,6},{8,9},{9,8},{10,11... | collective-permute-start | bytes 1572872 | tf_op jit(solution)/shard_map/ppermute | solution.py:318
  29.4 16.3 %collective-permute-start.8 = (bf16[1024,256]{1,0:T(8,128)(2,1)S(1)}, bf16[1024,256]{1,0:T(8,128)(2,1)S(1)}, u32[]{:S(2)}, u32[]{:S(2)}) collective-permute-start(bf16[1024,256]{1,0:T(8,128)(2,1)S(1)} %copy-done.11), channel_id=1, source_target_pairs={{0,4},{2,6},{4,0},{6,2},{8,12},{10,14},{12,8},{14,10},{16,20},{18,... | collective-permute-start | bytes 1572872 | tf_op jit(solution)/shard_map/ppermute | solution.py:312
  35.3 22.1 %collective-permute-start.7 = (bf16[128,2048]{1,0:T(8,128)(2,1)S(1)}, bf16[128,2048]{1,0:T(8,128)(2,1)S(1)}, u32[]{:S(2)}, u32[]{:S(2)}) collective-permute-start(bf16[128,2048]{1,0:T(8,128)(2,1)S(1)} %collective-permute-done.2.refs_0_), channel_id=1, source_target_pairs={{0,8},{2,10},{4,12},{6,14},{8,0},{10,2},{12,4},{14,6},{16,24},{18,... | collective-permute-start | bytes 1572872 | tf_op jit(solution)/shard_map/ppermute | solution.py:305
  37.1 19.3 %collective-permute-start.6 = (bf16[272,768]{1,0:T(8,128)(2,1)S(1)}, bf16[272,768]{1,0:T(8,128)(2,1)S(1)}, u32[]{:S(2)}, u32[]{:S(2)}) collective-permute-start(bf16[272,768]{1,0:T(8,128)(2,1)S(1)} %get-tuple-element.68), channel_id=1, source_target_pairs={{0,16},{2,18},{4,20},{6,22},{8,24},{10,26},{12,28},{14,30},{16,0},... | collective-permute-start | bytes 1253384 | tf_op jit(solution)/shard_map/ppermute | solution.py:305
  39.7 24.2 %collective-permute-start.5 = (bf16[128,2048]{1,0:T(8,128)(2,1)S(1)}, bf16[128,2048]{1,0:T(8,128)(2,1)S(1)}, u32[]{:S(2)}, u32[]{:S(2)}) collective-permute-start(bf16[128,2048]{1,0:T(8,128)(2,1)S(1)} %collective-permute-done.2.refs_0_), channel_id=1, source_target_pairs={{0,1},{1,0},{2,3},{3,2},{4,5},{5,4},{6,7},{7,6},{8,9},{9,8},{10,11... | collective-permute-start | bytes 1572872 | tf_op jit(solution)/shard_map/ppermute | solution.py:318
  42.2 20.2 %collective-permute-start.13 = (bf16[272,768]{1,0:T(8,128)(2,1)S(1)}, bf16[272,768]{1,0:T(8,128)(2,1)S(1)}, u32[]{:S(2)}, u32[]{:S(2)}) collective-permute-start(bf16[272,768]{1,0:T(8,128)(2,1)S(1)} %collective-permute-done.4.refs_8_), channel_id=1, source_target_pairs={{0,4},{2,6},{4,0},{6,2},{8,12},{10,14},{12,8},{14,10},{16,20},{18,... | collective-permute-start | bytes 1253384 | tf_op jit(solution)/shard_map/ppermute | solution.py:312
  57.4 14.4 %collective-permute-start.11 = (bf16[272,768]{1,0:T(8,128)(2,1)S(1)}, bf16[272,768]{1,0:T(8,128)(2,1)S(1)}, u32[]{:S(2)}, u32[]{:S(2)}) collective-permute-start(bf16[272,768]{1,0:T(8,128)(2,1)S(1)} %get-tuple-element.76), channel_id=1, source_target_pairs={{0,24},{2,26},{4,28},{6,30},{8,16},{10,18},{12,20},{14,22},{16,8},... | collective-permute-start | bytes 1253384 | tf_op jit(solution)/shard_map/ppermute | solution.py:305
  60.9 20.0 %collective-permute-start.12 = (bf16[1024,256]{1,0:T(8,128)(2,1)S(1)}, bf16[1024,256]{1,0:T(8,128)(2,1)S(1)}, u32[]{:S(2)}, u32[]{:S(2)}) collective-permute-start(bf16[1024,256]{1,0:T(8,128)(2,1)S(1)} %copy-done.11), channel_id=1, source_target_pairs={{0,8},{2,10},{4,12},{6,14},{8,0},{10,2},{12,4},{14,6},{16,24},{18,... | collective-permute-start | bytes 1572872 | tf_op jit(solution)/shard_map/ppermute | solution.py:305
  60.9 20.0 %collective-permute-start.10 = (bf16[128,2048]{1,0:T(8,128)(2,1)S(1)}, bf16[128,2048]{1,0:T(8,128)(2,1)S(1)}, u32[]{:S(2)}, u32[]{:S(2)}) collective-permute-start(bf16[128,2048]{1,0:T(8,128)(2,1)S(1)} %collective-permute-done.7.refs_0_), channel_id=1, source_target_pairs={{0,1},{1,0},{2,3},{3,2},{4,5},{5,4},{6,7},{7,6},{8,9},{9,8},{10,11... | collective-permute-start | bytes 1572872 | tf_op jit(solution)/shard_map/ppermute | solution.py:318
  62.4 20.9 %collective-permute-start.21 = (bf16[272,768]{1,0:T(8,128)(2,1)S(1)}, bf16[272,768]{1,0:T(8,128)(2,1)S(1)}, u32[]{:S(2)}, u32[]{:S(2)}) collective-permute-start(bf16[272,768]{1,0:T(8,128)(2,1)S(1)} %collective-permute-done.6.refs_12_), channel_id=1, source_target_pairs={{0,4},{2,6},{4,0},{6,2},{8,12},{10,14},{12,8},{14,10},{16,20},{18,... | collective-permute-start | bytes 1253384 | tf_op jit(solution)/shard_map/ppermute | solution.py:312
  63.9 19.5 %collective-permute-start.16 = (bf16[272,768]{1,0:T(8,128)(2,1)S(1)}, bf16[272,768]{1,0:T(8,128)(2,1)S(1)}, u32[]{:S(2)}, u32[]{:S(2)}) collective-permute-start(bf16[272,768]{1,0:T(8,128)(2,1)S(1)} %get-tuple-element.69.refs_4_), channel_id=1, source_target_pairs={{0,2},{2,0},{4,6},{6,4},{8,10},{10,8},{12,14},{14,12},{16,18},{18,... | collective-permute-start | bytes 1253384 | tf_op jit(solution)/shard_map/ppermute | solution.py:315
  100.6 31.1 %collective-permute-start.27 = (bf16[1024,256]{1,0:T(8,128)(2,1)S(1)}, bf16[1024,256]{1,0:T(8,128)(2,1)S(1)}, u32[]{:S(2)}, u32[]{:S(2)}) collective-permute-start(bf16[1024,256]{1,0:T(8,128)(2,1)S(1)} %copy-done.11), channel_id=1, source_target_pairs={{0,16},{2,18},{4,20},{6,22},{8,24},{10,26},{12,28},{14,30},{16,0},... | collective-permute-start | bytes 1572872 | tf_op jit(solution)/shard_map/ppermute | solution.py:305
  116.0 15.8 %collective-permute-start.29 = (bf16[2,128,128]{2,1,0:T(8,128)(2,1)S(1)}, bf16[2,128,128]{2,1,0:T(8,128)(2,1)S(1)}, u32[]{:S(2)}, u32[]{:S(2)}) collective-permute-start(bf16[2,128,128]{2,1,0:T(8,128)(2,1)S(1)} %get-tuple-element.99), channel_id=1, source_target_pairs={{0,16},{2,18},{4,20},{6,22},{8,24},{10,26},{12,28},{14,30},{16,0},... | collective-permute-start | bytes 196616 | tf_op jit(solution)/shard_map/ppermute | solution.py:305
  117.3 14.5 %collective-permute-start.28 = (bf16[2,128,128]{2,1,0:T(8,128)(2,1)S(1)}, bf16[2,128,128]{2,1,0:T(8,128)(2,1)S(1)}, u32[]{:S(2)}, u32[]{:S(2)}) collective-permute-start(bf16[2,128,128]{2,1,0:T(8,128)(2,1)S(1)} %get-tuple-element.98), channel_id=1, source_target_pairs={{0,24},{2,26},{4,28},{6,30},{8,16},{10,18},{12,20},{14,22},{16,8},... | collective-permute-start | bytes 196616 | tf_op jit(solution)/shard_map/ppermute | solution.py:305
  131.7 13.1 %collective-permute-start.31 = (bf16[1024,256]{1,0:T(8,128)(2,1)S(1)}, bf16[1024,256]{1,0:T(8,128)(2,1)S(1)}, u32[]{:S(2)}, u32[]{:S(2)}) collective-permute-start(bf16[1024,256]{1,0:T(8,128)(2,1)S(1)} %collective-permute-done.27.refs_12_), channel_id=1, source_target_pairs={{0,8},{2,10},{4,12},{6,14},{8,0},{10,2},{12,4},{14,6},{16,24},{18,... | collective-permute-start | bytes 1572872 | tf_op jit(solution)/shard_map/ppermute | solution.py:305
  133.2 15.8 %collective-permute-start.35 = (bf16[1024,256]{1,0:T(8,128)(2,1)S(1)}, bf16[1024,256]{1,0:T(8,128)(2,1)S(1)}, u32[]{:S(2)}, u32[]{:S(2)}) collective-permute-start(bf16[1024,256]{1,0:T(8,128)(2,1)S(1)} %collective-permute-done.12.refs_10_), channel_id=1, source_target_pairs={{0,4},{2,6},{4,0},{6,2},{8,12},{10,14},{12,8},{14,10},{16,20},{18,... | collective-permute-start | bytes 1572872 | tf_op jit(solution)/shard_map/ppermute | solution.py:312
  134.7 24.6 %collective-permute-start.36 = (bf16[1024,256]{1,0:T(8,128)(2,1)S(1)}, bf16[1024,256]{1,0:T(8,128)(2,1)S(1)}, u32[]{:S(2)}, u32[]{:S(2)}) collective-permute-start(bf16[1024,256]{1,0:T(8,128)(2,1)S(1)} %collective-permute-done.27.refs_12_), channel_id=1, source_target_pairs={{0,4},{2,6},{4,0},{6,2},{8,12},{10,14},{12,8},{14,10},{16,20},{18,... | collective-permute-start | bytes 1572872 | tf_op jit(solution)/shard_map/ppermute | solution.py:312
  144.8 23.9 %collective-permute-start.37 = (bf16[1024,256]{1,0:T(8,128)(2,1)S(1)}, bf16[1024,256]{1,0:T(8,128)(2,1)S(1)}, u32[]{:S(2)}, u32[]{:S(2)}) collective-permute-start(bf16[1024,256]{1,0:T(8,128)(2,1)S(1)} %collective-permute-done.31.refs_14_), channel_id=1, source_target_pairs={{0,4},{2,6},{4,0},{6,2},{8,12},{10,14},{12,8},{14,10},{16,20},{18,... | collective-permute-start | bytes 1572872 | tf_op jit(solution)/shard_map/ppermute | solution.py:312
  175.0 12.4 %collective-permute-start.41 = (bf16[4,128,256]{2,1,0:T(8,128)(2,1)S(1)}, bf16[4,128,256]{2,1,0:T(8,128)(2,1)S(1)}, u32[]{:S(2)}, u32[]{:S(2)}) collective-permute-start(bf16[4,128,256]{2,1,0:T(8,128)(2,1)S(1)} %collective-permute-done.40), channel_id=1, source_target_pairs={{0,1},{1,0},{2,3},{3,2},{4,5},{5,4},{6,7},{7,6},{8,9},{9,8},{10,11... | collective-permute-start | bytes 786440 | tf_op jit(solution)/shard_map/ppermute | solution.py:318
  (34 other events, 209.2 us)

commit v4 on v3

--- a/solution.py
+++ b/solution.py
@@ -326,10 +326,13 @@
     def done(a):
         return mark(lax.optimization_barrier((a, *chain))[0])
 
-    def done_all(parts):
-        parts = lax.optimization_barrier((*parts, *chain))[: len(parts)]
-        mark(parts[-1])
-        return parts
+    def done_all(*lists):
+        flat = [part for parts in lists for part in parts]
+        if flat:
+            flat = lax.optimization_barrier((*flat, *chain))[: len(flat)]
+            mark(flat[-1])
+        flat = iter(flat)
+        return [[next(flat) for _ in parts] for parts in lists]
 
     def after(a, b):
         return lax.optimization_barrier((a, b))[0]
@@ -346,11 +349,10 @@
     def begin_y(j):
         started["y", j] = [over_y(tok[j], k) for k in range(1, n_head)]
 
-    def end_y(j):
-        parts = [tok[j]] + [done(part) for part in started["y", j]]
+    def end_y(j, others):
         (rows[j],) = call(
             functools.partial(norm_kernel, n_head),
-            (at, gain[None], *parts),
+            (at, gain[None], tok[j], *others),
             [shape((seg_rows, width))],
         )
         mark(rows[j])
@@ -362,9 +364,9 @@
         started["x", j] = [over_x(packs[j], k) for k in range(1, xn)]
         pieces[j] = both(packs[j])
 
-    def end_x(j):
-        for part in started["x", j]:
-            pieces[j] += both(done(part))
+    def end_x(j, others):
+        for part in others:
+            pieces[j] += both(part)
 
     def begin_out(j, source):
         started["o", j] = [over_x(source, k) for k in range(1, xn)]
@@ -390,39 +392,48 @@
 
     bits = [1 << n for n in range(zn.bit_length() - 1)]
     more = [j for j in range(1, zn) if j not in bits]
-    if bits:
-        for b, part in zip(bits, done_all([started[b] for b in bits])):
-            tok[b] = part
-            begin_y(b)
+    parts, first, whole, columns[0][1:] = done_all(
+        [started[b] for b in bits], started["y", 0], started["x", 0], started["o", 0]
+    )
+    tok.update(zip(bits, parts))
+    end_x(0, whole)
+    for b in bits:
+        begin_y(b)
     for j in more:
         begin_tok(j)
-    for j in range(2, min(3, zn)):
+    early = range(1, min(3, zn))
+    for j in early[1:]:
         started["w", j] = over_z(after(sent[j], tok[1]), j)
-    end_y(0)
-    ready = []
-    for j in range(1, zn):
-        if j == 2:
-            ready = done_all([started["w", 2], *(started[i] for i in more)])
-            packs[2] = ready[0]
-            for i, part in zip(more, ready[1:]):
-                tok[i] = part
-                begin_y(i)
-        elif j == last:
-            first = over_z(after(w_out, packs[j - 1]), 1)
-            packs[j], out_z[1] = done_all([started["w", j], first])
-        else:
-            packs[j] = done(started["w", j])
+    end_y(0, first)
+    parts, far, *near = done_all(
+        [started["w", j] for j in early],
+        [started[j] for j in more],
+        *(started["y", b] for b in bits),
+    )
+    packs.update(zip(early, parts))
+    tok.update(zip(more, far))
+    for j in range(len(early) + 1, zn):
+        started["w", j] = over_z(after(sent[j], packs[j - 1]), j)
+    for j in more:
+        begin_y(j)
+    for j in early:
         begin_x(j)
-        if j > 1 and j + 1 < zn:
-            started["w", j + 1] = over_z(after(sent[j + 1], packs[j]), j + 1)
-        end_y(j)
-        end_x(j - 1)
-        if j == 1:
-            end_out(0)
+    if last:
+        started["oz", 1] = over_z(after(w_out, packs[early[-1]]), 1)
+    for b, others in zip(bits, near):
+        end_y(b, others)
+    for j in more:
+        end_y(j, done_all(started["y", j])[0])
+    for j in range(len(early) + 1, zn):
+        packs[j] = done(started["w", j])
+        begin_x(j)
     for b in bits[1:]:
         started["oz", b] = over_z(after(w_out, packs[last]), b)
-    if not last:
-        end_out(0)
+    for j in range(1, last):
+        end_x(j, done_all(started["x", j])[0])
+    if last:
+        out_z[1] = done(started["oz", 1])
+        begin_out(1, out_z[1])
     rows = [rows[j] for j in range(zn)]
 
     chunk_rows = xn * cn * w_rows
@@ -441,7 +452,16 @@
             room=48,
         )
         mark(before[0])
-    end_x(last)
+    if last:
+        parts, others, columns[1][1:] = done_all(
+            [started["oz", b] for b in bits[1:]], started["x", last], started["o", 1]
+        )
+        end_x(last, others)
+        out_z.update(zip(bits[1:], parts))
+        for b in bits[1:]:
+            begin_out(b, out_z[b])
+        for j in more:
+            started["oz", j] = over_z(out_z[j ^ (j & -j)], j & -j)
     *parts, meta = call(
         functools.partial(finish_kernel, zn, xn, cn),
         (at, *rows, *pieces[last], *before[:1]),
@@ -451,8 +471,6 @@
         column=(chunk_rows, lambda at: at[0] ^ last),
         room=32,
     )
-    if last:
-        begin_out(1, out_z[1])
     parts = [done(over_c(part, m)) if m else part for m, part in enumerate(parts)]
     sums, written, group, group16, table = call(
         functools.partial(write_kernel, zn, xn, cn),
@@ -473,7 +491,9 @@
         scalars=2,
     )
     mark(token)
-    others = [done(other) for other in others]
+    others, parts = done_all(others, [started["oz", j] for j in more])
+    for j, part in zip(more, parts):
+        begin_out(j, part)
     attended = call(
         functools.partial(memory_kernel, zn, xn, cn),
         (at, score_scale, table, sums, token, written, group, *others),
@@ -486,21 +506,12 @@
     )
 
     here = [over_z(block, j) if j else block for j, block in enumerate(attended)]
-    swapped = {}
-    for j in range(zn):
-        here[j] = done(here[j]) if j else here[j]
-        swapped[j] = [over_c(here[j], m) for m in range(1, cn)]
-    for b in bits[1:]:
-        out_z[b] = done(started["oz", b])
-        begin_out(b, out_z[b])
     for j in range(1, zn):
-        if j not in out_z:
-            low = j & -j
-            out_z[j] = done(over_z(out_z[j ^ low], low))
-            begin_out(j, out_z[j])
+        here[j] = done(here[j])
+    swapped = [[over_c(here[j], m) for m in range(1, cn)] for j in range(zn)]
     here = sum(([here[j]] + [done(a) for a in swapped[j]] for j in range(zn)), [])
 
-    for j in range(1, zn):
+    for j in range(2, zn):
         end_out(j)
     columns = sum((columns[j] for j in range(zn)), [])
     out_cols = w_out.shape[1]

time: 189 us -> 169 us (0.89)
  waiting for transfers between devices: 111 us -> 99 us
  starting transfers between devices: 44.4 us -> 36.3 us
    ppermute x12, waiting for transfers between devices: 67.1 us -> 48.9 us  [over_z(): return lax.ppermute(a, 'seq', pairs)]
    ppermute x9, waiting for transfers between devices: 28 us -> 34.5 us  [over_x(): return lax.ppermute(a, 'seq', pairs)]
    ppermute x9, starting transfers between devices: 12.6 us -> 8.8 us  [over_x(): return lax.ppermute(a, 'seq', pairs)]
    ppermute x12, starting transfers between devices: 20.4 us -> 17 us  [over_z(): return lax.ppermute(a, 'seq', pairs)]
  transfers between devices with their start and end apart: 42 -> 42, of which waited for: 22 -> 16; matrix products, arithmetic and copies ran while one was open for 0% -> 0% of each run, Pallas kernels for 9% -> 10%
where the time goes in v4:
time: 169 us
  waiting for transfers between devices  99 us (59%)
  starting transfers between devices  36.3 us (21%)
  Pallas kernels  24.3 us (14%)
  local copies, waits for them, and re-layouts  8.16 us (5%)
    ppermute x12, waiting for transfers between devices, over_z(): return lax.ppermute(a, 'seq', pairs)  48.9 us
    ppermute x9, waiting for transfers between devices, over_x(): return lax.ppermute(a, 'seq', pairs)  34.5 us
    pallas_call x12, Pallas kernels, call(): pl.pallas_call(kernel, grid_spec=pltpu.PrefetchScalarGridSpec(num_scalar_...  24.3 us
    ppermute x12, starting transfers between devices, over_z(): return lax.ppermute(a, 'seq', pairs)  17 us
    ppermute x6, waiting for transfers between devices, over_y(): lax.ppermute(a, 'head', [(h, (h + k) % n_head) for h in range(n_head)])  11.4 us
    ppermute x9, starting transfers between devices, over_x(): return lax.ppermute(a, 'seq', pairs)  8.8 us
    unnamed x32, local copies, waits for them, and re-layouts  8.16 us
    ppermute x6, starting transfers between devices, over_y(): lax.ppermute(a, 'head', [(h, (h + k) % n_head) for h in range(n_head)])  7.61 us
  transfers between devices with their start and end apart: 42, of which 16 were waited for; matrix products, arithmetic and copies ran while one was open for 0% of the time, Pallas kernels for 10%

profile of v4, /device:TPU:0, one launch (start us, length us, event | category | flops | bytes accessed | tf_op | source)
XLA Modules:
  0.0 168.7 jit_solution(11600037983167329037)
XLA Ops:
  0.0 3.0 %collective-permute-start = (bf16[128,2048]{1,0:T(8,128)(2,1)}, bf16[128,2048]{1,0:T(8,128)(2,1)S(1)}, u32[]{:S(2)}, u32[]{:S(2)}) collective-permute-start(bf16[128,2048]{1,0:T(8,128)(2,1)} %refs_0_.3), channel_id=1, source_target_pairs={{0,8},{2,10},{4,12},{6,14},{8,0},{10,2},{12,4},{14,6},{16,24},{18,... | collective-permute-start | bytes 1572872 | tf_op jit(solution)/shard_map/ppermute | solution.py:305
  3.0 2.6 %collective-permute-start.1 = (bf16[128,2048]{1,0:T(8,128)(2,1)}, bf16[128,2048]{1,0:T(8,128)(2,1)S(1)}, u32[]{:S(2)}, u32[]{:S(2)}) collective-permute-start(bf16[128,2048]{1,0:T(8,128)(2,1)} %refs_0_.3), channel_id=1, source_target_pairs={{0,16},{2,18},{4,20},{6,22},{8,24},{10,26},{12,28},{14,30},{16,0},... | collective-permute-start | bytes 1572872 | tf_op jit(solution)/shard_map/ppermute | solution.py:305
  14.7 14.4 %collective-permute-done.3.refs_6_ = bf16[272,768]{1,0:T(8,128)(2,1)S(1)} collective-permute-done((bf16[272,768]{1,0:T(8,128)(2,1)S(1)}, bf16[272,768]{1,0:T(8,128)(2,1)S(1)}, u32[]{:S(2)}, u32[]{:S(2)}) %collective-permute-start.3) | collective-permute-done | bytes 417824 | tf_op jit(solution)/shard_map/ppermute | solution.py:312
  31.7 1.6 collective-permute-start.5
  35.0 24.0 %collective-permute-done.5.refs_8_ = bf16[272,768]{1,0:T(8,128)(2,1)S(1)} collective-permute-done((bf16[272,768]{1,0:T(8,128)(2,1)S(1)}, bf16[272,768]{1,0:T(8,128)(2,1)S(1)}, u32[]{:S(2)}, u32[]{:S(2)}) %collective-permute-start.5) | collective-permute-done | bytes 417824 | tf_op jit(solution)/shard_map/ppermute | solution.py:305
  65.0 8.5 %collective-permute-done.11.refs_4_ = bf16[272,768]{1,0:T(8,128)(2,1)S(1)} collective-permute-done((bf16[272,768]{1,0:T(8,128)(2,1)S(1)}, bf16[272,768]{1,0:T(8,128)(2,1)S(1)}, u32[]{:S(2)}, u32[]{:S(2)}) %collective-permute-start.11) | collective-permute-done | bytes 417824 | tf_op jit(solution)/shard_map/ppermute | solution.py:305
  74.0 3.5 %collective-permute-done.16.refs_14_ = bf16[272,768]{1,0:T(8,128)(2,1)S(1)} collective-permute-done((bf16[272,768]{1,0:T(8,128)(2,1)S(1)}, bf16[272,768]{1,0:T(8,128)(2,1)S(1)}, u32[]{:S(2)}, u32[]{:S(2)}) %collective-permute-start.16) | collective-permute-done | bytes 417824 | tf_op jit(solution)/shard_map/ppermute | solution.py:312
  84.0 1.7 %collective-permute-start.13 = (bf16[1024,256]{1,0:T(8,128)(2,1)S(1)}, bf16[1024,256]{1,0:T(8,128)(2,1)S(1)}, u32[]{:S(2)}, u32[]{:S(2)}) collective-permute-start(bf16[1024,256]{1,0:T(8,128)(2,1)S(1)} %copy-done.11), channel_id=1, source_target_pairs={{0,16},{2,18},{4,20},{6,22},{8,24},{10,26},{12,28},{14,30},{16,0},... | collective-permute-start | bytes 1572872 | tf_op jit(solution)/shard_map/ppermute | solution.py:305
  88.2 6.7 %shard_map.105 = (f32[4,128,768]{2,1,0:T(8,128)}, f32[3,2,2,16,128]{4,3,2,1,0:T(8,128)S(1)}) custom-call(s32[4]{0:T(128)S(1)} %pad_add_fusion.at, bf16[128,4096]{1,0:T(8,128)(2,1)S(1)} %shard_map.101.refs_0_, bf16[128,4096]{1,0:T(8,128)(2,1)} %copy-done.4, bf16[128,4096]{1,0:T(8,128)(2,1)} %copy-done, bf16[128,4096]{1,0:T(8,128)(2,1)} %copy-done.2, ...), custom_call_target="tpu_custom_call" | custom-call | flops 2415919104 | bytes 10878992 | tf_op jit(solution)/shard_map/pallas_call | solution.py:34
  95.0 10.4 %collective-permute-done.14.refs_6_ = bf16[272,768]{1,0:T(8,128)(2,1)S(1)} collective-permute-done((bf16[272,768]{1,0:T(8,128)(2,1)S(1)}, bf16[272,768]{1,0:T(8,128)(2,1)S(1)}, u32[]{:S(2)}, u32[]{:S(2)}) %collective-permute-start.14) | collective-permute-done | bytes 417824 | tf_op jit(solution)/shard_map/ppermute | solution.py:312
  105.3 4.4 %collective-permute-done.13.refs_12_ = bf16[1024,256]{1,0:T(8,128)(2,1)S(1)} collective-permute-done((bf16[1024,256]{1,0:T(8,128)(2,1)S(1)}, bf16[1024,256]{1,0:T(8,128)(2,1)S(1)}, u32[]{:S(2)}, u32[]{:S(2)}) %collective-permute-start.13) | collective-permute-done | bytes 524320 | tf_op jit(solution)/shard_map/ppermute | solution.py:305
  109.7 1.7 %collective-permute-done.25.refs_7_ = bf16[272,768]{1,0:T(8,128)(2,1)S(1)} collective-permute-done((bf16[272,768]{1,0:T(8,128)(2,1)S(1)}, bf16[272,768]{1,0:T(8,128)(2,1)S(1)}, u32[]{:S(2)}, u32[]{:S(2)}) %collective-permute-start.25) | collective-permute-done | bytes 417824 | tf_op jit(solution)/shard_map/ppermute | solution.py:315
  112.9 1.7 shard_map.106
  114.8 1.6 collective-permute-done.26.refs_1_
  119.9 2.0 %shard_map.108.token = f32[4,2,128,128]{3,2,1,0:T(8,128)S(1)} custom-call(s32[4]{0:T(128)S(1)} %pad_add_fusion.at, f32[8]{0:T(128)S(1)} %copy-done.14, f32[4,2,2,16,128]{4,3,2,1,0:T(8,128)S(1)} %get-tuple-element.91.table, bf16[4,2,128,384]{3,2,1,0:T(8,128)(2,1)S(1)} %get-tuple-element.92.sums), custom_call_target="tpu_custom_call" | custom-call | bytes 1441840 | tf_op jit(solution)/shard_map/pallas_call | solution.py:34
  121.9 7.1 %collective-permute-done.28.refs_14_ = bf16[1024,256]{1,0:T(8,128)(2,1)S(1)} collective-permute-done((bf16[1024,256]{1,0:T(8,128)(2,1)S(1)}, bf16[1024,256]{1,0:T(8,128)(2,1)S(1)}, u32[]{:S(2)}, u32[]{:S(2)}) %collective-permute-start.28) | collective-permute-done | bytes 524320 | tf_op jit(solution)/shard_map/ppermute | solution.py:305
  129.5 2.2 %shard_map.109 = (bf16[2,128,128]{2,1,0:T(8,128)(2,1)S(1)}, bf16[2,128,128]{2,1,0:T(8,128)(2,1)S(1)}, bf16[2,128,128]{2,1,0:T(8,128)(2,1)S(1)}, bf16[2,128,128]{2,1,0:T(8,128)(2,1)S(1)}) custom-call(s32[4]{0:T(128)S(1)} %pad_add_fusion.at, f32[8]{0:T(128)S(1)} %copy-done.14, f32[4,2,2,16,128]{4,3,2,1,0:T(8,128)S(1)} %get-tuple-element.91.table, ...), custom_call_target="tpu_custom_call" | custom-call | bytes 3538992 | tf_op jit(solution)/shard_map/pallas_call | solution.py:34
  132.1 2.9 %collective-permute-start.31 = (bf16[2,128,128]{2,1,0:T(8,128)(2,1)S(1)}, bf16[2,128,128]{2,1,0:T(8,128)(2,1)S(1)}, u32[]{:S(2)}, u32[]{:S(2)}) collective-permute-start(bf16[2,128,128]{2,1,0:T(8,128)(2,1)S(1)} %get-tuple-element.100), channel_id=1, source_target_pairs={{0,16},{2,18},{4,20},{6,22},{8,24},{10,26},{12,28},{14,30},{16,0},... | collective-permute-start | bytes 196616 | tf_op jit(solution)/shard_map/ppermute | solution.py:305
  136.2 3.1 %collective-permute-done.31.refs_4_ = bf16[2,128,128]{2,1,0:T(8,128)(2,1)S(1)} collective-permute-done((bf16[2,128,128]{2,1,0:T(8,128)(2,1)S(1)}, bf16[2,128,128]{2,1,0:T(8,128)(2,1)S(1)}, u32[]{:S(2)}, u32[]{:S(2)}) %collective-permute-start.31) | collective-permute-done | bytes 65568 | tf_op jit(solution)/shard_map/ppermute | solution.py:305
  139.3 1.7 %collective-permute-done.30.refs_6_ = bf16[2,128,128]{2,1,0:T(8,128)(2,1)S(1)} collective-permute-done((bf16[2,128,128]{2,1,0:T(8,128)(2,1)S(1)}, bf16[2,128,128]{2,1,0:T(8,128)(2,1)S(1)}, u32[]{:S(2)}, u32[]{:S(2)}) %collective-permute-start.30) | collective-permute-done | bytes 65568 | tf_op jit(solution)/shard_map/ppermute | solution.py:305
  142.5 6.2 %collective-permute-done.37.refs_15_ = bf16[1024,256]{1,0:T(8,128)(2,1)S(1)} collective-permute-done((bf16[1024,256]{1,0:T(8,128)(2,1)S(1)}, bf16[1024,256]{1,0:T(8,128)(2,1)S(1)}, u32[]{:S(2)}, u32[]{:S(2)}) %collective-permute-start.37) | collective-permute-done | bytes 524320 | tf_op jit(solution)/shard_map/ppermute | solution.py:312
  148.6 4.1 %shard_map.110 = (bf16[4,128,256]{2,1,0:T(8,128)(2,1)S(1)}, bf16[4,128,256]{2,1,0:T(8,128)(2,1)S(1)}, bf16[4,128,256]{2,1,0:T(8,128)(2,1)S(1)}, bf16[4,128,256]{2,1,0:T(8,128)(2,1)S(1)}) custom-call(s32[4]{0:T(128)S(1)} %pad_add_fusion.at, bf16[2,128,128]{2,1,0:T(8,128)(2,1)S(1)} %get-tuple-element.98.refs_0_, ...), custom_call_target="tpu_custom_call" | custom-call | flops 1073741824 | bytes 5767184 | tf_op jit(solution)/shard_map/pallas_call | solution.py:34
  155.9 6.6 %collective-permute-done.39.refs_2_ = bf16[4,128,256]{2,1,0:T(8,128)(2,1)S(1)} collective-permute-done((bf16[4,128,256]{2,1,0:T(8,128)(2,1)S(1)}, bf16[4,128,256]{2,1,0:T(8,128)(2,1)S(1)}, u32[]{:S(2)}, u32[]{:S(2)}) %collective-permute-start.39) | collective-permute-done | bytes 262176 | tf_op jit(solution)/shard_map/ppermute | solution.py:318
  162.5 4.7 %collective-permute-done.41.refs_3_ = bf16[4,128,256]{2,1,0:T(8,128)(2,1)S(1)} collective-permute-done((bf16[4,128,256]{2,1,0:T(8,128)(2,1)S(1)}, bf16[4,128,256]{2,1,0:T(8,128)(2,1)S(1)}, u32[]{:S(2)}, u32[]{:S(2)}) %collective-permute-start.41) | collective-permute-done | bytes 262176 | tf_op jit(solution)/shard_map/ppermute | solution.py:318
  (105 shorter events, 41.4 us)
Async XLA Ops:
  0.0 29.1 %collective-permute-start = (bf16[128,2048]{1,0:T(8,128)(2,1)}, bf16[128,2048]{1,0:T(8,128)(2,1)S(1)}, u32[]{:S(2)}, u32[]{:S(2)}) collective-permute-start(bf16[128,2048]{1,0:T(8,128)(2,1)} %refs_0_.3), channel_id=1, source_target_pairs={{0,8},{2,10},{4,12},{6,14},{8,0},{10,2},{12,4},{14,6},{16,24},{18,... | collective-permute-start | bytes 1572872 | tf_op jit(solution)/shard_map/ppermute | solution.py:305
  3.0 26.1 %collective-permute-start.1 = (bf16[128,2048]{1,0:T(8,128)(2,1)}, bf16[128,2048]{1,0:T(8,128)(2,1)S(1)}, u32[]{:S(2)}, u32[]{:S(2)}) collective-permute-start(bf16[128,2048]{1,0:T(8,128)(2,1)} %refs_0_.3), channel_id=1, source_target_pairs={{0,16},{2,18},{4,20},{6,22},{8,24},{10,26},{12,28},{14,30},{16,0},... | collective-permute-start | bytes 1572872 | tf_op jit(solution)/shard_map/ppermute | solution.py:305
  5.6 23.5 %collective-permute-start.2 = (bf16[128,2048]{1,0:T(8,128)(2,1)}, bf16[128,2048]{1,0:T(8,128)(2,1)S(1)}, u32[]{:S(2)}, u32[]{:S(2)}) collective-permute-start(bf16[128,2048]{1,0:T(8,128)(2,1)} %refs_0_.3), channel_id=1, source_target_pairs={{0,1},{1,0},{2,3},{3,2},{4,5},{5,4},{6,7},{7,6},{8,9},{9,8},{10,11... | collective-permute-start | bytes 1572872 | tf_op jit(solution)/shard_map/ppermute | solution.py:318
  7.1 22.0 %collective-permute-start.4 = (bf16[1024,256]{1,0:T(8,128)(2,1)}, bf16[1024,256]{1,0:T(8,128)(2,1)S(1)}, u32[]{:S(2)}, u32[]{:S(2)}) collective-permute-start(bf16[1024,256]{1,0:T(8,128)(2,1)} %refs_8_.1), channel_id=1, source_target_pairs={{0,4},{2,6},{4,0},{6,2},{8,12},{10,14},{12,8},{14,10},{16,20},{18,... | collective-permute-start | bytes 1572872 | tf_op jit(solution)/shard_map/ppermute | solution.py:312
  14.1 15.0 %collective-permute-start.3 = (bf16[272,768]{1,0:T(8,128)(2,1)S(1)}, bf16[272,768]{1,0:T(8,128)(2,1)S(1)}, u32[]{:S(2)}, u32[]{:S(2)}) collective-permute-start(bf16[272,768]{1,0:T(8,128)(2,1)S(1)} %get-tuple-element.61.refs_4_), channel_id=1, source_target_pairs={{0,4},{2,6},{4,0},{6,2},{8,12},{10,14},{12,8},{14,10},{16,20},{18,... | collective-permute-start | bytes 1253384 | tf_op jit(solution)/shard_map/ppermute | solution.py:312
  29.1 29.9 %collective-permute-start.7 = (bf16[128,2048]{1,0:T(8,128)(2,1)S(1)}, bf16[128,2048]{1,0:T(8,128)(2,1)S(1)}, u32[]{:S(2)}, u32[]{:S(2)}) collective-permute-start(bf16[128,2048]{1,0:T(8,128)(2,1)S(1)} %collective-permute-done.1.refs_0_), channel_id=1, source_target_pairs={{0,8},{2,10},{4,12},{6,14},{8,0},{10,2},{12,4},{14,6},{16,24},{18,... | collective-permute-start | bytes 1572872 | tf_op jit(solution)/shard_map/ppermute | solution.py:305
  29.7 29.4 %collective-permute-start.8 = (bf16[128,2048]{1,0:T(8,128)(2,1)S(1)}, bf16[128,2048]{1,0:T(8,128)(2,1)S(1)}, u32[]{:S(2)}, u32[]{:S(2)}) collective-permute-start(bf16[128,2048]{1,0:T(8,128)(2,1)S(1)} %collective-permute-done.refs_0_), channel_id=1, source_target_pairs={{0,1},{1,0},{2,3},{3,2},{4,5},{5,4},{6,7},{7,6},{8,9},{9,8},{10,11... | collective-permute-start | bytes 1572872 | tf_op jit(solution)/shard_map/ppermute | solution.py:318
  30.8 28.3 %collective-permute-start.9 = (bf16[128,2048]{1,0:T(8,128)(2,1)S(1)}, bf16[128,2048]{1,0:T(8,128)(2,1)S(1)}, u32[]{:S(2)}, u32[]{:S(2)}) collective-permute-start(bf16[128,2048]{1,0:T(8,128)(2,1)S(1)} %collective-permute-done.1.refs_0_), channel_id=1, source_target_pairs={{0,1},{1,0},{2,3},{3,2},{4,5},{5,4},{6,7},{7,6},{8,9},{9,8},{10,11... | collective-permute-start | bytes 1572872 | tf_op jit(solution)/shard_map/ppermute | solution.py:318
  31.7 27.3 %collective-permute-start.5 = (bf16[272,768]{1,0:T(8,128)(2,1)S(1)}, bf16[272,768]{1,0:T(8,128)(2,1)S(1)}, u32[]{:S(2)}, u32[]{:S(2)}) collective-permute-start(bf16[272,768]{1,0:T(8,128)(2,1)S(1)} %get-tuple-element.64), channel_id=1, source_target_pairs={{0,8},{2,10},{4,12},{6,14},{8,0},{10,2},{12,4},{14,6},{16,24},{18,... | collective-permute-start | bytes 1253384 | tf_op jit(solution)/shard_map/ppermute | solution.py:305
  33.3 25.8 %collective-permute-start.6 = (bf16[272,768]{1,0:T(8,128)(2,1)S(1)}, bf16[272,768]{1,0:T(8,128)(2,1)S(1)}, u32[]{:S(2)}, u32[]{:S(2)}) collective-permute-start(bf16[272,768]{1,0:T(8,128)(2,1)S(1)} %get-tuple-element.66), channel_id=1, source_target_pairs={{0,16},{2,18},{4,20},{6,22},{8,24},{10,26},{12,28},{14,30},{16,0},... | collective-permute-start | bytes 1253384 | tf_op jit(solution)/shard_map/ppermute | solution.py:305
  59.0 14.5 %collective-permute-start.11 = (bf16[272,768]{1,0:T(8,128)(2,1)S(1)}, bf16[272,768]{1,0:T(8,128)(2,1)S(1)}, u32[]{:S(2)}, u32[]{:S(2)}) collective-permute-start(bf16[272,768]{1,0:T(8,128)(2,1)S(1)} %get-tuple-element.74), channel_id=1, source_target_pairs={{0,24},{2,26},{4,28},{6,30},{8,16},{10,18},{12,20},{14,22},{16,8},... | collective-permute-start | bytes 1253384 | tf_op jit(solution)/shard_map/ppermute | solution.py:305
  60.5 13.0 %collective-permute-start.17 = (bf16[272,768]{1,0:T(8,128)(2,1)S(1)}, bf16[272,768]{1,0:T(8,128)(2,1)S(1)}, u32[]{:S(2)}, u32[]{:S(2)}) collective-permute-start(bf16[272,768]{1,0:T(8,128)(2,1)S(1)} %collective-permute-done.5.refs_8_), channel_id=1, source_target_pairs={{0,4},{2,6},{4,0},{6,2},{8,12},{10,14},{12,8},{14,10},{16,20},{18,... | collective-permute-start | bytes 1253384 | tf_op jit(solution)/shard_map/ppermute | solution.py:312
  62.0 15.6 %collective-permute-start.10 = (bf16[128,2048]{1,0:T(8,128)(2,1)S(1)}, bf16[128,2048]{1,0:T(8,128)(2,1)S(1)}, u32[]{:S(2)}, u32[]{:S(2)}) collective-permute-start(bf16[128,2048]{1,0:T(8,128)(2,1)S(1)} %collective-permute-done.7.refs_0_), channel_id=1, source_target_pairs={{0,1},{1,0},{2,3},{3,2},{4,5},{5,4},{6,7},{7,6},{8,9},{9,8},{10,11... | collective-permute-start | bytes 1572872 | tf_op jit(solution)/shard_map/ppermute | solution.py:318
  63.5 14.0 %collective-permute-start.16 = (bf16[272,768]{1,0:T(8,128)(2,1)S(1)}, bf16[272,768]{1,0:T(8,128)(2,1)S(1)}, u32[]{:S(2)}, u32[]{:S(2)}) collective-permute-start(bf16[272,768]{1,0:T(8,128)(2,1)S(1)} %collective-permute-done.6.refs_12_), channel_id=1, source_target_pairs={{0,4},{2,6},{4,0},{6,2},{8,12},{10,14},{12,8},{14,10},{16,20},{18,... | collective-permute-start | bytes 1253384 | tf_op jit(solution)/shard_map/ppermute | solution.py:312
  64.1 17.9 %collective-permute-start.15 = (bf16[1024,256]{1,0:T(8,128)(2,1)S(1)}, bf16[1024,256]{1,0:T(8,128)(2,1)S(1)}, u32[]{:S(2)}, u32[]{:S(2)}) collective-permute-start(bf16[1024,256]{1,0:T(8,128)(2,1)S(1)} %copy-done.11), channel_id=1, source_target_pairs={{0,8},{2,10},{4,12},{6,14},{8,0},{10,2},{12,4},{14,6},{16,24},{18,... | collective-permute-start | bytes 1572872 | tf_op jit(solution)/shard_map/ppermute | solution.py:305
  82.5 22.9 %collective-permute-start.18 = (bf16[1024,256]{1,0:T(8,128)(2,1)S(1)}, bf16[1024,256]{1,0:T(8,128)(2,1)S(1)}, u32[]{:S(2)}, u32[]{:S(2)}) collective-permute-start(bf16[1024,256]{1,0:T(8,128)(2,1)S(1)} %collective-permute-done.15.refs_10_), channel_id=1, source_target_pairs={{0,4},{2,6},{4,0},{6,2},{8,12},{10,14},{12,8},{14,10},{16,20},{18,... | collective-permute-start | bytes 1572872 | tf_op jit(solution)/shard_map/ppermute | solution.py:312
  84.0 25.8 %collective-permute-start.13 = (bf16[1024,256]{1,0:T(8,128)(2,1)S(1)}, bf16[1024,256]{1,0:T(8,128)(2,1)S(1)}, u32[]{:S(2)}, u32[]{:S(2)}) collective-permute-start(bf16[1024,256]{1,0:T(8,128)(2,1)S(1)} %copy-done.11), channel_id=1, source_target_pairs={{0,16},{2,18},{4,20},{6,22},{8,24},{10,26},{12,28},{14,30},{16,0},... | collective-permute-start | bytes 1572872 | tf_op jit(solution)/shard_map/ppermute | solution.py:305
  85.7 19.7 %collective-permute-start.14 = (bf16[272,768]{1,0:T(8,128)(2,1)S(1)}, bf16[272,768]{1,0:T(8,128)(2,1)S(1)}, u32[]{:S(2)}, u32[]{:S(2)}) collective-permute-start(bf16[272,768]{1,0:T(8,128)(2,1)S(1)} %collective-permute-done.11.refs_4_), channel_id=1, source_target_pairs={{0,4},{2,6},{4,0},{6,2},{8,12},{10,14},{12,8},{14,10},{16,20},{18,... | collective-permute-start | bytes 1253384 | tf_op jit(solution)/shard_map/ppermute | solution.py:312
  88.2 21.6 %collective-permute-start.12 = (bf16[272,768]{1,0:T(8,128)(2,1)S(1)}, bf16[272,768]{1,0:T(8,128)(2,1)S(1)}, u32[]{:S(2)}, u32[]{:S(2)}) collective-permute-start(bf16[272,768]{1,0:T(8,128)(2,1)S(1)} %collective-permute-done.11.refs_4_), channel_id=1, source_target_pairs={{0,2},{2,0},{4,6},{6,4},{8,10},{10,8},{12,14},{14,12},{16,18},{18,... | collective-permute-start | bytes 1253384 | tf_op jit(solution)/shard_map/ppermute | solution.py:315
  114.8 14.2 %collective-permute-start.28 = (bf16[1024,256]{1,0:T(8,128)(2,1)S(1)}, bf16[1024,256]{1,0:T(8,128)(2,1)S(1)}, u32[]{:S(2)}, u32[]{:S(2)}) collective-permute-start(bf16[1024,256]{1,0:T(8,128)(2,1)S(1)} %collective-permute-done.13.refs_12_), channel_id=1, source_target_pairs={{0,8},{2,10},{4,12},{6,14},{8,0},{10,2},{12,4},{14,6},{16,24},{18,... | collective-permute-start | bytes 1572872 | tf_op jit(solution)/shard_map/ppermute | solution.py:305
  117.8 11.2 %collective-permute-start.27 = (bf16[4,128,256]{2,1,0:T(8,128)(2,1)S(1)}, bf16[4,128,256]{2,1,0:T(8,128)(2,1)S(1)}, u32[]{:S(2)}, u32[]{:S(2)}) collective-permute-start(bf16[4,128,256]{2,1,0:T(8,128)(2,1)S(1)} %get-tuple-element.95), channel_id=1, source_target_pairs={{0,4},{2,6},{4,0},{6,2},{8,12},{10,14},{12,8},{14,10},{16,20},{18,... | collective-permute-start | bytes 786440 | tf_op jit(solution)/shard_map/ppermute | solution.py:312
  118.4 24.1 %collective-permute-start.36 = (bf16[1024,256]{1,0:T(8,128)(2,1)S(1)}, bf16[1024,256]{1,0:T(8,128)(2,1)S(1)}, u32[]{:S(2)}, u32[]{:S(2)}) collective-permute-start(bf16[1024,256]{1,0:T(8,128)(2,1)S(1)} %collective-permute-done.13.refs_12_), channel_id=1, source_target_pairs={{0,4},{2,6},{4,0},{6,2},{8,12},{10,14},{12,8},{14,10},{16,20},{18,... | collective-permute-start | bytes 1572872 | tf_op jit(solution)/shard_map/ppermute | solution.py:312
  129.0 19.6 %collective-permute-start.37 = (bf16[1024,256]{1,0:T(8,128)(2,1)S(1)}, bf16[1024,256]{1,0:T(8,128)(2,1)S(1)}, u32[]{:S(2)}, u32[]{:S(2)}) collective-permute-start(bf16[1024,256]{1,0:T(8,128)(2,1)S(1)} %collective-permute-done.28.refs_14_), channel_id=1, source_target_pairs={{0,4},{2,6},{4,0},{6,2},{8,12},{10,14},{12,8},{14,10},{16,20},{18,... | collective-permute-start | bytes 1572872 | tf_op jit(solution)/shard_map/ppermute | solution.py:312
  154.9 12.4 %collective-permute-start.41 = (bf16[4,128,256]{2,1,0:T(8,128)(2,1)S(1)}, bf16[4,128,256]{2,1,0:T(8,128)(2,1)S(1)}, u32[]{:S(2)}, u32[]{:S(2)}) collective-permute-start(bf16[4,128,256]{2,1,0:T(8,128)(2,1)S(1)} %collective-permute-done.40), channel_id=1, source_target_pairs={{0,1},{1,0},{2,3},{3,2},{4,5},{5,4},{6,7},{7,6},{8,9},{9,8},{10,11... | collective-permute-start | bytes 786440 | tf_op jit(solution)/shard_map/ppermute | solution.py:318
  (34 other events, 287.3 us)

commit v5 on v4

--- a/solution.py
+++ b/solution.py
@@ -19,7 +19,7 @@
     return lax.dot_general(a, b, dims, preferred_element_type=F32)
 
 
-def call(kernel, ins, outs, scratch=(), flops=0, scalars=1, column=None, room=20):
+def call(kernel, ins, outs, scratch=(), flops=0, scalars=1, column=None, room=12):
     moved = sum(math.prod(a.shape) * a.dtype.itemsize for a in (*ins, *outs))
 
     def whole(a):
@@ -232,9 +232,9 @@
             outs[j][m] = done[z ^ j, c ^ m]
 
 
-def out_kernel(zn, xn, cn, n_head, at, *refs):
+def out_kernel(zn, xn, cn, n_head, slots, at, *refs):
     attended = refs[: zn * cn]
-    weights = refs[zn * cn : zn * cn + zn * xn]
+    weights = refs[zn * cn : zn * cn + len(slots) * xn]
     outs, rows = refs[-1 - cn * n_head : -1], refs[-1]
     z, x, c, y = at[0], at[1], at[2], at[3]
     seg_rows = attended[0].shape[1]
@@ -245,11 +245,12 @@
                     attended[j * cn + e][m ^ e]
                 )
     blocks = outs[0].shape[0]
-    for j in range(zn):
+    share = zn * xn // n_head
+    for n, j in enumerate(slots):
         for k in range(xn):
-            product = dot(rows[...], weights[j * xn + k][...]).astype(BF16)
+            product = dot(rows[...], weights[n * xn + k][...]).astype(BF16)
             spot = (z ^ j) * xn + lax.rem(x + xn - k, xn)
-            turn = lax.rem(spot // blocks + n_head - y, n_head)
+            turn = lax.rem(spot // share + n_head - y, n_head)
             for r in range(n_head):
 
                 @pl.when(turn == r)
@@ -260,20 +261,23 @@
                         ]
 
 
-def sum_kernel(n_head, cn, at, *refs):
+def sum_kernel(n_head, cn, phases, at, *refs):
     out = refs[-1]
-    blocks, _, size = refs[0].shape
-    for b in range(blocks):
-        totals = [
-            sum(refs[r * cn + e][b].astype(F32) for r in range(n_head)).astype(BF16)
-            for e in range(cn)
-        ]
-        for m in range(cn):
-            total = totals[0]
-            for e in range(1, cn):
-                total = jnp.where((at[2] ^ e) == m, totals[e], total)
-            first = (b * cn + m) * size
-            out[:, first : first + size] = total
+    blocks, seg_rows, size = refs[0].shape
+    for p in range(phases):
+        few = refs[p * n_head * cn : (p + 1) * n_head * cn]
+        places = []
+        for b in range(blocks):
+            totals = [
+                sum(few[r * cn + e][b].astype(F32) for r in range(n_head)).astype(BF16)
+                for e in range(cn)
+            ]
+            for m in range(cn):
+                total = totals[0]
+                for e in range(1, cn):
+                    total = jnp.where((at[2] ^ e) == m, totals[e], total)
+                places.append(total)
+        out[:, lanes(lax.rem(at[0] ^ p, phases), blocks * cn * size)] = jnp.concatenate(places, 1)
 
 
 def body(tokens, gain, w_query, w_key, w_value, w_out, mem_query, score_scale, decay, seg_len):
@@ -392,9 +396,7 @@
 
     bits = [1 << n for n in range(zn.bit_length() - 1)]
     more = [j for j in range(1, zn) if j not in bits]
-    parts, first, whole, columns[0][1:] = done_all(
-        [started[b] for b in bits], started["y", 0], started["x", 0], started["o", 0]
-    )
+    parts, first, whole = done_all([started[b] for b in bits], started["y", 0], started["x", 0])
     tok.update(zip(bits, parts))
     end_x(0, whole)
     for b in bits:
@@ -405,9 +407,10 @@
     for j in early[1:]:
         started["w", j] = over_z(after(sent[j], tok[1]), j)
     end_y(0, first)
-    parts, far, *near = done_all(
+    parts, far, columns[0][1:], *near = done_all(
         [started["w", j] for j in early],
         [started[j] for j in more],
+        started["o", 0],
         *(started["y", b] for b in bits),
     )
     packs.update(zip(early, parts))
@@ -416,19 +419,21 @@
         started["w", j] = over_z(after(sent[j], packs[j - 1]), j)
     for j in more:
         begin_y(j)
-    for j in early:
-        begin_x(j)
     if last:
+        begin_x(1)
         started["oz", 1] = over_z(after(w_out, packs[early[-1]]), 1)
     for b, others in zip(bits, near):
         end_y(b, others)
-    for j in more:
-        end_y(j, done_all(started["y", j])[0])
+    for j in early[1:]:
+        packs[j] = lax.optimization_barrier((packs[j], *(rows[b] for b in bits)))[0]
+        begin_x(j)
     for j in range(len(early) + 1, zn):
         packs[j] = done(started["w", j])
         begin_x(j)
     for b in bits[1:]:
         started["oz", b] = over_z(after(w_out, packs[last]), b)
+    for j in more:
+        end_y(j, done_all(started["y", j])[0])
     for j in range(1, last):
         end_x(j, done_all(started["x", j])[0])
     if last:
@@ -449,7 +454,7 @@
             ],
             [pltpu.VMEM((last, chunk_rows, cn * 3 * DH), BF16)],
             flops * last,
-            room=48,
+            room=30,
         )
         mark(before[0])
     if last:
@@ -469,7 +474,7 @@
         [pltpu.VMEM((chunk_rows, cn * 3 * DH), BF16)],
         flops,
         column=(chunk_rows, lambda at: at[0] ^ last),
-        room=32,
+        room=20,
     )
     parts = [done(over_c(part, m)) if m else part for m, part in enumerate(parts)]
     sums, written, group, group16, table = call(
@@ -513,25 +518,27 @@
 
     for j in range(2, zn):
         end_out(j)
-    columns = sum((columns[j] for j in range(zn)), [])
     out_cols = w_out.shape[1]
-    blocks = feat_local // (cn * out_cols)
-    products = call(
-        functools.partial(out_kernel, zn, xn, cn, n_head),
-        (at, *here, *columns),
-        [shape((blocks, seg_rows, out_cols))] * (cn * n_head),
-        [pltpu.VMEM((cn * seg_rows, heads * DH), BF16)],
-        2 * cn * seg_rows * heads * DH * zn * xn * out_cols,
-        room=32,
-    )
+    phases = zn // n_head if zn % n_head == 0 else 1
+    blocks = feat_local // (cn * out_cols * phases)
     mine = []
-    for r in range(n_head):
-        for m in range(cn):
-            block = products[r * cn + m]
-            block = over_c(block, m) if m else block
-            mine.append(over_y(block, r) if r else block)
+    for p in range(phases):
+        few = range(p, zn, phases)
+        products = call(
+            functools.partial(out_kernel, zn, xn, cn, n_head, few),
+            (at, *here, *sum((columns[j] for j in few), [])),
+            [shape((blocks, seg_rows, out_cols))] * (cn * n_head),
+            [pltpu.VMEM((cn * seg_rows, heads * DH), BF16)],
+            2 * cn * seg_rows * heads * DH * len(few) * xn * out_cols,
+            room=20,
+        )
+        for r in range(n_head):
+            for m in range(cn):
+                block = products[r * cn + m]
+                block = over_c(block, m) if m else block
+                mine.append(over_y(block, r) if r else block)
     (branch,) = call(
-        functools.partial(sum_kernel, n_head, cn),
+        functools.partial(sum_kernel, n_head, cn, phases),
         (at, *mine),
         [shape((seg_rows, feat_local))],
     )

time: 169 us -> 164 us (0.970)
  starting transfers between devices: 36.3 us -> 43.6 us
  waiting for transfers between devices: 99 us -> 93.8 us
  local copies, waits for them, and re-layouts: 8.16 us -> 3.8 us
  Pallas kernels: 24.3 us -> 21.7 us
    ppermute x12, waiting for transfers between devices: 48.9 us -> 39.9 us  [over_z(): return lax.ppermute(a, 'seq', pairs)]
    ppermute x9, waiting for transfers between devices: 34.5 us -> 39.5 us  [over_x(): return lax.ppermute(a, 'seq', pairs)]
    unnamed x32 -> x18, local copies, waits for them, and re-layouts: 8.16 us -> 3.8 us
    ppermute x12, starting transfers between devices: 17 us -> 21.1 us  [over_z(): return lax.ppermute(a, 'seq', pairs)]
    pallas_call x12 -> x13, Pallas kernels: 24.3 us -> 21.7 us  [call(): pl.pallas_call(kernel, grid_spec=pltpu.PrefetchScalarGridSpec(num_scalar_...]
    ppermute x9, starting transfers between devices: 8.8 us -> 10.7 us  [over_x(): return lax.ppermute(a, 'seq', pairs)]
    ppermute x6 -> x8, starting transfers between devices: 7.61 us -> 9.25 us  [over_y(): lax.ppermute(a, 'head', [(h, (h + k) % n_head) for h in range(n_head)])]
    ppermute x6 -> x8, waiting for transfers between devices: 11.4 us -> 10.2 us  [over_y(): lax.ppermute(a, 'head', [(h, (h + k) % n_head) for h in range(n_head)])]
  transfers between devices with their start and end apart: 42 -> 46, of which waited for: 16 -> 23; matrix products, arithmetic and copies ran while one was open for 0% -> 0% of each run, Pallas kernels for 10% -> 11%
where the time goes in v5:
time: 164 us
  waiting for transfers between devices  93.8 us (57%)
  starting transfers between devices  43.6 us (27%)
  Pallas kernels  21.7 us (13%)
  local copies, waits for them, and re-layouts  3.8 us (2%)
    ppermute x12, waiting for transfers between devices, over_z(): return lax.ppermute(a, 'seq', pairs)  39.9 us
    ppermute x9, waiting for transfers between devices, over_x(): return lax.ppermute(a, 'seq', pairs)  39.5 us
    pallas_call x13, Pallas kernels, call(): pl.pallas_call(kernel, grid_spec=pltpu.PrefetchScalarGridSpec(num_scalar_...  21.7 us
    ppermute x12, starting transfers between devices, over_z(): return lax.ppermute(a, 'seq', pairs)  21.1 us
    ppermute x9, starting transfers between devices, over_x(): return lax.ppermute(a, 'seq', pairs)  10.7 us
    ppermute x8, waiting for transfers between devices, over_y(): lax.ppermute(a, 'head', [(h, (h + k) % n_head) for h in range(n_head)])  10.2 us
    ppermute x8, starting transfers between devices, over_y(): lax.ppermute(a, 'head', [(h, (h + k) % n_head) for h in range(n_head)])  9.25 us
    ppermute x17, waiting for transfers between devices, over_c(): return lax.ppermute(a, 'seq', [(s, s ^ m) for s in range(n_seq)])  4.25 us
  transfers between devices with their start and end apart: 46, of which 23 were waited for; matrix products, arithmetic and copies ran while one was open for 0% of the time, Pallas kernels for 11%

profile of v5, /device:TPU:0, one launch (start us, length us, event | category | flops | bytes accessed | tf_op | source)
XLA Modules:
  0.0 163.8 jit_solution(15510705832492505843)
XLA Ops:
  0.0 3.0 %collective-permute-start = (bf16[128,2048]{1,0:T(8,128)(2,1)}, bf16[128,2048]{1,0:T(8,128)(2,1)S(1)}, u32[]{:S(2)}, u32[]{:S(2)}) collective-permute-start(bf16[128,2048]{1,0:T(8,128)(2,1)} %refs_0_.3), channel_id=1, source_target_pairs={{0,8},{2,10},{4,12},{6,14},{8,0},{10,2},{12,4},{14,6},{16,24},{18,... | collective-permute-start | bytes 1572872 | tf_op jit(solution)/shard_map/ppermute | solution.py:309
  3.0 2.6 %collective-permute-start.1 = (bf16[128,2048]{1,0:T(8,128)(2,1)}, bf16[128,2048]{1,0:T(8,128)(2,1)S(1)}, u32[]{:S(2)}, u32[]{:S(2)}) collective-permute-start(bf16[128,2048]{1,0:T(8,128)(2,1)} %refs_0_.3), channel_id=1, source_target_pairs={{0,16},{2,18},{4,20},{6,22},{8,24},{10,26},{12,28},{14,30},{16,0},... | collective-permute-start | bytes 1572872 | tf_op jit(solution)/shard_map/ppermute | solution.py:309
  14.6 8.6 %collective-permute-done.3.refs_6_ = bf16[272,768]{1,0:T(8,128)(2,1)S(1)} collective-permute-done((bf16[272,768]{1,0:T(8,128)(2,1)S(1)}, bf16[272,768]{1,0:T(8,128)(2,1)S(1)}, u32[]{:S(2)}, u32[]{:S(2)}) %collective-permute-start.3) | collective-permute-done | bytes 417824 | tf_op jit(solution)/shard_map/ppermute | solution.py:316
  24.7 2.4 %collective-permute-done.refs_0_ = bf16[128,2048]{1,0:T(8,128)(2,1)S(1)} collective-permute-done((bf16[128,2048]{1,0:T(8,128)(2,1)}, bf16[128,2048]{1,0:T(8,128)(2,1)S(1)}, u32[]{:S(2)}, u32[]{:S(2)}) %collective-permute-start) | collective-permute-done | bytes 524320 | tf_op jit(solution)/shard_map/ppermute | solution.py:309
  27.9 2.5 %collective-permute-start.6 = (bf16[128,2048]{1,0:T(8,128)(2,1)S(1)}, bf16[128,2048]{1,0:T(8,128)(2,1)S(1)}, u32[]{:S(2)}, u32[]{:S(2)}) collective-permute-start(bf16[128,2048]{1,0:T(8,128)(2,1)S(1)} %collective-permute-done.1.refs_0_), channel_id=1, source_target_pairs={{0,8},{2,10},{4,12},{6,14},{8,0},{10,2},{12,4},{14,6},{16,24},{18,... | collective-permute-start | bytes 1572872 | tf_op jit(solution)/shard_map/ppermute | solution.py:309
  32.4 3.8 %collective-permute-done.4.refs_8_ = bf16[272,768]{1,0:T(8,128)(2,1)S(1)} collective-permute-done((bf16[272,768]{1,0:T(8,128)(2,1)S(1)}, bf16[272,768]{1,0:T(8,128)(2,1)S(1)}, u32[]{:S(2)}, u32[]{:S(2)}) %collective-permute-start.4) | collective-permute-done | bytes 417824 | tf_op jit(solution)/shard_map/ppermute | solution.py:309
  36.2 3.1 %collective-permute-start.5 = (bf16[272,768]{1,0:T(8,128)(2,1)S(1)}, bf16[272,768]{1,0:T(8,128)(2,1)S(1)}, u32[]{:S(2)}, u32[]{:S(2)}) collective-permute-start(bf16[272,768]{1,0:T(8,128)(2,1)S(1)} %get-tuple-element.71), channel_id=1, source_target_pairs={{0,16},{2,18},{4,20},{6,22},{8,24},{10,26},{12,28},{14,30},{16,0},... | collective-permute-start | bytes 1253384 | tf_op jit(solution)/shard_map/ppermute | solution.py:309
  40.3 14.6 %collective-permute-done.5.refs_12_ = bf16[272,768]{1,0:T(8,128)(2,1)S(1)} collective-permute-done((bf16[272,768]{1,0:T(8,128)(2,1)S(1)}, bf16[272,768]{1,0:T(8,128)(2,1)S(1)}, u32[]{:S(2)}, u32[]{:S(2)}) %collective-permute-start.5) | collective-permute-done | bytes 417824 | tf_op jit(solution)/shard_map/ppermute | solution.py:309
  55.5 4.1 %collective-permute-start.11 = (bf16[272,768]{1,0:T(8,128)(2,1)S(1)}, bf16[272,768]{1,0:T(8,128)(2,1)S(1)}, u32[]{:S(2)}, u32[]{:S(2)}) collective-permute-start(bf16[272,768]{1,0:T(8,128)(2,1)S(1)} %get-tuple-element.78), channel_id=1, source_target_pairs={{0,24},{2,26},{4,28},{6,30},{8,16},{10,18},{12,20},{14,22},{16,8},... | collective-permute-start | bytes 1253384 | tf_op jit(solution)/shard_map/ppermute | solution.py:309
  65.2 5.0 %collective-permute-done.11.refs_4_ = bf16[272,768]{1,0:T(8,128)(2,1)S(1)} collective-permute-done((bf16[272,768]{1,0:T(8,128)(2,1)S(1)}, bf16[272,768]{1,0:T(8,128)(2,1)S(1)}, u32[]{:S(2)}, u32[]{:S(2)}) %collective-permute-start.11) | collective-permute-done | bytes 417824 | tf_op jit(solution)/shard_map/ppermute | solution.py:309
  70.2 4.5 %collective-permute-done.17.refs_10_ = bf16[272,768]{1,0:T(8,128)(2,1)S(1)} collective-permute-done((bf16[272,768]{1,0:T(8,128)(2,1)S(1)}, bf16[272,768]{1,0:T(8,128)(2,1)S(1)}, u32[]{:S(2)}, u32[]{:S(2)}) %collective-permute-start.17) | collective-permute-done | bytes 417824 | tf_op jit(solution)/shard_map/ppermute | solution.py:316
  74.7 5.7 %collective-permute-done.16.refs_14_ = bf16[272,768]{1,0:T(8,128)(2,1)S(1)} collective-permute-done((bf16[272,768]{1,0:T(8,128)(2,1)S(1)}, bf16[272,768]{1,0:T(8,128)(2,1)S(1)}, u32[]{:S(2)}, u32[]{:S(2)}) %collective-permute-start.16) | collective-permute-done | bytes 417824 | tf_op jit(solution)/shard_map/ppermute | solution.py:316
  85.4 3.4 %shard_map.105 = (f32[4,128,768]{2,1,0:T(8,128)S(1)}, f32[3,2,2,16,128]{4,3,2,1,0:T(8,128)S(1)}) custom-call(s32[4]{0:T(128)S(1)} %pad_add_fusion.at, bf16[128,4096]{1,0:T(8,128)(2,1)S(1)} %shard_map.101.refs_0_, bf16[128,4096]{1,0:T(8,128)(2,1)S(1)} %shard_map.102.refs_1_, bf16[128,4096]{1,0:T(8,128)(2,1)S(1)} %shard_map.103.refs_2_, ...), custom_call_target="tpu_custom_call" | custom-call | flops 2415919104 | bytes 10878992 | tf_op jit(solution)/shard_map/pallas_call | solution.py:34
  88.8 17.1 %collective-permute-done.14.refs_6_ = bf16[272,768]{1,0:T(8,128)(2,1)S(1)} collective-permute-done((bf16[272,768]{1,0:T(8,128)(2,1)S(1)}, bf16[272,768]{1,0:T(8,128)(2,1)S(1)}, u32[]{:S(2)}, u32[]{:S(2)}) %collective-permute-start.14) | collective-permute-done | bytes 417824 | tf_op jit(solution)/shard_map/ppermute | solution.py:316
  118.7 7.2 %collective-permute-done.28.refs_10_ = bf16[1024,256]{1,0:T(8,128)(2,1)S(1)} collective-permute-done((bf16[1024,256]{1,0:T(8,128)(2,1)S(1)}, bf16[1024,256]{1,0:T(8,128)(2,1)S(1)}, u32[]{:S(2)}, u32[]{:S(2)}) %collective-permute-start.28) | collective-permute-done | bytes 524320 | tf_op jit(solution)/shard_map/ppermute | solution.py:309
  131.4 2.6 %collective-permute-start.30 = (bf16[2,128,128]{2,1,0:T(8,128)(2,1)S(1)}, bf16[2,128,128]{2,1,0:T(8,128)(2,1)S(1)}, u32[]{:S(2)}, u32[]{:S(2)}) collective-permute-start(bf16[2,128,128]{2,1,0:T(8,128)(2,1)S(1)} %get-tuple-element.105), channel_id=1, source_target_pairs={{0,24},{2,26},{4,28},{6,30},{8,16},{10,18},{12,20},{14,22},{16,8},... | collective-permute-start | bytes 196616 | tf_op jit(solution)/shard_map/ppermute | solution.py:309
  134.0 2.8 %collective-permute-done.31.refs_4_ = bf16[2,128,128]{2,1,0:T(8,128)(2,1)S(1)} collective-permute-done((bf16[2,128,128]{2,1,0:T(8,128)(2,1)S(1)}, bf16[2,128,128]{2,1,0:T(8,128)(2,1)S(1)}, u32[]{:S(2)}, u32[]{:S(2)}) %collective-permute-start.31) | collective-permute-done | bytes 65568 | tf_op jit(solution)/shard_map/ppermute | solution.py:309
  139.0 2.4 %shard_map.110 = (bf16[2,128,256]{2,1,0:T(8,128)(2,1)S(1)}, bf16[2,128,256]{2,1,0:T(8,128)(2,1)S(1)}, bf16[2,128,256]{2,1,0:T(8,128)(2,1)S(1)}, bf16[2,128,256]{2,1,0:T(8,128)(2,1)S(1)}) custom-call(s32[4]{0:T(128)S(1)} %pad_add_fusion.at, bf16[2,128,128]{2,1,0:T(8,128)(2,1)S(1)} %get-tuple-element.104.refs_0_, ...), custom_call_target="tpu_custom_call" | custom-call | flops 536870912 | bytes 3145744 | tf_op jit(solution)/shard_map/pallas_call | solution.py:34
  142.0 3.5 %collective-permute-done.41.refs_11_ = bf16[1024,256]{1,0:T(8,128)(2,1)S(1)} collective-permute-done((bf16[1024,256]{1,0:T(8,128)(2,1)S(1)}, bf16[1024,256]{1,0:T(8,128)(2,1)S(1)}, u32[]{:S(2)}, u32[]{:S(2)}) %collective-permute-start.41) | collective-permute-done | bytes 524320 | tf_op jit(solution)/shard_map/ppermute | solution.py:316
  145.5 2.4 %shard_map.111 = (bf16[2,128,256]{2,1,0:T(8,128)(2,1)S(1)}, bf16[2,128,256]{2,1,0:T(8,128)(2,1)S(1)}, bf16[2,128,256]{2,1,0:T(8,128)(2,1)S(1)}, bf16[2,128,256]{2,1,0:T(8,128)(2,1)S(1)}) custom-call(s32[4]{0:T(128)S(1)} %pad_add_fusion.at, bf16[2,128,128]{2,1,0:T(8,128)(2,1)S(1)} %get-tuple-element.104.refs_0_, ...), custom_call_target="tpu_custom_call" | custom-call | flops 536870912 | bytes 3145744 | tf_op jit(solution)/shard_map/pallas_call | solution.py:34
  152.1 2.2 %collective-permute-done.38.refs_2_ = bf16[2,128,256]{2,1,0:T(8,128)(2,1)S(1)} collective-permute-done((bf16[2,128,256]{2,1,0:T(8,128)(2,1)S(1)}, bf16[2,128,256]{2,1,0:T(8,128)(2,1)S(1)}, u32[]{:S(2)}, u32[]{:S(2)}) %collective-permute-start.38) | collective-permute-done | bytes 131104 | tf_op jit(solution)/shard_map/ppermute | solution.py:322
  154.3 2.8 %collective-permute-done.40.refs_3_ = bf16[2,128,256]{2,1,0:T(8,128)(2,1)S(1)} collective-permute-done((bf16[2,128,256]{2,1,0:T(8,128)(2,1)S(1)}, bf16[2,128,256]{2,1,0:T(8,128)(2,1)S(1)}, u32[]{:S(2)}, u32[]{:S(2)}) %collective-permute-start.40) | collective-permute-done | bytes 131104 | tf_op jit(solution)/shard_map/ppermute | solution.py:322
  157.1 2.8 %collective-permute-done.43.refs_6_ = bf16[2,128,256]{2,1,0:T(8,128)(2,1)S(1)} collective-permute-done((bf16[2,128,256]{2,1,0:T(8,128)(2,1)S(1)}, bf16[2,128,256]{2,1,0:T(8,128)(2,1)S(1)}, u32[]{:S(2)}, u32[]{:S(2)}) %collective-permute-start.43) | collective-permute-done | bytes 131104 | tf_op jit(solution)/shard_map/ppermute | solution.py:322
  159.9 2.4 %collective-permute-done.45.refs_7_ = bf16[2,128,256]{2,1,0:T(8,128)(2,1)S(1)} collective-permute-done((bf16[2,128,256]{2,1,0:T(8,128)(2,1)S(1)}, bf16[2,128,256]{2,1,0:T(8,128)(2,1)S(1)}, u32[]{:S(2)}, u32[]{:S(2)}) %collective-permute-start.45) | collective-permute-done | bytes 131104 | tf_op jit(solution)/shard_map/ppermute | solution.py:322
  (100 shorter events, 51.4 us)
Async XLA Ops:
  0.0 27.1 %collective-permute-start = (bf16[128,2048]{1,0:T(8,128)(2,1)}, bf16[128,2048]{1,0:T(8,128)(2,1)S(1)}, u32[]{:S(2)}, u32[]{:S(2)}) collective-permute-start(bf16[128,2048]{1,0:T(8,128)(2,1)} %refs_0_.3), channel_id=1, source_target_pairs={{0,8},{2,10},{4,12},{6,14},{8,0},{10,2},{12,4},{14,6},{16,24},{18,... | collective-permute-start | bytes 1572872 | tf_op jit(solution)/shard_map/ppermute | solution.py:309
  3.0 24.8 %collective-permute-start.1 = (bf16[128,2048]{1,0:T(8,128)(2,1)}, bf16[128,2048]{1,0:T(8,128)(2,1)S(1)}, u32[]{:S(2)}, u32[]{:S(2)}) collective-permute-start(bf16[128,2048]{1,0:T(8,128)(2,1)} %refs_0_.3), channel_id=1, source_target_pairs={{0,16},{2,18},{4,20},{6,22},{8,24},{10,26},{12,28},{14,30},{16,0},... | collective-permute-start | bytes 1572872 | tf_op jit(solution)/shard_map/ppermute | solution.py:309
  5.6 22.2 %collective-permute-start.2 = (bf16[128,2048]{1,0:T(8,128)(2,1)}, bf16[128,2048]{1,0:T(8,128)(2,1)S(1)}, u32[]{:S(2)}, u32[]{:S(2)}) collective-permute-start(bf16[128,2048]{1,0:T(8,128)(2,1)} %refs_0_.3), channel_id=1, source_target_pairs={{0,1},{1,0},{2,3},{3,2},{4,5},{5,4},{6,7},{7,6},{8,9},{9,8},{10,11... | collective-permute-start | bytes 1572872 | tf_op jit(solution)/shard_map/ppermute | solution.py:322
  14.2 22.0 %collective-permute-start.4 = (bf16[272,768]{1,0:T(8,128)(2,1)S(1)}, bf16[272,768]{1,0:T(8,128)(2,1)S(1)}, u32[]{:S(2)}, u32[]{:S(2)}) collective-permute-start(bf16[272,768]{1,0:T(8,128)(2,1)S(1)} %get-tuple-element.69), channel_id=1, source_target_pairs={{0,8},{2,10},{4,12},{6,14},{8,0},{10,2},{12,4},{14,6},{16,24},{18,... | collective-permute-start | bytes 1253384 | tf_op jit(solution)/shard_map/ppermute | solution.py:309
  23.2 17.0 %collective-permute-start.7 = (bf16[1024,256]{1,0:T(8,128)(2,1)S(1)}, bf16[1024,256]{1,0:T(8,128)(2,1)S(1)}, u32[]{:S(2)}, u32[]{:S(2)}) collective-permute-start(bf16[1024,256]{1,0:T(8,128)(2,1)S(1)} %copy-done.4), channel_id=1, source_target_pairs={{0,4},{2,6},{4,0},{6,2},{8,12},{10,14},{12,8},{14,10},{16,20},{18,... | collective-permute-start | bytes 1572872 | tf_op jit(solution)/shard_map/ppermute | solution.py:316
  27.9 27.7 %collective-permute-start.6 = (bf16[128,2048]{1,0:T(8,128)(2,1)S(1)}, bf16[128,2048]{1,0:T(8,128)(2,1)S(1)}, u32[]{:S(2)}, u32[]{:S(2)}) collective-permute-start(bf16[128,2048]{1,0:T(8,128)(2,1)S(1)} %collective-permute-done.1.refs_0_), channel_id=1, source_target_pairs={{0,8},{2,10},{4,12},{6,14},{8,0},{10,2},{12,4},{14,6},{16,24},{18,... | collective-permute-start | bytes 1572872 | tf_op jit(solution)/shard_map/ppermute | solution.py:309
  30.3 25.2 %collective-permute-start.8 = (bf16[128,2048]{1,0:T(8,128)(2,1)S(1)}, bf16[128,2048]{1,0:T(8,128)(2,1)S(1)}, u32[]{:S(2)}, u32[]{:S(2)}) collective-permute-start(bf16[128,2048]{1,0:T(8,128)(2,1)S(1)} %collective-permute-done.refs_0_), channel_id=1, source_target_pairs={{0,1},{1,0},{2,3},{3,2},{4,5},{5,4},{6,7},{7,6},{8,9},{9,8},{10,11... | collective-permute-start | bytes 1572872 | tf_op jit(solution)/shard_map/ppermute | solution.py:322
  31.9 23.7 %collective-permute-start.9 = (bf16[128,2048]{1,0:T(8,128)(2,1)S(1)}, bf16[128,2048]{1,0:T(8,128)(2,1)S(1)}, u32[]{:S(2)}, u32[]{:S(2)}) collective-permute-start(bf16[128,2048]{1,0:T(8,128)(2,1)S(1)} %collective-permute-done.1.refs_0_), channel_id=1, source_target_pairs={{0,1},{1,0},{2,3},{3,2},{4,5},{5,4},{6,7},{7,6},{8,9},{9,8},{10,11... | collective-permute-start | bytes 1572872 | tf_op jit(solution)/shard_map/ppermute | solution.py:322
  36.2 18.7 %collective-permute-start.5 = (bf16[272,768]{1,0:T(8,128)(2,1)S(1)}, bf16[272,768]{1,0:T(8,128)(2,1)S(1)}, u32[]{:S(2)}, u32[]{:S(2)}) collective-permute-start(bf16[272,768]{1,0:T(8,128)(2,1)S(1)} %get-tuple-element.71), channel_id=1, source_target_pairs={{0,16},{2,18},{4,20},{6,22},{8,24},{10,26},{12,28},{14,30},{16,0},... | collective-permute-start | bytes 1253384 | tf_op jit(solution)/shard_map/ppermute | solution.py:309
  55.5 14.6 %collective-permute-start.11 = (bf16[272,768]{1,0:T(8,128)(2,1)S(1)}, bf16[272,768]{1,0:T(8,128)(2,1)S(1)}, u32[]{:S(2)}, u32[]{:S(2)}) collective-permute-start(bf16[272,768]{1,0:T(8,128)(2,1)S(1)} %get-tuple-element.78), channel_id=1, source_target_pairs={{0,24},{2,26},{4,28},{6,30},{8,16},{10,18},{12,20},{14,22},{16,8},... | collective-permute-start | bytes 1253384 | tf_op jit(solution)/shard_map/ppermute | solution.py:309
  60.6 19.9 %collective-permute-start.10 = (bf16[128,2048]{1,0:T(8,128)(2,1)S(1)}, bf16[128,2048]{1,0:T(8,128)(2,1)S(1)}, u32[]{:S(2)}, u32[]{:S(2)}) collective-permute-start(bf16[128,2048]{1,0:T(8,128)(2,1)S(1)} %collective-permute-done.6.refs_0_), channel_id=1, source_target_pairs={{0,1},{1,0},{2,3},{3,2},{4,5},{5,4},{6,7},{7,6},{8,9},{9,8},{10,11... | collective-permute-start | bytes 1572872 | tf_op jit(solution)/shard_map/ppermute | solution.py:322
  62.1 12.6 %collective-permute-start.17 = (bf16[272,768]{1,0:T(8,128)(2,1)S(1)}, bf16[272,768]{1,0:T(8,128)(2,1)S(1)}, u32[]{:S(2)}, u32[]{:S(2)}) collective-permute-start(bf16[272,768]{1,0:T(8,128)(2,1)S(1)} %collective-permute-done.4.refs_8_), channel_id=1, source_target_pairs={{0,4},{2,6},{4,0},{6,2},{8,12},{10,14},{12,8},{14,10},{16,20},{18,... | collective-permute-start | bytes 1253384 | tf_op jit(solution)/shard_map/ppermute | solution.py:316
  64.6 15.9 %collective-permute-start.16 = (bf16[272,768]{1,0:T(8,128)(2,1)S(1)}, bf16[272,768]{1,0:T(8,128)(2,1)S(1)}, u32[]{:S(2)}, u32[]{:S(2)}) collective-permute-start(bf16[272,768]{1,0:T(8,128)(2,1)S(1)} %collective-permute-done.5.refs_12_), channel_id=1, source_target_pairs={{0,4},{2,6},{4,0},{6,2},{8,12},{10,14},{12,8},{14,10},{16,20},{18,... | collective-permute-start | bytes 1253384 | tf_op jit(solution)/shard_map/ppermute | solution.py:316
  65.2 16.8 %collective-permute-start.15 = (bf16[1024,256]{1,0:T(8,128)(2,1)S(1)}, bf16[1024,256]{1,0:T(8,128)(2,1)S(1)}, u32[]{:S(2)}, u32[]{:S(2)}) collective-permute-start(bf16[1024,256]{1,0:T(8,128)(2,1)S(1)} %copy-done.4), channel_id=1, source_target_pairs={{0,8},{2,10},{4,12},{6,14},{8,0},{10,2},{12,4},{14,6},{16,24},{18,... | collective-permute-start | bytes 1572872 | tf_op jit(solution)/shard_map/ppermute | solution.py:309
  70.2 11.7 %collective-permute-start.19 = (bf16[272,768]{1,0:T(8,128)(2,1)S(1)}, bf16[272,768]{1,0:T(8,128)(2,1)S(1)}, u32[]{:S(2)}, u32[]{:S(2)}) collective-permute-start(bf16[272,768]{1,0:T(8,128)(2,1)S(1)} %get-tuple-element.66.refs_4_), channel_id=1, source_target_pairs={{0,2},{2,0},{4,6},{6,4},{8,10},{10,8},{12,14},{14,12},{16,18},{18,... | collective-permute-start | bytes 1253384 | tf_op jit(solution)/shard_map/ppermute | solution.py:319
  82.5 25.4 %collective-permute-start.13 = (bf16[1024,256]{1,0:T(8,128)(2,1)S(1)}, bf16[1024,256]{1,0:T(8,128)(2,1)S(1)}, u32[]{:S(2)}, u32[]{:S(2)}) collective-permute-start(bf16[1024,256]{1,0:T(8,128)(2,1)S(1)} %copy-done.4), channel_id=1, source_target_pairs={{0,16},{2,18},{4,20},{6,22},{8,24},{10,26},{12,28},{14,30},{16,0},... | collective-permute-start | bytes 1572872 | tf_op jit(solution)/shard_map/ppermute | solution.py:309
  83.4 24.5 %collective-permute-start.18 = (bf16[1024,256]{1,0:T(8,128)(2,1)S(1)}, bf16[1024,256]{1,0:T(8,128)(2,1)S(1)}, u32[]{:S(2)}, u32[]{:S(2)}) collective-permute-start(bf16[1024,256]{1,0:T(8,128)(2,1)S(1)} %collective-permute-done.15.refs_8_), channel_id=1, source_target_pairs={{0,4},{2,6},{4,0},{6,2},{8,12},{10,14},{12,8},{14,10},{16,20},{18,... | collective-permute-start | bytes 1572872 | tf_op jit(solution)/shard_map/ppermute | solution.py:316
  84.9 21.1 %collective-permute-start.14 = (bf16[272,768]{1,0:T(8,128)(2,1)S(1)}, bf16[272,768]{1,0:T(8,128)(2,1)S(1)}, u32[]{:S(2)}, u32[]{:S(2)}) collective-permute-start(bf16[272,768]{1,0:T(8,128)(2,1)S(1)} %collective-permute-done.11.refs_4_), channel_id=1, source_target_pairs={{0,4},{2,6},{4,0},{6,2},{8,12},{10,14},{12,8},{14,10},{16,20},{18,... | collective-permute-start | bytes 1253384 | tf_op jit(solution)/shard_map/ppermute | solution.py:316
  85.4 22.6 %collective-permute-start.12 = (bf16[272,768]{1,0:T(8,128)(2,1)S(1)}, bf16[272,768]{1,0:T(8,128)(2,1)S(1)}, u32[]{:S(2)}, u32[]{:S(2)}) collective-permute-start(bf16[272,768]{1,0:T(8,128)(2,1)S(1)} %collective-permute-done.11.refs_4_), channel_id=1, source_target_pairs={{0,2},{2,0},{4,6},{6,4},{8,10},{10,8},{12,14},{14,12},{16,18},{18,... | collective-permute-start | bytes 1253384 | tf_op jit(solution)/shard_map/ppermute | solution.py:319
  111.6 14.2 %collective-permute-start.28 = (bf16[1024,256]{1,0:T(8,128)(2,1)S(1)}, bf16[1024,256]{1,0:T(8,128)(2,1)S(1)}, u32[]{:S(2)}, u32[]{:S(2)}) collective-permute-start(bf16[1024,256]{1,0:T(8,128)(2,1)S(1)} %collective-permute-done.13.refs_10_), channel_id=1, source_target_pairs={{0,8},{2,10},{4,12},{6,14},{8,0},{10,2},{12,4},{14,6},{16,24},{18,... | collective-permute-start | bytes 1572872 | tf_op jit(solution)/shard_map/ppermute | solution.py:309
  114.6 11.2 %collective-permute-start.27 = (bf16[4,128,256]{2,1,0:T(8,128)(2,1)S(1)}, bf16[4,128,256]{2,1,0:T(8,128)(2,1)S(1)}, u32[]{:S(2)}, u32[]{:S(2)}) collective-permute-start(bf16[4,128,256]{2,1,0:T(8,128)(2,1)S(1)} %get-tuple-element.101), channel_id=1, source_target_pairs={{0,4},{2,6},{4,0},{6,2},{8,12},{10,14},{12,8},{14,10},{16,20},{18,... | collective-permute-start | bytes 786440 | tf_op jit(solution)/shard_map/ppermute | solution.py:316
  116.2 22.8 %collective-permute-start.36 = (bf16[1024,256]{1,0:T(8,128)(2,1)S(1)}, bf16[1024,256]{1,0:T(8,128)(2,1)S(1)}, u32[]{:S(2)}, u32[]{:S(2)}) collective-permute-start(bf16[1024,256]{1,0:T(8,128)(2,1)S(1)} %collective-permute-done.13.refs_10_), channel_id=1, source_target_pairs={{0,4},{2,6},{4,0},{6,2},{8,12},{10,14},{12,8},{14,10},{16,20},{18,... | collective-permute-start | bytes 1572872 | tf_op jit(solution)/shard_map/ppermute | solution.py:316
  125.8 19.6 %collective-permute-start.41 = (bf16[1024,256]{1,0:T(8,128)(2,1)S(1)}, bf16[1024,256]{1,0:T(8,128)(2,1)S(1)}, u32[]{:S(2)}, u32[]{:S(2)}) collective-permute-start(bf16[1024,256]{1,0:T(8,128)(2,1)S(1)} %collective-permute-done.28.refs_10_), channel_id=1, source_target_pairs={{0,4},{2,6},{4,0},{6,2},{8,12},{10,14},{12,8},{14,10},{16,20},{18,... | collective-permute-start | bytes 1572872 | tf_op jit(solution)/shard_map/ppermute | solution.py:316
  150.6 11.7 %collective-permute-start.45 = (bf16[2,128,256]{2,1,0:T(8,128)(2,1)S(1)}, bf16[2,128,256]{2,1,0:T(8,128)(2,1)S(1)}, u32[]{:S(2)}, u32[]{:S(2)}) collective-permute-start(bf16[2,128,256]{2,1,0:T(8,128)(2,1)S(1)} %collective-permute-done.44), channel_id=1, source_target_pairs={{0,1},{1,0},{2,3},{3,2},{4,5},{5,4},{6,7},{7,6},{8,9},{9,8},{10,11... | collective-permute-start | bytes 393224 | tf_op jit(solution)/shard_map/ppermute | solution.py:322
  (31 other events, 207.7 us)

commit v6 on v5

--- a/solution.py
+++ b/solution.py
@@ -118,18 +118,20 @@
     rows = refs[:zn]
     weights = refs[zn : zn + xn * cn]
     before = refs[zn + xn * cn] if zn > 1 else None
-    outs, meta, chunk = refs[-2 - cn : -2], refs[-2], refs[-1]
+    meta, chunk = refs[-2:]
+    outs = refs[zn + xn * cn + (before is not None) : -2]
     c = at[2]
 
     def each(i, sums):
         sums = (sums if before is None else sums + before[i]).astype(BF16)
         heads = [sums[:, e * 3 * DH : (e + 1) * 3 * DH] for e in range(cn)]
-        for m, out in enumerate(outs):
+        half = outs[0].shape[0]
+        for m in range(cn):
             pick = heads[m]
             for e in range(cn):
                 if e != m:
                     pick = jnp.where((c ^ m) == e, heads[e], pick)
-            out[i] = pick
+            outs[i // half * cn + m][i % half] = pick
 
     project(xn, cn, at, rows, weights, chunk, meta.at[0], each)
 
@@ -144,8 +146,9 @@
     return retain, length
 
 
-def write_kernel(zn, xn, cn, at, *refs):
-    parts, query, metas = refs[:cn], refs[cn], refs[cn + 1 : -5]
+def write_kernel(zn, xn, cn, halves, at, *refs):
+    count = cn * halves
+    parts, query, metas = refs[:count], refs[count], refs[count + 1 : -5]
     sums, written, group, group16, table = refs[-5:]
     z, x, c = at[0], at[1], at[2]
     j = 0
@@ -155,9 +158,10 @@
             j += 1
     retain, length = segment_info(table)
     seg_rows = sums.shape[2]
+    half = zn // halves
     for i in range(zn):
         for m in range(cn):
-            sums[z ^ i, c ^ m] = parts[m][i]
+            sums[z ^ i, c ^ m] = parts[i // half * cn + m][i % half]
     own = query[:, lanes(z * cn + c, DH)]
     slots = own.shape[0]
     position = lax.broadcasted_iota(jnp.int32, (slots, seg_rows), 1).astype(F32)
@@ -232,10 +236,10 @@
             outs[j][m] = done[z ^ j, c ^ m]
 
 
-def out_kernel(zn, xn, cn, n_head, slots, at, *refs):
+def out_kernel(zn, xn, cn, n_head, slots, turns, phases, at, *refs):
     attended = refs[: zn * cn]
     weights = refs[zn * cn : zn * cn + len(slots) * xn]
-    outs, rows = refs[-1 - cn * n_head : -1], refs[-1]
+    outs, rows = refs[zn * cn + len(weights) : -1], refs[-1]
     z, x, c, y = at[0], at[1], at[2], at[3]
     seg_rows = attended[0].shape[1]
     for j in range(zn):
@@ -248,24 +252,24 @@
     share = zn * xn // n_head
     for n, j in enumerate(slots):
         for k in range(xn):
-            product = dot(rows[...], weights[n * xn + k][...]).astype(BF16)
             spot = (z ^ j) * xn + lax.rem(x + xn - k, xn)
             turn = lax.rem(spot // share + n_head - y, n_head)
-            for r in range(n_head):
+            for i, r in enumerate(turns):
 
                 @pl.when(turn == r)
                 def _():
+                    product = dot(rows[...], weights[n * xn + k][...]).astype(BF16)
                     for m in range(cn):
-                        outs[r * cn + m][lax.rem(spot, blocks)] = product[
-                            m * seg_rows : (m + 1) * seg_rows
-                        ]
+                        out = outs[(j % phases * len(turns) + i) * cn + m if len(slots) == zn else i * cn + m]
+                        out[lax.rem(spot, blocks)] = product[m * seg_rows : (m + 1) * seg_rows]
 
 
 def sum_kernel(n_head, cn, phases, at, *refs):
     out = refs[-1]
     blocks, seg_rows, size = refs[0].shape
     for p in range(phases):
-        few = refs[p * n_head * cn : (p + 1) * n_head * cn]
+        count = (n_head - 1) * cn
+        few = refs[(phases * (n_head - 1) + p) * cn :][:cn] + refs[p * count : (p + 1) * count]
         places = []
         for b in range(blocks):
             totals = [
@@ -434,11 +438,11 @@
         started["oz", b] = over_z(after(w_out, packs[last]), b)
     for j in more:
         end_y(j, done_all(started["y", j])[0])
-    for j in range(1, last):
-        end_x(j, done_all(started["x", j])[0])
     if last:
         out_z[1] = done(started["oz", 1])
         begin_out(1, out_z[1])
+    for j in range(1, last):
+        end_x(j, done_all(started["x", j])[0])
     rows = [rows[j] for j in range(zn)]
 
     chunk_rows = xn * cn * w_rows
@@ -458,27 +462,31 @@
         )
         mark(before[0])
     if last:
-        parts, others, columns[1][1:] = done_all(
-            [started["oz", b] for b in bits[1:]], started["x", last], started["o", 1]
+        end_x(last, done_all(started["x", last])[0])
+        parts, columns[1][1:], held = done_all(
+            [started["oz", b] for b in bits[1:]], started["o", 1], before[:1]
         )
-        end_x(last, others)
+        before = [*held, *before[1:]]
         out_z.update(zip(bits[1:], parts))
         for b in bits[1:]:
             begin_out(b, out_z[b])
         for j in more:
             started["oz", j] = over_z(out_z[j ^ (j & -j)], j & -j)
+    halves = 2 if zn % 2 == 0 else 1
     *parts, meta = call(
         functools.partial(finish_kernel, zn, xn, cn),
         (at, *rows, *pieces[last], *before[:1]),
-        [shape((zn, seg_rows, 3 * DH))] * cn + [shape((1, xn, cn, META, DH), F32)],
+        [shape((zn // halves, seg_rows, 3 * DH))] * (cn * halves)
+        + [shape((1, xn, cn, META, DH), F32)],
         [pltpu.VMEM((chunk_rows, cn * 3 * DH), BF16)],
         flops,
         column=(chunk_rows, lambda at: at[0] ^ last),
         room=20,
     )
-    parts = [done(over_c(part, m)) if m else part for m, part in enumerate(parts)]
+    parts = [over_c(part, n % cn) if n % cn else part for n, part in enumerate(parts)]
+    (parts,) = done_all(parts)
     sums, written, group, group16, table = call(
-        functools.partial(write_kernel, zn, xn, cn),
+        functools.partial(write_kernel, zn, xn, cn, halves),
         (at, *parts, mem_query, *before[1:], meta),
         [
             shape((zn, cn, seg_rows, 3 * DH)),
@@ -496,7 +504,11 @@
         scalars=2,
     )
     mark(token)
-    others, parts = done_all(others, [started["oz", j] for j in more])
+    others, parts, *shares = done_all(
+        others, [started["oz", j] for j in more], *(started["o", b] for b in bits[1:])
+    )
+    for b, share in zip(bits[1:], shares):
+        columns[b] += share
     for j, part in zip(more, parts):
         begin_out(j, part)
     attended = call(
@@ -516,27 +528,31 @@
     swapped = [[over_c(here[j], m) for m in range(1, cn)] for j in range(zn)]
     here = sum(([here[j]] + [done(a) for a in swapped[j]] for j in range(zn)), [])
 
-    for j in range(2, zn):
+    for j in more:
         end_out(j)
     out_cols = w_out.shape[1]
     phases = zn // n_head if zn % n_head == 0 else 1
     blocks = feat_local // (cn * out_cols * phases)
-    mine = []
-    for p in range(phases):
-        few = range(p, zn, phases)
-        products = call(
-            functools.partial(out_kernel, zn, xn, cn, n_head, few),
+    def multiply(few, turns, outs):
+        return call(
+            functools.partial(out_kernel, zn, xn, cn, n_head, few, turns, phases),
             (at, *here, *sum((columns[j] for j in few), [])),
-            [shape((blocks, seg_rows, out_cols))] * (cn * n_head),
+            [shape((blocks, seg_rows, out_cols))] * outs,
             [pltpu.VMEM((cn * seg_rows, heads * DH), BF16)],
             2 * cn * seg_rows * heads * DH * len(few) * xn * out_cols,
             room=20,
         )
-        for r in range(n_head):
-            for m in range(cn):
-                block = products[r * cn + m]
-                block = over_c(block, m) if m else block
-                mine.append(over_y(block, r) if r else block)
+
+    mine = []
+    others = range(1, n_head)
+    for p in range(phases):
+        products = multiply(range(p, zn, phases), others, cn * len(others))
+        for n, block in enumerate(products):
+            block = over_c(block, n % cn) if n % cn else block
+            mine.append(over_y(block, others[n // cn]))
+    products = multiply(range(zn), (0,), cn * phases)
+    for n, block in enumerate(products):
+        mine.append(over_c(block, n % cn) if n % cn else block)
     (branch,) = call(
         functools.partial(sum_kernel, n_head, cn, phases),
         (at, *mine),

time: 164 us -> 159 us (0.970)
  waiting for transfers between devices: 93.8 us -> 89 us
    ppermute x9, waiting for transfers between devices: 39.5 us -> 20.5 us  [over_x(): return lax.ppermute(a, 'seq', pairs)]
    ppermute x12, waiting for transfers between devices: 39.9 us -> 58.4 us  [over_z(): return lax.ppermute(a, 'seq', pairs)]
    ppermute x8, waiting for transfers between devices: 10.2 us -> 7.63 us  [over_y(): lax.ppermute(a, 'head', [(h, (h + k) % n_head) for h in range(n_head)])]
    ppermute x17 -> x18, waiting for transfers between devices: 4.25 us -> 2.49 us  [over_c(): return lax.ppermute(a, 'seq', [(s, s ^ m) for s in range(n_seq)])]
    pallas_call x13 -> x14, Pallas kernels: 21.7 us -> 21.7 us  [call(): pl.pallas_call(kernel, grid_spec=pltpu.PrefetchScalarGridSpec(num_scalar_...]
  transfers between devices with their start and end apart: 46 -> 47, of which waited for: 23 -> 24; matrix products, arithmetic and copies ran while one was open for 0% -> 0% of each run, Pallas kernels for 11% -> 13%
where the time goes in v6:
time: 159 us
  waiting for transfers between devices  89 us (56%)
  starting transfers between devices  43.3 us (27%)
  Pallas kernels  21.7 us (14%)
  local copies, waits for them, and re-layouts  3.8 us (2%)
    ppermute x12, waiting for transfers between devices, over_z(): return lax.ppermute(a, 'seq', pairs)  58.4 us
    pallas_call x14, Pallas kernels, call(): pl.pallas_call(kernel, grid_spec=pltpu.PrefetchScalarGridSpec(num_scalar_...  21.7 us
    ppermute x12, starting transfers between devices, over_z(): return lax.ppermute(a, 'seq', pairs)  21.1 us
    ppermute x9, waiting for transfers between devices, over_x(): return lax.ppermute(a, 'seq', pairs)  20.5 us
    ppermute x9, starting transfers between devices, over_x(): return lax.ppermute(a, 'seq', pairs)  10 us
    ppermute x8, starting transfers between devices, over_y(): lax.ppermute(a, 'head', [(h, (h + k) % n_head) for h in range(n_head)])  9.14 us
    ppermute x8, waiting for transfers between devices, over_y(): lax.ppermute(a, 'head', [(h, (h + k) % n_head) for h in range(n_head)])  7.63 us
    unnamed x18, local copies, waits for them, and re-layouts  3.8 us
  transfers between devices with their start and end apart: 47, of which 24 were waited for; matrix products, arithmetic and copies ran while one was open for 0% of the time, Pallas kernels for 13%

profile of v6, /device:TPU:0, one launch (start us, length us, event | category | flops | bytes accessed | tf_op | source)
XLA Modules:
  0.0 158.7 jit_solution(1992967390240654997)
XLA Ops:
  0.0 3.0 %collective-permute-start = (bf16[128,2048]{1,0:T(8,128)(2,1)}, bf16[128,2048]{1,0:T(8,128)(2,1)S(1)}, u32[]{:S(2)}, u32[]{:S(2)}) collective-permute-start(bf16[128,2048]{1,0:T(8,128)(2,1)} %refs_0_.3), channel_id=1, source_target_pairs={{0,8},{2,10},{4,12},{6,14},{8,0},{10,2},{12,4},{14,6},{16,24},{18,... | collective-permute-start | bytes 1572872 | tf_op jit(solution)/shard_map/ppermute | solution.py:313
  3.0 2.6 %collective-permute-start.1 = (bf16[128,2048]{1,0:T(8,128)(2,1)}, bf16[128,2048]{1,0:T(8,128)(2,1)S(1)}, u32[]{:S(2)}, u32[]{:S(2)}) collective-permute-start(bf16[128,2048]{1,0:T(8,128)(2,1)} %refs_0_.3), channel_id=1, source_target_pairs={{0,16},{2,18},{4,20},{6,22},{8,24},{10,26},{12,28},{14,30},{16,0},... | collective-permute-start | bytes 1572872 | tf_op jit(solution)/shard_map/ppermute | solution.py:313
  14.6 8.6 %collective-permute-done.3.refs_6_ = bf16[272,768]{1,0:T(8,128)(2,1)S(1)} collective-permute-done((bf16[272,768]{1,0:T(8,128)(2,1)S(1)}, bf16[272,768]{1,0:T(8,128)(2,1)S(1)}, u32[]{:S(2)}, u32[]{:S(2)}) %collective-permute-start.3) | collective-permute-done | bytes 417824 | tf_op jit(solution)/shard_map/ppermute | solution.py:320
  24.7 2.4 %collective-permute-done.refs_0_ = bf16[128,2048]{1,0:T(8,128)(2,1)S(1)} collective-permute-done((bf16[128,2048]{1,0:T(8,128)(2,1)}, bf16[128,2048]{1,0:T(8,128)(2,1)S(1)}, u32[]{:S(2)}, u32[]{:S(2)}) %collective-permute-start) | collective-permute-done | bytes 524320 | tf_op jit(solution)/shard_map/ppermute | solution.py:313
  27.9 2.5 %collective-permute-start.6 = (bf16[128,2048]{1,0:T(8,128)(2,1)S(1)}, bf16[128,2048]{1,0:T(8,128)(2,1)S(1)}, u32[]{:S(2)}, u32[]{:S(2)}) collective-permute-start(bf16[128,2048]{1,0:T(8,128)(2,1)S(1)} %collective-permute-done.1.refs_0_), channel_id=1, source_target_pairs={{0,8},{2,10},{4,12},{6,14},{8,0},{10,2},{12,4},{14,6},{16,24},{18,... | collective-permute-start | bytes 1572872 | tf_op jit(solution)/shard_map/ppermute | solution.py:313
  32.4 3.8 %collective-permute-done.4.refs_8_ = bf16[272,768]{1,0:T(8,128)(2,1)S(1)} collective-permute-done((bf16[272,768]{1,0:T(8,128)(2,1)S(1)}, bf16[272,768]{1,0:T(8,128)(2,1)S(1)}, u32[]{:S(2)}, u32[]{:S(2)}) %collective-permute-start.4) | collective-permute-done | bytes 417824 | tf_op jit(solution)/shard_map/ppermute | solution.py:313
  36.2 3.1 %collective-permute-start.5 = (bf16[272,768]{1,0:T(8,128)(2,1)S(1)}, bf16[272,768]{1,0:T(8,128)(2,1)S(1)}, u32[]{:S(2)}, u32[]{:S(2)}) collective-permute-start(bf16[272,768]{1,0:T(8,128)(2,1)S(1)} %get-tuple-element.77), channel_id=1, source_target_pairs={{0,16},{2,18},{4,20},{6,22},{8,24},{10,26},{12,28},{14,30},{16,0},... | collective-permute-start | bytes 1253384 | tf_op jit(solution)/shard_map/ppermute | solution.py:313
  40.3 14.6 %collective-permute-done.5.refs_12_ = bf16[272,768]{1,0:T(8,128)(2,1)S(1)} collective-permute-done((bf16[272,768]{1,0:T(8,128)(2,1)S(1)}, bf16[272,768]{1,0:T(8,128)(2,1)S(1)}, u32[]{:S(2)}, u32[]{:S(2)}) %collective-permute-start.5) | collective-permute-done | bytes 417824 | tf_op jit(solution)/shard_map/ppermute | solution.py:313
  55.5 4.1 %collective-permute-start.11 = (bf16[272,768]{1,0:T(8,128)(2,1)S(1)}, bf16[272,768]{1,0:T(8,128)(2,1)S(1)}, u32[]{:S(2)}, u32[]{:S(2)}) collective-permute-start(bf16[272,768]{1,0:T(8,128)(2,1)S(1)} %get-tuple-element.84), channel_id=1, source_target_pairs={{0,24},{2,26},{4,28},{6,30},{8,16},{10,18},{12,20},{14,22},{16,8},... | collective-permute-start | bytes 1253384 | tf_op jit(solution)/shard_map/ppermute | solution.py:313
  65.2 5.0 %collective-permute-done.11.refs_4_ = bf16[272,768]{1,0:T(8,128)(2,1)S(1)} collective-permute-done((bf16[272,768]{1,0:T(8,128)(2,1)S(1)}, bf16[272,768]{1,0:T(8,128)(2,1)S(1)}, u32[]{:S(2)}, u32[]{:S(2)}) %collective-permute-start.11) | collective-permute-done | bytes 417824 | tf_op jit(solution)/shard_map/ppermute | solution.py:313
  72.5 7.0 %collective-permute-done.18.refs_8_.refs_10_ = bf16[1024,256]{1,0:T(8,128)(2,1)S(1)} collective-permute-done((bf16[1024,256]{1,0:T(8,128)(2,1)S(1)}, bf16[1024,256]{1,0:T(8,128)(2,1)S(1)}, u32[]{:S(2)}, u32[]{:S(2)}) %collective-permute-start.18) | collective-permute-done | bytes 524320 | tf_op jit(solution)/shard_map/ppermute | solution.py:313
  84.2 3.4 %shard_map.105 = (f32[4,128,768]{2,1,0:T(8,128)S(1)}, f32[3,2,2,16,128]{4,3,2,1,0:T(8,128)S(1)}) custom-call(s32[4]{0:T(128)S(1)} %pad_add_fusion.at, bf16[128,4096]{1,0:T(8,128)(2,1)S(1)} %shard_map.101.refs_0_, bf16[128,4096]{1,0:T(8,128)(2,1)S(1)} %shard_map.102.refs_1_, bf16[128,4096]{1,0:T(8,128)(2,1)S(1)} %shard_map.103.refs_2_, ...), custom_call_target="tpu_custom_call" | custom-call | flops 2415919104 | bytes 10878992 | tf_op jit(solution)/shard_map/pallas_call | solution.py:34
  87.6 5.8 %collective-permute-done.13.refs_6_ = bf16[272,768]{1,0:T(8,128)(2,1)S(1)} collective-permute-done((bf16[272,768]{1,0:T(8,128)(2,1)S(1)}, bf16[272,768]{1,0:T(8,128)(2,1)S(1)}, u32[]{:S(2)}, u32[]{:S(2)}) %collective-permute-start.13) | collective-permute-done | bytes 417824 | tf_op jit(solution)/shard_map/ppermute | solution.py:320
  93.5 15.5 %collective-permute-done.24.refs_10_.refs_12_ = bf16[1024,256]{1,0:T(8,128)(2,1)S(1)} collective-permute-done((bf16[1024,256]{1,0:T(8,128)(2,1)S(1)}, bf16[1024,256]{1,0:T(8,128)(2,1)S(1)}, u32[]{:S(2)}, u32[]{:S(2)}) %collective-permute-start.24) | collective-permute-done | bytes 524320 | tf_op jit(solution)/shard_map/ppermute | solution.py:313
  109.5 1.7 %shard_map.106 = (bf16[2,128,384]{2,1,0:T(8,128)(2,1)S(1)}, bf16[2,128,384]{2,1,0:T(8,128)(2,1)S(1)}, bf16[2,128,384]{2,1,0:T(8,128)(2,1)S(1)}, bf16[2,128,384]{...) custom-call(s32[4]{0:T(128)S(1)} %pad_add_fusion.at, bf16[128,4096]{1,0:T(8,128)(2,1)S(1)} %shard_map.101.refs_0_, ...), custom_call_target="tpu_custom_call" | custom-call | flops 805306368 | bytes 8257552 | tf_op jit(solution)/shard_map/pallas_call | solution.py:34
  115.9 2.0 %shard_map.108.token = f32[4,2,128,128]{3,2,1,0:T(8,128)S(1)} custom-call(s32[4]{0:T(128)S(1)} %pad_add_fusion.at, f32[8]{0:T(128)S(1)} %copy-done.7, f32[4,2,2,16,128]{4,3,2,1,0:T(8,128)S(1)} %get-tuple-element.108.table, bf16[4,2,128,384]{3,2,1,0:T(8,128)(2,1)S(1)} %get-tuple-element.109.sums), custom_call_target="tpu_custom_call" | custom-call | bytes 1441840 | tf_op jit(solution)/shard_map/pallas_call | solution.py:34
  117.9 4.5 %collective-permute-done.29.refs_10_.refs_14_ = bf16[1024,256]{1,0:T(8,128)(2,1)S(1)} collective-permute-done((bf16[1024,256]{1,0:T(8,128)(2,1)S(1)}, bf16[1024,256]{1,0:T(8,128)(2,1)S(1)}, u32[]{:S(2)}, u32[]{:S(2)}) %collective-permute-start.29) | collective-permute-done | bytes 524320 | tf_op jit(solution)/shard_map/ppermute | solution.py:313
  123.8 4.3 %collective-permute-done.28.refs_0_ = bf16[4,128,256]{2,1,0:T(8,128)(2,1)S(1)} collective-permute-done((bf16[4,128,256]{2,1,0:T(8,128)(2,1)S(1)}, bf16[4,128,256]{2,1,0:T(8,128)(2,1)S(1)}, u32[]{:S(2)}, u32[]{:S(2)}) %collective-permute-start.28) | collective-permute-done | bytes 262176 | tf_op jit(solution)/shard_map/ppermute | solution.py:320
  128.4 2.2 %shard_map.109 = (bf16[2,128,128]{2,1,0:T(8,128)(2,1)S(1)}, bf16[2,128,128]{2,1,0:T(8,128)(2,1)S(1)}, bf16[2,128,128]{2,1,0:T(8,128)(2,1)S(1)}, bf16[2,128,128]{2,1,0:T(8,128)(2,1)S(1)}) custom-call(s32[4]{0:T(128)S(1)} %pad_add_fusion.at, f32[8]{0:T(128)S(1)} %copy-done.7, f32[4,2,2,16,128]{4,3,2,1,0:T(8,128)S(1)} %get-tuple-element.108.table, ...), custom_call_target="tpu_custom_call" | custom-call | bytes 3538992 | tf_op jit(solution)/shard_map/pallas_call | solution.py:34
  130.7 1.8 %collective-permute-start.34 = (bf16[2,128,128]{2,1,0:T(8,128)(2,1)S(1)}, bf16[2,128,128]{2,1,0:T(8,128)(2,1)S(1)}, u32[]{:S(2)}, u32[]{:S(2)}) collective-permute-start(bf16[2,128,128]{2,1,0:T(8,128)(2,1)S(1)} %get-tuple-element.118), channel_id=1, source_target_pairs={{0,8},{2,10},{4,12},{6,14},{8,0},{10,2},{12,4},{14,6},{16,24},{18,... | collective-permute-start | bytes 196616 | tf_op jit(solution)/shard_map/ppermute | solution.py:313
  135.6 3.1 %collective-permute-done.33.refs_4_ = bf16[2,128,128]{2,1,0:T(8,128)(2,1)S(1)} collective-permute-done((bf16[2,128,128]{2,1,0:T(8,128)(2,1)S(1)}, bf16[2,128,128]{2,1,0:T(8,128)(2,1)S(1)}, u32[]{:S(2)}, u32[]{:S(2)}) %collective-permute-start.33) | collective-permute-done | bytes 65568 | tf_op jit(solution)/shard_map/ppermute | solution.py:313
  146.2 2.0 %shard_map.112 = (bf16[2,128,256]{2,1,0:T(8,128)(2,1)S(1)}, bf16[2,128,256]{2,1,0:T(8,128)(2,1)S(1)}, bf16[2,128,256]{2,1,0:T(8,128)(2,1)S(1)}, bf16[2,128,256]{2,1,0:T(8,128)(2,1)S(1)}) custom-call(s32[4]{0:T(128)S(1)} %pad_add_fusion.at, bf16[2,128,128]{2,1,0:T(8,128)(2,1)S(1)} %get-tuple-element.115.refs_0_, ...), custom_call_target="tpu_custom_call" | custom-call | flops 1073741824 | bytes 5242896 | tf_op jit(solution)/shard_map/pallas_call | solution.py:34
  151.1 4.1 %collective-permute-done.42.refs_2_ = bf16[2,128,256]{2,1,0:T(8,128)(2,1)S(1)} collective-permute-done((bf16[2,128,256]{2,1,0:T(8,128)(2,1)S(1)}, bf16[2,128,256]{2,1,0:T(8,128)(2,1)S(1)}, u32[]{:S(2)}, u32[]{:S(2)}) %collective-permute-start.42) | collective-permute-done | bytes 131104 | tf_op jit(solution)/shard_map/ppermute | solution.py:326
  155.2 2.0 %collective-permute-done.44.refs_3_ = bf16[2,128,256]{2,1,0:T(8,128)(2,1)S(1)} collective-permute-done((bf16[2,128,256]{2,1,0:T(8,128)(2,1)S(1)}, bf16[2,128,256]{2,1,0:T(8,128)(2,1)S(1)}, u32[]{:S(2)}, u32[]{:S(2)}) %collective-permute-start.44) | collective-permute-done | bytes 131104 | tf_op jit(solution)/shard_map/ppermute | solution.py:326
  (103 shorter events, 48.7 us)
Async XLA Ops:
  0.0 27.1 %collective-permute-start = (bf16[128,2048]{1,0:T(8,128)(2,1)}, bf16[128,2048]{1,0:T(8,128)(2,1)S(1)}, u32[]{:S(2)}, u32[]{:S(2)}) collective-permute-start(bf16[128,2048]{1,0:T(8,128)(2,1)} %refs_0_.3), channel_id=1, source_target_pairs={{0,8},{2,10},{4,12},{6,14},{8,0},{10,2},{12,4},{14,6},{16,24},{18,... | collective-permute-start | bytes 1572872 | tf_op jit(solution)/shard_map/ppermute | solution.py:313
  3.0 24.8 %collective-permute-start.1 = (bf16[128,2048]{1,0:T(8,128)(2,1)}, bf16[128,2048]{1,0:T(8,128)(2,1)S(1)}, u32[]{:S(2)}, u32[]{:S(2)}) collective-permute-start(bf16[128,2048]{1,0:T(8,128)(2,1)} %refs_0_.3), channel_id=1, source_target_pairs={{0,16},{2,18},{4,20},{6,22},{8,24},{10,26},{12,28},{14,30},{16,0},... | collective-permute-start | bytes 1572872 | tf_op jit(solution)/shard_map/ppermute | solution.py:313
  5.6 22.2 %collective-permute-start.2 = (bf16[128,2048]{1,0:T(8,128)(2,1)}, bf16[128,2048]{1,0:T(8,128)(2,1)S(1)}, u32[]{:S(2)}, u32[]{:S(2)}) collective-permute-start(bf16[128,2048]{1,0:T(8,128)(2,1)} %refs_0_.3), channel_id=1, source_target_pairs={{0,1},{1,0},{2,3},{3,2},{4,5},{5,4},{6,7},{7,6},{8,9},{9,8},{10,11... | collective-permute-start | bytes 1572872 | tf_op jit(solution)/shard_map/ppermute | solution.py:326
  12.6 10.6 %collective-permute-start.3 = (bf16[272,768]{1,0:T(8,128)(2,1)S(1)}, bf16[272,768]{1,0:T(8,128)(2,1)S(1)}, u32[]{:S(2)}, u32[]{:S(2)}) collective-permute-start(bf16[272,768]{1,0:T(8,128)(2,1)S(1)} %get-tuple-element.72.refs_4_), channel_id=1, source_target_pairs={{0,4},{2,6},{4,0},{6,2},{8,12},{10,14},{12,8},{14,10},{16,20},{18,... | collective-permute-start | bytes 1253384 | tf_op jit(solution)/shard_map/ppermute | solution.py:320
  14.2 22.0 %collective-permute-start.4 = (bf16[272,768]{1,0:T(8,128)(2,1)S(1)}, bf16[272,768]{1,0:T(8,128)(2,1)S(1)}, u32[]{:S(2)}, u32[]{:S(2)}) collective-permute-start(bf16[272,768]{1,0:T(8,128)(2,1)S(1)} %get-tuple-element.75), channel_id=1, source_target_pairs={{0,8},{2,10},{4,12},{6,14},{8,0},{10,2},{12,4},{14,6},{16,24},{18,... | collective-permute-start | bytes 1253384 | tf_op jit(solution)/shard_map/ppermute | solution.py:313
  23.2 17.0 %collective-permute-start.7 = (bf16[1024,256]{1,0:T(8,128)(2,1)S(1)}, bf16[1024,256]{1,0:T(8,128)(2,1)S(1)}, u32[]{:S(2)}, u32[]{:S(2)}) collective-permute-start(bf16[1024,256]{1,0:T(8,128)(2,1)S(1)} %copy-done), channel_id=1, source_target_pairs={{0,4},{2,6},{4,0},{6,2},{8,12},{10,14},{12,8},{14,10},{16,20},{18,... | collective-permute-start | bytes 1572872 | tf_op jit(solution)/shard_map/ppermute | solution.py:320
  27.9 27.7 %collective-permute-start.6 = (bf16[128,2048]{1,0:T(8,128)(2,1)S(1)}, bf16[128,2048]{1,0:T(8,128)(2,1)S(1)}, u32[]{:S(2)}, u32[]{:S(2)}) collective-permute-start(bf16[128,2048]{1,0:T(8,128)(2,1)S(1)} %collective-permute-done.1.refs_0_), channel_id=1, source_target_pairs={{0,8},{2,10},{4,12},{6,14},{8,0},{10,2},{12,4},{14,6},{16,24},{18,... | collective-permute-start | bytes 1572872 | tf_op jit(solution)/shard_map/ppermute | solution.py:313
  30.3 25.2 %collective-permute-start.8 = (bf16[128,2048]{1,0:T(8,128)(2,1)S(1)}, bf16[128,2048]{1,0:T(8,128)(2,1)S(1)}, u32[]{:S(2)}, u32[]{:S(2)}) collective-permute-start(bf16[128,2048]{1,0:T(8,128)(2,1)S(1)} %collective-permute-done.refs_0_), channel_id=1, source_target_pairs={{0,1},{1,0},{2,3},{3,2},{4,5},{5,4},{6,7},{7,6},{8,9},{9,8},{10,11... | collective-permute-start | bytes 1572872 | tf_op jit(solution)/shard_map/ppermute | solution.py:326
  31.9 23.7 %collective-permute-start.9 = (bf16[128,2048]{1,0:T(8,128)(2,1)S(1)}, bf16[128,2048]{1,0:T(8,128)(2,1)S(1)}, u32[]{:S(2)}, u32[]{:S(2)}) collective-permute-start(bf16[128,2048]{1,0:T(8,128)(2,1)S(1)} %collective-permute-done.1.refs_0_), channel_id=1, source_target_pairs={{0,1},{1,0},{2,3},{3,2},{4,5},{5,4},{6,7},{7,6},{8,9},{9,8},{10,11... | collective-permute-start | bytes 1572872 | tf_op jit(solution)/shard_map/ppermute | solution.py:326
  36.2 18.7 %collective-permute-start.5 = (bf16[272,768]{1,0:T(8,128)(2,1)S(1)}, bf16[272,768]{1,0:T(8,128)(2,1)S(1)}, u32[]{:S(2)}, u32[]{:S(2)}) collective-permute-start(bf16[272,768]{1,0:T(8,128)(2,1)S(1)} %get-tuple-element.77), channel_id=1, source_target_pairs={{0,16},{2,18},{4,20},{6,22},{8,24},{10,26},{12,28},{14,30},{16,0},... | collective-permute-start | bytes 1253384 | tf_op jit(solution)/shard_map/ppermute | solution.py:313
  55.5 14.7 %collective-permute-start.11 = (bf16[272,768]{1,0:T(8,128)(2,1)S(1)}, bf16[272,768]{1,0:T(8,128)(2,1)S(1)}, u32[]{:S(2)}, u32[]{:S(2)}) collective-permute-start(bf16[272,768]{1,0:T(8,128)(2,1)S(1)} %get-tuple-element.84), channel_id=1, source_target_pairs={{0,24},{2,26},{4,28},{6,30},{8,16},{10,18},{12,20},{14,22},{16,8},... | collective-permute-start | bytes 1253384 | tf_op jit(solution)/shard_map/ppermute | solution.py:313
  59.6 11.9 %collective-permute-start.10 = (bf16[128,2048]{1,0:T(8,128)(2,1)S(1)}, bf16[128,2048]{1,0:T(8,128)(2,1)S(1)}, u32[]{:S(2)}, u32[]{:S(2)}) collective-permute-start(bf16[128,2048]{1,0:T(8,128)(2,1)S(1)} %collective-permute-done.6.refs_0_), channel_id=1, source_target_pairs={{0,1},{1,0},{2,3},{3,2},{4,5},{5,4},{6,7},{7,6},{8,9},{9,8},{10,11... | collective-permute-start | bytes 1572872 | tf_op jit(solution)/shard_map/ppermute | solution.py:326
  61.1 18.4 %collective-permute-start.18 = (bf16[1024,256]{1,0:T(8,128)(2,1)S(1)}, bf16[1024,256]{1,0:T(8,128)(2,1)S(1)}, u32[]{:S(2)}, u32[]{:S(2)}) collective-permute-start(bf16[1024,256]{1,0:T(8,128)(2,1)S(1)} %copy-done), channel_id=1, source_target_pairs={{0,8},{2,10},{4,12},{6,14},{8,0},{10,2},{12,4},{14,6},{16,24},{18,... | collective-permute-start | bytes 1572872 | tf_op jit(solution)/shard_map/ppermute | solution.py:313
  62.1 17.4 %collective-permute-start.17 = (bf16[272,768]{1,0:T(8,128)(2,1)S(1)}, bf16[272,768]{1,0:T(8,128)(2,1)S(1)}, u32[]{:S(2)}, u32[]{:S(2)}) collective-permute-start(bf16[272,768]{1,0:T(8,128)(2,1)S(1)} %collective-permute-done.4.refs_8_), channel_id=1, source_target_pairs={{0,4},{2,6},{4,0},{6,2},{8,12},{10,14},{12,8},{14,10},{16,20},{18,... | collective-permute-start | bytes 1253384 | tf_op jit(solution)/shard_map/ppermute | solution.py:320
  64.6 15.9 %collective-permute-start.21 = (bf16[272,768]{1,0:T(8,128)(2,1)S(1)}, bf16[272,768]{1,0:T(8,128)(2,1)S(1)}, u32[]{:S(2)}, u32[]{:S(2)}) collective-permute-start(bf16[272,768]{1,0:T(8,128)(2,1)S(1)} %collective-permute-done.5.refs_12_), channel_id=1, source_target_pairs={{0,4},{2,6},{4,0},{6,2},{8,12},{10,14},{12,8},{14,10},{16,20},{18,... | collective-permute-start | bytes 1253384 | tf_op jit(solution)/shard_map/ppermute | solution.py:320
  81.0 12.5 %collective-permute-start.13 = (bf16[272,768]{1,0:T(8,128)(2,1)S(1)}, bf16[272,768]{1,0:T(8,128)(2,1)S(1)}, u32[]{:S(2)}, u32[]{:S(2)}) collective-permute-start(bf16[272,768]{1,0:T(8,128)(2,1)S(1)} %collective-permute-done.11.refs_4_), channel_id=1, source_target_pairs={{0,4},{2,6},{4,0},{6,2},{8,12},{10,14},{12,8},{14,10},{16,20},{18,... | collective-permute-start | bytes 1253384 | tf_op jit(solution)/shard_map/ppermute | solution.py:320
  82.5 27.0 %collective-permute-start.12 = (bf16[272,768]{1,0:T(8,128)(2,1)S(1)}, bf16[272,768]{1,0:T(8,128)(2,1)S(1)}, u32[]{:S(2)}, u32[]{:S(2)}) collective-permute-start(bf16[272,768]{1,0:T(8,128)(2,1)S(1)} %collective-permute-done.11.refs_4_), channel_id=1, source_target_pairs={{0,2},{2,0},{4,6},{6,4},{8,10},{10,8},{12,14},{14,12},{16,18},{18,... | collective-permute-start | bytes 1253384 | tf_op jit(solution)/shard_map/ppermute | solution.py:323
  82.5 26.5 %collective-permute-start.24 = (bf16[1024,256]{1,0:T(8,128)(2,1)S(1)}, bf16[1024,256]{1,0:T(8,128)(2,1)S(1)}, u32[]{:S(2)}, u32[]{:S(2)}) collective-permute-start(bf16[1024,256]{1,0:T(8,128)(2,1)S(1)} %copy-done), channel_id=1, source_target_pairs={{0,16},{2,18},{4,20},{6,22},{8,24},{10,26},{12,28},{14,30},{16,0},... | collective-permute-start | bytes 1572872 | tf_op jit(solution)/shard_map/ppermute | solution.py:313
  83.4 25.5 %collective-permute-start.25 = (bf16[1024,256]{1,0:T(8,128)(2,1)S(1)}, bf16[1024,256]{1,0:T(8,128)(2,1)S(1)}, u32[]{:S(2)}, u32[]{:S(2)}) collective-permute-start(bf16[1024,256]{1,0:T(8,128)(2,1)S(1)} %collective-permute-done.18.refs_8_.refs_10_), channel_id=1, source_target_pairs={{0,4},{2,6},{4,0},{6,2},{8,12},{10,14},{12,8},{14,10},{16,20},{18,... | collective-permute-start | bytes 1572872 | tf_op jit(solution)/shard_map/ppermute | solution.py:320
  93.5 16.0 %collective-permute-start.23 = (bf16[272,768]{1,0:T(8,128)(2,1)S(1)}, bf16[272,768]{1,0:T(8,128)(2,1)S(1)}, u32[]{:S(2)}, u32[]{:S(2)}) collective-permute-start(bf16[272,768]{1,0:T(8,128)(2,1)S(1)} %collective-permute-done.13.refs_6_), channel_id=1, source_target_pairs={{0,2},{2,0},{4,6},{6,4},{8,10},{10,8},{12,14},{14,12},{16,18},{18,... | collective-permute-start | bytes 1253384 | tf_op jit(solution)/shard_map/ppermute | solution.py:323
  108.9 13.5 %collective-permute-start.29 = (bf16[1024,256]{1,0:T(8,128)(2,1)S(1)}, bf16[1024,256]{1,0:T(8,128)(2,1)S(1)}, u32[]{:S(2)}, u32[]{:S(2)}) collective-permute-start(bf16[1024,256]{1,0:T(8,128)(2,1)S(1)} %collective-permute-done.24.refs_10_.refs_12_), channel_id=1, source_target_pairs={{0,8},{2,10},{4,12},{6,14},{8,0},{10,2},{12,4},{14,6},{16,24},{18,... | collective-permute-start | bytes 1572872 | tf_op jit(solution)/shard_map/ppermute | solution.py:313
  109.0 14.8 %collective-permute-start.30 = (bf16[1024,256]{1,0:T(8,128)(2,1)S(1)}, bf16[1024,256]{1,0:T(8,128)(2,1)S(1)}, u32[]{:S(2)}, u32[]{:S(2)}) collective-permute-start(bf16[1024,256]{1,0:T(8,128)(2,1)S(1)} %collective-permute-done.24.refs_10_.refs_12_), channel_id=1, source_target_pairs={{0,4},{2,6},{4,0},{6,2},{8,12},{10,14},{12,8},{14,10},{16,20},{18,... | collective-permute-start | bytes 1572872 | tf_op jit(solution)/shard_map/ppermute | solution.py:320
  114.4 13.7 %collective-permute-start.28 = (bf16[4,128,256]{2,1,0:T(8,128)(2,1)S(1)}, bf16[4,128,256]{2,1,0:T(8,128)(2,1)S(1)}, u32[]{:S(2)}, u32[]{:S(2)}) collective-permute-start(bf16[4,128,256]{2,1,0:T(8,128)(2,1)S(1)} %get-tuple-element.112), channel_id=1, source_target_pairs={{0,4},{2,6},{4,0},{6,2},{8,12},{10,14},{12,8},{14,10},{16,20},{18,... | collective-permute-start | bytes 786440 | tf_op jit(solution)/shard_map/ppermute | solution.py:320
  128.0 15.5 %collective-permute-start.41 = (bf16[1024,256]{1,0:T(8,128)(2,1)S(1)}, bf16[1024,256]{1,0:T(8,128)(2,1)S(1)}, u32[]{:S(2)}, u32[]{:S(2)}) collective-permute-start(bf16[1024,256]{1,0:T(8,128)(2,1)S(1)} %collective-permute-done.29.refs_10_.refs_14_), channel_id=1, source_target_pairs={{0,4},{2,6},{4,0},{6,2},{8,12},{10,14},{12,8},{14,10},{16,20},{18,... | collective-permute-start | bytes 1572872 | tf_op jit(solution)/shard_map/ppermute | solution.py:320
  (32 other events, 227.3 us)

commit v7 on v6

--- a/solution.py
+++ b/solution.py
@@ -236,10 +236,11 @@
             outs[j][m] = done[z ^ j, c ^ m]
 
 
-def out_kernel(zn, xn, cn, n_head, slots, turns, phases, at, *refs):
+def out_kernel(zn, xn, cn, n_head, slots, turns, phases, forms, at, *refs):
     attended = refs[: zn * cn]
-    weights = refs[zn * cn : zn * cn + len(slots) * xn]
-    outs, rows = refs[zn * cn + len(weights) : -1], refs[-1]
+    rest = iter(refs[zn * cn : -1])
+    weights = [[next(rest) for _ in range(form)] for form in forms]
+    outs, rows = list(rest), refs[-1]
     z, x, c, y = at[0], at[1], at[2], at[3]
     seg_rows = attended[0].shape[1]
     for j in range(zn):
@@ -255,13 +256,18 @@
             spot = (z ^ j) * xn + lax.rem(x + xn - k, xn)
             turn = lax.rem(spot // share + n_head - y, n_head)
             for i, r in enumerate(turns):
-
-                @pl.when(turn == r)
-                def _():
-                    product = dot(rows[...], weights[n * xn + k][...]).astype(BF16)
-                    for m in range(cn):
-                        out = outs[(j % phases * len(turns) + i) * cn + m if len(slots) == zn else i * cn + m]
-                        out[lax.rem(spot, blocks)] = product[m * seg_rows : (m + 1) * seg_rows]
+                for e, weight in enumerate(weights[n * xn + k]):
+                    here = turn == r
+                    if len(weights[n * xn + k]) > 1:
+                        here = here & (c == e)
+
+                    @pl.when(here)
+                    def _():
+                        product = dot(rows[...], weight[...]).astype(BF16)
+                        group = j % phases * len(turns) if len(slots) == zn else 0
+                        for m in range(cn):
+                            out = outs[(group + i) * cn + m]
+                            out[lax.rem(spot, blocks)] = product[m * seg_rows : (m + 1) * seg_rows]
 
 
 def sum_kernel(n_head, cn, phases, at, *refs):
@@ -312,11 +318,12 @@
         pairs = [(s, join(split(s)[0] ^ j, *split(s)[1:])) for s in range(n_seq)]
         return lax.ppermute(a, "seq", pairs)
 
-    def over_x(a, k):
+    def over_x(a, k, cores=None):
         pairs = []
         for s in range(n_seq):
             sz, sx, sc = split(s)
-            pairs.append((s, join(sz, (sx + k) % xn, sc)))
+            if cores is None or sc in cores:
+                pairs.append((s, join(sz, (sx + k) % xn, sc)))
         return lax.ppermute(a, "seq", pairs)
 
     def over_c(a, m):
@@ -469,7 +476,10 @@
         before = [*held, *before[1:]]
         out_z.update(zip(bits[1:], parts))
         for b in bits[1:]:
-            begin_out(b, out_z[b])
+            columns[b] = [out_z[b]]
+            started["o", b] = [
+                over_x(out_z[b], k, (e,)) for e in range(cn) for k in range(1, xn)
+            ]
         for j in more:
             started["oz", j] = over_z(out_z[j ^ (j & -j)], j & -j)
     halves = 2 if zn % 2 == 0 else 1
@@ -504,11 +514,10 @@
         scalars=2,
     )
     mark(token)
-    others, parts, *shares = done_all(
-        others, [started["oz", j] for j in more], *(started["o", b] for b in bits[1:])
-    )
-    for b, share in zip(bits[1:], shares):
-        columns[b] += share
+    count = xn - 1
+    others, parts, *early_x = done_all(
+        others, [started["oz", j] for j in more], *(started["o", b][:count] for b in bits[1:])
+    )
     for j, part in zip(more, parts):
         begin_out(j, part)
     attended = call(
@@ -523,8 +532,11 @@
     )
 
     here = [over_z(block, j) if j else block for j, block in enumerate(attended)]
-    for j in range(1, zn):
+    for j in reversed(range(1, zn)):
         here[j] = done(here[j])
+    for b, ready in zip(bits[1:], early_x):
+        ready = ready + done_all(started["o", b][count:])[0]
+        columns[b] += [ready[k::count] for k in range(count)]
     swapped = [[over_c(here[j], m) for m in range(1, cn)] for j in range(zn)]
     here = sum(([here[j]] + [done(a) for a in swapped[j]] for j in range(zn)), [])
 
@@ -534,9 +546,12 @@
     phases = zn // n_head if zn % n_head == 0 else 1
     blocks = feat_local // (cn * out_cols * phases)
     def multiply(few, turns, outs):
+        arrays = sum((columns[j] for j in few), [])
+        arrays = [a if isinstance(a, list) else [a] for a in arrays]
+        forms = tuple(len(a) for a in arrays)
         return call(
-            functools.partial(out_kernel, zn, xn, cn, n_head, few, turns, phases),
-            (at, *here, *sum((columns[j] for j in few), [])),
+            functools.partial(out_kernel, zn, xn, cn, n_head, few, turns, phases, forms),
+            (at, *here, *sum(arrays, [])),
             [shape((blocks, seg_rows, out_cols))] * outs,
             [pltpu.VMEM((cn * seg_rows, heads * DH), BF16)],
             2 * cn * seg_rows * heads * DH * len(few) * xn * out_cols,

time: 159 us -> 157 us (0.987)
  waiting for transfers between devices: 89 us -> 84.4 us
  starting transfers between devices: 43.3 us -> 46.2 us
    ppermute x12, waiting for transfers between devices: 58.4 us -> 55.5 us  [over_z(): return lax.ppermute(a, 'seq', pairs)]
    ppermute x9 -> x10, starting transfers between devices: 10 us -> 12.8 us  [over_x(): return lax.ppermute(a, 'seq', pairs)]
    ppermute x9 -> x10, waiting for transfers between devices: 20.5 us -> 18.9 us  [over_x(): return lax.ppermute(a, 'seq', pairs)]
  transfers between devices with their start and end apart: 47 -> 48, of which waited for: 24 -> 24; matrix products, arithmetic and copies ran while one was open for 0% -> 0% of each run, Pallas kernels for 13% -> 13%
where the time goes in v7:
time: 157 us
  waiting for transfers between devices  84.4 us (54%)
  starting transfers between devices  46.2 us (29%)
  Pallas kernels  21.7 us (14%)
  local copies, waits for them, and re-layouts  3.8 us (2%)
    ppermute x12, waiting for transfers between devices, over_z(): return lax.ppermute(a, 'seq', pairs)  55.5 us
    pallas_call x14, Pallas kernels, call(): pl.pallas_call(kernel, grid_spec=pltpu.PrefetchScalarGridSpec(num_scalar_...  21.7 us
    ppermute x12, starting transfers between devices, over_z(): return lax.ppermute(a, 'seq', pairs)  21.1 us
    ppermute x10, waiting for transfers between devices, over_x(): return lax.ppermute(a, 'seq', pairs)  18.9 us
    ppermute x10, starting transfers between devices, over_x(): return lax.ppermute(a, 'seq', pairs)  12.8 us
    ppermute x8, starting transfers between devices, over_y(): lax.ppermute(a, 'head', [(h, (h + k) % n_head) for h in range(n_head)])  9.24 us
    ppermute x8, waiting for transfers between devices, over_y(): lax.ppermute(a, 'head', [(h, (h + k) % n_head) for h in range(n_head)])  7.56 us
    unnamed x18, local copies, waits for them, and re-layouts  3.8 us
  transfers between devices with their start and end apart: 48, of which 24 were waited for; matrix products, arithmetic and copies ran while one was open for 0% of the time, Pallas kernels for 13%

profile of v7, /device:TPU:0, one launch (start us, length us, event | category | flops | bytes accessed | tf_op | source)
XLA Modules:
  0.0 157.1 jit_solution(9730652160020696340)
XLA Ops:
  0.0 3.0 %collective-permute-start = (bf16[128,2048]{1,0:T(8,128)(2,1)}, bf16[128,2048]{1,0:T(8,128)(2,1)S(1)}, u32[]{:S(2)}, u32[]{:S(2)}) collective-permute-start(bf16[128,2048]{1,0:T(8,128)(2,1)} %refs_0_.3), channel_id=1, source_target_pairs={{0,8},{2,10},{4,12},{6,14},{8,0},{10,2},{12,4},{14,6},{16,24},{18,... | collective-permute-start | bytes 1572872 | tf_op jit(solution)/shard_map/ppermute | solution.py:319
  3.0 2.6 %collective-permute-start.1 = (bf16[128,2048]{1,0:T(8,128)(2,1)}, bf16[128,2048]{1,0:T(8,128)(2,1)S(1)}, u32[]{:S(2)}, u32[]{:S(2)}) collective-permute-start(bf16[128,2048]{1,0:T(8,128)(2,1)} %refs_0_.3), channel_id=1, source_target_pairs={{0,16},{2,18},{4,20},{6,22},{8,24},{10,26},{12,28},{14,30},{16,0},... | collective-permute-start | bytes 1572872 | tf_op jit(solution)/shard_map/ppermute | solution.py:319
  14.6 8.6 %collective-permute-done.3.refs_6_ = bf16[272,768]{1,0:T(8,128)(2,1)S(1)} collective-permute-done((bf16[272,768]{1,0:T(8,128)(2,1)S(1)}, bf16[272,768]{1,0:T(8,128)(2,1)S(1)}, u32[]{:S(2)}, u32[]{:S(2)}) %collective-permute-start.3) | collective-permute-done | bytes 417824 | tf_op jit(solution)/shard_map/ppermute | solution.py:327
  24.7 2.4 %collective-permute-done.refs_0_ = bf16[128,2048]{1,0:T(8,128)(2,1)S(1)} collective-permute-done((bf16[128,2048]{1,0:T(8,128)(2,1)}, bf16[128,2048]{1,0:T(8,128)(2,1)S(1)}, u32[]{:S(2)}, u32[]{:S(2)}) %collective-permute-start) | collective-permute-done | bytes 524320 | tf_op jit(solution)/shard_map/ppermute | solution.py:319
  27.9 2.5 %collective-permute-start.6 = (bf16[128,2048]{1,0:T(8,128)(2,1)S(1)}, bf16[128,2048]{1,0:T(8,128)(2,1)S(1)}, u32[]{:S(2)}, u32[]{:S(2)}) collective-permute-start(bf16[128,2048]{1,0:T(8,128)(2,1)S(1)} %collective-permute-done.1.refs_0_), channel_id=1, source_target_pairs={{0,8},{2,10},{4,12},{6,14},{8,0},{10,2},{12,4},{14,6},{16,24},{18,... | collective-permute-start | bytes 1572872 | tf_op jit(solution)/shard_map/ppermute | solution.py:319
  32.4 3.8 %collective-permute-done.4.refs_8_ = bf16[272,768]{1,0:T(8,128)(2,1)S(1)} collective-permute-done((bf16[272,768]{1,0:T(8,128)(2,1)S(1)}, bf16[272,768]{1,0:T(8,128)(2,1)S(1)}, u32[]{:S(2)}, u32[]{:S(2)}) %collective-permute-start.4) | collective-permute-done | bytes 417824 | tf_op jit(solution)/shard_map/ppermute | solution.py:319
  36.2 3.1 %collective-permute-start.5 = (bf16[272,768]{1,0:T(8,128)(2,1)S(1)}, bf16[272,768]{1,0:T(8,128)(2,1)S(1)}, u32[]{:S(2)}, u32[]{:S(2)}) collective-permute-start(bf16[272,768]{1,0:T(8,128)(2,1)S(1)} %get-tuple-element.78), channel_id=1, source_target_pairs={{0,16},{2,18},{4,20},{6,22},{8,24},{10,26},{12,28},{14,30},{16,0},... | collective-permute-start | bytes 1253384 | tf_op jit(solution)/shard_map/ppermute | solution.py:319
  40.3 14.6 %collective-permute-done.5.refs_12_ = bf16[272,768]{1,0:T(8,128)(2,1)S(1)} collective-permute-done((bf16[272,768]{1,0:T(8,128)(2,1)S(1)}, bf16[272,768]{1,0:T(8,128)(2,1)S(1)}, u32[]{:S(2)}, u32[]{:S(2)}) %collective-permute-start.5) | collective-permute-done | bytes 417824 | tf_op jit(solution)/shard_map/ppermute | solution.py:319
  55.5 4.1 %collective-permute-start.11 = (bf16[272,768]{1,0:T(8,128)(2,1)S(1)}, bf16[272,768]{1,0:T(8,128)(2,1)S(1)}, u32[]{:S(2)}, u32[]{:S(2)}) collective-permute-start(bf16[272,768]{1,0:T(8,128)(2,1)S(1)} %get-tuple-element.85), channel_id=1, source_target_pairs={{0,24},{2,26},{4,28},{6,30},{8,16},{10,18},{12,20},{14,22},{16,8},... | collective-permute-start | bytes 1253384 | tf_op jit(solution)/shard_map/ppermute | solution.py:319
  65.2 5.0 %collective-permute-done.11.refs_4_ = bf16[272,768]{1,0:T(8,128)(2,1)S(1)} collective-permute-done((bf16[272,768]{1,0:T(8,128)(2,1)S(1)}, bf16[272,768]{1,0:T(8,128)(2,1)S(1)}, u32[]{:S(2)}, u32[]{:S(2)}) %collective-permute-start.11) | collective-permute-done | bytes 417824 | tf_op jit(solution)/shard_map/ppermute | solution.py:319
  72.5 7.0 %collective-permute-done.18.refs_8_.refs_10_ = bf16[1024,256]{1,0:T(8,128)(2,1)S(1)} collective-permute-done((bf16[1024,256]{1,0:T(8,128)(2,1)S(1)}, bf16[1024,256]{1,0:T(8,128)(2,1)S(1)}, u32[]{:S(2)}, u32[]{:S(2)}) %collective-permute-start.18) | collective-permute-done | bytes 524320 | tf_op jit(solution)/shard_map/ppermute | solution.py:319
  84.2 3.4 %shard_map.105 = (f32[4,128,768]{2,1,0:T(8,128)S(1)}, f32[3,2,2,16,128]{4,3,2,1,0:T(8,128)S(1)}) custom-call(s32[4]{0:T(128)S(1)} %pad_add_fusion.at, bf16[128,4096]{1,0:T(8,128)(2,1)S(1)} %shard_map.101.refs_0_, bf16[128,4096]{1,0:T(8,128)(2,1)S(1)} %shard_map.102.refs_1_, bf16[128,4096]{1,0:T(8,128)(2,1)S(1)} %shard_map.103.refs_2_, ...), custom_call_target="tpu_custom_call" | custom-call | flops 2415919104 | bytes 10878992 | tf_op jit(solution)/shard_map/pallas_call | solution.py:34
  87.6 5.8 %collective-permute-done.13.refs_6_ = bf16[272,768]{1,0:T(8,128)(2,1)S(1)} collective-permute-done((bf16[272,768]{1,0:T(8,128)(2,1)S(1)}, bf16[272,768]{1,0:T(8,128)(2,1)S(1)}, u32[]{:S(2)}, u32[]{:S(2)}) %collective-permute-start.13) | collective-permute-done | bytes 417824 | tf_op jit(solution)/shard_map/ppermute | solution.py:327
  93.5 15.5 %collective-permute-done.24.refs_10_.refs_12_ = bf16[1024,256]{1,0:T(8,128)(2,1)S(1)} collective-permute-done((bf16[1024,256]{1,0:T(8,128)(2,1)S(1)}, bf16[1024,256]{1,0:T(8,128)(2,1)S(1)}, u32[]{:S(2)}, u32[]{:S(2)}) %collective-permute-start.24) | collective-permute-done | bytes 524320 | tf_op jit(solution)/shard_map/ppermute | solution.py:319
  109.0 2.4 %collective-permute-start.30 = (bf16[1024,256]{1,0:T(8,128)(2,1)S(1)}, bf16[1024,256]{1,0:T(8,128)(2,1)S(1)}, u32[]{:S(2)}, u32[]{:S(2)}) collective-permute-start(bf16[1024,256]{1,0:T(8,128)(2,1)S(1)} %collective-permute-done.24.refs_10_.refs_12_), channel_id=1, source_target_pairs={{0,4},{4,0},{8,12},{12,8},{16,20},{20,16},{24,28},{28,24},{1,5},{5... | collective-permute-start | bytes 1572872 | tf_op jit(solution)/shard_map/ppermute | solution.py:327
  118.5 2.0 %shard_map.108.token = f32[4,2,128,128]{3,2,1,0:T(8,128)S(1)} custom-call(s32[4]{0:T(128)S(1)} %pad_add_fusion.at, f32[8]{0:T(128)S(1)} %copy-done.7, f32[4,2,2,16,128]{4,3,2,1,0:T(8,128)S(1)} %get-tuple-element.109.table, bf16[4,2,128,384]{3,2,1,0:T(8,128)(2,1)S(1)} %get-tuple-element.110.sums), custom_call_target="tpu_custom_call" | custom-call | bytes 1441840 | tf_op jit(solution)/shard_map/pallas_call | solution.py:34
  120.5 1.9 %collective-permute-done.29.refs_10_.refs_15_ = bf16[1024,256]{1,0:T(8,128)(2,1)S(1)} collective-permute-done((bf16[1024,256]{1,0:T(8,128)(2,1)S(1)}, bf16[1024,256]{1,0:T(8,128)(2,1)S(1)}, u32[]{:S(2)}, u32[]{:S(2)}) %collective-permute-start.29) | collective-permute-done | bytes 524320 | tf_op jit(solution)/shard_map/ppermute | solution.py:319
  122.4 4.0 %collective-permute-done.28.refs_0_ = bf16[4,128,256]{2,1,0:T(8,128)(2,1)S(1)} collective-permute-done((bf16[4,128,256]{2,1,0:T(8,128)(2,1)S(1)}, bf16[4,128,256]{2,1,0:T(8,128)(2,1)S(1)}, u32[]{:S(2)}, u32[]{:S(2)}) %collective-permute-start.28) | collective-permute-done | bytes 262176 | tf_op jit(solution)/shard_map/ppermute | solution.py:327
  127.0 2.2 %shard_map.109 = (bf16[2,128,128]{2,1,0:T(8,128)(2,1)S(1)}, bf16[2,128,128]{2,1,0:T(8,128)(2,1)S(1)}, bf16[2,128,128]{2,1,0:T(8,128)(2,1)S(1)}, bf16[2,128,128]{2,1,0:T(8,128)(2,1)S(1)}) custom-call(s32[4]{0:T(128)S(1)} %pad_add_fusion.at, f32[8]{0:T(128)S(1)} %copy-done.7, f32[4,2,2,16,128]{4,3,2,1,0:T(8,128)S(1)} %get-tuple-element.109.table, ...), custom_call_target="tpu_custom_call" | custom-call | bytes 3538992 | tf_op jit(solution)/shard_map/pallas_call | solution.py:34
  129.2 1.8 %collective-permute-start.35 = (bf16[2,128,128]{2,1,0:T(8,128)(2,1)S(1)}, bf16[2,128,128]{2,1,0:T(8,128)(2,1)S(1)}, u32[]{:S(2)}, u32[]{:S(2)}) collective-permute-start(bf16[2,128,128]{2,1,0:T(8,128)(2,1)S(1)} %get-tuple-element.119), channel_id=1, source_target_pairs={{0,24},{2,26},{4,28},{6,30},{8,16},{10,18},{12,20},{14,22},{16,8},... | collective-permute-start | bytes 196616 | tf_op jit(solution)/shard_map/ppermute | solution.py:319
  135.4 2.0 %collective-permute-done.34.refs_4_ = bf16[2,128,128]{2,1,0:T(8,128)(2,1)S(1)} collective-permute-done((bf16[2,128,128]{2,1,0:T(8,128)(2,1)S(1)}, bf16[2,128,128]{2,1,0:T(8,128)(2,1)S(1)}, u32[]{:S(2)}, u32[]{:S(2)}) %collective-permute-start.34) | collective-permute-done | bytes 65568 | tf_op jit(solution)/shard_map/ppermute | solution.py:319
  144.7 2.0 %shard_map.112 = (bf16[2,128,256]{2,1,0:T(8,128)(2,1)S(1)}, bf16[2,128,256]{2,1,0:T(8,128)(2,1)S(1)}, bf16[2,128,256]{2,1,0:T(8,128)(2,1)S(1)}, bf16[2,128,256]{2,1,0:T(8,128)(2,1)S(1)}) custom-call(s32[4]{0:T(128)S(1)} %pad_add_fusion.at, bf16[2,128,128]{2,1,0:T(8,128)(2,1)S(1)} %get-tuple-element.116.refs_0_, ...), custom_call_target="tpu_custom_call" | custom-call | flops 1073741824 | bytes 5767184 | tf_op jit(solution)/shard_map/pallas_call | solution.py:34
  150.0 3.7 %collective-permute-done.43.refs_2_ = bf16[2,128,256]{2,1,0:T(8,128)(2,1)S(1)} collective-permute-done((bf16[2,128,256]{2,1,0:T(8,128)(2,1)S(1)}, bf16[2,128,256]{2,1,0:T(8,128)(2,1)S(1)}, u32[]{:S(2)}, u32[]{:S(2)}) %collective-permute-start.43) | collective-permute-done | bytes 131104 | tf_op jit(solution)/shard_map/ppermute | solution.py:333
  153.6 1.9 %collective-permute-done.45.refs_3_ = bf16[2,128,256]{2,1,0:T(8,128)(2,1)S(1)} collective-permute-done((bf16[2,128,256]{2,1,0:T(8,128)(2,1)S(1)}, bf16[2,128,256]{2,1,0:T(8,128)(2,1)S(1)}, u32[]{:S(2)}, u32[]{:S(2)}) %collective-permute-start.45) | collective-permute-done | bytes 131104 | tf_op jit(solution)/shard_map/ppermute | solution.py:333
  (105 shorter events, 50.8 us)
Async XLA Ops:
  0.0 27.1 %collective-permute-start = (bf16[128,2048]{1,0:T(8,128)(2,1)}, bf16[128,2048]{1,0:T(8,128)(2,1)S(1)}, u32[]{:S(2)}, u32[]{:S(2)}) collective-permute-start(bf16[128,2048]{1,0:T(8,128)(2,1)} %refs_0_.3), channel_id=1, source_target_pairs={{0,8},{2,10},{4,12},{6,14},{8,0},{10,2},{12,4},{14,6},{16,24},{18,... | collective-permute-start | bytes 1572872 | tf_op jit(solution)/shard_map/ppermute | solution.py:319
  3.0 24.8 %collective-permute-start.1 = (bf16[128,2048]{1,0:T(8,128)(2,1)}, bf16[128,2048]{1,0:T(8,128)(2,1)S(1)}, u32[]{:S(2)}, u32[]{:S(2)}) collective-permute-start(bf16[128,2048]{1,0:T(8,128)(2,1)} %refs_0_.3), channel_id=1, source_target_pairs={{0,16},{2,18},{4,20},{6,22},{8,24},{10,26},{12,28},{14,30},{16,0},... | collective-permute-start | bytes 1572872 | tf_op jit(solution)/shard_map/ppermute | solution.py:319
  5.6 22.2 %collective-permute-start.2 = (bf16[128,2048]{1,0:T(8,128)(2,1)}, bf16[128,2048]{1,0:T(8,128)(2,1)S(1)}, u32[]{:S(2)}, u32[]{:S(2)}) collective-permute-start(bf16[128,2048]{1,0:T(8,128)(2,1)} %refs_0_.3), channel_id=1, source_target_pairs={{0,1},{1,0},{2,3},{3,2},{4,5},{5,4},{6,7},{7,6},{8,9},{9,8},{10,11... | collective-permute-start | bytes 1572872 | tf_op jit(solution)/shard_map/ppermute | solution.py:333
  12.6 10.6 %collective-permute-start.3 = (bf16[272,768]{1,0:T(8,128)(2,1)S(1)}, bf16[272,768]{1,0:T(8,128)(2,1)S(1)}, u32[]{:S(2)}, u32[]{:S(2)}) collective-permute-start(bf16[272,768]{1,0:T(8,128)(2,1)S(1)} %get-tuple-element.73.refs_4_), channel_id=1, source_target_pairs={{0,4},{2,6},{4,0},{6,2},{8,12},{10,14},{12,8},{14,10},{16,20},{18,... | collective-permute-start | bytes 1253384 | tf_op jit(solution)/shard_map/ppermute | solution.py:327
  14.2 22.0 %collective-permute-start.4 = (bf16[272,768]{1,0:T(8,128)(2,1)S(1)}, bf16[272,768]{1,0:T(8,128)(2,1)S(1)}, u32[]{:S(2)}, u32[]{:S(2)}) collective-permute-start(bf16[272,768]{1,0:T(8,128)(2,1)S(1)} %get-tuple-element.76), channel_id=1, source_target_pairs={{0,8},{2,10},{4,12},{6,14},{8,0},{10,2},{12,4},{14,6},{16,24},{18,... | collective-permute-start | bytes 1253384 | tf_op jit(solution)/shard_map/ppermute | solution.py:319
  23.2 17.0 %collective-permute-start.7 = (bf16[1024,256]{1,0:T(8,128)(2,1)S(1)}, bf16[1024,256]{1,0:T(8,128)(2,1)S(1)}, u32[]{:S(2)}, u32[]{:S(2)}) collective-permute-start(bf16[1024,256]{1,0:T(8,128)(2,1)S(1)} %copy-done), channel_id=1, source_target_pairs={{0,4},{2,6},{4,0},{6,2},{8,12},{10,14},{12,8},{14,10},{16,20},{18,... | collective-permute-start | bytes 1572872 | tf_op jit(solution)/shard_map/ppermute | solution.py:327
  27.9 27.7 %collective-permute-start.6 = (bf16[128,2048]{1,0:T(8,128)(2,1)S(1)}, bf16[128,2048]{1,0:T(8,128)(2,1)S(1)}, u32[]{:S(2)}, u32[]{:S(2)}) collective-permute-start(bf16[128,2048]{1,0:T(8,128)(2,1)S(1)} %collective-permute-done.1.refs_0_), channel_id=1, source_target_pairs={{0,8},{2,10},{4,12},{6,14},{8,0},{10,2},{12,4},{14,6},{16,24},{18,... | collective-permute-start | bytes 1572872 | tf_op jit(solution)/shard_map/ppermute | solution.py:319
  30.3 25.2 %collective-permute-start.8 = (bf16[128,2048]{1,0:T(8,128)(2,1)S(1)}, bf16[128,2048]{1,0:T(8,128)(2,1)S(1)}, u32[]{:S(2)}, u32[]{:S(2)}) collective-permute-start(bf16[128,2048]{1,0:T(8,128)(2,1)S(1)} %collective-permute-done.refs_0_), channel_id=1, source_target_pairs={{0,1},{1,0},{2,3},{3,2},{4,5},{5,4},{6,7},{7,6},{8,9},{9,8},{10,11... | collective-permute-start | bytes 1572872 | tf_op jit(solution)/shard_map/ppermute | solution.py:333
  31.9 23.7 %collective-permute-start.9 = (bf16[128,2048]{1,0:T(8,128)(2,1)S(1)}, bf16[128,2048]{1,0:T(8,128)(2,1)S(1)}, u32[]{:S(2)}, u32[]{:S(2)}) collective-permute-start(bf16[128,2048]{1,0:T(8,128)(2,1)S(1)} %collective-permute-done.1.refs_0_), channel_id=1, source_target_pairs={{0,1},{1,0},{2,3},{3,2},{4,5},{5,4},{6,7},{7,6},{8,9},{9,8},{10,11... | collective-permute-start | bytes 1572872 | tf_op jit(solution)/shard_map/ppermute | solution.py:333
  36.2 18.7 %collective-permute-start.5 = (bf16[272,768]{1,0:T(8,128)(2,1)S(1)}, bf16[272,768]{1,0:T(8,128)(2,1)S(1)}, u32[]{:S(2)}, u32[]{:S(2)}) collective-permute-start(bf16[272,768]{1,0:T(8,128)(2,1)S(1)} %get-tuple-element.78), channel_id=1, source_target_pairs={{0,16},{2,18},{4,20},{6,22},{8,24},{10,26},{12,28},{14,30},{16,0},... | collective-permute-start | bytes 1253384 | tf_op jit(solution)/shard_map/ppermute | solution.py:319
  55.5 14.7 %collective-permute-start.11 = (bf16[272,768]{1,0:T(8,128)(2,1)S(1)}, bf16[272,768]{1,0:T(8,128)(2,1)S(1)}, u32[]{:S(2)}, u32[]{:S(2)}) collective-permute-start(bf16[272,768]{1,0:T(8,128)(2,1)S(1)} %get-tuple-element.85), channel_id=1, source_target_pairs={{0,24},{2,26},{4,28},{6,30},{8,16},{10,18},{12,20},{14,22},{16,8},... | collective-permute-start | bytes 1253384 | tf_op jit(solution)/shard_map/ppermute | solution.py:319
  59.6 11.9 %collective-permute-start.10 = (bf16[128,2048]{1,0:T(8,128)(2,1)S(1)}, bf16[128,2048]{1,0:T(8,128)(2,1)S(1)}, u32[]{:S(2)}, u32[]{:S(2)}) collective-permute-start(bf16[128,2048]{1,0:T(8,128)(2,1)S(1)} %collective-permute-done.6.refs_0_), channel_id=1, source_target_pairs={{0,1},{1,0},{2,3},{3,2},{4,5},{5,4},{6,7},{7,6},{8,9},{9,8},{10,11... | collective-permute-start | bytes 1572872 | tf_op jit(solution)/shard_map/ppermute | solution.py:333
  61.1 18.4 %collective-permute-start.18 = (bf16[1024,256]{1,0:T(8,128)(2,1)S(1)}, bf16[1024,256]{1,0:T(8,128)(2,1)S(1)}, u32[]{:S(2)}, u32[]{:S(2)}) collective-permute-start(bf16[1024,256]{1,0:T(8,128)(2,1)S(1)} %copy-done), channel_id=1, source_target_pairs={{0,8},{2,10},{4,12},{6,14},{8,0},{10,2},{12,4},{14,6},{16,24},{18,... | collective-permute-start | bytes 1572872 | tf_op jit(solution)/shard_map/ppermute | solution.py:319
  62.1 17.4 %collective-permute-start.17 = (bf16[272,768]{1,0:T(8,128)(2,1)S(1)}, bf16[272,768]{1,0:T(8,128)(2,1)S(1)}, u32[]{:S(2)}, u32[]{:S(2)}) collective-permute-start(bf16[272,768]{1,0:T(8,128)(2,1)S(1)} %collective-permute-done.4.refs_8_), channel_id=1, source_target_pairs={{0,4},{2,6},{4,0},{6,2},{8,12},{10,14},{12,8},{14,10},{16,20},{18,... | collective-permute-start | bytes 1253384 | tf_op jit(solution)/shard_map/ppermute | solution.py:327
  64.6 15.9 %collective-permute-start.21 = (bf16[272,768]{1,0:T(8,128)(2,1)S(1)}, bf16[272,768]{1,0:T(8,128)(2,1)S(1)}, u32[]{:S(2)}, u32[]{:S(2)}) collective-permute-start(bf16[272,768]{1,0:T(8,128)(2,1)S(1)} %collective-permute-done.5.refs_12_), channel_id=1, source_target_pairs={{0,4},{2,6},{4,0},{6,2},{8,12},{10,14},{12,8},{14,10},{16,20},{18,... | collective-permute-start | bytes 1253384 | tf_op jit(solution)/shard_map/ppermute | solution.py:327
  81.0 12.5 %collective-permute-start.13 = (bf16[272,768]{1,0:T(8,128)(2,1)S(1)}, bf16[272,768]{1,0:T(8,128)(2,1)S(1)}, u32[]{:S(2)}, u32[]{:S(2)}) collective-permute-start(bf16[272,768]{1,0:T(8,128)(2,1)S(1)} %collective-permute-done.11.refs_4_), channel_id=1, source_target_pairs={{0,4},{2,6},{4,0},{6,2},{8,12},{10,14},{12,8},{14,10},{16,20},{18,... | collective-permute-start | bytes 1253384 | tf_op jit(solution)/shard_map/ppermute | solution.py:327
  82.5 28.9 %collective-permute-start.12 = (bf16[272,768]{1,0:T(8,128)(2,1)S(1)}, bf16[272,768]{1,0:T(8,128)(2,1)S(1)}, u32[]{:S(2)}, u32[]{:S(2)}) collective-permute-start(bf16[272,768]{1,0:T(8,128)(2,1)S(1)} %collective-permute-done.11.refs_4_), channel_id=1, source_target_pairs={{0,2},{2,0},{4,6},{6,4},{8,10},{10,8},{12,14},{14,12},{16,18},{18,... | collective-permute-start | bytes 1253384 | tf_op jit(solution)/shard_map/ppermute | solution.py:330
  82.5 26.5 %collective-permute-start.24 = (bf16[1024,256]{1,0:T(8,128)(2,1)S(1)}, bf16[1024,256]{1,0:T(8,128)(2,1)S(1)}, u32[]{:S(2)}, u32[]{:S(2)}) collective-permute-start(bf16[1024,256]{1,0:T(8,128)(2,1)S(1)} %copy-done), channel_id=1, source_target_pairs={{0,16},{2,18},{4,20},{6,22},{8,24},{10,26},{12,28},{14,30},{16,0},... | collective-permute-start | bytes 1572872 | tf_op jit(solution)/shard_map/ppermute | solution.py:319
  83.4 25.5 %collective-permute-start.25 = (bf16[1024,256]{1,0:T(8,128)(2,1)S(1)}, bf16[1024,256]{1,0:T(8,128)(2,1)S(1)}, u32[]{:S(2)}, u32[]{:S(2)}) collective-permute-start(bf16[1024,256]{1,0:T(8,128)(2,1)S(1)} %collective-permute-done.18.refs_8_.refs_10_), channel_id=1, source_target_pairs={{0,4},{2,6},{4,0},{6,2},{8,12},{10,14},{12,8},{14,10},{16,20},{18,... | collective-permute-start | bytes 1572872 | tf_op jit(solution)/shard_map/ppermute | solution.py:327
  93.5 17.9 %collective-permute-start.23 = (bf16[272,768]{1,0:T(8,128)(2,1)S(1)}, bf16[272,768]{1,0:T(8,128)(2,1)S(1)}, u32[]{:S(2)}, u32[]{:S(2)}) collective-permute-start(bf16[272,768]{1,0:T(8,128)(2,1)S(1)} %collective-permute-done.13.refs_6_), channel_id=1, source_target_pairs={{0,2},{2,0},{4,6},{6,4},{8,10},{10,8},{12,14},{14,12},{16,18},{18,... | collective-permute-start | bytes 1253384 | tf_op jit(solution)/shard_map/ppermute | solution.py:330
  108.9 13.5 %collective-permute-start.29 = (bf16[1024,256]{1,0:T(8,128)(2,1)S(1)}, bf16[1024,256]{1,0:T(8,128)(2,1)S(1)}, u32[]{:S(2)}, u32[]{:S(2)}) collective-permute-start(bf16[1024,256]{1,0:T(8,128)(2,1)S(1)} %collective-permute-done.24.refs_10_.refs_12_), channel_id=1, source_target_pairs={{0,8},{2,10},{4,12},{6,14},{8,0},{10,2},{12,4},{14,6},{16,24},{18,... | collective-permute-start | bytes 1572872 | tf_op jit(solution)/shard_map/ppermute | solution.py:319
  109.0 13.5 %collective-permute-start.30 = (bf16[1024,256]{1,0:T(8,128)(2,1)S(1)}, bf16[1024,256]{1,0:T(8,128)(2,1)S(1)}, u32[]{:S(2)}, u32[]{:S(2)}) collective-permute-start(bf16[1024,256]{1,0:T(8,128)(2,1)S(1)} %collective-permute-done.24.refs_10_.refs_12_), channel_id=1, source_target_pairs={{0,4},{4,0},{8,12},{12,8},{16,20},{20,16},{24,28},{28,24},{1,5},{5... | collective-permute-start | bytes 1572872 | tf_op jit(solution)/shard_map/ppermute | solution.py:327
  117.8 20.2 %collective-permute-start.32 = (bf16[1024,256]{1,0:T(8,128)(2,1)S(1)}, bf16[1024,256]{1,0:T(8,128)(2,1)S(1)}, u32[]{:S(2)}, u32[]{:S(2)}) collective-permute-start(bf16[1024,256]{1,0:T(8,128)(2,1)S(1)} %collective-permute-done.24.refs_10_.refs_12_), channel_id=1, source_target_pairs={{2,6},{6,2},{10,14},{14,10},{18,22},{22,18},{26,30},{30,26},{3,7},... | collective-permute-start | bytes 1572872 | tf_op jit(solution)/shard_map/ppermute | solution.py:327
  126.4 16.2 %collective-permute-start.42 = (bf16[1024,256]{1,0:T(8,128)(2,1)S(1)}, bf16[1024,256]{1,0:T(8,128)(2,1)S(1)}, u32[]{:S(2)}, u32[]{:S(2)}) collective-permute-start(bf16[1024,256]{1,0:T(8,128)(2,1)S(1)} %collective-permute-done.29.refs_10_.refs_15_), channel_id=1, source_target_pairs={{0,4},{2,6},{4,0},{6,2},{8,12},{10,14},{12,8},{14,10},{16,20},{18,... | collective-permute-start | bytes 1572872 | tf_op jit(solution)/shard_map/ppermute | solution.py:327
  (33 other events, 238.2 us)

commit v8 on v7

--- a/solution.py
+++ b/solution.py
@@ -478,7 +478,7 @@
         for b in bits[1:]:
             columns[b] = [out_z[b]]
             started["o", b] = [
-                over_x(out_z[b], k, (e,)) for e in range(cn) for k in range(1, xn)
+                over_x(out_z[b], k, (e,)) for e in reversed(range(cn)) for k in range(1, xn)
             ]
         for j in more:
             started["oz", j] = over_z(out_z[j ^ (j & -j)], j & -j)
@@ -536,7 +536,7 @@
         here[j] = done(here[j])
     for b, ready in zip(bits[1:], early_x):
         ready = ready + done_all(started["o", b][count:])[0]
-        columns[b] += [ready[k::count] for k in range(count)]
+        columns[b] += [ready[k::count][::-1] for k in range(count)]
     swapped = [[over_c(here[j], m) for m in range(1, cn)] for j in range(zn)]
     here = sum(([here[j]] + [done(a) for a in swapped[j]] for j in range(zn)), [])
 

time: 157 us -> 156 us (level)
  waiting for transfers between devices: 84.4 us -> 82.8 us
    ppermute x10, waiting for transfers between devices: 18.9 us -> 17.2 us  [over_x(): return lax.ppermute(a, 'seq', pairs)]
  transfers between devices with their start and end apart: 48 -> 48, of which waited for: 24 -> 25; matrix products, arithmetic and copies ran while one was open for 0% -> 0% of each run, Pallas kernels for 13% -> 13%
where the time goes in v8:
time: 156 us
  waiting for transfers between devices  82.8 us (53%)
  starting transfers between devices  46.8 us (30%)
  Pallas kernels  21.7 us (14%)
  local copies, waits for them, and re-layouts  3.8 us (2%)
    ppermute x12, waiting for transfers between devices, over_z(): return lax.ppermute(a, 'seq', pairs)  55.4 us
    pallas_call x14, Pallas kernels, call(): pl.pallas_call(kernel, grid_spec=pltpu.PrefetchScalarGridSpec(num_scalar_...  21.7 us
    ppermute x12, starting transfers between devices, over_z(): return lax.ppermute(a, 'seq', pairs)  21.1 us
    ppermute x10, waiting for transfers between devices, over_x(): return lax.ppermute(a, 'seq', pairs)  17.2 us
    ppermute x10, starting transfers between devices, over_x(): return lax.ppermute(a, 'seq', pairs)  13.3 us
    ppermute x8, starting transfers between devices, over_y(): lax.ppermute(a, 'head', [(h, (h + k) % n_head) for h in range(n_head)])  8.82 us
    ppermute x8, waiting for transfers between devices, over_y(): lax.ppermute(a, 'head', [(h, (h + k) % n_head) for h in range(n_head)])  7.63 us
    unnamed x18, local copies, waits for them, and re-layouts  3.8 us
  transfers between devices with their start and end apart: 48, of which 25 were waited for; matrix products, arithmetic and copies ran while one was open for 0% of the time, Pallas kernels for 13%

profile of v8, /device:TPU:0, one launch (start us, length us, event | category | flops | bytes accessed | tf_op | source)
XLA Modules:
  0.0 156.1 jit_solution(11281265237390857954)
XLA Ops:
  0.0 3.0 %collective-permute-start = (bf16[128,2048]{1,0:T(8,128)(2,1)}, bf16[128,2048]{1,0:T(8,128)(2,1)S(1)}, u32[]{:S(2)}, u32[]{:S(2)}) collective-permute-start(bf16[128,2048]{1,0:T(8,128)(2,1)} %refs_0_.3), channel_id=1, source_target_pairs={{0,8},{2,10},{4,12},{6,14},{8,0},{10,2},{12,4},{14,6},{16,24},{18,... | collective-permute-start | bytes 1572872 | tf_op jit(solution)/shard_map/ppermute | solution.py:319
  3.0 2.6 %collective-permute-start.1 = (bf16[128,2048]{1,0:T(8,128)(2,1)}, bf16[128,2048]{1,0:T(8,128)(2,1)S(1)}, u32[]{:S(2)}, u32[]{:S(2)}) collective-permute-start(bf16[128,2048]{1,0:T(8,128)(2,1)} %refs_0_.3), channel_id=1, source_target_pairs={{0,16},{2,18},{4,20},{6,22},{8,24},{10,26},{12,28},{14,30},{16,0},... | collective-permute-start | bytes 1572872 | tf_op jit(solution)/shard_map/ppermute | solution.py:319
  14.6 8.6 %collective-permute-done.3.refs_6_ = bf16[272,768]{1,0:T(8,128)(2,1)S(1)} collective-permute-done((bf16[272,768]{1,0:T(8,128)(2,1)S(1)}, bf16[272,768]{1,0:T(8,128)(2,1)S(1)}, u32[]{:S(2)}, u32[]{:S(2)}) %collective-permute-start.3) | collective-permute-done | bytes 417824 | tf_op jit(solution)/shard_map/ppermute | solution.py:327
  24.7 2.4 %collective-permute-done.refs_0_ = bf16[128,2048]{1,0:T(8,128)(2,1)S(1)} collective-permute-done((bf16[128,2048]{1,0:T(8,128)(2,1)}, bf16[128,2048]{1,0:T(8,128)(2,1)S(1)}, u32[]{:S(2)}, u32[]{:S(2)}) %collective-permute-start) | collective-permute-done | bytes 524320 | tf_op jit(solution)/shard_map/ppermute | solution.py:319
  27.9 2.5 %collective-permute-start.6 = (bf16[128,2048]{1,0:T(8,128)(2,1)S(1)}, bf16[128,2048]{1,0:T(8,128)(2,1)S(1)}, u32[]{:S(2)}, u32[]{:S(2)}) collective-permute-start(bf16[128,2048]{1,0:T(8,128)(2,1)S(1)} %collective-permute-done.1.refs_0_), channel_id=1, source_target_pairs={{0,8},{2,10},{4,12},{6,14},{8,0},{10,2},{12,4},{14,6},{16,24},{18,... | collective-permute-start | bytes 1572872 | tf_op jit(solution)/shard_map/ppermute | solution.py:319
  32.4 3.8 %collective-permute-done.4.refs_8_ = bf16[272,768]{1,0:T(8,128)(2,1)S(1)} collective-permute-done((bf16[272,768]{1,0:T(8,128)(2,1)S(1)}, bf16[272,768]{1,0:T(8,128)(2,1)S(1)}, u32[]{:S(2)}, u32[]{:S(2)}) %collective-permute-start.4) | collective-permute-done | bytes 417824 | tf_op jit(solution)/shard_map/ppermute | solution.py:319
  36.2 3.1 %collective-permute-start.5 = (bf16[272,768]{1,0:T(8,128)(2,1)S(1)}, bf16[272,768]{1,0:T(8,128)(2,1)S(1)}, u32[]{:S(2)}, u32[]{:S(2)}) collective-permute-start(bf16[272,768]{1,0:T(8,128)(2,1)S(1)} %get-tuple-element.78), channel_id=1, source_target_pairs={{0,16},{2,18},{4,20},{6,22},{8,24},{10,26},{12,28},{14,30},{16,0},... | collective-permute-start | bytes 1253384 | tf_op jit(solution)/shard_map/ppermute | solution.py:319
  40.3 14.6 %collective-permute-done.5.refs_12_ = bf16[272,768]{1,0:T(8,128)(2,1)S(1)} collective-permute-done((bf16[272,768]{1,0:T(8,128)(2,1)S(1)}, bf16[272,768]{1,0:T(8,128)(2,1)S(1)}, u32[]{:S(2)}, u32[]{:S(2)}) %collective-permute-start.5) | collective-permute-done | bytes 417824 | tf_op jit(solution)/shard_map/ppermute | solution.py:319
  55.5 4.1 %collective-permute-start.11 = (bf16[272,768]{1,0:T(8,128)(2,1)S(1)}, bf16[272,768]{1,0:T(8,128)(2,1)S(1)}, u32[]{:S(2)}, u32[]{:S(2)}) collective-permute-start(bf16[272,768]{1,0:T(8,128)(2,1)S(1)} %get-tuple-element.85), channel_id=1, source_target_pairs={{0,24},{2,26},{4,28},{6,30},{8,16},{10,18},{12,20},{14,22},{16,8},... | collective-permute-start | bytes 1253384 | tf_op jit(solution)/shard_map/ppermute | solution.py:319
  65.2 5.0 %collective-permute-done.11.refs_4_ = bf16[272,768]{1,0:T(8,128)(2,1)S(1)} collective-permute-done((bf16[272,768]{1,0:T(8,128)(2,1)S(1)}, bf16[272,768]{1,0:T(8,128)(2,1)S(1)}, u32[]{:S(2)}, u32[]{:S(2)}) %collective-permute-start.11) | collective-permute-done | bytes 417824 | tf_op jit(solution)/shard_map/ppermute | solution.py:319
  72.5 7.0 %collective-permute-done.18.refs_8_.refs_10_ = bf16[1024,256]{1,0:T(8,128)(2,1)S(1)} collective-permute-done((bf16[1024,256]{1,0:T(8,128)(2,1)S(1)}, bf16[1024,256]{1,0:T(8,128)(2,1)S(1)}, u32[]{:S(2)}, u32[]{:S(2)}) %collective-permute-start.18) | collective-permute-done | bytes 524320 | tf_op jit(solution)/shard_map/ppermute | solution.py:319
  84.2 3.4 %shard_map.105 = (f32[4,128,768]{2,1,0:T(8,128)S(1)}, f32[3,2,2,16,128]{4,3,2,1,0:T(8,128)S(1)}) custom-call(s32[4]{0:T(128)S(1)} %pad_add_fusion.at, bf16[128,4096]{1,0:T(8,128)(2,1)S(1)} %shard_map.101.refs_0_, bf16[128,4096]{1,0:T(8,128)(2,1)S(1)} %shard_map.102.refs_1_, bf16[128,4096]{1,0:T(8,128)(2,1)S(1)} %shard_map.103.refs_2_, ...), custom_call_target="tpu_custom_call" | custom-call | flops 2415919104 | bytes 10878992 | tf_op jit(solution)/shard_map/pallas_call | solution.py:34
  87.6 5.8 %collective-permute-done.13.refs_6_ = bf16[272,768]{1,0:T(8,128)(2,1)S(1)} collective-permute-done((bf16[272,768]{1,0:T(8,128)(2,1)S(1)}, bf16[272,768]{1,0:T(8,128)(2,1)S(1)}, u32[]{:S(2)}, u32[]{:S(2)}) %collective-permute-start.13) | collective-permute-done | bytes 417824 | tf_op jit(solution)/shard_map/ppermute | solution.py:327
  93.5 15.5 %collective-permute-done.24.refs_10_.refs_12_ = bf16[1024,256]{1,0:T(8,128)(2,1)S(1)} collective-permute-done((bf16[1024,256]{1,0:T(8,128)(2,1)S(1)}, bf16[1024,256]{1,0:T(8,128)(2,1)S(1)}, u32[]{:S(2)}, u32[]{:S(2)}) %collective-permute-start.24) | collective-permute-done | bytes 524320 | tf_op jit(solution)/shard_map/ppermute | solution.py:319
  116.9 2.3 %collective-permute-start.32 = (bf16[1024,256]{1,0:T(8,128)(2,1)S(1)}, bf16[1024,256]{1,0:T(8,128)(2,1)S(1)}, u32[]{:S(2)}, u32[]{:S(2)}) collective-permute-start(bf16[1024,256]{1,0:T(8,128)(2,1)S(1)} %collective-permute-done.24.refs_10_.refs_12_), channel_id=1, source_target_pairs={{0,4},{4,0},{8,12},{12,8},{16,20},{20,16},{24,28},{28,24},{1,5},{5... | collective-permute-start | bytes 1572872 | tf_op jit(solution)/shard_map/ppermute | solution.py:327
  119.2 2.0 %shard_map.108.token = f32[4,2,128,128]{3,2,1,0:T(8,128)S(1)} custom-call(s32[4]{0:T(128)S(1)} %pad_add_fusion.at, f32[8]{0:T(128)S(1)} %copy-done.7, f32[4,2,2,16,128]{4,3,2,1,0:T(8,128)S(1)} %get-tuple-element.109.table, bf16[4,2,128,384]{3,2,1,0:T(8,128)(2,1)S(1)} %get-tuple-element.110.sums), custom_call_target="tpu_custom_call" | custom-call | bytes 1441840 | tf_op jit(solution)/shard_map/pallas_call | solution.py:34
  122.4 1.9 %collective-permute-done.28.refs_0_ = bf16[4,128,256]{2,1,0:T(8,128)(2,1)S(1)} collective-permute-done((bf16[4,128,256]{2,1,0:T(8,128)(2,1)S(1)}, bf16[4,128,256]{2,1,0:T(8,128)(2,1)S(1)}, u32[]{:S(2)}, u32[]{:S(2)}) %collective-permute-start.28) | collective-permute-done | bytes 262176 | tf_op jit(solution)/shard_map/ppermute | solution.py:327
  125.4 2.2 %shard_map.109 = (bf16[2,128,128]{2,1,0:T(8,128)(2,1)S(1)}, bf16[2,128,128]{2,1,0:T(8,128)(2,1)S(1)}, bf16[2,128,128]{2,1,0:T(8,128)(2,1)S(1)}, bf16[2,128,128]{2,1,0:T(8,128)(2,1)S(1)}) custom-call(s32[4]{0:T(128)S(1)} %pad_add_fusion.at, f32[8]{0:T(128)S(1)} %copy-done.7, f32[4,2,2,16,128]{4,3,2,1,0:T(8,128)S(1)} %get-tuple-element.109.table, ...), custom_call_target="tpu_custom_call" | custom-call | bytes 3538992 | tf_op jit(solution)/shard_map/pallas_call | solution.py:34
  127.6 2.3 %collective-permute-start.35 = (bf16[2,128,128]{2,1,0:T(8,128)(2,1)S(1)}, bf16[2,128,128]{2,1,0:T(8,128)(2,1)S(1)}, u32[]{:S(2)}, u32[]{:S(2)}) collective-permute-start(bf16[2,128,128]{2,1,0:T(8,128)(2,1)S(1)} %get-tuple-element.119), channel_id=1, source_target_pairs={{0,24},{2,26},{4,28},{6,30},{8,16},{10,18},{12,20},{14,22},{16,8},... | collective-permute-start | bytes 196616 | tf_op jit(solution)/shard_map/ppermute | solution.py:319
  132.1 2.4 %collective-permute-done.35.refs_6_ = bf16[2,128,128]{2,1,0:T(8,128)(2,1)S(1)} collective-permute-done((bf16[2,128,128]{2,1,0:T(8,128)(2,1)S(1)}, bf16[2,128,128]{2,1,0:T(8,128)(2,1)S(1)}, u32[]{:S(2)}, u32[]{:S(2)}) %collective-permute-start.35) | collective-permute-done | bytes 65568 | tf_op jit(solution)/shard_map/ppermute | solution.py:319
  134.4 2.1 %collective-permute-done.34.refs_4_ = bf16[2,128,128]{2,1,0:T(8,128)(2,1)S(1)} collective-permute-done((bf16[2,128,128]{2,1,0:T(8,128)(2,1)S(1)}, bf16[2,128,128]{2,1,0:T(8,128)(2,1)S(1)}, u32[]{:S(2)}, u32[]{:S(2)}) %collective-permute-start.34) | collective-permute-done | bytes 65568 | tf_op jit(solution)/shard_map/ppermute | solution.py:319
  143.6 2.0 %shard_map.112 = (bf16[2,128,256]{2,1,0:T(8,128)(2,1)S(1)}, bf16[2,128,256]{2,1,0:T(8,128)(2,1)S(1)}, bf16[2,128,256]{2,1,0:T(8,128)(2,1)S(1)}, bf16[2,128,256]{2,1,0:T(8,128)(2,1)S(1)}) custom-call(s32[4]{0:T(128)S(1)} %pad_add_fusion.at, bf16[2,128,128]{2,1,0:T(8,128)(2,1)S(1)} %get-tuple-element.116.refs_0_, ...), custom_call_target="tpu_custom_call" | custom-call | flops 1073741824 | bytes 5767184 | tf_op jit(solution)/shard_map/pallas_call | solution.py:34
  148.6 4.0 %collective-permute-done.43.refs_2_ = bf16[2,128,256]{2,1,0:T(8,128)(2,1)S(1)} collective-permute-done((bf16[2,128,256]{2,1,0:T(8,128)(2,1)S(1)}, bf16[2,128,256]{2,1,0:T(8,128)(2,1)S(1)}, u32[]{:S(2)}, u32[]{:S(2)}) %collective-permute-start.43) | collective-permute-done | bytes 131104 | tf_op jit(solution)/shard_map/ppermute | solution.py:333
  152.6 2.0 %collective-permute-done.45.refs_3_ = bf16[2,128,256]{2,1,0:T(8,128)(2,1)S(1)} collective-permute-done((bf16[2,128,256]{2,1,0:T(8,128)(2,1)S(1)}, bf16[2,128,256]{2,1,0:T(8,128)(2,1)S(1)}, u32[]{:S(2)}, u32[]{:S(2)}) %collective-permute-start.45) | collective-permute-done | bytes 131104 | tf_op jit(solution)/shard_map/ppermute | solution.py:333
  (105 shorter events, 50.7 us)
Async XLA Ops:
  0.0 27.1 %collective-permute-start = (bf16[128,2048]{1,0:T(8,128)(2,1)}, bf16[128,2048]{1,0:T(8,128)(2,1)S(1)}, u32[]{:S(2)}, u32[]{:S(2)}) collective-permute-start(bf16[128,2048]{1,0:T(8,128)(2,1)} %refs_0_.3), channel_id=1, source_target_pairs={{0,8},{2,10},{4,12},{6,14},{8,0},{10,2},{12,4},{14,6},{16,24},{18,... | collective-permute-start | bytes 1572872 | tf_op jit(solution)/shard_map/ppermute | solution.py:319
  3.0 24.8 %collective-permute-start.1 = (bf16[128,2048]{1,0:T(8,128)(2,1)}, bf16[128,2048]{1,0:T(8,128)(2,1)S(1)}, u32[]{:S(2)}, u32[]{:S(2)}) collective-permute-start(bf16[128,2048]{1,0:T(8,128)(2,1)} %refs_0_.3), channel_id=1, source_target_pairs={{0,16},{2,18},{4,20},{6,22},{8,24},{10,26},{12,28},{14,30},{16,0},... | collective-permute-start | bytes 1572872 | tf_op jit(solution)/shard_map/ppermute | solution.py:319
  5.6 22.2 %collective-permute-start.2 = (bf16[128,2048]{1,0:T(8,128)(2,1)}, bf16[128,2048]{1,0:T(8,128)(2,1)S(1)}, u32[]{:S(2)}, u32[]{:S(2)}) collective-permute-start(bf16[128,2048]{1,0:T(8,128)(2,1)} %refs_0_.3), channel_id=1, source_target_pairs={{0,1},{1,0},{2,3},{3,2},{4,5},{5,4},{6,7},{7,6},{8,9},{9,8},{10,11... | collective-permute-start | bytes 1572872 | tf_op jit(solution)/shard_map/ppermute | solution.py:333
  12.6 10.6 %collective-permute-start.3 = (bf16[272,768]{1,0:T(8,128)(2,1)S(1)}, bf16[272,768]{1,0:T(8,128)(2,1)S(1)}, u32[]{:S(2)}, u32[]{:S(2)}) collective-permute-start(bf16[272,768]{1,0:T(8,128)(2,1)S(1)} %get-tuple-element.73.refs_4_), channel_id=1, source_target_pairs={{0,4},{2,6},{4,0},{6,2},{8,12},{10,14},{12,8},{14,10},{16,20},{18,... | collective-permute-start | bytes 1253384 | tf_op jit(solution)/shard_map/ppermute | solution.py:327
  14.2 22.0 %collective-permute-start.4 = (bf16[272,768]{1,0:T(8,128)(2,1)S(1)}, bf16[272,768]{1,0:T(8,128)(2,1)S(1)}, u32[]{:S(2)}, u32[]{:S(2)}) collective-permute-start(bf16[272,768]{1,0:T(8,128)(2,1)S(1)} %get-tuple-element.76), channel_id=1, source_target_pairs={{0,8},{2,10},{4,12},{6,14},{8,0},{10,2},{12,4},{14,6},{16,24},{18,... | collective-permute-start | bytes 1253384 | tf_op jit(solution)/shard_map/ppermute | solution.py:319
  23.2 17.0 %collective-permute-start.7 = (bf16[1024,256]{1,0:T(8,128)(2,1)S(1)}, bf16[1024,256]{1,0:T(8,128)(2,1)S(1)}, u32[]{:S(2)}, u32[]{:S(2)}) collective-permute-start(bf16[1024,256]{1,0:T(8,128)(2,1)S(1)} %copy-done), channel_id=1, source_target_pairs={{0,4},{2,6},{4,0},{6,2},{8,12},{10,14},{12,8},{14,10},{16,20},{18,... | collective-permute-start | bytes 1572872 | tf_op jit(solution)/shard_map/ppermute | solution.py:327
  27.9 27.7 %collective-permute-start.6 = (bf16[128,2048]{1,0:T(8,128)(2,1)S(1)}, bf16[128,2048]{1,0:T(8,128)(2,1)S(1)}, u32[]{:S(2)}, u32[]{:S(2)}) collective-permute-start(bf16[128,2048]{1,0:T(8,128)(2,1)S(1)} %collective-permute-done.1.refs_0_), channel_id=1, source_target_pairs={{0,8},{2,10},{4,12},{6,14},{8,0},{10,2},{12,4},{14,6},{16,24},{18,... | collective-permute-start | bytes 1572872 | tf_op jit(solution)/shard_map/ppermute | solution.py:319
  30.3 25.2 %collective-permute-start.8 = (bf16[128,2048]{1,0:T(8,128)(2,1)S(1)}, bf16[128,2048]{1,0:T(8,128)(2,1)S(1)}, u32[]{:S(2)}, u32[]{:S(2)}) collective-permute-start(bf16[128,2048]{1,0:T(8,128)(2,1)S(1)} %collective-permute-done.refs_0_), channel_id=1, source_target_pairs={{0,1},{1,0},{2,3},{3,2},{4,5},{5,4},{6,7},{7,6},{8,9},{9,8},{10,11... | collective-permute-start | bytes 1572872 | tf_op jit(solution)/shard_map/ppermute | solution.py:333
  31.9 23.7 %collective-permute-start.9 = (bf16[128,2048]{1,0:T(8,128)(2,1)S(1)}, bf16[128,2048]{1,0:T(8,128)(2,1)S(1)}, u32[]{:S(2)}, u32[]{:S(2)}) collective-permute-start(bf16[128,2048]{1,0:T(8,128)(2,1)S(1)} %collective-permute-done.1.refs_0_), channel_id=1, source_target_pairs={{0,1},{1,0},{2,3},{3,2},{4,5},{5,4},{6,7},{7,6},{8,9},{9,8},{10,11... | collective-permute-start | bytes 1572872 | tf_op jit(solution)/shard_map/ppermute | solution.py:333
  36.2 18.7 %collective-permute-start.5 = (bf16[272,768]{1,0:T(8,128)(2,1)S(1)}, bf16[272,768]{1,0:T(8,128)(2,1)S(1)}, u32[]{:S(2)}, u32[]{:S(2)}) collective-permute-start(bf16[272,768]{1,0:T(8,128)(2,1)S(1)} %get-tuple-element.78), channel_id=1, source_target_pairs={{0,16},{2,18},{4,20},{6,22},{8,24},{10,26},{12,28},{14,30},{16,0},... | collective-permute-start | bytes 1253384 | tf_op jit(solution)/shard_map/ppermute | solution.py:319
  55.5 14.7 %collective-permute-start.11 = (bf16[272,768]{1,0:T(8,128)(2,1)S(1)}, bf16[272,768]{1,0:T(8,128)(2,1)S(1)}, u32[]{:S(2)}, u32[]{:S(2)}) collective-permute-start(bf16[272,768]{1,0:T(8,128)(2,1)S(1)} %get-tuple-element.85), channel_id=1, source_target_pairs={{0,24},{2,26},{4,28},{6,30},{8,16},{10,18},{12,20},{14,22},{16,8},... | collective-permute-start | bytes 1253384 | tf_op jit(solution)/shard_map/ppermute | solution.py:319
  59.6 11.9 %collective-permute-start.10 = (bf16[128,2048]{1,0:T(8,128)(2,1)S(1)}, bf16[128,2048]{1,0:T(8,128)(2,1)S(1)}, u32[]{:S(2)}, u32[]{:S(2)}) collective-permute-start(bf16[128,2048]{1,0:T(8,128)(2,1)S(1)} %collective-permute-done.6.refs_0_), channel_id=1, source_target_pairs={{0,1},{1,0},{2,3},{3,2},{4,5},{5,4},{6,7},{7,6},{8,9},{9,8},{10,11... | collective-permute-start | bytes 1572872 | tf_op jit(solution)/shard_map/ppermute | solution.py:333
  61.1 18.4 %collective-permute-start.18 = (bf16[1024,256]{1,0:T(8,128)(2,1)S(1)}, bf16[1024,256]{1,0:T(8,128)(2,1)S(1)}, u32[]{:S(2)}, u32[]{:S(2)}) collective-permute-start(bf16[1024,256]{1,0:T(8,128)(2,1)S(1)} %copy-done), channel_id=1, source_target_pairs={{0,8},{2,10},{4,12},{6,14},{8,0},{10,2},{12,4},{14,6},{16,24},{18,... | collective-permute-start | bytes 1572872 | tf_op jit(solution)/shard_map/ppermute | solution.py:319
  62.1 17.4 %collective-permute-start.17 = (bf16[272,768]{1,0:T(8,128)(2,1)S(1)}, bf16[272,768]{1,0:T(8,128)(2,1)S(1)}, u32[]{:S(2)}, u32[]{:S(2)}) collective-permute-start(bf16[272,768]{1,0:T(8,128)(2,1)S(1)} %collective-permute-done.4.refs_8_), channel_id=1, source_target_pairs={{0,4},{2,6},{4,0},{6,2},{8,12},{10,14},{12,8},{14,10},{16,20},{18,... | collective-permute-start | bytes 1253384 | tf_op jit(solution)/shard_map/ppermute | solution.py:327
  64.6 15.9 %collective-permute-start.21 = (bf16[272,768]{1,0:T(8,128)(2,1)S(1)}, bf16[272,768]{1,0:T(8,128)(2,1)S(1)}, u32[]{:S(2)}, u32[]{:S(2)}) collective-permute-start(bf16[272,768]{1,0:T(8,128)(2,1)S(1)} %collective-permute-done.5.refs_12_), channel_id=1, source_target_pairs={{0,4},{2,6},{4,0},{6,2},{8,12},{10,14},{12,8},{14,10},{16,20},{18,... | collective-permute-start | bytes 1253384 | tf_op jit(solution)/shard_map/ppermute | solution.py:327
  81.0 12.5 %collective-permute-start.13 = (bf16[272,768]{1,0:T(8,128)(2,1)S(1)}, bf16[272,768]{1,0:T(8,128)(2,1)S(1)}, u32[]{:S(2)}, u32[]{:S(2)}) collective-permute-start(bf16[272,768]{1,0:T(8,128)(2,1)S(1)} %collective-permute-done.11.refs_4_), channel_id=1, source_target_pairs={{0,4},{2,6},{4,0},{6,2},{8,12},{10,14},{12,8},{14,10},{16,20},{18,... | collective-permute-start | bytes 1253384 | tf_op jit(solution)/shard_map/ppermute | solution.py:327
  82.5 27.2 %collective-permute-start.12 = (bf16[272,768]{1,0:T(8,128)(2,1)S(1)}, bf16[272,768]{1,0:T(8,128)(2,1)S(1)}, u32[]{:S(2)}, u32[]{:S(2)}) collective-permute-start(bf16[272,768]{1,0:T(8,128)(2,1)S(1)} %collective-permute-done.11.refs_4_), channel_id=1, source_target_pairs={{0,2},{2,0},{4,6},{6,4},{8,10},{10,8},{12,14},{14,12},{16,18},{18,... | collective-permute-start | bytes 1253384 | tf_op jit(solution)/shard_map/ppermute | solution.py:330
  82.5 26.5 %collective-permute-start.24 = (bf16[1024,256]{1,0:T(8,128)(2,1)S(1)}, bf16[1024,256]{1,0:T(8,128)(2,1)S(1)}, u32[]{:S(2)}, u32[]{:S(2)}) collective-permute-start(bf16[1024,256]{1,0:T(8,128)(2,1)S(1)} %copy-done), channel_id=1, source_target_pairs={{0,16},{2,18},{4,20},{6,22},{8,24},{10,26},{12,28},{14,30},{16,0},... | collective-permute-start | bytes 1572872 | tf_op jit(solution)/shard_map/ppermute | solution.py:319
  83.4 25.5 %collective-permute-start.25 = (bf16[1024,256]{1,0:T(8,128)(2,1)S(1)}, bf16[1024,256]{1,0:T(8,128)(2,1)S(1)}, u32[]{:S(2)}, u32[]{:S(2)}) collective-permute-start(bf16[1024,256]{1,0:T(8,128)(2,1)S(1)} %collective-permute-done.18.refs_8_.refs_10_), channel_id=1, source_target_pairs={{0,4},{2,6},{4,0},{6,2},{8,12},{10,14},{12,8},{14,10},{16,20},{18,... | collective-permute-start | bytes 1572872 | tf_op jit(solution)/shard_map/ppermute | solution.py:327
  93.5 16.2 %collective-permute-start.23 = (bf16[272,768]{1,0:T(8,128)(2,1)S(1)}, bf16[272,768]{1,0:T(8,128)(2,1)S(1)}, u32[]{:S(2)}, u32[]{:S(2)}) collective-permute-start(bf16[272,768]{1,0:T(8,128)(2,1)S(1)} %collective-permute-done.13.refs_6_), channel_id=1, source_target_pairs={{0,2},{2,0},{4,6},{6,4},{8,10},{10,8},{12,14},{14,12},{16,18},{18,... | collective-permute-start | bytes 1253384 | tf_op jit(solution)/shard_map/ppermute | solution.py:330
  108.9 13.5 %collective-permute-start.29 = (bf16[1024,256]{1,0:T(8,128)(2,1)S(1)}, bf16[1024,256]{1,0:T(8,128)(2,1)S(1)}, u32[]{:S(2)}, u32[]{:S(2)}) collective-permute-start(bf16[1024,256]{1,0:T(8,128)(2,1)S(1)} %collective-permute-done.24.refs_10_.refs_12_), channel_id=1, source_target_pairs={{0,8},{2,10},{4,12},{6,14},{8,0},{10,2},{12,4},{14,6},{16,24},{18,... | collective-permute-start | bytes 1572872 | tf_op jit(solution)/shard_map/ppermute | solution.py:319
  109.0 13.5 %collective-permute-start.30 = (bf16[1024,256]{1,0:T(8,128)(2,1)S(1)}, bf16[1024,256]{1,0:T(8,128)(2,1)S(1)}, u32[]{:S(2)}, u32[]{:S(2)}) collective-permute-start(bf16[1024,256]{1,0:T(8,128)(2,1)S(1)} %collective-permute-done.24.refs_10_.refs_12_), channel_id=1, source_target_pairs={{2,6},{6,2},{10,14},{14,10},{18,22},{22,18},{26,30},{30,26},{3,7},... | collective-permute-start | bytes 1572872 | tf_op jit(solution)/shard_map/ppermute | solution.py:327
  116.9 20.1 %collective-permute-start.32 = (bf16[1024,256]{1,0:T(8,128)(2,1)S(1)}, bf16[1024,256]{1,0:T(8,128)(2,1)S(1)}, u32[]{:S(2)}, u32[]{:S(2)}) collective-permute-start(bf16[1024,256]{1,0:T(8,128)(2,1)S(1)} %collective-permute-done.24.refs_10_.refs_12_), channel_id=1, source_target_pairs={{0,4},{4,0},{8,12},{12,8},{16,20},{20,16},{24,28},{28,24},{1,5},{5... | collective-permute-start | bytes 1572872 | tf_op jit(solution)/shard_map/ppermute | solution.py:327
  124.3 16.9 %collective-permute-start.42 = (bf16[1024,256]{1,0:T(8,128)(2,1)S(1)}, bf16[1024,256]{1,0:T(8,128)(2,1)S(1)}, u32[]{:S(2)}, u32[]{:S(2)}) collective-permute-start(bf16[1024,256]{1,0:T(8,128)(2,1)S(1)} %collective-permute-done.29.refs_10_.refs_15_), channel_id=1, source_target_pairs={{0,4},{2,6},{4,0},{6,2},{8,12},{10,14},{12,8},{14,10},{16,20},{18,... | collective-permute-start | bytes 1572872 | tf_op jit(solution)/shard_map/ppermute | solution.py:327
  (33 other events, 238.0 us)

commit v9 on v8

--- a/solution.py
+++ b/solution.py
@@ -111,7 +111,7 @@
 
         part = [row.at[:, lanes(at[0] ^ j, size)] for row in rows]
         few = weights[n * xn * cn : (n + 1) * xn * cn]
-        project(xn, cn, at, part, few, chunk.at[n], meta.at[n], each)
+        project(xn, cn, at, part, few, chunk.at[n], meta.at[j], each)
 
 
 def finish_kernel(zn, xn, cn, at, *refs):
@@ -418,6 +418,8 @@
     for j in early[1:]:
         started["w", j] = over_z(after(sent[j], tok[1]), j)
     end_y(0, first)
+    if last:
+        pieces[0] = done_all(pieces[0])[0]
     parts, far, columns[0][1:], *near = done_all(
         [started["w", j] for j in early],
         [started[j] for j in more],
@@ -457,8 +459,8 @@
     before = []
     if last:
         before = call(
-            functools.partial(project_kernel, zn, xn, cn, range(last)),
-            (at, *rows, *sum((pieces[j] for j in range(last)), [])),
+            functools.partial(project_kernel, zn, xn, cn, range(last)[::-1]),
+            (at, *rows, *sum((pieces[j] for j in range(last)[::-1]), [])),
             [
                 shape((zn, seg_rows, cn * 3 * DH), F32),
                 shape((last, xn, cn, META, DH), F32),
@@ -469,11 +471,10 @@
         )
         mark(before[0])
     if last:
-        end_x(last, done_all(started["x", last])[0])
-        parts, columns[1][1:], held = done_all(
-            [started["oz", b] for b in bits[1:]], started["o", 1], before[:1]
+        parts, others, columns[1][1:] = done_all(
+            [started["oz", b] for b in bits[1:]], started["x", last], started["o", 1]
         )
-        before = [*held, *before[1:]]
+        end_x(last, others)
         out_z.update(zip(bits[1:], parts))
         for b in bits[1:]:
             columns[b] = [out_z[b]]

time: 156 us -> 156 us (level)
    ppermute x12, waiting for transfers between devices: 55.4 us -> 42.1 us  [over_z(): return lax.ppermute(a, 'seq', pairs)]
    ppermute x10, waiting for transfers between devices: 17.2 us -> 29.3 us  [over_x(): return lax.ppermute(a, 'seq', pairs)]
  transfers between devices with their start and end apart: 48 -> 48, of which waited for: 25 -> 26; matrix products, arithmetic and copies ran while one was open for 0% -> 0% of each run, Pallas kernels for 13% -> 13%
where the time goes in v9:
time: 156 us
  waiting for transfers between devices  82.7 us (53%)
  starting transfers between devices  46.5 us (30%)
  Pallas kernels  21.8 us (14%)
  local copies, waits for them, and re-layouts  3.79 us (2%)
    ppermute x12, waiting for transfers between devices, over_z(): return lax.ppermute(a, 'seq', pairs)  42.1 us
    ppermute x10, waiting for transfers between devices, over_x(): return lax.ppermute(a, 'seq', pairs)  29.3 us
    pallas_call x14, Pallas kernels, call(): pl.pallas_call(kernel, grid_spec=pltpu.PrefetchScalarGridSpec(num_scalar_...  21.8 us
    ppermute x12, starting transfers between devices, over_z(): return lax.ppermute(a, 'seq', pairs)  19.6 us
    ppermute x10, starting transfers between devices, over_x(): return lax.ppermute(a, 'seq', pairs)  13 us
    ppermute x8, starting transfers between devices, over_y(): lax.ppermute(a, 'head', [(h, (h + k) % n_head) for h in range(n_head)])  9.81 us
    ppermute x8, waiting for transfers between devices, over_y(): lax.ppermute(a, 'head', [(h, (h + k) % n_head) for h in range(n_head)])  7.66 us
    ppermute x18, starting transfers between devices, over_c(): return lax.ppermute(a, 'seq', [(s, s ^ m) for s in range(n_seq)])  4.01 us
  transfers between devices with their start and end apart: 48, of which 26 were waited for; matrix products, arithmetic and copies ran while one was open for 0% of the time, Pallas kernels for 13%

profile of v9, /device:TPU:0, one launch (start us, length us, event | category | flops | bytes accessed | tf_op | source)
XLA Modules:
  0.0 155.7 jit_solution(850662748416049830)
XLA Ops:
  0.0 3.0 %collective-permute-start = (bf16[128,2048]{1,0:T(8,128)(2,1)}, bf16[128,2048]{1,0:T(8,128)(2,1)S(1)}, u32[]{:S(2)}, u32[]{:S(2)}) collective-permute-start(bf16[128,2048]{1,0:T(8,128)(2,1)} %refs_0_.3), channel_id=1, source_target_pairs={{0,8},{2,10},{4,12},{6,14},{8,0},{10,2},{12,4},{14,6},{16,24},{18,... | collective-permute-start | bytes 1572872 | tf_op jit(solution)/shard_map/ppermute | solution.py:319
  3.0 2.6 %collective-permute-start.1 = (bf16[128,2048]{1,0:T(8,128)(2,1)}, bf16[128,2048]{1,0:T(8,128)(2,1)S(1)}, u32[]{:S(2)}, u32[]{:S(2)}) collective-permute-start(bf16[128,2048]{1,0:T(8,128)(2,1)} %refs_0_.3), channel_id=1, source_target_pairs={{0,16},{2,18},{4,20},{6,22},{8,24},{10,26},{12,28},{14,30},{16,0},... | collective-permute-start | bytes 1572872 | tf_op jit(solution)/shard_map/ppermute | solution.py:319
  14.2 9.0 %collective-permute-done.3.refs_14_ = bf16[272,768]{1,0:T(8,128)(2,1)S(1)} collective-permute-done((bf16[272,768]{1,0:T(8,128)(2,1)S(1)}, bf16[272,768]{1,0:T(8,128)(2,1)S(1)}, u32[]{:S(2)}, u32[]{:S(2)}) %collective-permute-start.3) | collective-permute-done | bytes 417824 | tf_op jit(solution)/shard_map/ppermute | solution.py:327
  23.7 3.4 %collective-permute-done.refs_0_ = bf16[128,2048]{1,0:T(8,128)(2,1)S(1)} collective-permute-done((bf16[128,2048]{1,0:T(8,128)(2,1)}, bf16[128,2048]{1,0:T(8,128)(2,1)S(1)}, u32[]{:S(2)}, u32[]{:S(2)}) %collective-permute-start) | collective-permute-done | bytes 524320 | tf_op jit(solution)/shard_map/ppermute | solution.py:319
  29.4 2.5 %collective-permute-start.6 = (bf16[128,2048]{1,0:T(8,128)(2,1)S(1)}, bf16[128,2048]{1,0:T(8,128)(2,1)S(1)}, u32[]{:S(2)}, u32[]{:S(2)}) collective-permute-start(bf16[128,2048]{1,0:T(8,128)(2,1)S(1)} %collective-permute-done.1.refs_0_), channel_id=1, source_target_pairs={{0,8},{2,10},{4,12},{6,14},{8,0},{10,2},{12,4},{14,6},{16,24},{18,... | collective-permute-start | bytes 1572872 | tf_op jit(solution)/shard_map/ppermute | solution.py:319
  33.4 2.7 %collective-permute-done.4.refs_8_ = bf16[272,768]{1,0:T(8,128)(2,1)S(1)} collective-permute-done((bf16[272,768]{1,0:T(8,128)(2,1)S(1)}, bf16[272,768]{1,0:T(8,128)(2,1)S(1)}, u32[]{:S(2)}, u32[]{:S(2)}) %collective-permute-start.4) | collective-permute-done | bytes 417824 | tf_op jit(solution)/shard_map/ppermute | solution.py:319
  36.2 2.0 %collective-permute-start.9 = (bf16[128,2048]{1,0:T(8,128)(2,1)S(1)}, bf16[128,2048]{1,0:T(8,128)(2,1)S(1)}, u32[]{:S(2)}, u32[]{:S(2)}) collective-permute-start(bf16[128,2048]{1,0:T(8,128)(2,1)S(1)} %collective-permute-done.1.refs_0_), channel_id=1, source_target_pairs={{0,1},{1,0},{2,3},{3,2},{4,5},{5,4},{6,7},{7,6},{8,9},{9,8},{10,11... | collective-permute-start | bytes 1572872 | tf_op jit(solution)/shard_map/ppermute | solution.py:333
  38.2 2.6 %collective-permute-start.5 = (bf16[272,768]{1,0:T(8,128)(2,1)S(1)}, bf16[272,768]{1,0:T(8,128)(2,1)S(1)}, u32[]{:S(2)}, u32[]{:S(2)}) collective-permute-start(bf16[272,768]{1,0:T(8,128)(2,1)S(1)} %get-tuple-element.81), channel_id=1, source_target_pairs={{0,16},{2,18},{4,20},{6,22},{8,24},{10,26},{12,28},{14,30},{16,0},... | collective-permute-start | bytes 1253384 | tf_op jit(solution)/shard_map/ppermute | solution.py:319
  42.2 12.7 %collective-permute-done.5.refs_4_ = bf16[272,768]{1,0:T(8,128)(2,1)S(1)} collective-permute-done((bf16[272,768]{1,0:T(8,128)(2,1)S(1)}, bf16[272,768]{1,0:T(8,128)(2,1)S(1)}, u32[]{:S(2)}, u32[]{:S(2)}) %collective-permute-start.5) | collective-permute-done | bytes 417824 | tf_op jit(solution)/shard_map/ppermute | solution.py:319
  58.4 3.0 %collective-permute-start.13 = (bf16[272,768]{1,0:T(8,128)(2,1)S(1)}, bf16[272,768]{1,0:T(8,128)(2,1)S(1)}, u32[]{:S(2)}, u32[]{:S(2)}) collective-permute-start(bf16[272,768]{1,0:T(8,128)(2,1)S(1)} %get-tuple-element.90), channel_id=1, source_target_pairs={{0,24},{2,26},{4,28},{6,30},{8,16},{10,18},{12,20},{14,22},{16,8},... | collective-permute-start | bytes 1253384 | tf_op jit(solution)/shard_map/ppermute | solution.py:319
  65.4 7.3 %collective-permute-done.13.refs_4_ = bf16[272,768]{1,0:T(8,128)(2,1)S(1)} collective-permute-done((bf16[272,768]{1,0:T(8,128)(2,1)S(1)}, bf16[272,768]{1,0:T(8,128)(2,1)S(1)}, u32[]{:S(2)}, u32[]{:S(2)}) %collective-permute-start.13) | collective-permute-done | bytes 417824 | tf_op jit(solution)/shard_map/ppermute | solution.py:319
  74.2 7.3 %collective-permute-done.17.refs_8_.refs_10_ = bf16[1024,256]{1,0:T(8,128)(2,1)S(1)} collective-permute-done((bf16[1024,256]{1,0:T(8,128)(2,1)S(1)}, bf16[1024,256]{1,0:T(8,128)(2,1)S(1)}, u32[]{:S(2)}, u32[]{:S(2)}) %collective-permute-start.17) | collective-permute-done | bytes 524320 | tf_op jit(solution)/shard_map/ppermute | solution.py:319
  85.0 3.4 %shard_map.105 = (f32[4,128,768]{2,1,0:T(8,128)S(1)}, f32[3,2,2,16,128]{4,3,2,1,0:T(8,128)S(1)}) custom-call(s32[4]{0:T(128)S(1)} %pad_add_fusion.at, bf16[128,4096]{1,0:T(8,128)(2,1)S(1)} %shard_map.101.refs_0_, bf16[128,4096]{1,0:T(8,128)(2,1)S(1)} %shard_map.102.refs_1_, bf16[128,4096]{1,0:T(8,128)(2,1)S(1)} %shard_map.103.refs_2_, ...), custom_call_target="tpu_custom_call" | custom-call | flops 2415919104 | bytes 10878992 | tf_op jit(solution)/shard_map/pallas_call | solution.py:34
  88.4 17.0 %collective-permute-done.16.refs_6_ = bf16[272,768]{1,0:T(8,128)(2,1)S(1)} collective-permute-done((bf16[272,768]{1,0:T(8,128)(2,1)S(1)}, bf16[272,768]{1,0:T(8,128)(2,1)S(1)}, u32[]{:S(2)}, u32[]{:S(2)}) %collective-permute-start.16) | collective-permute-done | bytes 417824 | tf_op jit(solution)/shard_map/ppermute | solution.py:327
  105.5 2.4 %collective-permute-done.15.refs_10_.refs_12_ = bf16[1024,256]{1,0:T(8,128)(2,1)S(1)} collective-permute-done((bf16[1024,256]{1,0:T(8,128)(2,1)S(1)}, bf16[1024,256]{1,0:T(8,128)(2,1)S(1)}, u32[]{:S(2)}, u32[]{:S(2)}) %collective-permute-start.15) | collective-permute-done | bytes 524320 | tf_op jit(solution)/shard_map/ppermute | solution.py:319
  116.8 2.9 %collective-permute-start.32 = (bf16[1024,256]{1,0:T(8,128)(2,1)S(1)}, bf16[1024,256]{1,0:T(8,128)(2,1)S(1)}, u32[]{:S(2)}, u32[]{:S(2)}) collective-permute-start(bf16[1024,256]{1,0:T(8,128)(2,1)S(1)} %collective-permute-done.15.refs_10_.refs_12_), channel_id=1, source_target_pairs={{0,4},{4,0},{8,12},{12,8},{16,20},{20,16},{24,28},{28,24},{1,5},{5... | collective-permute-start | bytes 1572872 | tf_op jit(solution)/shard_map/ppermute | solution.py:327
  119.7 2.0 %shard_map.108.token = f32[4,2,128,128]{3,2,1,0:T(8,128)S(1)} custom-call(s32[4]{0:T(128)S(1)} %pad_add_fusion.at, f32[8]{0:T(128)S(1)} %copy-done.7, f32[4,2,2,16,128]{4,3,2,1,0:T(8,128)S(1)} %get-tuple-element.116.table, bf16[4,2,128,384]{3,2,1,0:T(8,128)(2,1)S(1)} %get-tuple-element.117.sums), custom_call_target="tpu_custom_call" | custom-call | bytes 1441840 | tf_op jit(solution)/shard_map/pallas_call | solution.py:34
  125.3 2.2 %shard_map.109 = (bf16[2,128,128]{2,1,0:T(8,128)(2,1)S(1)}, bf16[2,128,128]{2,1,0:T(8,128)(2,1)S(1)}, bf16[2,128,128]{2,1,0:T(8,128)(2,1)S(1)}, bf16[2,128,128]{2,1,0:T(8,128)(2,1)S(1)}) custom-call(s32[4]{0:T(128)S(1)} %pad_add_fusion.at, f32[8]{0:T(128)S(1)} %copy-done.7, f32[4,2,2,16,128]{4,3,2,1,0:T(8,128)S(1)} %get-tuple-element.116.table, ...), custom_call_target="tpu_custom_call" | custom-call | bytes 3538992 | tf_op jit(solution)/shard_map/pallas_call | solution.py:34
  127.5 2.0 %collective-permute-start.35 = (bf16[2,128,128]{2,1,0:T(8,128)(2,1)S(1)}, bf16[2,128,128]{2,1,0:T(8,128)(2,1)S(1)}, u32[]{:S(2)}, u32[]{:S(2)}) collective-permute-start(bf16[2,128,128]{2,1,0:T(8,128)(2,1)S(1)} %get-tuple-element.126), channel_id=1, source_target_pairs={{0,24},{2,26},{4,28},{6,30},{8,16},{10,18},{12,20},{14,22},{16,8},... | collective-permute-start | bytes 196616 | tf_op jit(solution)/shard_map/ppermute | solution.py:319
  131.9 2.2 %collective-permute-done.35.refs_6_ = bf16[2,128,128]{2,1,0:T(8,128)(2,1)S(1)} collective-permute-done((bf16[2,128,128]{2,1,0:T(8,128)(2,1)S(1)}, bf16[2,128,128]{2,1,0:T(8,128)(2,1)S(1)}, u32[]{:S(2)}, u32[]{:S(2)}) %collective-permute-start.35) | collective-permute-done | bytes 65568 | tf_op jit(solution)/shard_map/ppermute | solution.py:319
  134.1 2.0 %collective-permute-done.34.refs_4_ = bf16[2,128,128]{2,1,0:T(8,128)(2,1)S(1)} collective-permute-done((bf16[2,128,128]{2,1,0:T(8,128)(2,1)S(1)}, bf16[2,128,128]{2,1,0:T(8,128)(2,1)S(1)}, u32[]{:S(2)}, u32[]{:S(2)}) %collective-permute-start.34) | collective-permute-done | bytes 65568 | tf_op jit(solution)/shard_map/ppermute | solution.py:319
  143.2 2.0 %shard_map.112 = (bf16[2,128,256]{2,1,0:T(8,128)(2,1)S(1)}, bf16[2,128,256]{2,1,0:T(8,128)(2,1)S(1)}, bf16[2,128,256]{2,1,0:T(8,128)(2,1)S(1)}, bf16[2,128,256]{2,1,0:T(8,128)(2,1)S(1)}) custom-call(s32[4]{0:T(128)S(1)} %pad_add_fusion.at, bf16[2,128,128]{2,1,0:T(8,128)(2,1)S(1)} %get-tuple-element.123.refs_0_, ...), custom_call_target="tpu_custom_call" | custom-call | flops 1073741824 | bytes 5767184 | tf_op jit(solution)/shard_map/pallas_call | solution.py:34
  148.4 3.8 %collective-permute-done.43.refs_2_ = bf16[2,128,256]{2,1,0:T(8,128)(2,1)S(1)} collective-permute-done((bf16[2,128,256]{2,1,0:T(8,128)(2,1)S(1)}, bf16[2,128,256]{2,1,0:T(8,128)(2,1)S(1)}, u32[]{:S(2)}, u32[]{:S(2)}) %collective-permute-start.43) | collective-permute-done | bytes 131104 | tf_op jit(solution)/shard_map/ppermute | solution.py:333
  152.2 2.0 %collective-permute-done.45.refs_3_ = bf16[2,128,256]{2,1,0:T(8,128)(2,1)S(1)} collective-permute-done((bf16[2,128,256]{2,1,0:T(8,128)(2,1)S(1)}, bf16[2,128,256]{2,1,0:T(8,128)(2,1)S(1)}, u32[]{:S(2)}, u32[]{:S(2)}) %collective-permute-start.45) | collective-permute-done | bytes 131104 | tf_op jit(solution)/shard_map/ppermute | solution.py:333
  (105 shorter events, 52.7 us)
Async XLA Ops:
  0.0 27.1 %collective-permute-start = (bf16[128,2048]{1,0:T(8,128)(2,1)}, bf16[128,2048]{1,0:T(8,128)(2,1)S(1)}, u32[]{:S(2)}, u32[]{:S(2)}) collective-permute-start(bf16[128,2048]{1,0:T(8,128)(2,1)} %refs_0_.3), channel_id=1, source_target_pairs={{0,8},{2,10},{4,12},{6,14},{8,0},{10,2},{12,4},{14,6},{16,24},{18,... | collective-permute-start | bytes 1572872 | tf_op jit(solution)/shard_map/ppermute | solution.py:319
  3.0 24.8 %collective-permute-start.1 = (bf16[128,2048]{1,0:T(8,128)(2,1)}, bf16[128,2048]{1,0:T(8,128)(2,1)S(1)}, u32[]{:S(2)}, u32[]{:S(2)}) collective-permute-start(bf16[128,2048]{1,0:T(8,128)(2,1)} %refs_0_.3), channel_id=1, source_target_pairs={{0,16},{2,18},{4,20},{6,22},{8,24},{10,26},{12,28},{14,30},{16,0},... | collective-permute-start | bytes 1572872 | tf_op jit(solution)/shard_map/ppermute | solution.py:319
  5.6 22.2 %collective-permute-start.2 = (bf16[128,2048]{1,0:T(8,128)(2,1)}, bf16[128,2048]{1,0:T(8,128)(2,1)S(1)}, u32[]{:S(2)}, u32[]{:S(2)}) collective-permute-start(bf16[128,2048]{1,0:T(8,128)(2,1)} %refs_0_.3), channel_id=1, source_target_pairs={{0,1},{1,0},{2,3},{3,2},{4,5},{5,4},{6,7},{7,6},{8,9},{9,8},{10,11... | collective-permute-start | bytes 1572872 | tf_op jit(solution)/shard_map/ppermute | solution.py:333
  14.2 17.7 %collective-permute-start.10 = (bf16[272,768]{1,0:T(8,128)(2,1)S(1)}, bf16[272,768]{1,0:T(8,128)(2,1)S(1)}, u32[]{:S(2)}, u32[]{:S(2)}) collective-permute-start(bf16[272,768]{1,0:T(8,128)(2,1)S(1)} %get-tuple-element.100.refs_12_), channel_id=1, source_target_pairs={{0,2},{2,0},{4,6},{6,4},{8,10},{10,8},{12,14},{14,12},{16,18},{18,... | collective-permute-start | bytes 1253384 | tf_op jit(solution)/shard_map/ppermute | solution.py:330
  23.2 13.0 %collective-permute-start.4 = (bf16[272,768]{1,0:T(8,128)(2,1)S(1)}, bf16[272,768]{1,0:T(8,128)(2,1)S(1)}, u32[]{:S(2)}, u32[]{:S(2)}) collective-permute-start(bf16[272,768]{1,0:T(8,128)(2,1)S(1)} %get-tuple-element.79), channel_id=1, source_target_pairs={{0,8},{2,10},{4,12},{6,14},{8,0},{10,2},{12,4},{14,6},{16,24},{18,... | collective-permute-start | bytes 1253384 | tf_op jit(solution)/shard_map/ppermute | solution.py:319
  27.9 14.3 %collective-permute-start.7 = (bf16[1024,256]{1,0:T(8,128)(2,1)S(1)}, bf16[1024,256]{1,0:T(8,128)(2,1)S(1)}, u32[]{:S(2)}, u32[]{:S(2)}) collective-permute-start(bf16[1024,256]{1,0:T(8,128)(2,1)S(1)} %copy-done), channel_id=1, source_target_pairs={{0,4},{2,6},{4,0},{6,2},{8,12},{10,14},{12,8},{14,10},{16,20},{18,... | collective-permute-start | bytes 1572872 | tf_op jit(solution)/shard_map/ppermute | solution.py:327
  29.4 26.1 %collective-permute-start.6 = (bf16[128,2048]{1,0:T(8,128)(2,1)S(1)}, bf16[128,2048]{1,0:T(8,128)(2,1)S(1)}, u32[]{:S(2)}, u32[]{:S(2)}) collective-permute-start(bf16[128,2048]{1,0:T(8,128)(2,1)S(1)} %collective-permute-done.1.refs_0_), channel_id=1, source_target_pairs={{0,8},{2,10},{4,12},{6,14},{8,0},{10,2},{12,4},{14,6},{16,24},{18,... | collective-permute-start | bytes 1572872 | tf_op jit(solution)/shard_map/ppermute | solution.py:319
  31.9 23.6 %collective-permute-start.8 = (bf16[128,2048]{1,0:T(8,128)(2,1)S(1)}, bf16[128,2048]{1,0:T(8,128)(2,1)S(1)}, u32[]{:S(2)}, u32[]{:S(2)}) collective-permute-start(bf16[128,2048]{1,0:T(8,128)(2,1)S(1)} %collective-permute-done.refs_0_), channel_id=1, source_target_pairs={{0,1},{1,0},{2,3},{3,2},{4,5},{5,4},{6,7},{7,6},{8,9},{9,8},{10,11... | collective-permute-start | bytes 1572872 | tf_op jit(solution)/shard_map/ppermute | solution.py:333
  36.2 20.7 %collective-permute-start.9 = (bf16[128,2048]{1,0:T(8,128)(2,1)S(1)}, bf16[128,2048]{1,0:T(8,128)(2,1)S(1)}, u32[]{:S(2)}, u32[]{:S(2)}) collective-permute-start(bf16[128,2048]{1,0:T(8,128)(2,1)S(1)} %collective-permute-done.1.refs_0_), channel_id=1, source_target_pairs={{0,1},{1,0},{2,3},{3,2},{4,5},{5,4},{6,7},{7,6},{8,9},{9,8},{10,11... | collective-permute-start | bytes 1572872 | tf_op jit(solution)/shard_map/ppermute | solution.py:333
  38.2 16.7 %collective-permute-start.5 = (bf16[272,768]{1,0:T(8,128)(2,1)S(1)}, bf16[272,768]{1,0:T(8,128)(2,1)S(1)}, u32[]{:S(2)}, u32[]{:S(2)}) collective-permute-start(bf16[272,768]{1,0:T(8,128)(2,1)S(1)} %get-tuple-element.81), channel_id=1, source_target_pairs={{0,16},{2,18},{4,20},{6,22},{8,24},{10,26},{12,28},{14,30},{16,0},... | collective-permute-start | bytes 1253384 | tf_op jit(solution)/shard_map/ppermute | solution.py:319
  56.9 15.9 %collective-permute-start.12 = (bf16[128,2048]{1,0:T(8,128)(2,1)S(1)}, bf16[128,2048]{1,0:T(8,128)(2,1)S(1)}, u32[]{:S(2)}, u32[]{:S(2)}) collective-permute-start(bf16[128,2048]{1,0:T(8,128)(2,1)S(1)} %collective-permute-done.6.refs_0_), channel_id=1, source_target_pairs={{0,1},{1,0},{2,3},{3,2},{4,5},{5,4},{6,7},{7,6},{8,9},{9,8},{10,11... | collective-permute-start | bytes 1572872 | tf_op jit(solution)/shard_map/ppermute | solution.py:333
  58.4 14.4 %collective-permute-start.13 = (bf16[272,768]{1,0:T(8,128)(2,1)S(1)}, bf16[272,768]{1,0:T(8,128)(2,1)S(1)}, u32[]{:S(2)}, u32[]{:S(2)}) collective-permute-start(bf16[272,768]{1,0:T(8,128)(2,1)S(1)} %get-tuple-element.90), channel_id=1, source_target_pairs={{0,24},{2,26},{4,28},{6,30},{8,16},{10,18},{12,20},{14,22},{16,8},... | collective-permute-start | bytes 1253384 | tf_op jit(solution)/shard_map/ppermute | solution.py:319
  61.4 20.1 %collective-permute-start.17 = (bf16[1024,256]{1,0:T(8,128)(2,1)S(1)}, bf16[1024,256]{1,0:T(8,128)(2,1)S(1)}, u32[]{:S(2)}, u32[]{:S(2)}) collective-permute-start(bf16[1024,256]{1,0:T(8,128)(2,1)S(1)} %copy-done), channel_id=1, source_target_pairs={{0,8},{2,10},{4,12},{6,14},{8,0},{10,2},{12,4},{14,6},{16,24},{18,... | collective-permute-start | bytes 1572872 | tf_op jit(solution)/shard_map/ppermute | solution.py:319
  62.3 19.2 %collective-permute-start.21 = (bf16[272,768]{1,0:T(8,128)(2,1)S(1)}, bf16[272,768]{1,0:T(8,128)(2,1)S(1)}, u32[]{:S(2)}, u32[]{:S(2)}) collective-permute-start(bf16[272,768]{1,0:T(8,128)(2,1)S(1)} %collective-permute-done.4.refs_8_), channel_id=1, source_target_pairs={{0,4},{2,6},{4,0},{6,2},{8,12},{10,14},{12,8},{14,10},{16,20},{18,... | collective-permute-start | bytes 1253384 | tf_op jit(solution)/shard_map/ppermute | solution.py:327
  64.8 16.7 %collective-permute-start.20 = (bf16[272,768]{1,0:T(8,128)(2,1)S(1)}, bf16[272,768]{1,0:T(8,128)(2,1)S(1)}, u32[]{:S(2)}, u32[]{:S(2)}) collective-permute-start(bf16[272,768]{1,0:T(8,128)(2,1)S(1)} %collective-permute-done.5.refs_4_), channel_id=1, source_target_pairs={{0,4},{2,6},{4,0},{6,2},{8,12},{10,14},{12,8},{14,10},{16,20},{18,... | collective-permute-start | bytes 1253384 | tf_op jit(solution)/shard_map/ppermute | solution.py:327
  72.8 10.7 %collective-permute-start.23 = (bf16[272,768]{1,0:T(8,128)(2,1)S(1)}, bf16[272,768]{1,0:T(8,128)(2,1)S(1)}, u32[]{:S(2)}, u32[]{:S(2)}) collective-permute-start(bf16[272,768]{1,0:T(8,128)(2,1)S(1)} %collective-permute-done.4.refs_8_), channel_id=1, source_target_pairs={{0,2},{2,0},{4,6},{6,4},{8,10},{10,8},{12,14},{14,12},{16,18},{18,... | collective-permute-start | bytes 1253384 | tf_op jit(solution)/shard_map/ppermute | solution.py:330
  82.0 25.9 %collective-permute-start.15 = (bf16[1024,256]{1,0:T(8,128)(2,1)S(1)}, bf16[1024,256]{1,0:T(8,128)(2,1)S(1)}, u32[]{:S(2)}, u32[]{:S(2)}) collective-permute-start(bf16[1024,256]{1,0:T(8,128)(2,1)S(1)} %copy-done), channel_id=1, source_target_pairs={{0,16},{2,18},{4,20},{6,22},{8,24},{10,26},{12,28},{14,30},{16,0},... | collective-permute-start | bytes 1572872 | tf_op jit(solution)/shard_map/ppermute | solution.py:319
  83.0 24.9 %collective-permute-start.18 = (bf16[1024,256]{1,0:T(8,128)(2,1)S(1)}, bf16[1024,256]{1,0:T(8,128)(2,1)S(1)}, u32[]{:S(2)}, u32[]{:S(2)}) collective-permute-start(bf16[1024,256]{1,0:T(8,128)(2,1)S(1)} %collective-permute-done.17.refs_8_.refs_10_), channel_id=1, source_target_pairs={{0,4},{2,6},{4,0},{6,2},{8,12},{10,14},{12,8},{14,10},{16,20},{18,... | collective-permute-start | bytes 1572872 | tf_op jit(solution)/shard_map/ppermute | solution.py:327
  83.5 22.0 %collective-permute-start.16 = (bf16[272,768]{1,0:T(8,128)(2,1)S(1)}, bf16[272,768]{1,0:T(8,128)(2,1)S(1)}, u32[]{:S(2)}, u32[]{:S(2)}) collective-permute-start(bf16[272,768]{1,0:T(8,128)(2,1)S(1)} %collective-permute-done.13.refs_4_), channel_id=1, source_target_pairs={{0,4},{2,6},{4,0},{6,2},{8,12},{10,14},{12,8},{14,10},{16,20},{18,... | collective-permute-start | bytes 1253384 | tf_op jit(solution)/shard_map/ppermute | solution.py:327
  85.0 23.7 %collective-permute-start.14 = (bf16[272,768]{1,0:T(8,128)(2,1)S(1)}, bf16[272,768]{1,0:T(8,128)(2,1)S(1)}, u32[]{:S(2)}, u32[]{:S(2)}) collective-permute-start(bf16[272,768]{1,0:T(8,128)(2,1)S(1)} %collective-permute-done.13.refs_4_), channel_id=1, source_target_pairs={{0,2},{2,0},{4,6},{6,4},{8,10},{10,8},{12,14},{14,12},{16,18},{18,... | collective-permute-start | bytes 1253384 | tf_op jit(solution)/shard_map/ppermute | solution.py:330
  108.0 14.3 %collective-permute-start.29 = (bf16[1024,256]{1,0:T(8,128)(2,1)S(1)}, bf16[1024,256]{1,0:T(8,128)(2,1)S(1)}, u32[]{:S(2)}, u32[]{:S(2)}) collective-permute-start(bf16[1024,256]{1,0:T(8,128)(2,1)S(1)} %collective-permute-done.15.refs_10_.refs_12_), channel_id=1, source_target_pairs={{0,8},{2,10},{4,12},{6,14},{8,0},{10,2},{12,4},{14,6},{16,24},{18,... | collective-permute-start | bytes 1572872 | tf_op jit(solution)/shard_map/ppermute | solution.py:319
  108.0 14.3 %collective-permute-start.30 = (bf16[1024,256]{1,0:T(8,128)(2,1)S(1)}, bf16[1024,256]{1,0:T(8,128)(2,1)S(1)}, u32[]{:S(2)}, u32[]{:S(2)}) collective-permute-start(bf16[1024,256]{1,0:T(8,128)(2,1)S(1)} %collective-permute-done.15.refs_10_.refs_12_), channel_id=1, source_target_pairs={{2,6},{6,2},{10,14},{14,10},{18,22},{22,18},{26,30},{30,26},{3,7},... | collective-permute-start | bytes 1572872 | tf_op jit(solution)/shard_map/ppermute | solution.py:327
  116.8 19.9 %collective-permute-start.32 = (bf16[1024,256]{1,0:T(8,128)(2,1)S(1)}, bf16[1024,256]{1,0:T(8,128)(2,1)S(1)}, u32[]{:S(2)}, u32[]{:S(2)}) collective-permute-start(bf16[1024,256]{1,0:T(8,128)(2,1)S(1)} %collective-permute-done.15.refs_10_.refs_12_), channel_id=1, source_target_pairs={{0,4},{4,0},{8,12},{12,8},{16,20},{20,16},{24,28},{28,24},{1,5},{5... | collective-permute-start | bytes 1572872 | tf_op jit(solution)/shard_map/ppermute | solution.py:327
  124.2 16.9 %collective-permute-start.42 = (bf16[1024,256]{1,0:T(8,128)(2,1)S(1)}, bf16[1024,256]{1,0:T(8,128)(2,1)S(1)}, u32[]{:S(2)}, u32[]{:S(2)}) collective-permute-start(bf16[1024,256]{1,0:T(8,128)(2,1)S(1)} %collective-permute-done.29.refs_10_.refs_15_), channel_id=1, source_target_pairs={{0,4},{2,6},{4,0},{6,2},{8,12},{10,14},{12,8},{14,10},{16,20},{18,... | collective-permute-start | bytes 1572872 | tf_op jit(solution)/shard_map/ppermute | solution.py:327
  (33 other events, 225.1 us)

commit v10 on v9

--- a/solution.py
+++ b/solution.py
@@ -399,6 +399,7 @@
         (at, decay[0], seg_len, w_query, w_key, w_value),
         [shape((w_rows + META, cn * 3 * DH))] * zn,
         scalars=3,
+        room=60,
     )
     packs[0] = sent[0]
     begin_x(0)

time: 156 us -> 156 us (level)
  local copies, waits for them, and re-layouts: 3.79 us -> 0.03 us
  Pallas kernels: 21.8 us -> 24.3 us
    unnamed x18 -> x16, local copies, waits for them, and re-layouts: 3.79 us -> 0.03 us
    pallas_call x14, Pallas kernels: 21.8 us -> 24.3 us  [call(): pl.pallas_call(kernel, grid_spec=pltpu.PrefetchScalarGridSpec(num_scalar_...]
  transfers between devices with their start and end apart: 48 -> 48, of which waited for: 26 -> 26; matrix products, arithmetic and copies ran while one was open for 0% -> 0% of each run, Pallas kernels for 13% -> 15%
where the time goes in v10:
time: 156 us
  waiting for transfers between devices  82.9 us (53%)
  starting transfers between devices  47 us (30%)
  Pallas kernels  24.3 us (16%)
    ppermute x12, waiting for transfers between devices, over_z(): return lax.ppermute(a, 'seq', pairs)  42 us
    ppermute x10, waiting for transfers between devices, over_x(): return lax.ppermute(a, 'seq', pairs)  29.7 us
    pallas_call x14, Pallas kernels, call(): pl.pallas_call(kernel, grid_spec=pltpu.PrefetchScalarGridSpec(num_scalar_...  24.3 us
    ppermute x12, starting transfers between devices, over_z(): return lax.ppermute(a, 'seq', pairs)  20.1 us
    ppermute x10, starting transfers between devices, over_x(): return lax.ppermute(a, 'seq', pairs)  12.8 us
    ppermute x8, starting transfers between devices, over_y(): lax.ppermute(a, 'head', [(h, (h + k) % n_head) for h in range(n_head)])  9.82 us
    ppermute x8, waiting for transfers between devices, over_y(): lax.ppermute(a, 'head', [(h, (h + k) % n_head) for h in range(n_head)])  7.66 us
    ppermute x18, starting transfers between devices, over_c(): return lax.ppermute(a, 'seq', [(s, s ^ m) for s in range(n_seq)])  4.2 us
  transfers between devices with their start and end apart: 48, of which 26 were waited for; matrix products, arithmetic and copies ran while one was open for 0% of the time, Pallas kernels for 15%

profile of v10, /device:TPU:0, one launch (start us, length us, event | category | flops | bytes accessed | tf_op | source)
XLA Modules:
  0.0 155.7 jit_solution(17648188301673012875)
XLA Ops:
  0.0 3.1 %collective-permute-start = (bf16[128,2048]{1,0:T(8,128)(2,1)}, bf16[128,2048]{1,0:T(8,128)(2,1)S(1)}, u32[]{:S(2)}, u32[]{:S(2)}) collective-permute-start(bf16[128,2048]{1,0:T(8,128)(2,1)} %refs_0_.3), channel_id=1, source_target_pairs={{0,8},{2,10},{4,12},{6,14},{8,0},{10,2},{12,4},{14,6},{16,24},{18,... | collective-permute-start | bytes 1572872 | tf_op jit(solution)/shard_map/ppermute | solution.py:319
  3.1 2.6 %collective-permute-start.1 = (bf16[128,2048]{1,0:T(8,128)(2,1)}, bf16[128,2048]{1,0:T(8,128)(2,1)S(1)}, u32[]{:S(2)}, u32[]{:S(2)}) collective-permute-start(bf16[128,2048]{1,0:T(8,128)(2,1)} %refs_0_.3), channel_id=1, source_target_pairs={{0,16},{2,18},{4,20},{6,22},{8,24},{10,26},{12,28},{14,30},{16,0},... | collective-permute-start | bytes 1572872 | tf_op jit(solution)/shard_map/ppermute | solution.py:319
  8.5 3.5 %shard_map.100 = (bf16[272,768]{1,0:T(8,128)(2,1)}, bf16[272,768]{1,0:T(8,128)(2,1)}, bf16[272,768]{1,0:T(8,128)(2,1)}, bf16[272,768]{1,0:T(8,128)(2,1)}) custom-call(s32[4]{0:T(128)} %pad_add_fusion.at, f32[8]{0:T(128)} %bitcast.10, s32[1]{0:T(128)S(6)} %copy.11.seg_len, bf16[256,1024]{1,0:T(8,128)(2,1)} %refs_0_.2, bf16[256,1024]{1,0:T(8,128)(2,1)} %refs_1_.1, ...), custom_call_target="tpu_custom_call" | custom-call | bytes 3244084 | tf_op jit(solution)/shard_map/pallas_call | solution.py:34
  13.5 9.3 %collective-permute-done.3.refs_14_ = bf16[272,768]{1,0:T(8,128)(2,1)S(1)} collective-permute-done((bf16[272,768]{1,0:T(8,128)(2,1)}, bf16[272,768]{1,0:T(8,128)(2,1)S(1)}, u32[]{:S(2)}, u32[]{:S(2)}) %collective-permute-start.3) | collective-permute-done | bytes 417824 | tf_op jit(solution)/shard_map/ppermute | solution.py:327
  23.2 4.0 %collective-permute-done.refs_0_ = bf16[128,2048]{1,0:T(8,128)(2,1)S(1)} collective-permute-done((bf16[128,2048]{1,0:T(8,128)(2,1)}, bf16[128,2048]{1,0:T(8,128)(2,1)S(1)}, u32[]{:S(2)}, u32[]{:S(2)}) %collective-permute-start) | collective-permute-done | bytes 524320 | tf_op jit(solution)/shard_map/ppermute | solution.py:319
  29.5 2.5 %collective-permute-start.6 = (bf16[128,2048]{1,0:T(8,128)(2,1)S(1)}, bf16[128,2048]{1,0:T(8,128)(2,1)S(1)}, u32[]{:S(2)}, u32[]{:S(2)}) collective-permute-start(bf16[128,2048]{1,0:T(8,128)(2,1)S(1)} %collective-permute-done.1.refs_0_), channel_id=1, source_target_pairs={{0,8},{2,10},{4,12},{6,14},{8,0},{10,2},{12,4},{14,6},{16,24},{18,... | collective-permute-start | bytes 1572872 | tf_op jit(solution)/shard_map/ppermute | solution.py:319
  33.5 2.7 %collective-permute-done.4.refs_8_ = bf16[272,768]{1,0:T(8,128)(2,1)S(1)} collective-permute-done((bf16[272,768]{1,0:T(8,128)(2,1)}, bf16[272,768]{1,0:T(8,128)(2,1)S(1)}, u32[]{:S(2)}, u32[]{:S(2)}) %collective-permute-start.4) | collective-permute-done | bytes 417824 | tf_op jit(solution)/shard_map/ppermute | solution.py:319
  38.3 2.6 %collective-permute-start.5 = (bf16[272,768]{1,0:T(8,128)(2,1)}, bf16[272,768]{1,0:T(8,128)(2,1)S(1)}, u32[]{:S(2)}, u32[]{:S(2)}) collective-permute-start(bf16[272,768]{1,0:T(8,128)(2,1)} %get-tuple-element.81), channel_id=1, source_target_pairs={{0,16},{2,18},{4,20},{6,22},{8,24},{10,26},{12,28},{14,30},{16,0},... | collective-permute-start | bytes 1253384 | tf_op jit(solution)/shard_map/ppermute | solution.py:319
  42.3 12.8 %collective-permute-done.5.refs_4_ = bf16[272,768]{1,0:T(8,128)(2,1)S(1)} collective-permute-done((bf16[272,768]{1,0:T(8,128)(2,1)}, bf16[272,768]{1,0:T(8,128)(2,1)S(1)}, u32[]{:S(2)}, u32[]{:S(2)}) %collective-permute-start.5) | collective-permute-done | bytes 417824 | tf_op jit(solution)/shard_map/ppermute | solution.py:319
  58.5 3.2 %collective-permute-start.13 = (bf16[272,768]{1,0:T(8,128)(2,1)S(1)}, bf16[272,768]{1,0:T(8,128)(2,1)S(1)}, u32[]{:S(2)}, u32[]{:S(2)}) collective-permute-start(bf16[272,768]{1,0:T(8,128)(2,1)S(1)} %copy-done.7), channel_id=1, source_target_pairs={{0,24},{2,26},{4,28},{6,30},{8,16},{10,18},{12,20},{14,22},{16,8},... | collective-permute-start | bytes 1253384 | tf_op jit(solution)/shard_map/ppermute | solution.py:319
  65.7 7.1 %collective-permute-done.13.refs_4_ = bf16[272,768]{1,0:T(8,128)(2,1)S(1)} collective-permute-done((bf16[272,768]{1,0:T(8,128)(2,1)S(1)}, bf16[272,768]{1,0:T(8,128)(2,1)S(1)}, u32[]{:S(2)}, u32[]{:S(2)}) %collective-permute-start.13) | collective-permute-done | bytes 417824 | tf_op jit(solution)/shard_map/ppermute | solution.py:319
  74.3 7.0 %collective-permute-done.17.refs_8_.refs_10_ = bf16[1024,256]{1,0:T(8,128)(2,1)S(1)} collective-permute-done((bf16[1024,256]{1,0:T(8,128)(2,1)S(1)}, bf16[1024,256]{1,0:T(8,128)(2,1)S(1)}, u32[]{:S(2)}, u32[]{:S(2)}) %collective-permute-start.17) | collective-permute-done | bytes 524320 | tf_op jit(solution)/shard_map/ppermute | solution.py:319
  85.1 3.4 %shard_map.105 = (f32[4,128,768]{2,1,0:T(8,128)S(1)}, f32[3,2,2,16,128]{4,3,2,1,0:T(8,128)S(1)}) custom-call(s32[4]{0:T(128)S(1)} %copy-done.5, bf16[128,4096]{1,0:T(8,128)(2,1)S(1)} %shard_map.101.refs_0_, bf16[128,4096]{1,0:T(8,128)(2,1)S(1)} %shard_map.102.refs_1_, bf16[128,4096]{1,0:T(8,128)(2,1)S(1)} %shard_map.103.refs_2_, ...), custom_call_target="tpu_custom_call" | custom-call | flops 2415919104 | bytes 10878992 | tf_op jit(solution)/shard_map/pallas_call | solution.py:34
  88.5 17.0 %collective-permute-done.16.refs_6_ = bf16[272,768]{1,0:T(8,128)(2,1)S(1)} collective-permute-done((bf16[272,768]{1,0:T(8,128)(2,1)S(1)}, bf16[272,768]{1,0:T(8,128)(2,1)S(1)}, u32[]{:S(2)}, u32[]{:S(2)}) %collective-permute-start.16) | collective-permute-done | bytes 417824 | tf_op jit(solution)/shard_map/ppermute | solution.py:327
  105.6 2.2 %collective-permute-done.15.refs_10_.refs_12_ = bf16[1024,256]{1,0:T(8,128)(2,1)S(1)} collective-permute-done((bf16[1024,256]{1,0:T(8,128)(2,1)S(1)}, bf16[1024,256]{1,0:T(8,128)(2,1)S(1)}, u32[]{:S(2)}, u32[]{:S(2)}) %collective-permute-start.15) | collective-permute-done | bytes 524320 | tf_op jit(solution)/shard_map/ppermute | solution.py:319
  116.6 3.1 %collective-permute-start.32 = (bf16[1024,256]{1,0:T(8,128)(2,1)S(1)}, bf16[1024,256]{1,0:T(8,128)(2,1)S(1)}, u32[]{:S(2)}, u32[]{:S(2)}) collective-permute-start(bf16[1024,256]{1,0:T(8,128)(2,1)S(1)} %collective-permute-done.15.refs_10_.refs_12_), channel_id=1, source_target_pairs={{0,4},{4,0},{8,12},{12,8},{16,20},{20,16},{24,28},{28,24},{1,5},{5... | collective-permute-start | bytes 1572872 | tf_op jit(solution)/shard_map/ppermute | solution.py:327
  122.2 2.1 %collective-permute-done.28.refs_0_ = bf16[4,128,256]{2,1,0:T(8,128)(2,1)S(1)} collective-permute-done((bf16[4,128,256]{2,1,0:T(8,128)(2,1)S(1)}, bf16[4,128,256]{2,1,0:T(8,128)(2,1)S(1)}, u32[]{:S(2)}, u32[]{:S(2)}) %collective-permute-start.28) | collective-permute-done | bytes 262176 | tf_op jit(solution)/shard_map/ppermute | solution.py:327
  125.2 2.2 %shard_map.109 = (bf16[2,128,128]{2,1,0:T(8,128)(2,1)S(1)}, bf16[2,128,128]{2,1,0:T(8,128)(2,1)S(1)}, bf16[2,128,128]{2,1,0:T(8,128)(2,1)S(1)}, bf16[2,128,128]{2,1,0:T(8,128)(2,1)S(1)}) custom-call(s32[4]{0:T(128)S(1)} %copy-done.5, f32[8]{0:T(128)S(1)} %copy-done.6, f32[4,2,2,16,128]{4,3,2,1,0:T(8,128)S(1)} %get-tuple-element.116.table, ...), custom_call_target="tpu_custom_call" | custom-call | bytes 3538992 | tf_op jit(solution)/shard_map/pallas_call | solution.py:34
  127.4 2.2 %collective-permute-start.35 = (bf16[2,128,128]{2,1,0:T(8,128)(2,1)S(1)}, bf16[2,128,128]{2,1,0:T(8,128)(2,1)S(1)}, u32[]{:S(2)}, u32[]{:S(2)}) collective-permute-start(bf16[2,128,128]{2,1,0:T(8,128)(2,1)S(1)} %get-tuple-element.126), channel_id=1, source_target_pairs={{0,24},{2,26},{4,28},{6,30},{8,16},{10,18},{12,20},{14,22},{16,8},... | collective-permute-start | bytes 196616 | tf_op jit(solution)/shard_map/ppermute | solution.py:319
  131.9 2.3 %collective-permute-done.35.refs_6_ = bf16[2,128,128]{2,1,0:T(8,128)(2,1)S(1)} collective-permute-done((bf16[2,128,128]{2,1,0:T(8,128)(2,1)S(1)}, bf16[2,128,128]{2,1,0:T(8,128)(2,1)S(1)}, u32[]{:S(2)}, u32[]{:S(2)}) %collective-permute-start.35) | collective-permute-done | bytes 65568 | tf_op jit(solution)/shard_map/ppermute | solution.py:319
  134.2 2.0 %collective-permute-done.34.refs_4_ = bf16[2,128,128]{2,1,0:T(8,128)(2,1)S(1)} collective-permute-done((bf16[2,128,128]{2,1,0:T(8,128)(2,1)S(1)}, bf16[2,128,128]{2,1,0:T(8,128)(2,1)S(1)}, u32[]{:S(2)}, u32[]{:S(2)}) %collective-permute-start.34) | collective-permute-done | bytes 65568 | tf_op jit(solution)/shard_map/ppermute | solution.py:319
  143.3 2.0 %shard_map.112 = (bf16[2,128,256]{2,1,0:T(8,128)(2,1)S(1)}, bf16[2,128,256]{2,1,0:T(8,128)(2,1)S(1)}, bf16[2,128,256]{2,1,0:T(8,128)(2,1)S(1)}, bf16[2,128,256]{2,1,0:T(8,128)(2,1)S(1)}) custom-call(s32[4]{0:T(128)S(1)} %copy-done.5, bf16[2,128,128]{2,1,0:T(8,128)(2,1)S(1)} %get-tuple-element.123.refs_0_, ...), custom_call_target="tpu_custom_call" | custom-call | flops 1073741824 | bytes 5767184 | tf_op jit(solution)/shard_map/pallas_call | solution.py:34
  148.5 3.8 %collective-permute-done.43.refs_2_ = bf16[2,128,256]{2,1,0:T(8,128)(2,1)S(1)} collective-permute-done((bf16[2,128,256]{2,1,0:T(8,128)(2,1)S(1)}, bf16[2,128,256]{2,1,0:T(8,128)(2,1)S(1)}, u32[]{:S(2)}, u32[]{:S(2)}) %collective-permute-start.43) | collective-permute-done | bytes 131104 | tf_op jit(solution)/shard_map/ppermute | solution.py:333
  152.2 2.0 %collective-permute-done.45.refs_3_ = bf16[2,128,256]{2,1,0:T(8,128)(2,1)S(1)} collective-permute-done((bf16[2,128,256]{2,1,0:T(8,128)(2,1)S(1)}, bf16[2,128,256]{2,1,0:T(8,128)(2,1)S(1)}, u32[]{:S(2)}, u32[]{:S(2)}) %collective-permute-start.45) | collective-permute-done | bytes 131104 | tf_op jit(solution)/shard_map/ppermute | solution.py:333
  (103 shorter events, 50.1 us)
Async XLA Ops:
  0.0 27.2 %collective-permute-start = (bf16[128,2048]{1,0:T(8,128)(2,1)}, bf16[128,2048]{1,0:T(8,128)(2,1)S(1)}, u32[]{:S(2)}, u32[]{:S(2)}) collective-permute-start(bf16[128,2048]{1,0:T(8,128)(2,1)} %refs_0_.3), channel_id=1, source_target_pairs={{0,8},{2,10},{4,12},{6,14},{8,0},{10,2},{12,4},{14,6},{16,24},{18,... | collective-permute-start | bytes 1572872 | tf_op jit(solution)/shard_map/ppermute | solution.py:319
  3.1 24.8 %collective-permute-start.1 = (bf16[128,2048]{1,0:T(8,128)(2,1)}, bf16[128,2048]{1,0:T(8,128)(2,1)S(1)}, u32[]{:S(2)}, u32[]{:S(2)}) collective-permute-start(bf16[128,2048]{1,0:T(8,128)(2,1)} %refs_0_.3), channel_id=1, source_target_pairs={{0,16},{2,18},{4,20},{6,22},{8,24},{10,26},{12,28},{14,30},{16,0},... | collective-permute-start | bytes 1572872 | tf_op jit(solution)/shard_map/ppermute | solution.py:319
  5.7 22.2 %collective-permute-start.2 = (bf16[128,2048]{1,0:T(8,128)(2,1)}, bf16[128,2048]{1,0:T(8,128)(2,1)S(1)}, u32[]{:S(2)}, u32[]{:S(2)}) collective-permute-start(bf16[128,2048]{1,0:T(8,128)(2,1)} %refs_0_.3), channel_id=1, source_target_pairs={{0,1},{1,0},{2,3},{3,2},{4,5},{5,4},{6,7},{7,6},{8,9},{9,8},{10,11... | collective-permute-start | bytes 1572872 | tf_op jit(solution)/shard_map/ppermute | solution.py:333
  12.0 10.8 %collective-permute-start.3 = (bf16[272,768]{1,0:T(8,128)(2,1)}, bf16[272,768]{1,0:T(8,128)(2,1)S(1)}, u32[]{:S(2)}, u32[]{:S(2)}) collective-permute-start(bf16[272,768]{1,0:T(8,128)(2,1)} %get-tuple-element.100.refs_12_), channel_id=1, source_target_pairs={{0,4},{2,6},{4,0},{6,2},{8,12},{10,14},{12,8},{14,10},{16,20},{18,... | collective-permute-start | bytes 1253384 | tf_op jit(solution)/shard_map/ppermute | solution.py:327
  13.5 18.5 %collective-permute-start.10 = (bf16[272,768]{1,0:T(8,128)(2,1)}, bf16[272,768]{1,0:T(8,128)(2,1)S(1)}, u32[]{:S(2)}, u32[]{:S(2)}) collective-permute-start(bf16[272,768]{1,0:T(8,128)(2,1)} %get-tuple-element.100.refs_12_), channel_id=1, source_target_pairs={{0,2},{2,0},{4,6},{6,4},{8,10},{10,8},{12,14},{14,12},{16,18},{18,... | collective-permute-start | bytes 1253384 | tf_op jit(solution)/shard_map/ppermute | solution.py:330
  22.7 13.5 %collective-permute-start.4 = (bf16[272,768]{1,0:T(8,128)(2,1)}, bf16[272,768]{1,0:T(8,128)(2,1)S(1)}, u32[]{:S(2)}, u32[]{:S(2)}) collective-permute-start(bf16[272,768]{1,0:T(8,128)(2,1)} %get-tuple-element.79), channel_id=1, source_target_pairs={{0,8},{2,10},{4,12},{6,14},{8,0},{10,2},{12,4},{14,6},{16,24},{18,... | collective-permute-start | bytes 1253384 | tf_op jit(solution)/shard_map/ppermute | solution.py:319
  27.9 14.3 %collective-permute-start.7 = (bf16[1024,256]{1,0:T(8,128)(2,1)S(1)}, bf16[1024,256]{1,0:T(8,128)(2,1)S(1)}, u32[]{:S(2)}, u32[]{:S(2)}) collective-permute-start(bf16[1024,256]{1,0:T(8,128)(2,1)S(1)} %copy-done), channel_id=1, source_target_pairs={{0,4},{2,6},{4,0},{6,2},{8,12},{10,14},{12,8},{14,10},{16,20},{18,... | collective-permute-start | bytes 1572872 | tf_op jit(solution)/shard_map/ppermute | solution.py:327
  29.5 26.1 %collective-permute-start.6 = (bf16[128,2048]{1,0:T(8,128)(2,1)S(1)}, bf16[128,2048]{1,0:T(8,128)(2,1)S(1)}, u32[]{:S(2)}, u32[]{:S(2)}) collective-permute-start(bf16[128,2048]{1,0:T(8,128)(2,1)S(1)} %collective-permute-done.1.refs_0_), channel_id=1, source_target_pairs={{0,8},{2,10},{4,12},{6,14},{8,0},{10,2},{12,4},{14,6},{16,24},{18,... | collective-permute-start | bytes 1572872 | tf_op jit(solution)/shard_map/ppermute | solution.py:319
  32.0 23.6 %collective-permute-start.8 = (bf16[128,2048]{1,0:T(8,128)(2,1)S(1)}, bf16[128,2048]{1,0:T(8,128)(2,1)S(1)}, u32[]{:S(2)}, u32[]{:S(2)}) collective-permute-start(bf16[128,2048]{1,0:T(8,128)(2,1)S(1)} %collective-permute-done.refs_0_), channel_id=1, source_target_pairs={{0,1},{1,0},{2,3},{3,2},{4,5},{5,4},{6,7},{7,6},{8,9},{9,8},{10,11... | collective-permute-start | bytes 1572872 | tf_op jit(solution)/shard_map/ppermute | solution.py:333
  36.2 20.7 %collective-permute-start.9 = (bf16[128,2048]{1,0:T(8,128)(2,1)S(1)}, bf16[128,2048]{1,0:T(8,128)(2,1)S(1)}, u32[]{:S(2)}, u32[]{:S(2)}) collective-permute-start(bf16[128,2048]{1,0:T(8,128)(2,1)S(1)} %collective-permute-done.1.refs_0_), channel_id=1, source_target_pairs={{0,1},{1,0},{2,3},{3,2},{4,5},{5,4},{6,7},{7,6},{8,9},{9,8},{10,11... | collective-permute-start | bytes 1572872 | tf_op jit(solution)/shard_map/ppermute | solution.py:333
  38.3 16.8 %collective-permute-start.5 = (bf16[272,768]{1,0:T(8,128)(2,1)}, bf16[272,768]{1,0:T(8,128)(2,1)S(1)}, u32[]{:S(2)}, u32[]{:S(2)}) collective-permute-start(bf16[272,768]{1,0:T(8,128)(2,1)} %get-tuple-element.81), channel_id=1, source_target_pairs={{0,16},{2,18},{4,20},{6,22},{8,24},{10,26},{12,28},{14,30},{16,0},... | collective-permute-start | bytes 1253384 | tf_op jit(solution)/shard_map/ppermute | solution.py:319
  56.9 15.9 %collective-permute-start.12 = (bf16[128,2048]{1,0:T(8,128)(2,1)S(1)}, bf16[128,2048]{1,0:T(8,128)(2,1)S(1)}, u32[]{:S(2)}, u32[]{:S(2)}) collective-permute-start(bf16[128,2048]{1,0:T(8,128)(2,1)S(1)} %collective-permute-done.6.refs_0_), channel_id=1, source_target_pairs={{0,1},{1,0},{2,3},{3,2},{4,5},{5,4},{6,7},{7,6},{8,9},{9,8},{10,11... | collective-permute-start | bytes 1572872 | tf_op jit(solution)/shard_map/ppermute | solution.py:333
  58.5 14.4 %collective-permute-start.13 = (bf16[272,768]{1,0:T(8,128)(2,1)S(1)}, bf16[272,768]{1,0:T(8,128)(2,1)S(1)}, u32[]{:S(2)}, u32[]{:S(2)}) collective-permute-start(bf16[272,768]{1,0:T(8,128)(2,1)S(1)} %copy-done.7), channel_id=1, source_target_pairs={{0,24},{2,26},{4,28},{6,30},{8,16},{10,18},{12,20},{14,22},{16,8},... | collective-permute-start | bytes 1253384 | tf_op jit(solution)/shard_map/ppermute | solution.py:319
  61.7 19.7 %collective-permute-start.17 = (bf16[1024,256]{1,0:T(8,128)(2,1)S(1)}, bf16[1024,256]{1,0:T(8,128)(2,1)S(1)}, u32[]{:S(2)}, u32[]{:S(2)}) collective-permute-start(bf16[1024,256]{1,0:T(8,128)(2,1)S(1)} %copy-done), channel_id=1, source_target_pairs={{0,8},{2,10},{4,12},{6,14},{8,0},{10,2},{12,4},{14,6},{16,24},{18,... | collective-permute-start | bytes 1572872 | tf_op jit(solution)/shard_map/ppermute | solution.py:319
  62.6 18.7 %collective-permute-start.21 = (bf16[272,768]{1,0:T(8,128)(2,1)S(1)}, bf16[272,768]{1,0:T(8,128)(2,1)S(1)}, u32[]{:S(2)}, u32[]{:S(2)}) collective-permute-start(bf16[272,768]{1,0:T(8,128)(2,1)S(1)} %collective-permute-done.4.refs_8_), channel_id=1, source_target_pairs={{0,4},{2,6},{4,0},{6,2},{8,12},{10,14},{12,8},{14,10},{16,20},{18,... | collective-permute-start | bytes 1253384 | tf_op jit(solution)/shard_map/ppermute | solution.py:327
  65.1 16.2 %collective-permute-start.20 = (bf16[272,768]{1,0:T(8,128)(2,1)S(1)}, bf16[272,768]{1,0:T(8,128)(2,1)S(1)}, u32[]{:S(2)}, u32[]{:S(2)}) collective-permute-start(bf16[272,768]{1,0:T(8,128)(2,1)S(1)} %collective-permute-done.5.refs_4_), channel_id=1, source_target_pairs={{0,4},{2,6},{4,0},{6,2},{8,12},{10,14},{12,8},{14,10},{16,20},{18,... | collective-permute-start | bytes 1253384 | tf_op jit(solution)/shard_map/ppermute | solution.py:327
  81.9 25.9 %collective-permute-start.15 = (bf16[1024,256]{1,0:T(8,128)(2,1)S(1)}, bf16[1024,256]{1,0:T(8,128)(2,1)S(1)}, u32[]{:S(2)}, u32[]{:S(2)}) collective-permute-start(bf16[1024,256]{1,0:T(8,128)(2,1)S(1)} %copy-done), channel_id=1, source_target_pairs={{0,16},{2,18},{4,20},{6,22},{8,24},{10,26},{12,28},{14,30},{16,0},... | collective-permute-start | bytes 1572872 | tf_op jit(solution)/shard_map/ppermute | solution.py:319
  83.0 24.7 %collective-permute-start.18 = (bf16[1024,256]{1,0:T(8,128)(2,1)S(1)}, bf16[1024,256]{1,0:T(8,128)(2,1)S(1)}, u32[]{:S(2)}, u32[]{:S(2)}) collective-permute-start(bf16[1024,256]{1,0:T(8,128)(2,1)S(1)} %collective-permute-done.17.refs_8_.refs_10_), channel_id=1, source_target_pairs={{0,4},{2,6},{4,0},{6,2},{8,12},{10,14},{12,8},{14,10},{16,20},{18,... | collective-permute-start | bytes 1572872 | tf_op jit(solution)/shard_map/ppermute | solution.py:327
  83.6 22.0 %collective-permute-start.16 = (bf16[272,768]{1,0:T(8,128)(2,1)S(1)}, bf16[272,768]{1,0:T(8,128)(2,1)S(1)}, u32[]{:S(2)}, u32[]{:S(2)}) collective-permute-start(bf16[272,768]{1,0:T(8,128)(2,1)S(1)} %collective-permute-done.13.refs_4_), channel_id=1, source_target_pairs={{0,4},{2,6},{4,0},{6,2},{8,12},{10,14},{12,8},{14,10},{16,20},{18,... | collective-permute-start | bytes 1253384 | tf_op jit(solution)/shard_map/ppermute | solution.py:327
  85.1 23.5 %collective-permute-start.14 = (bf16[272,768]{1,0:T(8,128)(2,1)S(1)}, bf16[272,768]{1,0:T(8,128)(2,1)S(1)}, u32[]{:S(2)}, u32[]{:S(2)}) collective-permute-start(bf16[272,768]{1,0:T(8,128)(2,1)S(1)} %collective-permute-done.13.refs_4_), channel_id=1, source_target_pairs={{0,2},{2,0},{4,6},{6,4},{8,10},{10,8},{12,14},{14,12},{16,18},{18,... | collective-permute-start | bytes 1253384 | tf_op jit(solution)/shard_map/ppermute | solution.py:330
  107.8 14.3 %collective-permute-start.29 = (bf16[1024,256]{1,0:T(8,128)(2,1)S(1)}, bf16[1024,256]{1,0:T(8,128)(2,1)S(1)}, u32[]{:S(2)}, u32[]{:S(2)}) collective-permute-start(bf16[1024,256]{1,0:T(8,128)(2,1)S(1)} %collective-permute-done.15.refs_10_.refs_12_), channel_id=1, source_target_pairs={{0,8},{2,10},{4,12},{6,14},{8,0},{10,2},{12,4},{14,6},{16,24},{18,... | collective-permute-start | bytes 1572872 | tf_op jit(solution)/shard_map/ppermute | solution.py:319
  107.9 14.3 %collective-permute-start.30 = (bf16[1024,256]{1,0:T(8,128)(2,1)S(1)}, bf16[1024,256]{1,0:T(8,128)(2,1)S(1)}, u32[]{:S(2)}, u32[]{:S(2)}) collective-permute-start(bf16[1024,256]{1,0:T(8,128)(2,1)S(1)} %collective-permute-done.15.refs_10_.refs_12_), channel_id=1, source_target_pairs={{2,6},{6,2},{10,14},{14,10},{18,22},{22,18},{26,30},{30,26},{3,7},... | collective-permute-start | bytes 1572872 | tf_op jit(solution)/shard_map/ppermute | solution.py:327
  116.6 20.1 %collective-permute-start.32 = (bf16[1024,256]{1,0:T(8,128)(2,1)S(1)}, bf16[1024,256]{1,0:T(8,128)(2,1)S(1)}, u32[]{:S(2)}, u32[]{:S(2)}) collective-permute-start(bf16[1024,256]{1,0:T(8,128)(2,1)S(1)} %collective-permute-done.15.refs_10_.refs_12_), channel_id=1, source_target_pairs={{0,4},{4,0},{8,12},{12,8},{16,20},{20,16},{24,28},{28,24},{1,5},{5... | collective-permute-start | bytes 1572872 | tf_op jit(solution)/shard_map/ppermute | solution.py:327
  124.3 16.9 %collective-permute-start.42 = (bf16[1024,256]{1,0:T(8,128)(2,1)S(1)}, bf16[1024,256]{1,0:T(8,128)(2,1)S(1)}, u32[]{:S(2)}, u32[]{:S(2)}) collective-permute-start(bf16[1024,256]{1,0:T(8,128)(2,1)S(1)} %collective-permute-done.29.refs_10_.refs_15_), channel_id=1, source_target_pairs={{0,4},{2,6},{4,0},{6,2},{8,12},{10,14},{12,8},{14,10},{16,20},{18,... | collective-permute-start | bytes 1572872 | tf_op jit(solution)/shard_map/ppermute | solution.py:327
  (32 other events, 345.7 us)
